TPU v7x, 32 devices: a whole 2x2x4 slice. The times are simulated.
32 devices in a mesh: dp: 8 (over z, x), mp: 4 (over y, core).
Axes of the slice: x: 2, y: 2, z: 4, core: 2. Of those that a mesh axis runs over, the one named last changes fastest.
Arguments:
- char_input: bfloat16 [8192, 4096], P(('dp', 'mp')), may hold values from -6 to 6
- char_counts: int32 [8192], P(('dp', 'mp')), may hold values from 1 to 16, as said below
- word_source: int32 [8192], P(('dp', 'mp')), may hold values from 0 to 8191, as said below
- segment_ids: int32 [8192], P(('dp', 'mp')), may hold values from 0 to 4, as said below
- cotangent: bfloat16 [8192, 512], P(('dp', 'mp')), may hold values from -6 to 6
- char_norm_gains: bfloat16 [2, 256], replicated, may hold values from 0.099609375 to 1.8984375
- char_qkv: bfloat16 [256, 768], replicated, may hold values from -0.375 to 0.375
- char_out: bfloat16 [256, 256], replicated, may hold values from -0.75 to 0.75
- char_up: bfloat16 [256, 1024], replicated, may hold values from -0.375 to 0.375
- char_down: bfloat16 [1024, 256], replicated, may hold values from -0.1875 to 0.1875
- pool_vector: bfloat16 [256], replicated, may hold values from -0.375 to 0.375
- char_proj: bfloat16 [256, 512], replicated, may hold values from -0.375 to 0.375
- word_norm_gains: bfloat16 [2, 512], replicated, may hold values from 0.099609375 to 1.8984375
- word_qkv: bfloat16 [3, 512, 512], P(None, None, 'mp'), may hold values from -0.25 to 0.25
- word_out: bfloat16 [512, 512], P('mp'), may hold values from -3 to 3
- word_up: bfloat16 [512, 2048], P(None, 'mp'), may hold values from -0.25 to 0.25
- word_down: bfloat16 [2048, 512], P('mp'), may hold values from -0.125 to 0.125
Outputs:
- word_output: bfloat16 [8192, 512], P(('dp', 'mp'))
- char_input_grad: float32 [8192, 4096], P(('dp', 'mp'))
- grad_char_qkv: float32 [256, 768], P('dp', 'mp')
- grad_char_out: float32 [256, 256], P('dp', 'mp')
- grad_char_up: float32 [256, 1024], P('dp', 'mp')
- grad_char_down: float32 [1024, 256], P('dp', 'mp')
- grad_char_proj: float32 [256, 512], P('dp', 'mp')
- grad_word_qkv: float32 [3, 512, 512], P(None, 'dp', 'mp')
- grad_word_out: float32 [512, 512], P('mp', 'dp')
- grad_word_up: float32 [512, 2048], P('dp', 'mp')
- grad_word_down: float32 [2048, 512], P('mp', 'dp')
- grad_char_gains: float32 [2, 256], replicated
- grad_pool_vector: float32 [256], replicated
- grad_word_gains: float32 [2, 512], replicated
Inputs may be any that keep to these rules, and one draw needn't show every extreme that they name: `char_counts`: each word has 1 to 16 present character slots, the first ones; some word has all 16 in every draw. `word_source`: a permutation of the sequence-layout positions; a bucket row and the position it names stand at the same index of mp; at most 64 of the words held by one device belong to one sequence, and exactly 64 for some pair in every draw. `segment_ids`: each sequence holds five documents numbered 0 to 4 in order; document 2 begins at or before position 128 of its sequence and ends at or after position 895.
All inputs are finite; a program needn't handle non-finite values.
Results may differ from a plain program's by a relative error of at most 0.022.
The roundings to bfloat16 on the way count: a program that leaves them out, or rounds other values in their place, can miss the bound.
Values may be sent and summed in bfloat16 or wider, within the bound.
A program may use at most 256 MiB of HBM per device.

v0:
```python
from functools import partial

import jax
import jax.numpy as jnp
from jax import lax
from jax.sharding import PartitionSpec as P

HEADS = 8
CHAR_HEADS = 4
CHARS = 16


EPSILON = 1e-05
NEGATIVE = -1e30


def norm_rows(values, gain_vec):
    row_mean = jnp.mean(values, -1, keepdims=True)
    centered = values - row_mean
    variance = jnp.mean(centered * centered, -1, keepdims=True)
    return centered * lax.rsqrt(variance + EPSILON) * gain_vec


def pool_words(final_rows, pool_vec, present):
    pool_scores = jnp.sum(final_rows * pool_vec, -1)
    pool_scores = jnp.where(present, pool_scores, NEGATIVE)
    pool_weights = jax.nn.softmax(pool_scores, axis=-1)
    return jnp.sum(pool_weights[..., None] * final_rows, 1)


def flat_dot(left, right):
    return jnp.dot(left, right, preferred_element_type=jnp.float32)


def inner_dot(left, right):
    return lax.dot_general(
        left, right, (((0,), (0,)), ((), ())), preferred_element_type=jnp.float32
    )


def outer_dot(left, right):
    return lax.dot_general(
        left, right, (((1,), (1,)), ((), ())), preferred_element_type=jnp.float32
    )


def gather_rows(rows_in):
    return lax.all_gather(rows_in, "mp", axis=0, tiled=True)


def sum_rows(partial_rows):
    return lax.psum_scatter(partial_rows, "mp", scatter_dimension=0, tiled=True)


def char_forward(chars_flat, present, char_weights):
    norm_gains, qkv_weight, out_weight, up_weight, down_weight, pool_weight, proj_weight = (
        char_weights
    )
    word_count = present.shape[0]
    char_width = chars_flat.shape[1]
    head_size = char_width // CHAR_HEADS
    scale_value = head_size ** (-0.5)
    normed = norm_rows(chars_flat, norm_gains[0].astype(jnp.float32)).astype(jnp.bfloat16)
    projected = (
        flat_dot(normed, qkv_weight)
        .astype(jnp.bfloat16)
        .reshape(word_count, CHARS, 3, CHAR_HEADS, head_size)
    )
    scores = (
        jnp.einsum(
            "wqhe,wkhe->whqk",
            projected[:, :, 0],
            projected[:, :, 1],
            preferred_element_type=jnp.float32,
        )
        * scale_value
    )
    scores = jnp.where(present[:, None, None, :], scores, NEGATIVE)
    softmaxed = jax.nn.softmax(scores, axis=-1)
    mixed_heads = jnp.einsum(
        "whqk,wkhe->wqhe",
        softmaxed.astype(jnp.bfloat16),
        projected[:, :, 2],
        preferred_element_type=jnp.float32,
    )
    mixed_heads = mixed_heads.astype(jnp.bfloat16).reshape(word_count * CHARS, char_width)
    middle = chars_flat + flat_dot(mixed_heads, out_weight)
    normed_two = norm_rows(middle, norm_gains[1].astype(jnp.float32)).astype(jnp.bfloat16)
    hidden = flat_dot(normed_two, up_weight)
    activated = jax.nn.gelu(hidden).astype(jnp.bfloat16)
    final_rows = (middle + flat_dot(activated, down_weight)).reshape(word_count, CHARS, char_width)
    pooled = pool_words(final_rows, pool_weight.astype(jnp.float32), present).astype(jnp.bfloat16)
    word_vec = flat_dot(pooled, proj_weight)
    char_kept = (
        normed,
        projected,
        softmaxed,
        mixed_heads,
        middle,
        normed_two,
        hidden,
        activated,
        final_rows,
        pooled,
    )
    return (word_vec, char_kept)


def char_backward(chars_flat, present, char_weights, char_kept, d_word):
    norm_gains, qkv_weight, out_weight, up_weight, down_weight, pool_weight, proj_weight = (
        char_weights
    )
    (
        normed,
        projected,
        softmaxed,
        mixed_heads,
        middle,
        normed_two,
        hidden,
        activated,
        final_rows,
        pooled,
    ) = char_kept
    word_count = present.shape[0]
    char_width = chars_flat.shape[1]
    head_size = char_width // CHAR_HEADS
    scale_value = head_size ** (-0.5)
    grad_proj = inner_dot(pooled, d_word)
    d_pooled = outer_dot(d_word, proj_weight)
    pool_vec = pool_weight.astype(jnp.float32)
    unused_pool, pool_back = jax.vjp(partial(pool_words, present=present), final_rows, pool_vec)
    d_final3, grad_pool = pool_back(d_pooled)
    d_final = d_final3.reshape(word_count * CHARS, char_width)
    d_branch = d_final.astype(jnp.bfloat16)
    grad_down = inner_dot(activated, d_branch)
    d_activated = outer_dot(d_branch, down_weight)
    unused_gelu, gelu_back = jax.vjp(jax.nn.gelu, hidden)
    d_hidden = gelu_back(d_activated)[0].astype(jnp.bfloat16)
    grad_up = inner_dot(normed_two, d_hidden)
    d_normed_two = outer_dot(d_hidden, up_weight)
    unused_second, norm_back_second = jax.vjp(norm_rows, middle, norm_gains[1].astype(jnp.float32))
    d_middle_norm, grad_gain_second = norm_back_second(d_normed_two)
    d_middle = d_final + d_middle_norm
    d_attended = d_middle.astype(jnp.bfloat16)
    grad_out = inner_dot(mixed_heads, d_attended)
    d_mixed = (
        outer_dot(d_attended, out_weight)
        .astype(jnp.bfloat16)
        .reshape(word_count, CHARS, CHAR_HEADS, head_size)
    )
    queries = projected[:, :, 0]
    keys_in = projected[:, :, 1]
    values_in = projected[:, :, 2]
    d_soft = jnp.einsum("wqhe,wkhe->whqk", d_mixed, values_in, preferred_element_type=jnp.float32)
    row_delta = jnp.sum(softmaxed * d_soft, -1, keepdims=True)
    d_scores = (softmaxed * (d_soft - row_delta)).astype(jnp.bfloat16)
    d_queries = (
        jnp.einsum("whqk,wkhe->wqhe", d_scores, keys_in, preferred_element_type=jnp.float32)
        * scale_value
    )
    d_keys = (
        jnp.einsum("whqk,wqhe->wkhe", d_scores, queries, preferred_element_type=jnp.float32)
        * scale_value
    )
    d_values = jnp.einsum(
        "whqk,wqhe->wkhe",
        softmaxed.astype(jnp.bfloat16),
        d_mixed,
        preferred_element_type=jnp.float32,
    )
    d_projected = (
        jnp.stack([d_queries, d_keys, d_values], 2)
        .astype(jnp.bfloat16)
        .reshape(word_count * CHARS, 3 * char_width)
    )
    grad_qkv = inner_dot(normed, d_projected)
    d_normed = outer_dot(d_projected, qkv_weight)
    unused_first, norm_back_first = jax.vjp(
        norm_rows, chars_flat, norm_gains[0].astype(jnp.float32)
    )
    d_chars_norm, grad_gain_first = norm_back_first(d_normed)
    d_chars = d_middle + d_chars_norm
    grad_gains = jnp.stack([grad_gain_first, grad_gain_second], 0)
    return (d_chars, (grad_qkv, grad_out, grad_up, grad_down, grad_proj), grad_gains, grad_pool)


def attention_scores(q_block, keys_in, segments, seg_block, block_start, block_rows, scale_value):
    places = jnp.arange(segments.shape[0])
    rows_here = block_start + jnp.arange(block_rows)
    allowed = (places[None, :] <= rows_here[:, None]) & (segments[None, :] == seg_block[:, None])
    scores = (
        jnp.einsum("qhe,khe->hqk", q_block, keys_in, preferred_element_type=jnp.float32)
        * scale_value
    )
    return jnp.where(allowed[None], scores, NEGATIVE)


def word_attention(queries, keys_in, values_in, segments, block_rows):
    length = queries.shape[0]
    scale_value = queries.shape[-1] ** (-0.5)

    def one_block(block_start):
        q_block = lax.dynamic_slice_in_dim(queries, block_start, block_rows, 0)
        seg_block = lax.dynamic_slice_in_dim(segments, block_start, block_rows, 0)
        scores = attention_scores(
            q_block, keys_in, segments, seg_block, block_start, block_rows, scale_value
        )
        row_top = jnp.max(scores, -1, keepdims=True)
        raw_weights = jnp.exp(scores - row_top)
        row_total = jnp.sum(raw_weights, -1, keepdims=True)
        softmaxed = (raw_weights / row_total).astype(jnp.bfloat16)
        result = jnp.einsum(
            "hqk,khe->qhe", softmaxed, values_in, preferred_element_type=jnp.float32
        )
        return (result, (row_top + jnp.log(row_total))[..., 0])

    starts = jnp.arange(length // block_rows) * block_rows
    results, log_totals = lax.map(one_block, starts)
    return (results.reshape(length, queries.shape[1], queries.shape[2]), log_totals)


def word_attention_back(queries, keys_in, values_in, segments, log_totals, d_mixed, block_rows):
    length = queries.shape[0]
    scale_value = queries.shape[-1] ** (-0.5)

    def one_block(sums_carry, block_inputs):
        d_keys, d_values = sums_carry
        block_start, log_block = block_inputs
        q_block = lax.dynamic_slice_in_dim(queries, block_start, block_rows, 0)
        seg_block = lax.dynamic_slice_in_dim(segments, block_start, block_rows, 0)
        d_block = lax.dynamic_slice_in_dim(d_mixed, block_start, block_rows, 0)
        scores = attention_scores(
            q_block, keys_in, segments, seg_block, block_start, block_rows, scale_value
        )
        softmaxed = jnp.exp(scores - log_block[..., None])
        d_soft = jnp.einsum("qhe,khe->hqk", d_block, values_in, preferred_element_type=jnp.float32)
        row_delta = jnp.sum(softmaxed * d_soft, -1, keepdims=True)
        d_scores = (softmaxed * (d_soft - row_delta)).astype(jnp.bfloat16)
        d_query_block = (
            jnp.einsum("hqk,khe->qhe", d_scores, keys_in, preferred_element_type=jnp.float32)
            * scale_value
        )
        d_keys = (
            d_keys
            + jnp.einsum("hqk,qhe->khe", d_scores, q_block, preferred_element_type=jnp.float32)
            * scale_value
        )
        d_values = d_values + jnp.einsum(
            "hqk,qhe->khe",
            softmaxed.astype(jnp.bfloat16),
            d_block,
            preferred_element_type=jnp.float32,
        )
        return ((d_keys, d_values), d_query_block)

    starts = jnp.arange(length // block_rows) * block_rows
    empty = jnp.zeros(keys_in.shape, jnp.float32)
    (d_keys, d_values), d_queries = lax.scan(one_block, (empty, empty), (starts, log_totals))
    return (d_queries.reshape(queries.shape), d_keys, d_values)


def per_device(
    char_input,
    char_counts,
    word_source,
    segment_ids,
    cotangent,
    char_norm_gains,
    char_qkv,
    char_out,
    char_up,
    char_down,
    pool_vector,
    char_proj,
    word_norm_gains,
    word_qkv,
    word_out,
    word_up,
    word_down,
):
    words_here = char_counts.shape[0]
    char_width = char_proj.shape[0]
    model_width = word_out.shape[1]
    present = jnp.arange(CHARS)[None, :] < char_counts[:, None]
    chars_flat = char_input.astype(jnp.float32).reshape(words_here * CHARS, char_width)
    char_weights = (char_norm_gains, char_qkv, char_out, char_up, char_down, pool_vector, char_proj)
    word_vec, char_kept = char_forward(chars_flat, present, char_weights)
    groups = lax.axis_size("dp")
    capacity = (2 * words_here + groups - 1) // groups
    seq_length = words_here * lax.axis_size("mp")
    owner_index = word_source // seq_length
    row_in_owner = word_source % words_here
    owner_hits = (owner_index[:, None] == jnp.arange(groups)[None, :]).astype(jnp.int32)
    earlier_hits = jnp.cumsum(owner_hits, 0) - owner_hits
    slot_rank = jnp.sum(earlier_hits * owner_hits, 1)
    send_slot = owner_index * capacity + slot_rank
    send_vec = (
        jnp.zeros((groups * capacity, model_width), jnp.bfloat16)
        .at[send_slot]
        .set(word_vec.astype(jnp.bfloat16))
    )
    send_rows = (
        jnp.full((groups * capacity,), words_here, jnp.int32).at[send_slot].set(row_in_owner)
    )
    got_vec, got_rows = (
        lax.all_to_all(
            send_vec.reshape(groups, capacity, model_width),
            "dp",
            split_axis=0,
            concat_axis=0,
            tiled=True,
        ),
        lax.all_to_all(
            send_rows.reshape(groups, capacity), "dp", split_axis=0, concat_axis=0, tiled=True
        ),
    )
    got_rows = got_rows.reshape(groups * capacity)
    rows_low = (
        jnp.zeros((words_here, model_width), jnp.bfloat16)
        .at[got_rows]
        .set(got_vec.reshape(groups * capacity, model_width), mode="drop")
    )
    rows_in = rows_low.astype(jnp.float32)
    head_size = model_width // HEADS
    local_heads = word_qkv.shape[2] // head_size
    block_rows = min(512, seq_length)
    gain_first = word_norm_gains[0].astype(jnp.float32)
    gain_second = word_norm_gains[1].astype(jnp.float32)
    normed = norm_rows(rows_in, gain_first).astype(jnp.bfloat16)
    normed_all, segments_all = (
        lax.all_gather(normed, "mp", axis=0, tiled=True),
        lax.all_gather(segment_ids, "mp", axis=0, tiled=True),
    )
    projected = jnp.einsum(
        "ld,kde->kle", normed_all, word_qkv, preferred_element_type=jnp.float32
    ).astype(jnp.bfloat16)
    queries = projected[0].reshape(seq_length, local_heads, head_size)
    keys_in = projected[1].reshape(seq_length, local_heads, head_size)
    values_in = projected[2].reshape(seq_length, local_heads, head_size)
    attended, log_totals = word_attention(queries, keys_in, values_in, segments_all, block_rows)
    mixed_heads = attended.reshape(seq_length, local_heads * head_size).astype(jnp.bfloat16)
    middle = rows_in + sum_rows(flat_dot(mixed_heads, word_out))
    normed_two = norm_rows(middle, gain_second).astype(jnp.bfloat16)
    normed_two_all = gather_rows(normed_two)
    hidden = flat_dot(normed_two_all, word_up)
    activated = jax.nn.gelu(hidden).astype(jnp.bfloat16)
    output = middle + sum_rows(flat_dot(activated, word_down))
    d_output = cotangent.astype(jnp.float32)
    d_branch_all = gather_rows(cotangent)
    grad_word_down = inner_dot(activated, d_branch_all)
    d_activated = outer_dot(d_branch_all, word_down)
    unused_gelu, gelu_back = jax.vjp(jax.nn.gelu, hidden)
    d_hidden = gelu_back(d_activated)[0].astype(jnp.bfloat16)
    grad_word_up = inner_dot(normed_two_all, d_hidden)
    d_normed_two = sum_rows(outer_dot(d_hidden, word_up))
    unused_second, norm_back_second = jax.vjp(norm_rows, middle, gain_second)
    d_middle_norm, grad_gain_second = norm_back_second(d_normed_two)
    d_middle = d_output + d_middle_norm
    d_attended_all = gather_rows(d_middle.astype(jnp.bfloat16))
    grad_word_out = inner_dot(mixed_heads, d_attended_all)
    d_mixed = (
        outer_dot(d_attended_all, word_out)
        .astype(jnp.bfloat16)
        .reshape(seq_length, local_heads, head_size)
    )
    d_queries, d_keys, d_values = word_attention_back(
        queries, keys_in, values_in, segments_all, log_totals, d_mixed, block_rows
    )
    d_projected = (
        jnp.stack([d_queries, d_keys, d_values], 0)
        .reshape(3, seq_length, local_heads * head_size)
        .astype(jnp.bfloat16)
    )
    grad_word_qkv = jnp.einsum(
        "ld,kle->kde", normed_all, d_projected, preferred_element_type=jnp.float32
    )
    d_normed = sum_rows(
        jnp.einsum("kle,kde->ld", d_projected, word_qkv, preferred_element_type=jnp.float32)
    )
    unused_first, norm_back_first = jax.vjp(norm_rows, rows_in, gain_first)
    d_rows_norm, grad_gain_first = norm_back_first(d_normed)
    d_rows = (d_middle + d_rows_norm).astype(jnp.bfloat16)
    back_rows = jnp.take(d_rows, got_rows, axis=0, mode="fill", fill_value=0)
    returned = lax.all_to_all(
        back_rows.reshape(groups, capacity, model_width),
        "dp",
        split_axis=0,
        concat_axis=0,
        tiled=True,
    )
    d_word = returned.reshape(groups * capacity, model_width)[send_slot]
    d_chars, char_mats, grad_char_gains, grad_pool = char_backward(
        chars_flat, present, char_weights, char_kept, d_word
    )
    grad_word_gains = jnp.stack([grad_gain_first, grad_gain_second], 0)
    grad_char_gains, grad_pool, grad_word_gains = lax.psum(
        (grad_char_gains, grad_pool, grad_word_gains), ("dp", "mp")
    )
    grad_qkv, grad_out, grad_up, grad_down, grad_proj = char_mats
    reduced = (
        lax.psum_scatter(grad_qkv, "dp", scatter_dimension=0, tiled=True),
        lax.psum_scatter(grad_out, "dp", scatter_dimension=0, tiled=True),
        lax.psum_scatter(grad_up, "dp", scatter_dimension=0, tiled=True),
        lax.psum_scatter(grad_down, "dp", scatter_dimension=0, tiled=True),
        lax.psum_scatter(grad_proj, "dp", scatter_dimension=0, tiled=True),
        lax.psum_scatter(grad_word_qkv, "dp", scatter_dimension=1, tiled=True),
        lax.psum_scatter(grad_word_out, "dp", scatter_dimension=1, tiled=True),
        lax.psum_scatter(grad_word_up, "dp", scatter_dimension=0, tiled=True),
        lax.psum_scatter(grad_word_down, "dp", scatter_dimension=1, tiled=True),
    )
    grad_qkv, grad_out, grad_up, grad_down, grad_proj = (
        lax.psum_scatter(
            reduced[0].astype(jnp.bfloat16), "mp", scatter_dimension=1, tiled=True
        ).astype(jnp.float32),
        lax.psum_scatter(
            reduced[1].astype(jnp.bfloat16), "mp", scatter_dimension=1, tiled=True
        ).astype(jnp.float32),
        lax.psum_scatter(
            reduced[2].astype(jnp.bfloat16), "mp", scatter_dimension=1, tiled=True
        ).astype(jnp.float32),
        lax.psum_scatter(
            reduced[3].astype(jnp.bfloat16), "mp", scatter_dimension=1, tiled=True
        ).astype(jnp.float32),
        lax.psum_scatter(
            reduced[4].astype(jnp.bfloat16), "mp", scatter_dimension=1, tiled=True
        ).astype(jnp.float32),
    )
    grad_word_qkv, grad_word_out, grad_word_up, grad_word_down = (
        reduced[5],
        reduced[6],
        reduced[7],
        reduced[8],
    )
    return (
        output.astype(jnp.bfloat16),
        d_chars.reshape(words_here, CHARS * char_width),
        grad_qkv,
        grad_out,
        grad_up,
        grad_down,
        grad_proj,
        grad_word_qkv,
        grad_word_out,
        grad_word_up,
        grad_word_down,
        grad_char_gains,
        grad_pool,
        grad_word_gains,
    )


def solution(mesh):
    placed = (
        P(("dp", "mp"), None),
        P(("dp", "mp")),
        P(("dp", "mp")),
        P(("dp", "mp")),
        P(("dp", "mp"), None),
        P(),
        P(),
        P(),
        P(),
        P(),
        P(),
        P(),
        P(),
        P(None, None, "mp"),
        P("mp", None),
        P(None, "mp"),
        P("mp", None),
    )
    return jax.shard_map(
        per_device,
        mesh=mesh,
        in_specs=placed,
        out_specs=(
            P(("dp", "mp"), None),
            P(("dp", "mp"), None),
            P("dp", "mp"),
            P("dp", "mp"),
            P("dp", "mp"),
            P("dp", "mp"),
            P("dp", "mp"),
            P(None, "dp", "mp"),
            P("mp", "dp"),
            P("dp", "mp"),
            P("mp", "dp"),
            P(),
            P(),
            P(),
        ),
        check_vma=False,
    )
```

profile of v0, /device:TPU:0, one launch (start us, length us, event | category | flops | bytes accessed | tf_op | source)
XLA Modules:
  0.0 1233.4 jit_solution(5641197604273902447)
XLA Ops:
  36.4 18.6 %reshape.525 = bf16[256,16,3,4,64]{4,3,2,1,0:T(4,128)(2,1)} reshape(bf16[4096,768]{1,0:T(8,128)(2,1)} %convolution_convert_fusion) | data formatting | bytes 12582912 | tf_op jit(solution)/shard_map/reshape | solution.py:67
  144.7 15.0 %scatter_custom_fusion.2 = bf16[256,512]{1,0:T(8,128)(2,1)S(1)} fusion(s32[512]{0:T(512)S(1)} %bitcast.271, bf16[512,512]{1,0:T(8,128)(2,1)S(1)} %bitcast.248, bf16[]{:T(256)} %constant.88.clone.1), kind=kCustom, calls=%fused_computation.164 | custom fusion | bytes 262146 | tf_op jit(solution)/shard_map/scatter | solution.py:322
  179.0 15.2 %while.27 = (s32[]{:T(128)}, bf16[2,512,2,64]{1,3,2,0:T(8,128)(2,1)S(1)}, f32[2,2,512]{2,1,0:T(2,128)S(1)}, s32[2]{0:T(128)S(1)}, s32[1024]{0:T(1024)S(1)}, /*in...) while((s32[]{:T(128)}, ...), condition=%wide.region_21.22_spmd, body=%wide.region_18.21_spmd.sunk | while | flops 282590720 | bytes 15644855 | solution.py:219
  197.2 30.8 %reduce-scatter.26.cloned.1.call-done = f32[256,512]{1,0:T(8,128)} async-done(((f32[1024,512]{1,0:T(8,128)}), f32[256,512]{1,0:T(8,128)}) %reduce-scatter.26.cloned.1.call-update) | async-done | bytes 524304 | tf_op jit(solution)/shard_map/reduce_scatter | solution.py:52
  230.3 16.1 %all-gather.10.cloned.1.call-done = bf16[1024,512]{1,0:T(8,128)(2,1)} async-done(((bf16[256,512]{1,0:T(8,128)(2,1)}), bf16[1024,512]{1,0:T(8,128)(2,1)}) %all-gather.10.cloned.1.call-update) | async-done | bytes 1048592 | tf_op jit(solution)/shard_map/all_gather | solution.py:48
  249.7 15.5 %all-gather.8.cloned.1.call-done = bf16[1024,512]{1,0:T(8,128)(2,1)} async-done(((bf16[256,512]{1,0:T(8,128)(2,1)}), bf16[1024,512]{1,0:T(8,128)(2,1)}) %all-gather.8.cloned.1.call-update) | async-done | bytes 1048592 | tf_op jit(solution)/shard_map/all_gather | solution.py:48
  276.5 27.6 %reduce-scatter.30.cloned.1.call-done = f32[256,512]{1,0:T(8,128)} async-done(((f32[1024,512]{1,0:T(8,128)}), f32[256,512]{1,0:T(8,128)}) %reduce-scatter.30.cloned.1.call-update) | async-done | bytes 524304 | tf_op jit(solution)/shard_map/reduce_scatter | solution.py:52
  306.0 32.0 %reduce-scatter.28.cloned.1.call-done = f32[256,512]{1,0:T(8,128)} async-done(((f32[1024,512]{1,0:T(8,128)}), f32[256,512]{1,0:T(8,128)}) %reduce-scatter.28.cloned.1.call-update) | async-done | bytes 524304 | tf_op jit(solution)/shard_map/reduce_scatter | solution.py:52
  341.0 16.8 %all-gather.12.cloned.1.call-done = bf16[1024,512]{1,0:T(8,128)(2,1)} async-done(((bf16[256,512]{1,0:T(8,128)(2,1)}), bf16[1024,512]{1,0:T(8,128)(2,1)}) %all-gather.12.cloned.1.call-update) | async-done | bytes 1048592 | tf_op jit(solution)/shard_map/all_gather | solution.py:48
  359.6 23.0 %while.28 = (s32[]{:T(128)}, f32[1024,2,64]{0,2,1:T(8,128)S(1)}, f32[1024,2,64]{0,2,1:T(8,128)}, bf16[2,512,2,64]{1,3,2,0:T(8,128)(2,1)S(1)}, s32[2]{0:T(128)}, ...) while((s32[]{:T(128)}, f32[1024,2,64]{0,2,1:T(8,128)S(1)}, ...), condition=%wide.region_31.32_spmd.clone, body=%wide.region_29.31_spmd.clone.sunk | while | flops 689110528 | bytes 41462044 | solution.py:259
  401.6 18.3 %reduce-scatter.32.cloned.1.call-done = f32[256,512]{1,0:T(8,128)} async-done(((f32[1024,512]{1,0:T(8,128)}), f32[256,512]{1,0:T(8,128)}) %reduce-scatter.32.cloned.1.call-update) | async-done | bytes 524304 | tf_op jit(solution)/shard_map/reduce_scatter | solution.py:52
  455.4 15.4 %fusion.45 = bf16[4096,1024]{1,0:T(8,128)(2,1)S(1)} fusion(f32[4096,1024]{1,0:T(8,128)} %get-tuple-element.296, bf16[4096,256]{1,0:T(8,128)(2,1)S(1)} %fusion.49, bf16[1024,256]{1,0:T(8,128)(2,1)} %param.30), kind=kOutput, calls=%fused_computation.61 | convolution fusion | flops 2231369728 | bytes 27787264 | tf_op jit(solution)/shard_map/dot_general | solution.py:42
  570.8 20.1 %copy.113 = bf16[256,16,3,4,64]{4,3,2,1,0:T(4,128)(2,1)} copy(bf16[256,16,3,4,64]{0,4,3,2,1:T(8,128)(2,1)} %maximum_convert_fusion) | data formatting | bytes 12582912 | tf_op jit(solution)/shard_map/convert_element_type | solution.py:174
  591.0 18.4 %convert_element_type.201 = bf16[4096,768]{1,0:T(8,128)(2,1)} reshape(bf16[256,16,3,4,64]{4,3,2,1,0:T(4,128)(2,1)} %copy.113) | data formatting | bytes 12582912 | tf_op jit(solution)/shard_map/convert_element_type | solution.py:174
  642.5 63.4 %reduce-scatter.34.cloned.1.call-done = f32[32,768]{1,0:T(8,128)} async-done(((f32[256,768]{1,0:T(8,128)}), f32[32,768]{1,0:T(8,128)}) %reduce-scatter.34.cloned.1.call-update) | async-done | bytes 98320 | tf_op jit(solution)/shard_map/reduce_scatter | solution.py:402
  707.6 63.9 %reduce-scatter.42.cloned.1.call-done = f32[128,256]{1,0:T(8,128)} async-done(((f32[1024,256]{1,0:T(8,128)}), f32[128,256]{1,0:T(8,128)}) %reduce-scatter.42.cloned.1.call-update) | async-done | bytes 131088 | tf_op jit(solution)/shard_map/reduce_scatter | solution.py:405
  773.2 64.6 %reduce-scatter.38.cloned.1.call-done = f32[32,1024]{1,0:T(8,128)} async-done(((f32[256,1024]{1,0:T(8,128)}), f32[32,1024]{1,0:T(8,128)}) %reduce-scatter.38.cloned.1.call-update) | async-done | bytes 131088 | tf_op jit(solution)/shard_map/reduce_scatter | solution.py:404
  849.4 68.9 %all-reduce.4.cloned.1.call-done = f32[3,512,128]{2,0,1:T(4,128)} async-done(((f32[3,512,128]{2,0,1:T(4,128)}), f32[3,512,128]{2,0,1:T(4,128)}) %all-reduce.4.cloned.1.call-update) | async-done | bytes 786448
  938.0 39.7 %all-reduce.1 = (f32[2,256]{1,0:T(2,128)}, f32[256]{0:T(256)}, f32[2,512]{1,0:T(2,128)}) all-reduce(f32[2,256]{1,0:T(2,128)S(1)} %pad_maximum_fusion.4, f32[256]{0:T(256)S(1)} %copy-done.96, f32[2,512]{1,0:T(2,128)S(1)} %pad_maximum_fusion.3), channel_id=1, replica_groups=mesh['dp'=8,'mp'=4] {'dp','mp'}, use_global_device_ids=true, to_apply=%region_58.59 | all-reduce | flops 1792 | bytes 14336 | tf_op jit(solution)/shard_map/psum | solution.py:397
  985.4 20.3 %reduce-scatter.56.cloned.1.call-done = bf16[64,128]{1,0:T(8,128)(2,1)} async-done(((bf16[256,128]{1,0:T(8,128)(2,1)}), bf16[64,128]{1,0:T(8,128)(2,1)}) %reduce-scatter.56.cloned.1.call-update) | async-done | bytes 16400
  1007.3 20.3 %reduce-scatter.40.cloned.1.call-done = bf16[32,256]{1,0:T(8,128)(2,1)} async-done(((bf16[32,1024]{1,0:T(8,128)(2,1)}), bf16[32,256]{1,0:T(8,128)(2,1)}) %reduce-scatter.40.cloned.1.call-update) | async-done | bytes 16400 | tf_op jit(solution)/shard_map/reduce_scatter | solution.py:419
  1028.9 66.3 %reduce-scatter.50.cloned.1.call-done = f32[512,64]{0,1:T(8,128)} async-done(((f32[512,512]{0,1:T(8,128)}), f32[512,64]{0,1:T(8,128)}) %reduce-scatter.50.cloned.1.call-update) | async-done | bytes 131088 | tf_op jit(solution)/shard_map/reduce_scatter | solution.py:410
  1095.2 66.5 %reduce-scatter.48.cloned.1.call-done = f32[64,512]{1,0:T(8,128)} async-done(((f32[512,512]{1,0:T(8,128)}), f32[64,512]{1,0:T(8,128)}) %reduce-scatter.48.cloned.1.call-update) | async-done | bytes 131088 | tf_op jit(solution)/shard_map/reduce_scatter | solution.py:409
  1161.7 64.6 %reduce-scatter.46.cloned.1.call-done = f32[128,64]{0,1:T(8,128)} async-done(((f32[128,512]{0,1:T(8,128)}), f32[128,64]{0,1:T(8,128)}) %reduce-scatter.46.cloned.1.call-update) | async-done | bytes 32784 | tf_op jit(solution)/shard_map/reduce_scatter | solution.py:408
  (488 shorter events, 425.2 us)
Async XLA Ops:
  11.0 113.7 %all-to-all-start = ((s32[8,1,64]{2,1,0:T(1,128)}), s32[8,1,64]{2,1,0:T(1,128)S(1)}, u32[]{:S(2)}, u32[]{:S(2)}) async-start(s32[8,1,64]{2,1,0:T(1,128)} %all_to_all.12), calls=%async_computation | async-start | bytes 8192 | tf_op jit(solution)/shard_map/all_to_all | solution.py:314
  130.7 46.2 %all-gather.6.cloned.1.call-start = ((), (), s32[]{:S(2)}) async-start(), calls=%async_computation.20 | async-start | bytes 1310720 | tf_op jit(solution)/shard_map/all_gather | solution.py:332
  161.0 67.0 %reduce-scatter.26.cloned.1.call-start = ((), (), s32[]{:S(2)}) async-start(), calls=%async_computation.21 | async-start | bytes 2621440 | tf_op jit(solution)/shard_map/reduce_scatter | solution.py:52
  196.4 50.0 %all-gather.10.cloned.1.call-start = ((), (), s32[]{:S(2)}) async-start(), calls=%async_computation.24 | async-start | bytes 1310720 | tf_op jit(solution)/shard_map/all_gather | solution.py:48
  197.1 68.1 %all-gather.8.cloned.1.call-start = ((), (), s32[]{:S(2)}) async-start(), calls=%async_computation.22 | async-start | bytes 1310720 | tf_op jit(solution)/shard_map/all_gather | solution.py:48
  230.3 73.8 %reduce-scatter.30.cloned.1.call-start = ((), (), s32[]{:S(2)}) async-start(), calls=%async_computation.25 | async-start | bytes 2621440 | tf_op jit(solution)/shard_map/reduce_scatter | solution.py:52
  272.5 65.4 %reduce-scatter.28.cloned.1.call-start = ((), (), s32[]{:S(2)}) async-start(), calls=%async_computation.23 | async-start | bytes 2621440 | tf_op jit(solution)/shard_map/reduce_scatter | solution.py:52
  276.5 81.4 %all-gather.12.cloned.1.call-start = ((), (), s32[]{:S(2)}) async-start(), calls=%async_computation.26 | async-start | bytes 1310720 | tf_op jit(solution)/shard_map/all_gather | solution.py:48
  340.9 79.1 %reduce-scatter.32.cloned.1.call-start = ((), (), s32[]{:S(2)}) async-start(), calls=%async_computation.27 | async-start | bytes 2621440 | tf_op jit(solution)/shard_map/reduce_scatter | solution.py:52
  427.5 20.0 %all-to-all-start.2 = ((bf16[8,64,512]{2,1,0:T(8,128)(2,1)}), bf16[8,64,512]{2,1,0:T(8,128)(2,1)S(1)}, u32[]{:S(2)}, u32[]{:S(2)}) async-start(bf16[8,64,512]{2,1,0:T(8,128)(2,1)} %broadcast_select_fusion), calls=%async_computation.6 | async-start | bytes 1048576 | tf_op jit(solution)/shard_map/all_to_all | solution.py:385
  433.0 203.8 %reduce-scatter.36.cloned.1.call-start = ((), (), s32[]{:S(2)}) async-start(), calls=%async_computation.29 | async-start | bytes 294912 | tf_op jit(solution)/shard_map/reduce_scatter | solution.py:403
  517.1 123.7 %reduce-scatter.44.cloned.1.call-start = ((), (), s32[]{:S(2)}) async-start(), calls=%async_computation.33 | async-start | bytes 589824 | tf_op jit(solution)/shard_map/reduce_scatter | solution.py:406
  551.7 154.1 %reduce-scatter.34.cloned.1.call-start = ((), (), s32[]{:S(2)}) async-start(), calls=%async_computation.28 | async-start | bytes 884736 | tf_op jit(solution)/shard_map/reduce_scatter | solution.py:402
  615.0 156.6 %reduce-scatter.42.cloned.1.call-start = ((), (), s32[]{:S(2)}) async-start(), calls=%async_computation.32 | async-start | bytes 1179648 | tf_op jit(solution)/shard_map/reduce_scatter | solution.py:405
  622.4 215.4 %reduce-scatter.38.cloned.1.call-start = ((), (), s32[]{:S(2)}) async-start(), calls=%async_computation.30 | async-start | bytes 1179648 | tf_op jit(solution)/shard_map/reduce_scatter | solution.py:404
  631.6 286.6 %all-reduce.4.cloned.1.call-start = ((), (), s32[]{:S(2)}) async-start(), calls=%async_computation.41 | async-start | bytes 2097152
  636.7 341.1 %reduce-scatter.54.cloned.1.call-start = ((), (), s32[]{:S(2)}) async-start(), calls=%async_computation.38 | async-start | bytes 81920
  638.3 340.9 %reduce-scatter.58.cloned.1.call-start = ((), (), s32[]{:S(2)}) async-start(), calls=%async_computation.40 | async-start | bytes 163840
  642.4 341.4 %reduce-scatter.52.cloned.1.call-start = ((), (), s32[]{:S(2)}) async-start(), calls=%async_computation.37 | async-start | bytes 245760
  707.6 298.1 %reduce-scatter.56.cloned.1.call-start = ((), (), s32[]{:S(2)}) async-start(), calls=%async_computation.39 | async-start | bytes 81920
  773.2 254.4 %reduce-scatter.40.cloned.1.call-start = ((), (), s32[]{:S(2)}) async-start(), calls=%async_computation.31 | async-start | bytes 81920 | tf_op jit(solution)/shard_map/reduce_scatter | solution.py:419
  839.4 255.8 %reduce-scatter.50.cloned.1.call-start = ((), (), s32[]{:S(2)}) async-start(), calls=%async_computation.36 | async-start | bytes 1179648 | tf_op jit(solution)/shard_map/reduce_scatter | solution.py:410
  843.4 318.4 %reduce-scatter.48.cloned.1.call-start = ((), (), s32[]{:S(2)}) async-start(), calls=%async_computation.35 | async-start | bytes 1179648 | tf_op jit(solution)/shard_map/reduce_scatter | solution.py:409
  846.8 379.5 %reduce-scatter.46.cloned.1.call-start = ((), (), s32[]{:S(2)}) async-start(), calls=%async_computation.34 | async-start | bytes 294912 | tf_op jit(solution)/shard_map/reduce_scatter | solution.py:408
  (110 other events, 2155.1 us)
Sparse Core Ops, SparseCore 0:
  161.1 15.7 all-gather.5
  196.5 31.4 reduce-scatter.25
  229.6 16.7 all-gather.9
  248.4 16.7 all-gather.7
  272.6 31.4 reduce-scatter.29
  306.5 31.4 reduce-scatter.27
  341.0 16.7 all-gather.11
  388.5 31.4 reduce-scatter.31
  517.2 59.3 reduce-scatter.35
  579.8 60.9 reduce-scatter.43
  644.4 61.3 reduce-scatter.33
  709.1 62.3 reduce-scatter.41
  775.3 62.4 reduce-scatter.37
  841.2 77.0 all-reduce.3
  920.7 19.0 reduce-scatter.53
  942.0 19.5 reduce-scatter.57
  964.1 19.7 reduce-scatter.51
  986.3 19.3 reduce-scatter.55
  1008.1 19.4 reduce-scatter.39
  1031.8 63.3 reduce-scatter.49
  1099.2 62.4 reduce-scatter.47
  1166.0 60.2 reduce-scatter.45
where the time goes:
time: 1240 us; the launch traced here: 1230 us
  waiting for transfers between devices  688 us (55%)
  local copies, waits for them, and re-layouts  181 us (15%)
  matrix products  172 us (14%)
  other arithmetic  102 us (8%)
  blocking collectives  44.8 us (4%)
  starting transfers between devices  20 us (2%)
  between operations  17 us (1%)
    reduce_scatter x4, waiting for transfers between devices, sum_rows(): return lax.psum_scatter(partial_rows, 'mp', scatter_dimension=0, tiled=True)  109 us
    unnamed x27, waiting for transfers between devices  93.4 us
    reduce_scatter x1, waiting for transfers between devices, per_device(): lax.psum_scatter(grad_word_up, 'dp', scatter_dimension=0, tiled=True)  66.5 us
    reduce_scatter x1, waiting for transfers between devices, per_device(): lax.psum_scatter(grad_word_down, 'dp', scatter_dimension=1, tiled=True)  66.3 us
    reduce_scatter x1, waiting for transfers between devices, per_device(): lax.psum_scatter(grad_word_out, 'dp', scatter_dimension=1, tiled=True)  64.6 us
    reduce_scatter x1, waiting for transfers between devices, per_device(): lax.psum_scatter(grad_up, 'dp', scatter_dimension=0, tiled=True)  64.6 us
    reduce_scatter x1, waiting for transfers between devices, per_device(): lax.psum_scatter(grad_down, 'dp', scatter_dimension=0, tiled=True)  63.9 us
    reduce_scatter x1, waiting for transfers between devices, per_device(): lax.psum_scatter(grad_qkv, 'dp', scatter_dimension=0, tiled=True)  63.4 us
  transfers between devices with their start and end apart: 25, of which 21 were waited for; matrix products, arithmetic and copies ran while one was open for 25% of the time, Pallas kernels for 0%

commit v1 on v0

v1 whole, which is shorter than its diff:
```python
import functools
from functools import partial

import jax
import jax.numpy as jnp
from jax import lax
from jax.experimental import pallas as pl
from jax.experimental.pallas import tpu as pltpu
from jax.sharding import PartitionSpec as P

CHARS = 16
CHAR_HEADS = 4
EPSILON = 1e-05
NEGATIVE = -1e30
GELU_A = 0.7978845608028654
GELU_B = 0.044715
F32 = jnp.float32
BF16 = jnp.bfloat16
VMEM_LIMIT = 60 * 1024 * 1024


def dot_nn(left, right):
    return jnp.dot(left, right, preferred_element_type=F32)


def dot_nt(left, right):
    return lax.dot_general(left, right, (((1,), (1,)), ((), ())), preferred_element_type=F32)


def dot_tn(left, right):
    return lax.dot_general(left, right, (((0,), (0,)), ((), ())), preferred_element_type=F32)


def head_stack(values, heads, factor):
    width = values.shape[1] // heads
    lane = lax.broadcasted_iota(jnp.int32, (1, values.shape[1]), 1) // width
    return jnp.concatenate(
        [values * jnp.where(lane == h, factor, 0.0).astype(values.dtype) for h in range(heads)], 0
    )


def gelu_both(hidden):
    square = hidden * hidden
    inner = hidden * (GELU_A + (GELU_A * GELU_B) * square)
    tanh = jnp.tanh(inner)
    half = 0.5 + 0.5 * tanh
    slope = half + (0.5 * hidden) * (1.0 - tanh * tanh) * (GELU_A + (3.0 * GELU_A * GELU_B) * square)
    return hidden * half, slope


def char_fwd_body(
    x_ref, cnt_ref, gains_ref, wqkv_ref, wout_ref, wup_ref, wdown_ref, pool_ref, wproj_ref,
    e_ref, n1_ref, p_ref, a_ref, o_ref, n2_ref, rs1_ref, rs2_ref, act_ref, dg_ref, f_ref, aw_ref, pooled_ref,
):
    words, wide = x_ref.shape
    width = wide // CHARS
    blocks = words // 8
    gains = gains_ref[...].astype(F32)
    pieces = []
    for g in range(words // 16):
        xt = x_ref[16 * g : 16 * g + 16, :].astype(F32)
        for half in range(2):
            for c in range(CHARS):
                pieces.append(xt[8 * half : 8 * half + 8, width * c : width * c + width])
    x = jnp.concatenate(pieces, 0)

    def norm(v, gain):
        mean = jnp.mean(v, -1, keepdims=True)
        centered = v - mean
        rstd = lax.rsqrt(jnp.mean(centered * centered, -1, keepdims=True) + EPSILON)
        return (centered * rstd * gain).astype(BF16), rstd

    n1, rs1 = norm(x, gains[0:1])
    n1_ref[...] = n1
    rs1_ref[...] = rs1
    p_ref[...] = dot_nn(n1, wqkv_ref[...]).astype(BF16)
    row_w = lax.broadcasted_iota(jnp.int32, (8, 128), 0)
    lane_w = lax.broadcasted_iota(jnp.int32, (8, 128), 1) % 8
    same = row_w == lane_w
    slot = lax.broadcasted_iota(jnp.int32, (CHARS, 8, 128), 0)
    for b in range(blocks):
        rows = slice(128 * b, 128 * b + 128)
        counts = jnp.broadcast_to(cnt_ref[8 * b : 8 * b + 8, :], (8, 128))
        here = slot < counts[None]
        q = p_ref[rows, 0:width]
        k = p_ref[rows, width : 2 * width]
        v = p_ref[rows, 2 * width : 3 * width]
        st = dot_nt(head_stack(k, CHAR_HEADS, (width // CHAR_HEADS) ** -0.5), q)
        st = st.reshape(CHAR_HEADS, CHARS, 8, 128)
        st = jnp.where(here[None], st, NEGATIVE)
        e = jnp.exp(st - jnp.max(st, 1, keepdims=True))
        r = jnp.where(same[None, None], 1.0 / jnp.sum(e, 1, keepdims=True), 0.0)
        a = (e * r).reshape(CHAR_HEADS * 128, 128).astype(BF16)
        a_ref[CHAR_HEADS * 128 * b : CHAR_HEADS * 128 * (b + 1), :] = a
        o_ref[rows, :] = dot_tn(a, head_stack(v, CHAR_HEADS, 1.0)).astype(BF16)
    m = x + dot_nn(o_ref[...], wout_ref[...])
    n2, rs2 = norm(m, gains[1:2])
    n2_ref[...] = n2
    rs2_ref[...] = rs2
    act, slope = gelu_both(dot_nn(n2, wup_ref[...]))
    act = act.astype(BF16)
    act_ref[...] = act
    dg_ref[...] = slope.astype(BF16)
    f = m + dot_nn(act, wdown_ref[...])
    f_ref[...] = f.astype(BF16)
    t = jnp.sum(f * pool_ref[...].astype(F32), -1, keepdims=True).reshape(blocks, CHARS, 8, 1)
    counts = cnt_ref[...].reshape(blocks, 1, 8, 1)
    t = jnp.where(lax.broadcasted_iota(jnp.int32, t.shape, 1) < counts, t, NEGATIVE)
    et = jnp.exp(t - jnp.max(t, 1, keepdims=True))
    aw = et / jnp.sum(et, 1, keepdims=True)
    aw_ref[...] = aw.reshape(words * CHARS, 1)
    pooled = jnp.sum(aw * f.reshape(blocks, CHARS, 8, width), 1).reshape(words, width).astype(BF16)
    pooled_ref[...] = pooled
    e_ref[...] = dot_nn(pooled, wproj_ref[...]).astype(BF16)


def char_forward(x, counts, gains, wqkv, wout, wup, wdown, pool, wproj, step_words=32):
    words, wide = x.shape
    width = wide // CHARS
    rows = words * CHARS
    step_rows = step_words * CHARS
    full = lambda arr: pl.BlockSpec(arr.shape, lambda i: (0,) * arr.ndim)
    blk = lambda n, w: pl.BlockSpec((n, w), lambda i: (i, 0))
    hid = wup.shape[1]
    dw = wproj.shape[1]
    outs = [
        (words, step_words, dw, BF16), (rows, step_rows, width, BF16), (rows, step_rows, 3 * width, BF16),
        (rows * CHAR_HEADS, step_rows * CHAR_HEADS, 128, BF16), (rows, step_rows, width, BF16),
        (rows, step_rows, width, BF16), (rows, step_rows, 1, F32), (rows, step_rows, 1, F32),
        (rows, step_rows, hid, BF16), (rows, step_rows, hid, BF16), (rows, step_rows, width, BF16),
        (rows, step_rows, 1, F32), (words, step_words, width, BF16),
    ]
    return pl.pallas_call(
        char_fwd_body,
        grid=(words // step_words,),
        in_specs=[blk(step_words, wide), blk(step_words, 1)] + [full(w) for w in (gains, wqkv, wout, wup, wdown, pool, wproj)],
        out_specs=[blk(b, w) for _, b, w, _ in outs],
        out_shape=[jax.ShapeDtypeStruct((n, w), d) for n, _, w, d in outs],
        compiler_params=pltpu.CompilerParams(vmem_limit_bytes=VMEM_LIMIT),
        name="char_forward",
    )(x, counts, gains, wqkv, wout, wup, wdown, pool, wproj)


def char_bwd_body(
    de_ref, gains_ref, wqkv_ref, wout_ref, wup_ref, wdown_ref, pool_ref, wproj_ref,
    n1_ref, p_ref, a_ref, o_ref, n2_ref, rs1_ref, rs2_ref, act_ref, dg_ref, f_ref, aw_ref, pooled_ref,
    dx_ref, gqkv_ref, gout_ref, gup_ref, gdown_ref, gproj_ref, ggain_ref, gpool_ref,
    dp_ref, do_ref,
):
    words = de_ref.shape[0]
    width = n1_ref.shape[1]
    blocks = words // 8
    rows = words * CHARS
    gains = gains_ref[...].astype(F32)

    @pl.when(pl.program_id(0) == 0)
    def _():
        for ref in (gqkv_ref, gout_ref, gup_ref, gdown_ref, gproj_ref, ggain_ref, gpool_ref):
            ref[...] = jnp.zeros_like(ref)

    de = de_ref[...]
    gproj_ref[...] += dot_tn(pooled_ref[...], de)
    dpool = dot_nt(de, wproj_ref[...]).reshape(blocks, 1, 8, width)
    f = f_ref[...].astype(F32).reshape(blocks, CHARS, 8, width)
    aw = aw_ref[...].reshape(blocks, CHARS, 8, 1)
    g = jnp.sum(f * dpool, -1, keepdims=True)
    dt = aw * (g - jnp.sum(aw * g, 1, keepdims=True))
    gpool_ref[...] += jnp.sum((dt * f).reshape(rows // 8, 8, width), 0)
    df = (aw * dpool + dt * pool_ref[...].astype(F32)).reshape(rows, width)
    dfb = df.astype(BF16)
    gdown_ref[...] += dot_tn(act_ref[...], dfb)
    dh = (dg_ref[...].astype(F32) * dot_nt(dfb, wdown_ref[...])).astype(BF16)
    n2 = n2_ref[...]
    gup_ref[...] += dot_tn(n2, dh)
    dn2 = dot_nt(dh, wup_ref[...])

    def norm_back(dn, n, rstd, gain, row):
        d1 = dn * gain
        dnn = dn * n.astype(F32)
        ggain_ref[row] += jnp.sum(dnn.reshape(rows // 8, 8, width), 0)
        m1 = jnp.mean(d1, -1, keepdims=True)
        m2 = jnp.mean(dnn, -1, keepdims=True)
        return rstd * (d1 - m1 - n.astype(F32) * (1.0 / gain) * m2)

    dm = df + norm_back(dn2, n2, rs2_ref[...], gains[1:2], 1)
    dmb = dm.astype(BF16)
    gout_ref[...] += dot_tn(o_ref[...], dmb)
    do_ref[...] = dot_nt(dmb, wout_ref[...]).astype(BF16)
    scale = (width // CHAR_HEADS) ** -0.5
    for b in range(blocks):
        sl = slice(128 * b, 128 * b + 128)
        q = p_ref[sl, 0:width]
        k = p_ref[sl, width : 2 * width]
        v = p_ref[sl, 2 * width : 3 * width]
        do = do_ref[sl, :]
        ab = a_ref[CHAR_HEADS * 128 * b : CHAR_HEADS * 128 * (b + 1), :]
        a = ab.astype(F32).reshape(CHAR_HEADS, CHARS, 8, 128)
        dpt = dot_nt(head_stack(v, CHAR_HEADS, 1.0), do).reshape(CHAR_HEADS, CHARS, 8, 128)
        delta = jnp.sum(a * dpt, 1, keepdims=True)
        ds = (a * (dpt - delta)).reshape(CHAR_HEADS * 128, 128).astype(BF16)
        wide_ds = jnp.concatenate([ds[128 * h : 128 * h + 128] for h in range(CHAR_HEADS)], 1)
        wide_a = jnp.concatenate([ab[128 * h : 128 * h + 128] for h in range(CHAR_HEADS)], 1)
        dp_ref[sl, 0:width] = dot_tn(ds, head_stack(k, CHAR_HEADS, scale)).astype(BF16)
        dp_ref[sl, width : 2 * width] = dot_nn(wide_ds, head_stack(q, CHAR_HEADS, scale)).astype(BF16)
        dp_ref[sl, 2 * width : 3 * width] = dot_nn(wide_a, head_stack(do, CHAR_HEADS, 1.0)).astype(BF16)
    n1 = n1_ref[...]
    dp = dp_ref[...]
    gqkv_ref[...] += dot_tn(n1, dp)
    dn1 = dot_nt(dp, wqkv_ref[...])
    dx = dm + norm_back(dn1, n1, rs1_ref[...], gains[0:1], 0)
    for b in range(blocks):
        for c in range(CHARS):
            dx_ref[8 * b : 8 * b + 8, width * c : width * c + width] = dx[128 * b + 8 * c : 128 * b + 8 * c + 8]


def char_backward(de, kept, gains, wqkv, wout, wup, wdown, pool, wproj, step_words=32):
    words = de.shape[0]
    width = wout.shape[0]
    rows = words * CHARS
    step_rows = step_words * CHARS
    full = lambda arr: pl.BlockSpec(arr.shape, lambda i: (0,) * arr.ndim)
    blk = lambda n, w: pl.BlockSpec((n, w), lambda i: (i, 0))
    steps = words // step_words
    weights = (gains, wqkv, wout, wup, wdown, pool, wproj)
    outs = [wqkv.shape, wout.shape, wup.shape, wdown.shape, wproj.shape, (2, 8, width), (8, width)]
    return pl.pallas_call(
        char_bwd_body,
        grid=(steps,),
        in_specs=[blk(step_words, de.shape[1])] + [full(w) for w in weights]
        + [blk(r.shape[0] // steps, r.shape[1]) for r in kept],
        out_specs=[blk(step_words, CHARS * width)]
        + [pl.BlockSpec(s, lambda i, n=len(s): (0,) * n) for s in outs],
        out_shape=[jax.ShapeDtypeStruct((words, CHARS * width), F32)]
        + [jax.ShapeDtypeStruct(s, F32) for s in outs],
        scratch_shapes=[pltpu.VMEM((step_rows, 3 * width), BF16), pltpu.VMEM((step_rows, width), BF16)],
        compiler_params=pltpu.CompilerParams(vmem_limit_bytes=VMEM_LIMIT),
        name="char_backward",
    )(de, *weights, *kept)


MESH = pl.DeviceIdType.MESH
CHAR_ROWS = 224
WORD_ROWS = 768


def fold_half(block):
    half = block.shape[0] // 2
    return jnp.concatenate([block[:half], block[half:]], 1)


def unfold_half(block):
    return jnp.concatenate([block[:, :64], block[:, 64:]], 0)


def add_into(total_ref, other_ref, lead):
    def step(i, carry):
        total_ref[i] = (total_ref[i].astype(F32) + other_ref[i].astype(F32)).astype(total_ref.dtype)
        return carry
    lax.fori_loop(0, lead, step, 0)


def reduce_body(
    n_z,
    cqkv_ref, cout_ref, cup_ref, cdown_ref, cproj_ref, cgain_ref, cpool_ref, cg_ref,
    wqkv_ref, wout_ref, wup_ref, wdown_ref, wgain_ref,
    oqkv_ref, oout_ref, oup_ref, odown_ref, oproj_ref, owqkv_ref, owout_ref, owup_ref, owdown_ref,
    ocgain_ref, opool_ref, owgain_ref,
    cbuf, cr_a, cr_b, cr_c, cr_d, wbuf, wr_c, wr_d, small, sr, ssem, rsem,
):
    dp, mp = lax.axis_index("dp"), lax.axis_index("mp")
    z, x = dp // 2, dp % 2
    y, core = mp // 2, mp % 2
    peers = [(dp, y * 2 + 1 - core), (dp, (1 - y) * 2 + core), (z * 2 + 1 - x, mp)]
    z_peers = [(lax.rem(z + k, n_z) * 2 + x, mp) for k in range(1, n_z)]
    barrier = pltpu.get_barrier_semaphore()
    for peer in peers + z_peers:
        pl.semaphore_signal(barrier, inc=1, device_id=peer, device_id_type=MESH)

    def send(src, dst, slot, peer):
        copy = pltpu.make_async_remote_copy(
            src_ref=src, dst_ref=dst, send_sem=ssem.at[slot], recv_sem=rsem.at[slot],
            device_id=peer, device_id_type=MESH,
        )
        copy.start()
        return copy

    for d in range(2 * n_z):
        for t in range(3):
            wbuf[d % 2, d // 2, 64 * t : 64 * t + 64, :] = wqkv_ref[t, 64 * d : 64 * d + 64, :].astype(BF16)
        wbuf[d % 2, d // 2, 192:256, :] = wout_ref[64 * d : 64 * d + 64, :].astype(BF16)
        for t in range(4):
            wbuf[d % 2, d // 2, 256 + 64 * t : 320 + 64 * t, :] = wup_ref[64 * d : 64 * d + 64, 128 * t : 128 * t + 128].astype(BF16)
            wbuf[d % 2, d // 2, 512 + 64 * t : 576 + 64 * t, :] = wdown_ref[64 * d : 64 * d + 64, 128 * t : 128 * t + 128].astype(BF16)
    for d in range(2 * n_z):
        qkv = cqkv_ref[32 * d : 32 * d + 32, :]
        out = cout_ref[32 * d : 32 * d + 32, :]
        down = cdown_ref[128 * d : 128 * d + 128, :]
        for p in range(4):
            block = cbuf.at[p % 2, p // 2, d % 2, d // 2]
            part = qkv[:, 192 * p : 192 * p + 192]
            block[0:32, :] = part[:, 0:128].astype(BF16)
            block[32:48, :] = fold_half(part[:, 128:192]).astype(BF16)
            block[48:64, :] = fold_half(out[:, 64 * p : 64 * p + 64]).astype(BF16)
            block[64:96, :] = cup_ref[32 * d : 32 * d + 32, 256 * p : 256 * p + 128].astype(BF16)
            block[96:128, :] = cup_ref[32 * d : 32 * d + 32, 256 * p + 128 : 256 * p + 256].astype(BF16)
            block[128:192, :] = fold_half(down[:, 64 * p : 64 * p + 64]).astype(BF16)
            block[192:224, :] = cproj_ref[32 * d : 32 * d + 32, 128 * p : 128 * p + 128].astype(BF16)
    gains = cg_ref[...].astype(F32)
    rows = []
    for j in range(2):
        total = jnp.sum(cgain_ref[j], 0, keepdims=True) / gains[j : j + 1]
        rows += [total[:, 0:128], total[:, 128:256]]
    total = jnp.sum(cpool_ref[...], 0, keepdims=True)
    rows += [total[:, 0:128], total[:, 128:256]]
    for j in range(2):
        rows += [wgain_ref[j : j + 1, 128 * t : 128 * t + 128] for t in range(4)]
    rows.append(jnp.zeros((2, 128), F32))
    small[0] = jnp.concatenate(rows, 0)

    pl.semaphore_wait(barrier, len(peers) + len(z_peers))
    w_c = send(wbuf.at[1 - x], wr_c, 0, peers[2])
    c_a = send(cbuf.at[1 - core], cr_a, 1, peers[0])
    s_a = send(small.at[0], sr.at[0], 2, peers[0])
    s_a.wait()
    small[1] = small[0] + sr[0]
    s_b = send(small.at[1], sr.at[1], 3, peers[1])
    c_a.wait()
    mine = cbuf.at[core]
    for i in range(2):
        for j in range(2):
            add_into(mine.at[i, j], cr_a.at[i, j], n_z)
    c_b = send(mine.at[1 - y], cr_b, 4, peers[1])
    s_b.wait()
    small[2] = small[1] + sr[1]
    s_c = send(small.at[2], sr.at[2], 5, peers[2])
    w_c.wait()
    wmine = wbuf.at[x]
    add_into(wmine, wr_c, n_z)
    w_d = []
    for k in range(1, n_z):
        w_d.append(send(wmine.at[lax.rem(z + k, n_z)], wr_d.at[k - 1], 5 + k, z_peers[k - 1]))
    c_b.wait()
    mine2 = mine.at[y]
    for j in range(2):
        add_into(mine2.at[j], cr_b.at[j], n_z)
    c_c = send(mine2.at[1 - x], cr_c, 5 + n_z, peers[2])
    s_c.wait()
    small[3] = small[2] + sr[2]
    base = 5 + n_z
    s_d = [send(small.at[3], sr.at[2 + k], base + k, z_peers[k - 1]) for k in range(1, n_z)]
    c_c.wait()
    mine3 = mine2.at[x]
    add_into(mine3, cr_c, n_z)
    base = base + n_z - 1
    c_d = [send(mine3.at[lax.rem(z + k, n_z)], cr_d.at[k - 1], base + k, z_peers[k - 1]) for k in range(1, n_z)]
    for copy in w_d:
        copy.wait()
    word = wmine[z].astype(F32)
    for k in range(n_z - 1):
        word += wr_d[k].astype(F32)
    for t in range(3):
        owqkv_ref[t] = word[64 * t : 64 * t + 64]
    owout_ref[...] = word[192:256].T
    for t in range(4):
        owup_ref[:, 128 * t : 128 * t + 128] = word[256 + 64 * t : 320 + 64 * t]
        owdown_ref[128 * t : 128 * t + 128, :] = word[512 + 64 * t : 576 + 64 * t].T
    for copy in s_d:
        copy.wait()
    total = small[3]
    for k in range(n_z - 1):
        total += sr[3 + k]
    for j in range(2):
        for t in range(2):
            ocgain_ref[j : j + 1, 128 * t : 128 * t + 128] = total[2 * j + t : 2 * j + t + 1]
        for t in range(4):
            owgain_ref[j : j + 1, 128 * t : 128 * t + 128] = total[6 + 4 * j + t : 7 + 4 * j + t]
    for t in range(2):
        opool_ref[:, 128 * t : 128 * t + 128] = total[4 + t : 5 + t]
    for copy in c_d:
        copy.wait()
    char = mine3[z].astype(F32)
    for k in range(n_z - 1):
        char += cr_d[k].astype(F32)
    oqkv_ref[:, 0:128] = char[0:32]
    oqkv_ref[:, 128:192] = unfold_half(char[32:48])
    oout_ref[...] = unfold_half(char[48:64])
    oup_ref[:, 0:128] = char[64:96]
    oup_ref[:, 128:256] = char[96:128]
    odown_ref[...] = unfold_half(char[128:192])
    oproj_ref[...] = char[192:224]


def reduce_grads(n_dp, char_parts, char_gains, word_parts):
    n_z = n_dp // 2
    vm = pl.BlockSpec(memory_space=pltpu.VMEM)
    outs = [(32, 192), (32, 64), (32, 256), (128, 64), (32, 128), (3, 64, 128), (128, 64), (64, 512), (512, 64), (2, 256), (1, 256), (2, 512)]
    args = (*char_parts, char_gains, *word_parts)
    n_sem = 5 + n_z + 2 * (n_z - 1) + 1
    return pl.pallas_call(
        functools.partial(reduce_body, n_z),
        in_specs=[vm] * len(args),
        out_specs=[vm] * len(outs),
        out_shape=[jax.ShapeDtypeStruct(s, F32) for s in outs],
        scratch_shapes=[
            pltpu.VMEM((2, 2, 2, n_z, CHAR_ROWS, 128), BF16),
            pltpu.VMEM((2, 2, n_z, CHAR_ROWS, 128), BF16),
            pltpu.VMEM((2, n_z, CHAR_ROWS, 128), BF16),
            pltpu.VMEM((n_z, CHAR_ROWS, 128), BF16),
            pltpu.VMEM((n_z - 1, CHAR_ROWS, 128), BF16),
            pltpu.VMEM((2, n_z, WORD_ROWS, 128), BF16),
            pltpu.VMEM((n_z, WORD_ROWS, 128), BF16),
            pltpu.VMEM((n_z - 1, WORD_ROWS, 128), BF16),
            pltpu.VMEM((4, 16, 128), F32),
            pltpu.VMEM((2 + n_z, 16, 128), F32),
            pltpu.SemaphoreType.DMA((n_sem,)),
            pltpu.SemaphoreType.DMA((n_sem,)),
        ],
        compiler_params=pltpu.CompilerParams(collective_id=1, has_side_effects=True, vmem_limit_bytes=VMEM_LIMIT),
        name="reduce_gradients",
    )(*args)


HEADS = 8


def norm_rows(values, gain_vec):
    row_mean = jnp.mean(values, -1, keepdims=True)
    centered = values - row_mean
    variance = jnp.mean(centered * centered, -1, keepdims=True)
    return centered * lax.rsqrt(variance + EPSILON) * gain_vec


def flat_dot(left, right):
    return jnp.dot(left, right, preferred_element_type=jnp.float32)


def inner_dot(left, right):
    return lax.dot_general(
        left, right, (((0,), (0,)), ((), ())), preferred_element_type=jnp.float32
    )


def outer_dot(left, right):
    return lax.dot_general(
        left, right, (((1,), (1,)), ((), ())), preferred_element_type=jnp.float32
    )


def gather_rows(rows_in):
    return lax.all_gather(rows_in, "mp", axis=0, tiled=True)


def sum_rows(partial_rows):
    return lax.psum_scatter(partial_rows, "mp", scatter_dimension=0, tiled=True)


def attention_scores(q_block, keys_in, segments, seg_block, block_start, block_rows, scale_value):
    places = jnp.arange(segments.shape[0])
    rows_here = block_start + jnp.arange(block_rows)
    allowed = (places[None, :] <= rows_here[:, None]) & (segments[None, :] == seg_block[:, None])
    scores = (
        jnp.einsum("qhe,khe->hqk", q_block, keys_in, preferred_element_type=jnp.float32)
        * scale_value
    )
    return jnp.where(allowed[None], scores, NEGATIVE)


def word_attention(queries, keys_in, values_in, segments, block_rows):
    length = queries.shape[0]
    scale_value = queries.shape[-1] ** (-0.5)

    def one_block(block_start):
        q_block = lax.dynamic_slice_in_dim(queries, block_start, block_rows, 0)
        seg_block = lax.dynamic_slice_in_dim(segments, block_start, block_rows, 0)
        scores = attention_scores(
            q_block, keys_in, segments, seg_block, block_start, block_rows, scale_value
        )
        row_top = jnp.max(scores, -1, keepdims=True)
        raw_weights = jnp.exp(scores - row_top)
        row_total = jnp.sum(raw_weights, -1, keepdims=True)
        softmaxed = (raw_weights / row_total).astype(jnp.bfloat16)
        result = jnp.einsum(
            "hqk,khe->qhe", softmaxed, values_in, preferred_element_type=jnp.float32
        )
        return (result, (row_top + jnp.log(row_total))[..., 0])

    starts = jnp.arange(length // block_rows) * block_rows
    results, log_totals = lax.map(one_block, starts)
    return (results.reshape(length, queries.shape[1], queries.shape[2]), log_totals)


def word_attention_back(queries, keys_in, values_in, segments, log_totals, d_mixed, block_rows):
    length = queries.shape[0]
    scale_value = queries.shape[-1] ** (-0.5)

    def one_block(sums_carry, block_inputs):
        d_keys, d_values = sums_carry
        block_start, log_block = block_inputs
        q_block = lax.dynamic_slice_in_dim(queries, block_start, block_rows, 0)
        seg_block = lax.dynamic_slice_in_dim(segments, block_start, block_rows, 0)
        d_block = lax.dynamic_slice_in_dim(d_mixed, block_start, block_rows, 0)
        scores = attention_scores(
            q_block, keys_in, segments, seg_block, block_start, block_rows, scale_value
        )
        softmaxed = jnp.exp(scores - log_block[..., None])
        d_soft = jnp.einsum("qhe,khe->hqk", d_block, values_in, preferred_element_type=jnp.float32)
        row_delta = jnp.sum(softmaxed * d_soft, -1, keepdims=True)
        d_scores = (softmaxed * (d_soft - row_delta)).astype(jnp.bfloat16)
        d_query_block = (
            jnp.einsum("hqk,khe->qhe", d_scores, keys_in, preferred_element_type=jnp.float32)
            * scale_value
        )
        d_keys = (
            d_keys
            + jnp.einsum("hqk,qhe->khe", d_scores, q_block, preferred_element_type=jnp.float32)
            * scale_value
        )
        d_values = d_values + jnp.einsum(
            "hqk,qhe->khe",
            softmaxed.astype(jnp.bfloat16),
            d_block,
            preferred_element_type=jnp.float32,
        )
        return ((d_keys, d_values), d_query_block)

    starts = jnp.arange(length // block_rows) * block_rows
    empty = jnp.zeros(keys_in.shape, jnp.float32)
    (d_keys, d_values), d_queries = lax.scan(one_block, (empty, empty), (starts, log_totals))
    return (d_queries.reshape(queries.shape), d_keys, d_values)


def plain_reduce(char_parts, char_gains, word_parts):
    *char_mats, gain_rows, pool_rows = char_parts
    grad_word_qkv, grad_word_out, grad_word_up, grad_word_down, grad_word_gains = word_parts
    gain_sums = jnp.sum(gain_rows, 1) / char_gains.astype(F32)
    small = lax.psum((gain_sums, jnp.sum(pool_rows, 0), grad_word_gains), ("dp", "mp"))
    mats = []
    for grad in char_mats:
        part = lax.psum_scatter(grad, "dp", scatter_dimension=0, tiled=True)
        part = lax.psum_scatter(part.astype(BF16), "mp", scatter_dimension=1, tiled=True)
        mats.append(part.astype(F32))
    return (
        *mats,
        lax.psum_scatter(grad_word_qkv, "dp", scatter_dimension=1, tiled=True),
        lax.psum_scatter(grad_word_out, "dp", scatter_dimension=0, tiled=True).T,
        lax.psum_scatter(grad_word_up, "dp", scatter_dimension=0, tiled=True),
        lax.psum_scatter(grad_word_down, "dp", scatter_dimension=0, tiled=True).T,
        *small,
    )


def per_device(
    char_input,
    char_counts,
    word_source,
    segment_ids,
    cotangent,
    char_norm_gains,
    char_qkv,
    char_out,
    char_up,
    char_down,
    pool_vector,
    char_proj,
    word_norm_gains,
    word_qkv,
    word_out,
    word_up,
    word_down,
):
    words_here = char_counts.shape[0]
    char_width = char_proj.shape[0]
    model_width = word_out.shape[1]
    char_weights = (
        char_norm_gains, char_qkv, char_out, char_up, char_down, pool_vector.reshape(1, -1), char_proj
    )
    word_vec, *char_kept = char_forward(char_input, char_counts.reshape(-1, 1), *char_weights)
    groups = lax.axis_size("dp")
    capacity = (2 * words_here + groups - 1) // groups
    seq_length = words_here * lax.axis_size("mp")
    owner_index = word_source // seq_length
    row_in_owner = word_source % words_here
    owner_hits = (owner_index[:, None] == jnp.arange(groups)[None, :]).astype(jnp.int32)
    earlier_hits = jnp.cumsum(owner_hits, 0) - owner_hits
    slot_rank = jnp.sum(earlier_hits * owner_hits, 1)
    send_slot = owner_index * capacity + slot_rank
    send_vec = (
        jnp.zeros((groups * capacity, model_width), jnp.bfloat16)
        .at[send_slot]
        .set(word_vec.astype(jnp.bfloat16))
    )
    send_rows = (
        jnp.full((groups * capacity,), words_here, jnp.int32).at[send_slot].set(row_in_owner)
    )
    got_vec, got_rows = (
        lax.all_to_all(
            send_vec.reshape(groups, capacity, model_width),
            "dp",
            split_axis=0,
            concat_axis=0,
            tiled=True,
        ),
        lax.all_to_all(
            send_rows.reshape(groups, capacity), "dp", split_axis=0, concat_axis=0, tiled=True
        ),
    )
    got_rows = got_rows.reshape(groups * capacity)
    rows_low = (
        jnp.zeros((words_here, model_width), jnp.bfloat16)
        .at[got_rows]
        .set(got_vec.reshape(groups * capacity, model_width), mode="drop")
    )
    rows_in = rows_low.astype(jnp.float32)
    head_size = model_width // HEADS
    local_heads = word_qkv.shape[2] // head_size
    block_rows = min(512, seq_length)
    gain_first = word_norm_gains[0].astype(jnp.float32)
    gain_second = word_norm_gains[1].astype(jnp.float32)
    normed = norm_rows(rows_in, gain_first).astype(jnp.bfloat16)
    normed_all, segments_all = (
        lax.all_gather(normed, "mp", axis=0, tiled=True),
        lax.all_gather(segment_ids, "mp", axis=0, tiled=True),
    )
    projected = jnp.einsum(
        "ld,kde->kle", normed_all, word_qkv, preferred_element_type=jnp.float32
    ).astype(jnp.bfloat16)
    queries = projected[0].reshape(seq_length, local_heads, head_size)
    keys_in = projected[1].reshape(seq_length, local_heads, head_size)
    values_in = projected[2].reshape(seq_length, local_heads, head_size)
    attended, log_totals = word_attention(queries, keys_in, values_in, segments_all, block_rows)
    mixed_heads = attended.reshape(seq_length, local_heads * head_size).astype(jnp.bfloat16)
    middle = rows_in + sum_rows(flat_dot(mixed_heads, word_out))
    normed_two = norm_rows(middle, gain_second).astype(jnp.bfloat16)
    normed_two_all = gather_rows(normed_two)
    hidden = flat_dot(normed_two_all, word_up)
    activated = jax.nn.gelu(hidden).astype(jnp.bfloat16)
    output = middle + sum_rows(flat_dot(activated, word_down))
    d_output = cotangent.astype(jnp.float32)
    d_branch_all = gather_rows(cotangent)
    grad_word_down = inner_dot(d_branch_all, activated)
    d_activated = outer_dot(d_branch_all, word_down)
    unused_gelu, gelu_back = jax.vjp(jax.nn.gelu, hidden)
    d_hidden = gelu_back(d_activated)[0].astype(jnp.bfloat16)
    grad_word_up = inner_dot(normed_two_all, d_hidden)
    d_normed_two = sum_rows(outer_dot(d_hidden, word_up))
    unused_second, norm_back_second = jax.vjp(norm_rows, middle, gain_second)
    d_middle_norm, grad_gain_second = norm_back_second(d_normed_two)
    d_middle = d_output + d_middle_norm
    d_attended_all = gather_rows(d_middle.astype(jnp.bfloat16))
    grad_word_out = inner_dot(d_attended_all, mixed_heads)
    d_mixed = (
        outer_dot(d_attended_all, word_out)
        .astype(jnp.bfloat16)
        .reshape(seq_length, local_heads, head_size)
    )
    d_queries, d_keys, d_values = word_attention_back(
        queries, keys_in, values_in, segments_all, log_totals, d_mixed, block_rows
    )
    d_projected = (
        jnp.stack([d_queries, d_keys, d_values], 0)
        .reshape(3, seq_length, local_heads * head_size)
        .astype(jnp.bfloat16)
    )
    grad_word_qkv = jnp.einsum(
        "ld,kle->kde", normed_all, d_projected, preferred_element_type=jnp.float32
    )
    d_normed = sum_rows(
        jnp.einsum("kle,kde->ld", d_projected, word_qkv, preferred_element_type=jnp.float32)
    )
    unused_first, norm_back_first = jax.vjp(norm_rows, rows_in, gain_first)
    d_rows_norm, grad_gain_first = norm_back_first(d_normed)
    d_rows = (d_middle + d_rows_norm).astype(jnp.bfloat16)
    back_rows = jnp.take(d_rows, got_rows, axis=0, mode="fill", fill_value=0)
    returned = lax.all_to_all(
        back_rows.reshape(groups, capacity, model_width),
        "dp",
        split_axis=0,
        concat_axis=0,
        tiled=True,
    )
    d_word = returned.reshape(groups * capacity, model_width)[send_slot]
    d_chars, *char_parts = char_backward(d_word, char_kept, *char_weights)
    grad_word_gains = jnp.stack([grad_gain_first, grad_gain_second], 0)
    word_parts = (grad_word_qkv, grad_word_out, grad_word_up, grad_word_down, grad_word_gains)
    if groups == 8:
        reduced = reduce_grads(groups, char_parts, char_norm_gains, word_parts)
    else:
        reduced = plain_reduce(char_parts, char_norm_gains, word_parts)
    (
        grad_qkv, grad_out, grad_up, grad_down, grad_proj,
        grad_word_qkv, grad_word_out, grad_word_up, grad_word_down,
        grad_char_gains, grad_pool, grad_word_gains,
    ) = reduced
    return (
        output.astype(jnp.bfloat16),
        d_chars,
        grad_qkv,
        grad_out,
        grad_up,
        grad_down,
        grad_proj,
        grad_word_qkv,
        grad_word_out,
        grad_word_up,
        grad_word_down,
        grad_char_gains,
        grad_pool.reshape(-1),
        grad_word_gains,
    )


def solution(mesh):
    placed = (
        P(("dp", "mp"), None),
        P(("dp", "mp")),
        P(("dp", "mp")),
        P(("dp", "mp")),
        P(("dp", "mp"), None),
        P(),
        P(),
        P(),
        P(),
        P(),
        P(),
        P(),
        P(),
        P(None, None, "mp"),
        P("mp", None),
        P(None, "mp"),
        P("mp", None),
    )
    return jax.shard_map(
        per_device,
        mesh=mesh,
        in_specs=placed,
        out_specs=(
            P(("dp", "mp"), None),
            P(("dp", "mp"), None),
            P("dp", "mp"),
            P("dp", "mp"),
            P("dp", "mp"),
            P("dp", "mp"),
            P("dp", "mp"),
            P(None, "dp", "mp"),
            P("mp", "dp"),
            P("dp", "mp"),
            P("mp", "dp"),
            P(),
            P(),
            P(),
        ),
        check_vma=False,
    )
```

time: 1240 us -> 497 us (0.40)
  waiting for transfers between devices: 688 us -> 197 us
  local copies, waits for them, and re-layouts: 181 us -> 40.6 us
  Pallas kernels: 0 us -> 129 us
  matrix products: 172 us -> 47.6 us
  other arithmetic: 102 us -> 26.7 us
  blocking collectives: 44.8 us -> 5.24 us
    reduce_scatter x9 -> x0, waiting for transfers between devices: 412 us -> none  [the longest x1 66.5 us: per_device(): lax.psum_scatter(grad_word_up, 'dp', scatter_dimension=0, tiled=True)]
    pallas_call x0 -> x3, Pallas kernels: none -> 129 us  [the longest x1 46.4 us: reduce_grads(): pl.pallas_call(functools.partial(reduce_body, n_z), in_specs=[vm] * len(a...]
    unnamed x27 -> x8, waiting for transfers between devices: 93.4 us -> 0.8 us
    convert_element_type x4 -> x0, local copies, waits for them, and re-layouts: 45.7 us -> none  [the longest x2 38.6 us: char_backward(): d_projected = jnp.stack([d_queries, d_keys, d_values], 2).astype(jnp.bflo...]
    dot_general x6 -> x0, matrix products: 43.7 us -> none  [the longest x1 13.2 us: char_backward(): jnp.einsum('wqhe,wkhe->whqk', d_mixed, values_in, preferred_element_type=...]
    psum x1 -> x0, blocking collectives: 39.7 us -> none  [per_device(): lax.psum((grad_char_gains, grad_pool, grad_word_gains), ('dp', 'mp'))]
    reshape x5 -> x2, local copies, waits for them, and re-layouts: 41.3 us -> 2.69 us  [the longest x1 1.47 us: per_device(): char_counts.reshape(-1, 1)]
    dot_general x8 -> x3, matrix products: 38.3 us -> 7.11 us  [outer_dot(): lax.dot_general(left, right, (((1,), (1,)), ((), ())), preferred_element_...]
  transfers between devices with their start and end apart: 25 -> 11, of which waited for: 21 -> 10; matrix products, arithmetic and copies ran while one was open for 25% -> 6% of each run, Pallas kernels for 0% -> 8%
where the time goes in v1:
time: 497 us; the launch traced here: 489 us
  waiting for transfers between devices  197 us (40%)
  Pallas kernels  129 us (26%)
  matrix products  47.6 us (10%)
  local copies, waits for them, and re-layouts  40.6 us (8%)
  other arithmetic  26.7 us (5%)
  starting transfers between devices  19.6 us (4%)
  between operations  15.3 us (3%)
  loops' own time  7.87 us (2%)
  blocking collectives  5.24 us (1%)
    reduce_scatter x4, waiting for transfers between devices, sum_rows(): return lax.psum_scatter(partial_rows, 'mp', scatter_dimension=0, tiled=True)  117 us
    all_gather x3, waiting for transfers between devices, gather_rows(): return lax.all_gather(rows_in, 'mp', axis=0, tiled=True)  48.2 us
    pallas_call x1, Pallas kernels, reduce_grads(): pl.pallas_call(functools.partial(reduce_body, n_z), in_specs=[vm] * len(a...  46.4 us
    pallas_call x1, Pallas kernels, char_backward(): pl.pallas_call(char_bwd_body, grid=(steps,), in_specs=[blk(step_words, de...  43.5 us
    pallas_call x1, Pallas kernels, char_forward(): pl.pallas_call(char_fwd_body, grid=(words // step_words,), in_specs=[blk(...  39 us
    unnamed x84, local copies, waits for them, and re-layouts  20.2 us
    all_to_all x1, waiting for transfers between devices, per_device(): lax.all_to_all(send_vec.reshape(groups, capacity, model_width), 'dp', spl...  12.6 us
    dot_general x3, matrix products, flat_dot(): return jnp.dot(left, right, preferred_element_type=jnp.float32)  10.5 us
  transfers between devices with their start and end apart: 11, of which 10 were waited for; matrix products, arithmetic and copies ran while one was open for 6% of the time, Pallas kernels for 8%

profile of v1, /device:TPU:0, one launch (start us, length us, event | category | flops | bytes accessed | tf_op | source)
XLA Modules:
  0.0 488.8 jit_solution(4844293416363624795)
XLA Ops:
  11.0 7.3 %all-to-all-start = ((s32[8,1,64]{2,1,0:T(1,128)}), s32[8,1,64]{2,1,0:T(1,128)S(1)}, u32[]{:S(2)}, u32[]{:S(2)}) async-start(s32[8,1,64]{2,1,0:T(1,128)} %all_to_all.12), calls=%async_computation | async-start | bytes 8192 | tf_op jit(solution)/shard_map/all_to_all | solution.py:603
  20.9 39.0 %char_forward.1 = (bf16[256,512]{1,0:T(8,128)(2,1)}, bf16[4096,256]{1,0:T(8,128)(2,1)}, bf16[4096,768]{1,0:T(8,128)(2,1)}, bf16[16384,128]{1,0:T(8,128)(2,1)}, b...) custom-call(bf16[256,4096]{1,0:T(8,128)(2,1)} %x_ref.1, ...), custom_call_target="tpu_custom_call" | custom-call | tf_op jit(solution)/shard_map/char_forward/pallas_call | solution.py:133
  62.7 6.0 %all-to-all-start.1 = ((bf16[8,64,512]{2,1,0:T(8,128)(2,1)}), bf16[8,64,512]{2,1,0:T(8,128)(2,1)S(1)}, u32[]{:S(2)}, u32[]{:S(2)}) async-start(bf16[8,64,512]{2,1,0:T(8,128)(2,1)} %bitcast.9), calls=%async_computation.1 | async-start | bytes 1048576 | tf_op jit(solution)/shard_map/all_to_all | solution.py:596
  70.1 12.6 %all-to-all-done.1 = bf16[8,64,512]{2,1,0:T(8,128)(2,1)S(1)} async-done(((bf16[8,64,512]{2,1,0:T(8,128)(2,1)}), bf16[8,64,512]{2,1,0:T(8,128)(2,1)S(1)}, u32[]{:S(2)}, u32[]{:S(2)}) %all-to-all-start.1) | async-done | bytes 524320 | tf_op jit(solution)/shard_map/all_to_all | solution.py:596
  86.7 5.2 %all-gather = s32[4,1,256]{2,1,0:T(1,128)S(1)} all-gather(s32[1,1,256]{2,1,0:T(1,128)S(1)} %bitcast.163), channel_id=1, replica_groups=mesh['dp'=8,'mp'=4] {'mp'}, dimensions={0}, use_global_device_ids=true | all-gather | bytes 5120 | tf_op jit(solution)/shard_map/all_gather | solution.py:622
  91.9 10.4 %all-gather.6.cloned.1.call-done = bf16[1024,512]{1,0:T(8,128)(2,1)} async-done(((bf16[256,512]{1,0:T(8,128)(2,1)}), bf16[1024,512]{1,0:T(8,128)(2,1)}) %all-gather.6.cloned.1.call-update) | async-done | bytes 1048592 | tf_op jit(solution)/shard_map/all_gather | solution.py:621
  104.5 15.2 %while.27 = (s32[]{:T(128)}, bf16[2,512,2,64]{1,3,2,0:T(8,128)(2,1)S(1)}, f32[2,2,512]{2,1,0:T(2,128)S(1)}, s32[2]{0:T(128)S(1)}, s32[1024]{0:T(1024)S(1)}, /*in...) while((s32[]{:T(128)}, ...), condition=%wide.region_11.12_spmd, body=%wide.region_8.11_spmd.sunk | while | flops 282590720 | bytes 15644855 | solution.py:488
  122.7 30.8 %reduce-scatter.5.cloned.1.call-done = f32[256,512]{1,0:T(8,128)} async-done(((f32[1024,512]{1,0:T(8,128)}), f32[256,512]{1,0:T(8,128)}) %reduce-scatter.5.cloned.1.call-update) | async-done | bytes 524304 | tf_op jit(solution)/shard_map/reduce_scatter | solution.py:454
  155.8 16.1 %all-gather.10.cloned.1.call-done = bf16[1024,512]{1,0:T(8,128)(2,1)} async-done(((bf16[256,512]{1,0:T(8,128)(2,1)}), bf16[1024,512]{1,0:T(8,128)(2,1)}) %all-gather.10.cloned.1.call-update) | async-done | bytes 1048592 | tf_op jit(solution)/shard_map/all_gather | solution.py:450
  171.9 3.3 fusion.77
  175.2 15.5 %all-gather.8.cloned.1.call-done = bf16[1024,512]{1,0:T(8,128)(2,1)} async-done(((bf16[256,512]{1,0:T(8,128)(2,1)}), bf16[1024,512]{1,0:T(8,128)(2,1)}) %all-gather.8.cloned.1.call-update) | async-done | bytes 1048592 | tf_op jit(solution)/shard_map/all_gather | solution.py:450
  190.7 5.0 %fusion.44 = (bf16[1024,512]{1,0:T(8,128)(2,1)S(1)}, f32[1024,512]{1,0:T(8,128)}) fusion(f32[1024,512]{1,0:T(8,128)} %fusion.77, bf16[1024,512]{1,0:T(8,128)(2,1)} %all-gather.8.cloned.1.call-done, bf16[512,512]{1,0:T(8,128)(2,1)S(1)} %copy-done), kind=kOutput, calls=%fused_computation.60 | convolution fusion | flops 547356672 | bytes 6815744 | tf_op jit(solution)/shard_map/dot_general | solution.py:434
  198.9 3.7 fusion.71
  202.7 27.7 %reduce-scatter.9.cloned.1.call-done = f32[256,512]{1,0:T(8,128)} async-done(((f32[1024,512]{1,0:T(8,128)}), f32[256,512]{1,0:T(8,128)}) %reduce-scatter.9.cloned.1.call-update) | async-done | bytes 524304 | tf_op jit(solution)/shard_map/reduce_scatter | solution.py:454
  232.3 32.0 %reduce-scatter.7.cloned.1.call-done = f32[256,512]{1,0:T(8,128)} async-done(((f32[1024,512]{1,0:T(8,128)}), f32[256,512]{1,0:T(8,128)}) %reduce-scatter.7.cloned.1.call-update) | async-done | bytes 524304 | tf_op jit(solution)/shard_map/reduce_scatter | solution.py:454
  267.5 16.6 %all-gather.12.cloned.1.call-done = bf16[1024,512]{1,0:T(8,128)(2,1)} async-done(((bf16[256,512]{1,0:T(8,128)(2,1)}), bf16[1024,512]{1,0:T(8,128)(2,1)}) %all-gather.12.cloned.1.call-update) | async-done | bytes 1048592 | tf_op jit(solution)/shard_map/all_gather | solution.py:450
  285.8 23.1 %while.28 = (s32[]{:T(128)}, f32[1024,2,64]{0,2,1:T(8,128)S(1)}, f32[1024,2,64]{0,2,1:T(8,128)}, bf16[2,512,2,64]{1,3,2,0:T(8,128)(2,1)S(1)}, s32[2]{0:T(128)}, ...) while((s32[]{:T(128)}, f32[1024,2,64]{0,2,1:T(8,128)S(1)}, ...), condition=%wide.region_21.22_spmd.clone, body=%wide.region_19.21_spmd.clone.sunk | while | flops 689110528 | bytes 41462044 | solution.py:528
  315.2 3.7 convolution_bitcast_fusion.1.wdown_ref
  318.9 26.7 %reduce-scatter.11.cloned.1.call-done = f32[256,512]{1,0:T(8,128)} async-done(((f32[1024,512]{1,0:T(8,128)}), f32[256,512]{1,0:T(8,128)}) %reduce-scatter.11.cloned.1.call-update) | async-done | bytes 524304 | tf_op jit(solution)/shard_map/reduce_scatter | solution.py:454
  352.5 5.8 %all-to-all-start.2 = ((bf16[8,64,512]{2,1,0:T(8,128)(2,1)}), bf16[8,64,512]{2,1,0:T(8,128)(2,1)S(1)}, u32[]{:S(2)}, u32[]{:S(2)}) async-start(bf16[8,64,512]{2,1,0:T(8,128)(2,1)} %broadcast_select_fusion), calls=%async_computation.6 | async-start | bytes 1048576 | tf_op jit(solution)/shard_map/all_to_all | solution.py:674
  358.3 3.1 fusion.80.wup_ref
  364.9 7.8 %all-to-all-done.2 = bf16[8,64,512]{2,1,0:T(8,128)(2,1)S(1)} async-done(((bf16[8,64,512]{2,1,0:T(8,128)(2,1)}), bf16[8,64,512]{2,1,0:T(8,128)(2,1)S(1)}, u32[]{:S(2)}, u32[]{:S(2)}) %all-to-all-start.2) | async-done | bytes 524320 | tf_op jit(solution)/shard_map/all_to_all | solution.py:674
  374.6 43.5 %char_backward.1 = (f32[256,4096]{1,0:T(8,128)}, f32[256,768]{1,0:T(8,128)}, f32[256,256]{1,0:T(8,128)}, f32[256,1024]{1,0:T(8,128)}, f32[1024,256]{1,0:T(8,128)...) custom-call(bf16[256,512]{1,0:T(8,128)(2,1)} %gather_fusion.1, bf16[2,256]{1,0:T(2,128)(2,1)} %cg_ref.1, ...), custom_call_target="tpu_custom_call" | custom-call | tf_op jit(solution)/shard_map/char_backward/pallas_call | solution.py:226
  418.1 46.4 %reduce_gradients.1 = (f32[32,192]{1,0:T(8,128)}, f32[32,64]{1,0:T(8,128)}, f32[32,256]{1,0:T(8,128)}, f32[128,64]{1,0:T(8,128)}, f32[32,128]{1,0:T(8,128)}, /*i...) custom-call(f32[256,768]{1,0:T(8,128)} %get-tuple-element.168.cqkv_r, ...), custom_call_target="tpu_custom_call" | custom-call | tf_op jit(solution)/shard_map/reduce_gradients/pallas_call | solution.py:399
  (215 shorter events, 97.5 us)
Async XLA Ops:
  7.2 183.5 %copy-start = (bf16[512,512]{1,0:T(8,128)(2,1)S(1)}, bf16[512,512]{1,0:T(8,128)(2,1)}, u32[]{:S(2)}) copy-start(bf16[512,512]{1,0:T(8,128)(2,1)} %param.36) | copy-start | bytes 1572868
  8.9 51.1 %copy-start.33 = (s32[256]{0:T(256)}, s32[256]{0:T(256)S(1)}, u32[]{:S(2)}) copy-start(s32[256]{0:T(256)S(1)} %compare_select_fusion.2) | copy-start | bytes 3076
  11.0 51.7 %all-to-all-start = ((s32[8,1,64]{2,1,0:T(1,128)}), s32[8,1,64]{2,1,0:T(1,128)S(1)}, u32[]{:S(2)}, u32[]{:S(2)}) async-start(s32[8,1,64]{2,1,0:T(1,128)} %all_to_all.12), calls=%async_computation | async-start | bytes 8192 | tf_op jit(solution)/shard_map/all_to_all | solution.py:603
  20.9 47.8 %copy-start.32 = (bf16[2,512]{1,0:T(2,128)(2,1)S(1)}, bf16[2,512]{1,0:T(2,128)(2,1)}, u32[]{:S(2)}) copy-start(bf16[2,512]{1,0:T(2,128)(2,1)} %param.33) | copy-start | bytes 6148
  59.9 26.5 %copy-start.4 = (bf16[3,512,128]{2,1,0:T(8,128)(2,1)S(1)}, bf16[3,512,128]{2,1,0:T(8,128)(2,1)}, u32[]{:S(2)}) copy-start(bf16[3,512,128]{2,1,0:T(8,128)(2,1)} %param.34) | copy-start | bytes 1179652
  60.0 26.7 %copy-start.35 = (s32[256]{0:T(256)S(1)}, s32[256]{0:T(256)}, u32[]{:S(2)}) copy-start(s32[256]{0:T(256)} %param.24) | copy-start | bytes 3076
  62.7 20.0 %copy-start.21 = (s32[8,1,64]{2,1,0:T(1,128)}, s32[8,1,64]{2,1,0:T(1,128)S(1)}, u32[]{:S(2)}) copy-start(s32[8,1,64]{2,1,0:T(1,128)S(1)} %all-to-all-done) | copy-start | bytes 6148
  62.7 20.0 %all-to-all-start.1 = ((bf16[8,64,512]{2,1,0:T(8,128)(2,1)}), bf16[8,64,512]{2,1,0:T(8,128)(2,1)S(1)}, u32[]{:S(2)}, u32[]{:S(2)}) async-start(bf16[8,64,512]{2,1,0:T(8,128)(2,1)} %bitcast.9), calls=%async_computation.1 | async-start | bytes 1048576 | tf_op jit(solution)/shard_map/all_to_all | solution.py:596
  68.7 33.7 %all-gather.6.cloned.1.call-start = ((), (), s32[]{:S(2)}) async-start(), calls=%async_computation.7 | async-start | bytes 1310720 | tf_op jit(solution)/shard_map/all_gather | solution.py:621
  86.4 67.0 %reduce-scatter.5.cloned.1.call-start = ((), (), s32[]{:S(2)}) async-start(), calls=%async_computation.8 | async-start | bytes 2621440 | tf_op jit(solution)/shard_map/reduce_scatter | solution.py:454
  121.9 50.0 %copy-start.15 = (bf16[512,512]{1,0:T(8,128)(2,1)S(1)}, bf16[512,512]{1,0:T(8,128)(2,1)}, u32[]{:S(2)}) copy-start(bf16[512,512]{1,0:T(8,128)(2,1)} %param.37) | copy-start | bytes 1572868
  121.9 50.0 %all-gather.10.cloned.1.call-start = ((), (), s32[]{:S(2)}) async-start(), calls=%async_computation.11 | async-start | bytes 1310720 | tf_op jit(solution)/shard_map/all_gather | solution.py:450
  122.6 68.1 %all-gather.8.cloned.1.call-start = ((), (), s32[]{:S(2)}) async-start(), calls=%async_computation.9 | async-start | bytes 1310720 | tf_op jit(solution)/shard_map/all_gather | solution.py:450
  155.7 74.7 %reduce-scatter.9.cloned.1.call-start = ((), (), s32[]{:S(2)}) async-start(), calls=%async_computation.12 | async-start | bytes 2621440 | tf_op jit(solution)/shard_map/reduce_scatter | solution.py:454
  198.8 65.4 %reduce-scatter.7.cloned.1.call-start = ((), (), s32[]{:S(2)}) async-start(), calls=%async_computation.10 | async-start | bytes 2621440 | tf_op jit(solution)/shard_map/reduce_scatter | solution.py:454
  202.6 63.8 %copy-start.3 = (bf16[256,512]{1,0:T(8,128)(2,1)S(1)}, bf16[256,512]{1,0:T(8,128)(2,1)}, u32[]{:S(2)}) copy-start(bf16[256,512]{1,0:T(8,128)(2,1)} %param.25) | copy-start | bytes 786436
  202.6 81.5 %all-gather.12.cloned.1.call-start = ((), (), s32[]{:S(2)}) async-start(), calls=%async_computation.13 | async-start | bytes 1310720 | tf_op jit(solution)/shard_map/all_gather | solution.py:450
  267.2 78.4 %reduce-scatter.11.cloned.1.call-start = ((), (), s32[]{:S(2)}) async-start(), calls=%async_computation.14 | async-start | bytes 2621440 | tf_op jit(solution)/shard_map/reduce_scatter | solution.py:454
  315.2 30.4 %copy-start.20 = (f32[256]{0:T(256)S(1)}, f32[256]{0:T(256)}, u32[]{:S(2)}) copy-start(f32[256]{0:T(256)} %copy-done.19) | copy-start | bytes 3076
  315.2 31.6 %copy-start.28 = (f32[256]{0:T(256)S(1)}, f32[256]{0:T(256)}, u32[]{:S(2)}) copy-start(f32[256]{0:T(256)} %copy-done.27) | copy-start | bytes 3076
  315.2 31.7 %copy-start.24 = (f32[256]{0:T(256)S(1)}, f32[256]{0:T(256)}, u32[]{:S(2)}) copy-start(f32[256]{0:T(256)} %copy-done.23) | copy-start | bytes 3076
  315.2 33.1 %copy-start.26 = (f32[256]{0:T(256)S(1)}, f32[256]{0:T(256)}, u32[]{:S(2)}) copy-start(f32[256]{0:T(256)} %copy-done.25) | copy-start | bytes 3076
  352.5 20.2 %all-to-all-start.2 = ((bf16[8,64,512]{2,1,0:T(8,128)(2,1)}), bf16[8,64,512]{2,1,0:T(8,128)(2,1)S(1)}, u32[]{:S(2)}, u32[]{:S(2)}) async-start(bf16[8,64,512]{2,1,0:T(8,128)(2,1)} %broadcast_select_fusion), calls=%async_computation.6 | async-start | bytes 1048576 | tf_op jit(solution)/shard_map/all_to_all | solution.py:674
  418.1 63.5 %copy-start.1 = (bf16[512,512]{1,0:T(8,128)(2,1)S(1)}, bf16[512,512]{1,0:T(8,128)(2,1)}, u32[]{:S(2)}) copy-start(bf16[512,512]{1,0:T(8,128)(2,1)} %param.36) | copy-start | bytes 1572868
  (26 other events, 140.9 us)
Sparse Core Ops, SparseCore 0:
  86.5 15.7 all-gather.5
  122.0 31.4 reduce-scatter.4
  155.1 16.7 all-gather.9
  173.9 16.7 all-gather.7
  198.9 31.4 reduce-scatter.8
  232.8 31.4 reduce-scatter.6
  267.3 16.7 all-gather.11
  314.1 31.4 reduce-scatter.10

commit v2 on v1

v2 whole, which is shorter than its diff:
```python
import functools
import jax
import jax.numpy as jnp
from jax import lax
from jax.experimental import pallas as pl
from jax.experimental.pallas import tpu as pltpu
from jax.sharding import PartitionSpec as P

HEADS = 8
CHARS = 16
CHAR_HEADS = 4
EPSILON = 1e-05
NEGATIVE = -1e30
GELU_A = 0.7978845608028654
GELU_B = 0.044715
F32 = jnp.float32
BF16 = jnp.bfloat16
VMEM_LIMIT = 60 * 1024 * 1024


def dot_nn(left, right):
    return jnp.dot(left, right, preferred_element_type=F32)


def dot_nt(left, right):
    return lax.dot_general(left, right, (((1,), (1,)), ((), ())), preferred_element_type=F32)


def dot_tn(left, right):
    return lax.dot_general(left, right, (((0,), (0,)), ((), ())), preferred_element_type=F32)


def head_stack(values, heads, factor):
    width = values.shape[1] // heads
    lane = lax.broadcasted_iota(jnp.int32, (1, values.shape[1]), 1) // width
    return jnp.concatenate(
        [values * jnp.where(lane == h, factor, 0.0).astype(values.dtype) for h in range(heads)], 0
    )


def gelu_both(hidden):
    square = hidden * hidden
    inner = hidden * (GELU_A + (GELU_A * GELU_B) * square)
    tanh = jnp.tanh(inner)
    half = 0.5 + 0.5 * tanh
    slope = half + (0.5 * hidden) * (1.0 - tanh * tanh) * (GELU_A + (3.0 * GELU_A * GELU_B) * square)
    return hidden * half, slope


def char_fwd_body(
    x_ref, cnt_ref, gains_ref, wqkv_ref, wout_ref, wup_ref, wdown_ref, pool_ref, wproj_ref,
    e_ref, n1_ref, p_ref, a_ref, o_ref, n2_ref, rs1_ref, rs2_ref, act_ref, dg_ref, f_ref, aw_ref, pooled_ref,
):
    words, wide = x_ref.shape
    width = wide // CHARS
    blocks = words // 8
    gains = gains_ref[...].astype(F32)
    pieces = []
    for g in range(words // 16):
        xt = x_ref[16 * g : 16 * g + 16, :].astype(F32)
        for half in range(2):
            for c in range(CHARS):
                pieces.append(xt[8 * half : 8 * half + 8, width * c : width * c + width])
    x = jnp.concatenate(pieces, 0)

    def norm(v, gain):
        mean = jnp.mean(v, -1, keepdims=True)
        centered = v - mean
        rstd = lax.rsqrt(jnp.mean(centered * centered, -1, keepdims=True) + EPSILON)
        return (centered * rstd * gain).astype(BF16), rstd

    n1, rs1 = norm(x, gains[0:1])
    n1_ref[...] = n1
    rs1_ref[...] = rs1
    p_ref[...] = dot_nn(n1, wqkv_ref[...]).astype(BF16)
    row_w = lax.broadcasted_iota(jnp.int32, (8, 128), 0)
    lane_w = lax.broadcasted_iota(jnp.int32, (8, 128), 1) % 8
    same = row_w == lane_w
    slot = lax.broadcasted_iota(jnp.int32, (CHARS, 8, 128), 0)
    for b in range(blocks):
        rows = slice(128 * b, 128 * b + 128)
        counts = jnp.broadcast_to(cnt_ref[8 * b : 8 * b + 8, :], (8, 128))
        here = slot < counts[None]
        q = p_ref[rows, 0:width]
        k = p_ref[rows, width : 2 * width]
        v = p_ref[rows, 2 * width : 3 * width]
        st = dot_nt(head_stack(k, CHAR_HEADS, (width // CHAR_HEADS) ** -0.5), q)
        st = st.reshape(CHAR_HEADS, CHARS, 8, 128)
        st = jnp.where(here[None], st, NEGATIVE)
        e = jnp.exp(st - jnp.max(st, 1, keepdims=True))
        r = jnp.where(same[None, None], 1.0 / jnp.sum(e, 1, keepdims=True), 0.0)
        a = (e * r).reshape(CHAR_HEADS * 128, 128).astype(BF16)
        a_ref[CHAR_HEADS * 128 * b : CHAR_HEADS * 128 * (b + 1), :] = a
        o_ref[rows, :] = dot_tn(a, head_stack(v, CHAR_HEADS, 1.0)).astype(BF16)
    m = x + dot_nn(o_ref[...], wout_ref[...])
    n2, rs2 = norm(m, gains[1:2])
    n2_ref[...] = n2
    rs2_ref[...] = rs2
    act, slope = gelu_both(dot_nn(n2, wup_ref[...]))
    act = act.astype(BF16)
    act_ref[...] = act
    dg_ref[...] = slope.astype(BF16)
    f = m + dot_nn(act, wdown_ref[...])
    f_ref[...] = f.astype(BF16)
    t = jnp.sum(f * pool_ref[...].astype(F32), -1, keepdims=True).reshape(blocks, CHARS, 8, 1)
    counts = cnt_ref[...].reshape(blocks, 1, 8, 1)
    t = jnp.where(lax.broadcasted_iota(jnp.int32, t.shape, 1) < counts, t, NEGATIVE)
    et = jnp.exp(t - jnp.max(t, 1, keepdims=True))
    aw = et / jnp.sum(et, 1, keepdims=True)
    aw_ref[...] = aw.reshape(words * CHARS, 1)
    pooled = jnp.sum(aw * f.reshape(blocks, CHARS, 8, width), 1).reshape(words, width).astype(BF16)
    pooled_ref[...] = pooled
    e_ref[...] = dot_nn(pooled, wproj_ref[...]).astype(BF16)


def char_forward(x, counts, gains, wqkv, wout, wup, wdown, pool, wproj, step_words=32):
    words, wide = x.shape
    width = wide // CHARS
    rows = words * CHARS
    step_rows = step_words * CHARS
    full = lambda arr: pl.BlockSpec(arr.shape, lambda i: (0,) * arr.ndim)
    blk = lambda n, w: pl.BlockSpec((n, w), lambda i: (i, 0))
    hid = wup.shape[1]
    dw = wproj.shape[1]
    outs = [
        (words, step_words, dw, BF16), (rows, step_rows, width, BF16), (rows, step_rows, 3 * width, BF16),
        (rows * CHAR_HEADS, step_rows * CHAR_HEADS, 128, BF16), (rows, step_rows, width, BF16),
        (rows, step_rows, width, BF16), (rows, step_rows, 1, F32), (rows, step_rows, 1, F32),
        (rows, step_rows, hid, BF16), (rows, step_rows, hid, BF16), (rows, step_rows, width, BF16),
        (rows, step_rows, 1, F32), (words, step_words, width, BF16),
    ]
    return pl.pallas_call(
        char_fwd_body,
        grid=(words // step_words,),
        in_specs=[blk(step_words, wide), blk(step_words, 1)] + [full(w) for w in (gains, wqkv, wout, wup, wdown, pool, wproj)],
        out_specs=[blk(b, w) for _, b, w, _ in outs],
        out_shape=[jax.ShapeDtypeStruct((n, w), d) for n, _, w, d in outs],
        compiler_params=pltpu.CompilerParams(vmem_limit_bytes=VMEM_LIMIT),
        name="char_forward",
    )(x, counts, gains, wqkv, wout, wup, wdown, pool, wproj)


def char_bwd_body(
    de_ref, gains_ref, wqkv_ref, wout_ref, wup_ref, wdown_ref, pool_ref, wproj_ref,
    n1_ref, p_ref, a_ref, o_ref, n2_ref, rs1_ref, rs2_ref, act_ref, dg_ref, f_ref, aw_ref, pooled_ref,
    dx_ref, gqkv_ref, gout_ref, gup_ref, gdown_ref, gproj_ref, ggain_ref, gpool_ref,
    dp_ref, do_ref,
):
    words = de_ref.shape[0]
    width = n1_ref.shape[1]
    blocks = words // 8
    rows = words * CHARS
    gains = gains_ref[...].astype(F32)

    @pl.when(pl.program_id(0) == 0)
    def _():
        for ref in (gqkv_ref, gout_ref, gup_ref, gdown_ref, gproj_ref, ggain_ref, gpool_ref):
            ref[...] = jnp.zeros_like(ref)

    de = de_ref[...]
    gproj_ref[...] += dot_tn(pooled_ref[...], de)
    dpool = dot_nt(de, wproj_ref[...]).reshape(blocks, 1, 8, width)
    f = f_ref[...].astype(F32).reshape(blocks, CHARS, 8, width)
    aw = aw_ref[...].reshape(blocks, CHARS, 8, 1)
    g = jnp.sum(f * dpool, -1, keepdims=True)
    dt = aw * (g - jnp.sum(aw * g, 1, keepdims=True))
    gpool_ref[...] += jnp.sum((dt * f).reshape(rows // 8, 8, width), 0)
    df = (aw * dpool + dt * pool_ref[...].astype(F32)).reshape(rows, width)
    dfb = df.astype(BF16)
    gdown_ref[...] += dot_tn(act_ref[...], dfb)
    dh = (dg_ref[...].astype(F32) * dot_nt(dfb, wdown_ref[...])).astype(BF16)
    n2 = n2_ref[...]
    gup_ref[...] += dot_tn(n2, dh)
    dn2 = dot_nt(dh, wup_ref[...])

    def norm_back(dn, n, rstd, gain, row):
        d1 = dn * gain
        dnn = dn * n.astype(F32)
        ggain_ref[row] += jnp.sum(dnn.reshape(rows // 8, 8, width), 0)
        m1 = jnp.mean(d1, -1, keepdims=True)
        m2 = jnp.mean(dnn, -1, keepdims=True)
        return rstd * (d1 - m1 - n.astype(F32) * (1.0 / gain) * m2)

    dm = df + norm_back(dn2, n2, rs2_ref[...], gains[1:2], 1)
    dmb = dm.astype(BF16)
    gout_ref[...] += dot_tn(o_ref[...], dmb)
    do_ref[...] = dot_nt(dmb, wout_ref[...]).astype(BF16)
    scale = (width // CHAR_HEADS) ** -0.5
    for b in range(blocks):
        sl = slice(128 * b, 128 * b + 128)
        q = p_ref[sl, 0:width]
        k = p_ref[sl, width : 2 * width]
        v = p_ref[sl, 2 * width : 3 * width]
        do = do_ref[sl, :]
        ab = a_ref[CHAR_HEADS * 128 * b : CHAR_HEADS * 128 * (b + 1), :]
        a = ab.astype(F32).reshape(CHAR_HEADS, CHARS, 8, 128)
        dpt = dot_nt(head_stack(v, CHAR_HEADS, 1.0), do).reshape(CHAR_HEADS, CHARS, 8, 128)
        delta = jnp.sum(a * dpt, 1, keepdims=True)
        ds = (a * (dpt - delta)).reshape(CHAR_HEADS * 128, 128).astype(BF16)
        wide_ds = jnp.concatenate([ds[128 * h : 128 * h + 128] for h in range(CHAR_HEADS)], 1)
        wide_a = jnp.concatenate([ab[128 * h : 128 * h + 128] for h in range(CHAR_HEADS)], 1)
        dp_ref[sl, 0:width] = dot_tn(ds, head_stack(k, CHAR_HEADS, scale)).astype(BF16)
        dp_ref[sl, width : 2 * width] = dot_nn(wide_ds, head_stack(q, CHAR_HEADS, scale)).astype(BF16)
        dp_ref[sl, 2 * width : 3 * width] = dot_nn(wide_a, head_stack(do, CHAR_HEADS, 1.0)).astype(BF16)
    n1 = n1_ref[...]
    dp = dp_ref[...]
    gqkv_ref[...] += dot_tn(n1, dp)
    dn1 = dot_nt(dp, wqkv_ref[...])
    dx = dm + norm_back(dn1, n1, rs1_ref[...], gains[0:1], 0)
    for b in range(blocks):
        for c in range(CHARS):
            dx_ref[8 * b : 8 * b + 8, width * c : width * c + width] = dx[128 * b + 8 * c : 128 * b + 8 * c + 8]


def char_backward(de, kept, gains, wqkv, wout, wup, wdown, pool, wproj, step_words=32):
    words = de.shape[0]
    width = wout.shape[0]
    rows = words * CHARS
    step_rows = step_words * CHARS
    full = lambda arr: pl.BlockSpec(arr.shape, lambda i: (0,) * arr.ndim)
    blk = lambda n, w: pl.BlockSpec((n, w), lambda i: (i, 0))
    steps = words // step_words
    weights = (gains, wqkv, wout, wup, wdown, pool, wproj)
    outs = [wqkv.shape, wout.shape, wup.shape, wdown.shape, wproj.shape, (2, 8, width), (8, width)]
    return pl.pallas_call(
        char_bwd_body,
        grid=(steps,),
        in_specs=[blk(step_words, de.shape[1])] + [full(w) for w in weights]
        + [blk(r.shape[0] // steps, r.shape[1]) for r in kept],
        out_specs=[blk(step_words, CHARS * width)]
        + [pl.BlockSpec(s, lambda i, n=len(s): (0,) * n) for s in outs],
        out_shape=[jax.ShapeDtypeStruct((words, CHARS * width), F32)]
        + [jax.ShapeDtypeStruct(s, F32) for s in outs],
        scratch_shapes=[pltpu.VMEM((step_rows, 3 * width), BF16), pltpu.VMEM((step_rows, width), BF16)],
        compiler_params=pltpu.CompilerParams(vmem_limit_bytes=VMEM_LIMIT),
        name="char_backward",
    )(de, *weights, *kept)


MESH = pl.DeviceIdType.MESH
CHAR_ROWS = 224
WORD_ROWS = 768
SEMS = 8


def fold_half(block):
    half = block.shape[0] // 2
    return jnp.concatenate([block[:half], block[half:]], 1)


def unfold_half(block):
    return jnp.concatenate([block[:, :64], block[:, 64:]], 0)


def coordinates():
    dp, mp = lax.axis_index("dp"), lax.axis_index("mp")
    return dp // 2, dp % 2, mp // 2, mp % 2


def device_of(z, x, y, core):
    return (z * 2 + x, y * 2 + core)


def remote_copy(src, dst, ssem, rsem, slot, peer):
    return pltpu.make_async_remote_copy(
        src_ref=src, dst_ref=dst, send_sem=ssem.at[slot], recv_sem=rsem.at[slot],
        device_id=peer, device_id_type=MESH,
    )


class Halving:
    def __init__(self, n_z, work, got, ssem, rsem, base, order):
        self.n_z, self.work, self.got = n_z, work, got
        self.ssem, self.rsem, self.base, self.order = ssem, rsem, base, order
        self.z, self.x, self.y, self.core = coordinates()

    def copies(self, phase):
        z, x, y, core = self.z, self.x, self.y, self.core
        work = self.work
        slot = self.base + phase
        step = "c" if phase == 0 else self.order[phase - 1]
        if step == "c":
            pairs = [(work.at[1 - core], self.got[0], device_of(z, x, y, 1 - core))]
        elif step == "y":
            src = work.at[core, 1 - y] if phase == 1 else work.at[core, 1 - y, x]
            pairs = [(src, self.got[phase], device_of(z, x, 1 - y, core))]
        elif step == "x":
            src = work.at[core, :, 1 - x] if phase == 1 else work.at[core, y, 1 - x]
            pairs = [(src, self.got[phase], device_of(z, 1 - x, y, core))]
        else:
            pairs = []
            for k in range(1, self.n_z):
                other = lax.rem(z + k, self.n_z)
                pairs.append((work.at[core, y, x, other], self.got[3].at[k - 1], device_of(other, x, y, core)))
        return [remote_copy(s, d, self.ssem, self.rsem, slot + i, peer) for i, (s, d, peer) in enumerate(pairs)]

    def start(self, phase):
        for copy in self.copies(phase):
            copy.start()

    def finish(self, phase):
        for copy in self.copies(phase):
            copy.wait()
        x, y, core = self.x, self.y, self.core
        work, got, n_z = self.work, self.got[phase], self.n_z
        step = "c" if phase == 0 else self.order[phase - 1]

        def add(mine, other):
            def body(i, carry):
                mine[i] = (mine[i].astype(F32) + other[i].astype(F32)).astype(BF16)
                return carry
            lax.fori_loop(0, n_z, body, 0)

        if step == "c":
            for i in range(2):
                for j in range(2):
                    add(work.at[core, i, j], got.at[i, j])
        elif step == "y" and phase == 1:
            for j in range(2):
                add(work.at[core, y, j], got.at[j])
        elif step == "x" and phase == 1:
            for i in range(2):
                add(work.at[core, i, x], got.at[i])
        elif step in "yx":
            add(work.at[core, y, x], got)

    def total(self):
        value = self.work[self.core, self.y, self.x, self.z].astype(F32)
        for k in range(self.n_z - 1):
            value += self.got[3][k].astype(F32)
        return value

    @staticmethod
    def got_shapes(n_z, rows):
        return [
            pltpu.VMEM((2, 2, n_z, rows, 128), BF16), pltpu.VMEM((2, n_z, rows, 128), BF16),
            pltpu.VMEM((n_z, rows, 128), BF16), pltpu.VMEM((n_z - 1, rows, 128), BF16),
        ]


def pack_char(n_z, cqkv_ref, cout_ref, cup_ref, cdown_ref, cproj_ref, cbuf):
    for d in range(2 * n_z):
        qkv = cqkv_ref[32 * d : 32 * d + 32, :]
        out = cout_ref[32 * d : 32 * d + 32, :]
        down = cdown_ref[128 * d : 128 * d + 128, :]
        for p in range(4):
            block = cbuf.at[p % 2, p // 2, d % 2, d // 2]
            part = qkv[:, 192 * p : 192 * p + 192]
            block[0:32, :] = part[:, 0:128].astype(BF16)
            block[32:48, :] = fold_half(part[:, 128:192]).astype(BF16)
            block[48:64, :] = fold_half(out[:, 64 * p : 64 * p + 64]).astype(BF16)
            block[64:96, :] = cup_ref[32 * d : 32 * d + 32, 256 * p : 256 * p + 128].astype(BF16)
            block[96:128, :] = cup_ref[32 * d : 32 * d + 32, 256 * p + 128 : 256 * p + 256].astype(BF16)
            block[128:192, :] = fold_half(down[:, 64 * p : 64 * p + 64]).astype(BF16)
            block[192:224, :] = cproj_ref[32 * d : 32 * d + 32, 128 * p : 128 * p + 128].astype(BF16)


def pack_small(cgain_ref, cpool_ref, cg_ref, wgain_ref):
    gains = cg_ref[...].astype(F32)
    rows = []
    for j in range(2):
        total = jnp.sum(cgain_ref[j], 0, keepdims=True) / gains[j : j + 1]
        rows += [total[:, 0:128], total[:, 128:256]]
    total = jnp.sum(cpool_ref[...], 0, keepdims=True)
    rows += [total[:, 0:128], total[:, 128:256]]
    for j in range(2):
        rows += [wgain_ref[j : j + 1, 128 * t : 128 * t + 128] for t in range(4)]
    rows.append(jnp.zeros((2, 128), F32))
    return jnp.concatenate(rows, 0)


def reduce_body(
    n_z,
    cqkv_ref, cout_ref, cup_ref, cdown_ref, cproj_ref, cgain_ref, cpool_ref, cg_ref, wbuf_in, wgain_ref,
    char_ref, word_ref, small_ref,
    cbuf, *refs,
):
    c_got, wa_got, wb_got = refs[0:4], refs[4:8], refs[8:12]
    wbuf, small, sgot, ssem, rsem, lsem = refs[12:]
    z, x, y, core = coordinates()
    peers = [device_of(z, x, y, 1 - core), device_of(z, x, 1 - y, core), device_of(z, 1 - x, y, core)]
    z_peers = [device_of(lax.rem(z + k, n_z), x, y, core) for k in range(1, n_z)]
    barrier = pltpu.get_barrier_semaphore()
    for peer in peers + z_peers:
        pl.semaphore_signal(barrier, inc=1, device_id=peer, device_id_type=MESH)
    load = pltpu.make_async_copy(wbuf_in, wbuf, lsem)
    load.start()
    half = WORD_ROWS // 2
    first = Halving(n_z, wbuf.at[:, :, :, :, 0:half], wa_got, ssem, rsem, 0, "yxz")
    second = Halving(n_z, wbuf.at[:, :, :, :, half:], wb_got, ssem, rsem, SEMS, "xyz")
    chars = Halving(n_z, cbuf, c_got, ssem, rsem, 2 * SEMS, "yxz")
    tiny = 3 * SEMS
    load.wait()
    pl.semaphore_wait(barrier, len(peers) + len(z_peers))
    first.start(0)
    second.start(0)
    pack_char(n_z, cqkv_ref, cout_ref, cup_ref, cdown_ref, cproj_ref, cbuf)
    small[0] = pack_small(cgain_ref, cpool_ref, cg_ref, wgain_ref)
    chars.start(0)
    for i in range(3):
        copy = remote_copy(small.at[i], sgot.at[i], ssem, rsem, tiny + i, peers[i])
        copy.start()
        for part in (first, second, chars):
            part.finish(i)
            part.start(i + 1)
        copy.wait()
        small[i + 1] = small[i] + sgot[i]
    tail = [remote_copy(small.at[3], sgot.at[2 + k], ssem, rsem, tiny + 2 + k, z_peers[k - 1]) for k in range(1, n_z)]
    for copy in tail:
        copy.start()
    for copy in tail:
        copy.wait()
    total = small[3]
    for k in range(1, n_z):
        total += sgot[2 + k]
    small_ref[...] = total
    first.finish(3)
    word_ref[0:half, :] = first.total()
    second.finish(3)
    word_ref[half:, :] = second.total()
    chars.finish(3)
    char_ref[...] = chars.total()


def reduce_grads(n_dp, char_parts, char_gains, wbuf, wgain):
    n_z = n_dp // 2
    vm = pl.BlockSpec(memory_space=pltpu.VMEM)
    args = (*char_parts, char_gains, wbuf, wgain)
    specs = [vm] * len(args)
    specs[-2] = pl.BlockSpec(memory_space=pl.ANY)
    outs = [(CHAR_ROWS, 128), (WORD_ROWS, 128), (16, 128)]
    return pl.pallas_call(
        functools.partial(reduce_body, n_z),
        in_specs=specs,
        out_specs=[vm] * len(outs),
        out_shape=[jax.ShapeDtypeStruct(s, F32) for s in outs],
        scratch_shapes=[pltpu.VMEM((2, 2, 2, n_z, CHAR_ROWS, 128), BF16)]
        + Halving.got_shapes(n_z, CHAR_ROWS)
        + Halving.got_shapes(n_z, WORD_ROWS // 2) * 2
        + [
            pltpu.VMEM((2, 2, 2, n_z, WORD_ROWS, 128), BF16),
            pltpu.VMEM((4, 16, 128), F32),
            pltpu.VMEM((2 + n_z, 16, 128), F32),
            pltpu.SemaphoreType.DMA((4 * SEMS,)),
            pltpu.SemaphoreType.DMA((4 * SEMS,)),
            pltpu.SemaphoreType.DMA,
        ],
        compiler_params=pltpu.CompilerParams(collective_id=1, has_side_effects=True, vmem_limit_bytes=VMEM_LIMIT),
        name="reduce_gradients",
    )(*args)


def unpack_body(
    char_ref, word_ref, small_ref,
    oqkv_ref, oout_ref, oup_ref, odown_ref, oproj_ref, owqkv_ref, owout_ref, owup_ref, owdown_ref,
    ocgain_ref, opool_ref, owgain_ref,
):
    char, word, total = char_ref[...], word_ref[...], small_ref[...]
    oqkv_ref[:, 0:128] = char[0:32]
    oqkv_ref[:, 128:192] = unfold_half(char[32:48])
    oout_ref[...] = unfold_half(char[48:64])
    oup_ref[:, 0:128] = char[64:96]
    oup_ref[:, 128:256] = char[96:128]
    odown_ref[...] = unfold_half(char[128:192])
    oproj_ref[...] = char[192:224]
    for t in range(3):
        owqkv_ref[t] = word[64 * t : 64 * t + 64]
    owout_ref[...] = word[192:256].T
    for t in range(4):
        owup_ref[:, 128 * t : 128 * t + 128] = word[256 + 64 * t : 320 + 64 * t]
        owdown_ref[128 * t : 128 * t + 128, :] = word[512 + 64 * t : 576 + 64 * t].T
    for j in range(2):
        for t in range(2):
            ocgain_ref[j : j + 1, 128 * t : 128 * t + 128] = total[2 * j + t : 2 * j + t + 1]
        for t in range(4):
            owgain_ref[j : j + 1, 128 * t : 128 * t + 128] = total[6 + 4 * j + t : 7 + 4 * j + t]
    for t in range(2):
        opool_ref[:, 128 * t : 128 * t + 128] = total[4 + t : 5 + t]


def unpack_grads(char, word, small):
    vm = pl.BlockSpec(memory_space=pltpu.VMEM)
    outs = [(32, 192), (32, 64), (32, 256), (128, 64), (32, 128), (3, 64, 128), (128, 64), (64, 512), (512, 64), (2, 256), (1, 256), (2, 512)]
    return pl.pallas_call(
        unpack_body,
        in_specs=[vm] * 3,
        out_specs=[vm] * len(outs),
        out_shape=[jax.ShapeDtypeStruct(s, F32) for s in outs],
        name="unpack_gradients",
    )(char, word, small)


def norm_fwd(values, gain):
    mean = jnp.mean(values, -1, keepdims=True)
    centered = values - mean
    rstd = lax.rsqrt(jnp.mean(centered * centered, -1, keepdims=True) + EPSILON)
    return (centered * rstd * gain).astype(BF16), rstd


def norm_bwd(dn, n, rstd, gain):
    n = n.astype(F32)
    d1 = dn * gain
    dnn = dn * n
    m1 = jnp.mean(d1, -1, keepdims=True)
    m2 = jnp.mean(dnn, -1, keepdims=True)
    return rstd * (d1 - m1 - n * (1.0 / gain) * m2), jnp.sum(dnn, 0, keepdims=True) / gain


def as_column(row):
    return jnp.transpose(jnp.broadcast_to(row.astype(F32), (128, row.shape[1])))


def word_body(
    n_dp, cap, packed,
    e_ref, src_ref, seg_ref, cot_ref, gains_ref, wqkv_ref, wout_ref, wup_ref, wdown_ref,
    *refs,
):
    if packed:
        out_ref, de_ref, gbuf_ref, ggain_ref, *refs = refs
    else:
        out_ref, de_ref, gqkv_ref, gout_ref, gup_ref, gdown_ref, ggain_ref, *refs = refs
    (
        onehot, place, vec_send, vec_got, row_send, row_got, seg_all, segc_all, rows_ref, normed, rstd_a,
        qkv_send, qkv_all, weights, o_send, o_all, act_ref, dh_ref, dact_ref, dm_ref,
        do_send, do_all, dk_acc, dv_acc, dqkv_send, dqkv_all, back_send, ret,
        ssem, rsem,
    ) = refs
    dp, mp = lax.axis_index("dp"), lax.axis_index("mp")
    n_mp = 4
    words, width = e_ref.shape
    slots = n_dp * cap
    pair = 2 * (width // HEADS)
    scale = (width // HEADS) ** -0.5
    to_dp = [(lax.rem(dp + k, n_dp), mp) for k in range(n_dp)]
    from_dp = [(lax.rem(dp + n_dp - k, n_dp), mp) for k in range(n_dp)]
    mates = [(mp // 2 * 2 + (mp + 1) % 2), (mp + 2) % 4, ((mp // 2 * 2 + 2) % 4 + (mp + 1) % 2)]
    barrier = pltpu.get_barrier_semaphore()
    for k in range(1, n_dp):
        pl.semaphore_signal(barrier, inc=1, device_id=to_dp[k], device_id_type=MESH)
    for mate in mates:
        pl.semaphore_signal(barrier, inc=1, device_id=(dp, mate), device_id_type=MESH)
    next_slot = [0]

    def send(src, dst, peer):
        slot = next_slot[0]
        next_slot[0] += 1
        copy = pltpu.make_async_remote_copy(
            src_ref=src, dst_ref=dst, send_sem=ssem.at[slot], recv_sem=rsem.at[slot],
            device_id=peer, device_id_type=MESH,
        )
        copy.start()
        return copy

    source = src_ref[...]
    owner = source // (words * n_mp)
    owner_c = as_column(owner)[:, 0:1]
    index_r = lax.broadcasted_iota(jnp.int32, (words, words), 0)
    index_c = lax.broadcasted_iota(jnp.int32, (words, words), 1)
    earlier = (owner_c == owner.astype(F32)) & (index_r < index_c)
    rank = jnp.sum(jnp.where(earlier, 1.0, 0.0), 0, keepdims=True).astype(jnp.int32)
    slot_of = lax.rem(owner - dp + n_dp, n_dp) * cap + rank
    onehot[...] = jnp.where(lax.broadcasted_iota(jnp.int32, (slots, words), 0) == slot_of, 1.0, 0.0).astype(BF16)
    row_mat = as_column(lax.rem(source, words) + 1).astype(BF16)
    row_send[...] = dot_nn(onehot[...], row_mat).astype(BF16).reshape(n_dp, cap, 128)
    seg_all[mp] = jnp.broadcast_to(seg_ref[...], (8, words))
    vec_send[...] = dot_nn(onehot[...], e_ref[...]).astype(BF16).reshape(n_dp, cap, width)

    pl.semaphore_wait(barrier, n_dp - 1 + 3)
    row_copies = [send(row_send.at[k], row_got.at[k], to_dp[k]) for k in range(1, n_dp)]
    vec_copies = [send(vec_send.at[k], vec_got.at[k], to_dp[k]) for k in range(1, n_dp)]
    seg_copies = [send(seg_all.at[mp], seg_all.at[mp], (dp, mate)) for mate in mates]
    row_got[0] = row_send[0]
    vec_got[0] = vec_send[0]
    gains = gains_ref[...].astype(F32)
    cot = cot_ref[...]
    for p in range(n_mp):
        dact_ref[p] = dot_nt(cot, wdown_ref[p])
    for copy in seg_copies:
        copy.wait()
    for j in range(n_mp):
        segc_all[words * j : words * j + words, :] = as_column(seg_all[j, 0:1, :])
    for copy in row_copies:
        copy.wait()
    at_row = row_got[...].reshape(slots, 128)[:, 0:1].astype(F32) - 1.0
    lanes = lax.broadcasted_iota(jnp.int32, (slots, words), 1).astype(F32)
    place[...] = jnp.where(lanes == at_row, 1.0, 0.0).astype(BF16)
    for copy in vec_copies:
        copy.wait()
    rows = dot_tn(place[...], vec_got[...].reshape(slots, width))
    rows_ref[...] = rows
    n_w, rstd = norm_fwd(rows, gains[0:1])
    normed[0] = n_w
    rstd_a[0] = rstd
    qkv_copies = []
    for mate in reversed(mates):
        qkv_send[mate] = dot_nn(n_w, wqkv_ref[mate]).astype(BF16)
        qkv_copies.append(send(qkv_send.at[mate], qkv_all.at[mp], (dp, mate)))
    qkv_all[mp] = dot_nn(n_w, wqkv_ref[mp]).astype(BF16)
    for copy in qkv_copies:
        copy.wait()

    head_lane = lax.broadcasted_iota(jnp.int32, (1, pair), 1) // (pair // 2)
    head_mask = [jnp.where(head_lane == h, 1.0, 0.0).astype(BF16) for h in range(2)]
    o_copies = []
    for i in reversed(range(n_mp)):
        keys = words * (i + 1)
        q = qkv_all[i, :, 0:pair]
        k = qkv_all[0 : i + 1, :, pair : 2 * pair].reshape(keys, pair)
        v = qkv_all[0 : i + 1, :, 2 * pair : 3 * pair].reshape(keys, pair)
        same = segc_all[0:keys, 0:1] == seg_all[i, 0:1, :].astype(F32)
        key_at = lax.broadcasted_iota(jnp.int32, (keys, words), 0)
        query_at = lax.broadcasted_iota(jnp.int32, (keys, words), 1) + words * i
        allowed = same & (key_at <= query_at)
        total = None
        for h in range(2):
            st = dot_nt(k * (head_mask[h] * scale).astype(BF16), q)
            st = jnp.where(allowed, st, NEGATIVE)
            ex = jnp.exp(st - jnp.max(st, 0, keepdims=True))
            at = (ex * (1.0 / jnp.sum(ex, 0, keepdims=True))).astype(BF16)
            weights[i, h, 0:keys, :] = at
            part = dot_tn(at, v * head_mask[h])
            total = part if total is None else total + part
        o_send[i] = total.astype(BF16)
    for mate in reversed(mates):
        o_copies.append(send(o_send.at[mate], o_all.at[mp], (dp, mate)))
    o_all[mp] = o_send[mp]
    for copy in o_copies:
        copy.wait()
    attended = jnp.concatenate([o_all[p] for p in range(n_mp)], 1)
    mid = rows_ref[...] + dot_nn(attended, wout_ref[...].reshape(width, width))
    n_w2, rstd2 = norm_fwd(mid, gains[1:2])
    normed[1] = n_w2
    out = mid
    dn2 = jnp.zeros((words, width), F32)
    for p in range(n_mp):
        act, slope = gelu_both(dot_nn(n_w2, wup_ref[p]))
        act = act.astype(BF16)
        act_ref[p] = act
        dh = (slope * dact_ref[p]).astype(BF16)
        dh_ref[p] = dh
        out = out + dot_nn(act, wdown_ref[p])
        dn2 = dn2 + dot_nt(dh, wup_ref[p])
    out_ref[...] = out.astype(BF16)
    d_norm, gain_b = norm_bwd(dn2, n_w2, rstd2, gains[1:2])
    d_mid = cot.astype(F32) + d_norm
    dm_ref[...] = d_mid
    d_att = d_mid.astype(BF16)
    do_copies = []
    for mate in reversed(mates):
        do_send[mate] = dot_nt(d_att, wout_ref[mate]).astype(BF16)
        do_copies.append(send(do_send.at[mate], do_all.at[mp], (dp, mate)))
    do_all[mp] = dot_nt(d_att, wout_ref[mp]).astype(BF16)

    def put(base, p, grad):
        if packed:
            block = words // 4
            for d in range(n_dp):
                for t in range(grad.shape[1] // 128):
                    gbuf_ref[p % 2, p // 2, d % 2, d // 2, base + block * t : base + block * t + block, :] = (
                        grad[block * d : block * d + block, 128 * t : 128 * t + 128].astype(BF16)
                    )
        else:
            ref = {0: gqkv_ref, 192: gout_ref, 256: gup_ref, 512: gdown_ref}[base]
            ref[p] = grad

    for p in range(n_mp):
        put(512, p, dot_tn(cot, act_ref[p]))
        put(256, p, dot_tn(n_w2, dh_ref[p]))
        put(192, p, dot_tn(d_att, o_all[p]))
    dk_acc[...] = jnp.zeros_like(dk_acc)
    dv_acc[...] = jnp.zeros_like(dv_acc)
    for copy in do_copies:
        copy.wait()
    for i in reversed(range(n_mp)):
        keys = words * (i + 1)
        q = qkv_all[i, :, 0:pair]
        k = qkv_all[0 : i + 1, :, pair : 2 * pair].reshape(keys, pair)
        v = qkv_all[0 : i + 1, :, 2 * pair : 3 * pair].reshape(keys, pair)
        do = do_all[i]
        dq = None
        for h in range(2):
            at = weights[i, h, 0:keys, :]
            dpt = dot_nt(v * head_mask[h], do)
            af = at.astype(F32)
            delta = jnp.sum(af * dpt, 0, keepdims=True)
            ds = (af * (dpt - delta)).astype(BF16)
            scaled = (head_mask[h] * scale).astype(BF16)
            part = dot_tn(ds, k * scaled)
            dq = part if dq is None else dq + part
            dk_acc[0:keys, :] += dot_nn(ds, q * scaled)
            dv_acc[0:keys, :] += dot_nn(at, do * head_mask[h])
        dqkv_send[i, :, 0:pair] = dq.astype(BF16)
        dqkv_send[i, :, pair : 2 * pair] = dk_acc[words * i : keys, :].astype(BF16)
        dqkv_send[i, :, 2 * pair : 3 * pair] = dv_acc[words * i : keys, :].astype(BF16)
    dqkv_copies = []
    for mate in reversed(mates):
        dqkv_copies.append(send(dqkv_send.at[mate], dqkv_all.at[mp], (dp, mate)))
    dqkv_all[mp] = dqkv_send[mp]
    for copy in dqkv_copies:
        copy.wait()
    d_normed = jnp.zeros((words, width), F32)
    for p in range(n_mp):
        d_normed = d_normed + dot_nt(dqkv_all[p], wqkv_ref[p])
    d_first, gain_a = norm_bwd(d_normed, normed[0], rstd_a[0], gains[0:1])
    d_rows = (dm_ref[...] + d_first).astype(BF16)
    ggain_ref[0:1, :] = gain_a
    ggain_ref[1:2, :] = gain_b
    back_send[...] = dot_nn(place[...], d_rows).astype(BF16).reshape(n_dp, cap, width)
    back_copies = [send(back_send.at[k], ret.at[k], from_dp[k]) for k in range(1, n_dp)]
    ret[0] = back_send[0]
    for p in range(n_mp):
        put(0, p, dot_tn(normed[0], dqkv_all[p]))
    for copy in back_copies:
        copy.wait()
    de_ref[...] = dot_tn(onehot[...], ret[...].reshape(slots, width)).astype(BF16)


def word_layer(n_dp, word_vec, source, segments, cotangent, gains, wqkv, wout, wup, wdown):
    words, width = word_vec.shape
    n_mp = wqkv.shape[0]
    cap = -(-2 * words // n_dp // 16) * 16
    slots = cap * n_dp
    pair = 2 * (width // HEADS)
    packed = n_dp == 8
    outs = [((words, width), BF16), ((words, width), BF16)]
    if packed:
        outs.append(((2, 2, 2, n_dp // 2, WORD_ROWS, 128), BF16))
    else:
        outs += [((n_mp, width, n), F32) for n in (3 * pair, pair, wup.shape[2], wup.shape[2])]
    outs.append(((2, width), F32))
    hid = wup.shape[2]
    n_sem = 3 * (n_dp - 1) + 5 * 3
    vm = pl.BlockSpec(memory_space=pltpu.VMEM)
    args = (word_vec, source.reshape(1, -1), segments.reshape(1, -1), cotangent, gains, wqkv, wout, wup, wdown)
    shapes = [
        ((slots, words), BF16), ((slots, words), BF16), ((n_dp, cap, width), BF16), ((n_dp, cap, width), BF16),
        ((n_dp, cap, 128), BF16), ((n_dp, cap, 128), BF16), ((n_mp, 8, words), jnp.int32), ((n_mp * words, 128), F32),
        ((words, width), F32), ((2, words, width), BF16), ((1, words, 1), F32),
        ((n_mp, words, 3 * pair), BF16), ((n_mp, words, 3 * pair), BF16), ((n_mp, 2, n_mp * words, words), BF16),
        ((n_mp, words, pair), BF16), ((n_mp, words, pair), BF16),
        ((n_mp, words, hid), BF16), ((n_mp, words, hid), BF16), ((n_mp, words, hid), F32), ((words, width), F32),
        ((n_mp, words, pair), BF16), ((n_mp, words, pair), BF16), ((n_mp * words, pair), F32), ((n_mp * words, pair), F32),
        ((n_mp, words, 3 * pair), BF16), ((n_mp, words, 3 * pair), BF16), ((n_dp, cap, width), BF16), ((n_dp, cap, width), BF16),
    ]
    return pl.pallas_call(
        functools.partial(word_body, n_dp, cap, packed),
        in_specs=[vm] * len(args),
        out_specs=[vm] * len(outs),
        out_shape=[jax.ShapeDtypeStruct(s, d) for s, d in outs],
        scratch_shapes=[pltpu.VMEM(s, d) for s, d in shapes]
        + [pltpu.SemaphoreType.DMA((n_sem,)), pltpu.SemaphoreType.DMA((n_sem,))],
        compiler_params=pltpu.CompilerParams(collective_id=0, has_side_effects=True, vmem_limit_bytes=VMEM_LIMIT),
        name="word_layer",
    )(*args)


def plain_reduce(char_parts, char_gains, word_parts, word_gains):
    *char_mats, gain_rows, pool_rows = char_parts
    gain_sums = jnp.sum(gain_rows, 1) / char_gains.astype(F32)
    small = lax.psum((gain_sums, jnp.sum(pool_rows, 0), word_gains), ("dp", "mp"))
    mats = []
    for grad in char_mats:
        part = lax.psum_scatter(grad, "dp", scatter_dimension=0, tiled=True)
        part = lax.psum_scatter(part.astype(BF16), "mp", scatter_dimension=1, tiled=True)
        mats.append(part.astype(F32))
    words = []
    for grad in word_parts:
        part = lax.psum_scatter(grad, "dp", scatter_dimension=1, tiled=True)
        words.append(lax.psum_scatter(part, "mp", scatter_dimension=0, tiled=False))
    qkv, out, up, down = words
    qkv = jnp.transpose(qkv.reshape(qkv.shape[0], 3, -1), (1, 0, 2))
    return (*mats, qkv, out.T, up, down.T, *small)


def per_device(
    char_input,
    char_counts,
    word_source,
    segment_ids,
    cotangent,
    char_norm_gains,
    char_qkv,
    char_out,
    char_up,
    char_down,
    pool_vector,
    char_proj,
    word_norm_gains,
    word_qkv,
    word_out,
    word_up,
    word_down,
):
    groups = lax.axis_size("dp")
    char_weights = (
        char_norm_gains, char_qkv, char_out, char_up, char_down, pool_vector.reshape(1, -1), char_proj
    )
    word_weights = [
        lax.all_gather(w, "mp", axis=0, tiled=False)
        for w in (
            jnp.transpose(word_qkv, (1, 0, 2)).reshape(word_qkv.shape[1], -1), word_out, word_up, word_down,
        )
    ]
    word_vec, *char_kept = char_forward(char_input, char_counts.reshape(-1, 1), *char_weights)
    output, d_word, *word_parts, word_gains = word_layer(
        groups, word_vec, word_source, segment_ids, cotangent, word_norm_gains, *word_weights
    )
    d_chars, *char_parts = char_backward(d_word, char_kept, *char_weights)
    if groups == 8:
        sums = reduce_grads(groups, char_parts, char_norm_gains, word_parts[0], word_gains)
        grads = unpack_grads(*sums)
    else:
        grads = plain_reduce(char_parts, char_norm_gains, word_parts, word_gains)
    *mats, grad_char_gains, grad_pool, grad_word_gains = grads
    return (output, d_chars, *mats, grad_char_gains, grad_pool.reshape(-1), grad_word_gains)


def solution(mesh):
    placed = (
        P(("dp", "mp"), None),
        P(("dp", "mp")),
        P(("dp", "mp")),
        P(("dp", "mp")),
        P(("dp", "mp"), None),
        P(),
        P(),
        P(),
        P(),
        P(),
        P(),
        P(),
        P(),
        P(None, None, "mp"),
        P("mp", None),
        P(None, "mp"),
        P("mp", None),
    )
    return jax.shard_map(
        per_device,
        mesh=mesh,
        in_specs=placed,
        out_specs=(
            P(("dp", "mp"), None),
            P(("dp", "mp"), None),
            P("dp", "mp"),
            P("dp", "mp"),
            P("dp", "mp"),
            P("dp", "mp"),
            P("dp", "mp"),
            P(None, "dp", "mp"),
            P("mp", "dp"),
            P("dp", "mp"),
            P("mp", "dp"),
            P(),
            P(),
            P(),
        ),
        check_vma=False,
    )
```

time: 497 us -> 280 us (0.56); the launches traced: 489 us -> 280 us
  waiting for transfers between devices: 197 us -> 21.8 us
  Pallas kernels: 129 us -> 226 us
  matrix products: 47.6 us -> 0 us
  local copies, waits for them, and re-layouts: 40.6 us -> 8.96 us
  other arithmetic: 26.7 us -> 0 us
  starting transfers between devices: 19.6 us -> 0.12 us
  loops' own time: 7.87 us -> 0 us
    reduce_scatter x4 -> x0, waiting for transfers between devices: 117 us -> none  [sum_rows(): return lax.psum_scatter(partial_rows, 'mp', scatter_dimension=0, tiled=True)]
    pallas_call x1 -> x3, Pallas kernels: 46.4 us -> 143 us  [the longest x1 78.4 us: word_layer(): pl.pallas_call(functools.partial(word_body, n_dp, cap, packed), in_specs=...]
    dot_general x25 -> x0, matrix products: 45.7 us -> none  [the longest x3 10.5 us: flat_dot(): return jnp.dot(left, right, preferred_element_type=jnp.float32)]
    all_gather x4 -> x3, waiting for transfers between devices: 58.7 us -> 20.4 us  [per_device(): lax.all_gather(w, 'mp', axis=0, tiled=False)]
    all_to_all x3 -> x0, waiting for transfers between devices: 20.5 us -> none  [the longest x1 12.6 us: per_device(): lax.all_to_all(send_vec.reshape(groups, capacity, model_width), 'dp', spl...]
    all_to_all x3 -> x0, starting transfers between devices: 19 us -> none  [the longest x1 7.25 us: per_device(): lax.all_to_all(send_rows.reshape(groups, capacity), 'dp', split_axis=0, c...]
    unnamed x84 -> x13, local copies, waits for them, and re-layouts: 20.2 us -> 6.68 us
    reduce_sum x11 -> x0, other arithmetic: 10.7 us -> none  [the longest x3 4.46 us: norm_rows(): return centered * lax.rsqrt(variance + EPSILON) * gain_vec]
  transfers between devices with their start and end apart: 11 -> 3, of which waited for: 10 -> 1; matrix products, arithmetic and copies ran while one was open for 6% -> 0% of each run, Pallas kernels for 8% -> 14%
where the time goes in v2:
time: 280 us
  Pallas kernels  226 us (81%)
  waiting for transfers between devices  21.8 us (8%)
  between operations  13.8 us (5%)
  blocking collectives  9.28 us (3%)
  local copies, waits for them, and re-layouts  8.96 us (3%)
    pallas_call x1, Pallas kernels, word_layer(): pl.pallas_call(functools.partial(word_body, n_dp, cap, packed), in_specs=...  78.4 us
    pallas_call x1, Pallas kernels, reduce_grads(): pl.pallas_call(functools.partial(reduce_body, n_z), in_specs=specs, out_s...  62.8 us
    pallas_call x1, Pallas kernels, char_backward(): pl.pallas_call(char_bwd_body, grid=(steps,), in_specs=[blk(step_words, de...  43.6 us
    pallas_call x1, Pallas kernels, char_forward(): pl.pallas_call(char_fwd_body, grid=(words // step_words,), in_specs=[blk(...  39 us
    all_gather x3, waiting for transfers between devices, per_device(): lax.all_gather(w, 'mp', axis=0, tiled=False)  20.4 us
    all_gather x1, blocking collectives, per_device(): lax.all_gather(w, 'mp', axis=0, tiled=False)  9.28 us
    unnamed x13, local copies, waits for them, and re-layouts  6.68 us
  transfers between devices with their start and end apart: 3, of which 1 were waited for; matrix products, arithmetic and copies ran while one was open for 0% of the time, Pallas kernels for 14%

profile of v2, /device:TPU:0, one launch (start us, length us, event | category | flops | bytes accessed | tf_op | source)
XLA Modules:
  0.0 279.8 jit_solution(98236269329769489)
XLA Ops:
  7.2 0.0 copy-start.3
  7.2 0.0 all-gather.7.cloned.1.call-start
  7.2 1.2 copy.42
  8.4 0.9 copy.43
  9.3 0.0 all-gather.7.cloned.1.call-update
  9.4 0.0 all-gather.9.cloned.1.call-start
  9.4 0.7 all-gather.9.cloned.1.call-update
  10.1 0.0 all-gather.11.cloned.1.call-start
  10.2 0.7 all-gather.11.cloned.1.call-update
  10.8 0.0 copy-done.3
  10.9 0.6 reshape.44.pool_ref
  11.4 0.8 copy.41.cnt_ref
  12.2 39.0 %char_forward.1 = (bf16[256,512]{1,0:T(8,128)(2,1)}, bf16[4096,256]{1,0:T(8,128)(2,1)}, bf16[4096,768]{1,0:T(8,128)(2,1)}, bf16[16384,128]{1,0:T(8,128)(2,1)}, b...) custom-call(bf16[256,4096]{1,0:T(8,128)(2,1)} %x_ref.1, ...), custom_call_target="tpu_custom_call" | custom-call | tf_op jit(solution)/shard_map/char_forward/pallas_call | solution.py:132
  51.3 9.3 %all-gather = bf16[512,512]{1,0:T(8,128)(2,1)} all-gather(bf16[128,512]{1,0:T(8,128)(2,1)S(1)} %copy-done.1), channel_id=2, replica_groups=mesh['dp'=8,'mp'=4] {'mp'}, dimensions={0}, use_global_device_ids=true | all-gather | bytes 655360 | tf_op jit(solution)/shard_map/all_gather | solution.py:799
  60.5 20.4 %all-gather.11.cloned.1.call-done = bf16[2048,512]{1,0:T(8,128)(2,1)} async-done(((bf16[512,512]{1,0:T(8,128)(2,1)}), bf16[2048,512]{1,0:T(8,128)(2,1)}) %all-gather.11.cloned.1.call-update) | async-done | bytes 2097168 | tf_op jit(solution)/shard_map/all_gather | solution.py:799
  80.9 78.4 %word_layer.1 = (bf16[256,512]{1,0:T(8,128)(2,1)}, bf16[256,512]{1,0:T(8,128)(2,1)}, bf16[2,2,2,4,768,128]{5,4,3,2,1,0:T(8,128)(2,1)}, f32[2,512]{1,0:T(2,128)}) custom-call(bf16[256,512]{1,0:T(8,128)(2,1)} %get-tuple-element.54.e_ref, s32[1,256]{1,0:T(1,128)} %bitcast.15, s32[1,256]{1,0:T(1,128)} %bitcast.16, bf16[256,512]{1,0:T(8,128)(2,1)} %cot_ref.1, ...), custom_call_target="tpu_custom_call" | custom-call | tf_op jit(solution)/shard_map/word_layer/pallas_call | solution.py:745
  159.4 43.6 %char_backward.1 = (f32[256,4096]{1,0:T(8,128)}, f32[256,768]{1,0:T(8,128)}, f32[256,256]{1,0:T(8,128)}, f32[256,1024]{1,0:T(8,128)}, f32[1024,256]{1,0:T(8,128)...) custom-call(bf16[256,512]{1,0:T(8,128)(2,1)} %get-tuple-element.56.de_ref, bf16[2,256]{1,0:T(2,128)(2,1)} %cg_ref.1, ...), custom_call_target="tpu_custom_call" | custom-call | tf_op jit(solution)/shard_map/char_backward/pallas_call | solution.py:225
  202.9 62.8 %reduce_gradients.1 = (f32[224,128]{1,0:T(8,128)}, f32[768,128]{1,0:T(8,128)}, f32[16,128]{1,0:T(8,128)}) custom-call(f32[256,768]{1,0:T(8,128)} %get-tuple-element.70.cqkv_ref, f32[256,256]{1,0:T(8,128)} %get-tuple-element.71.cout_ref, f32[256,1024]{1,0:T(8,128)} %get-tuple-element.72.cup_ref, f32[1024,256]{1,0:T(8,128)} %get-tuple-element.73.cdown_ref, ...), custom_call_target="tpu_custom_call" | custom-call | tf_op jit(solution)/shard_map/reduce_gradients/pallas_call | solution.py:432
  265.8 2.0 unpack_gradients.1
  267.8 1.5 copy.44
  269.3 1.5 copy.45
  270.8 1.7 copy.46
  272.6 0.0 copy-done
  272.6 0.7 copy.48
  (7 shorter events, 0.0 us)
Async XLA Ops:
  7.2 3.7 %copy-start.3 = (bf16[256]{0:T(256)(128)(2,1)S(1)}, bf16[256]{0:T(256)(128)(2,1)}, u32[]{:S(2)}) copy-start(bf16[256]{0:T(256)(128)(2,1)} %param.27) | copy-start | bytes 1540
  7.2 4.2 %copy-start.2 = (s32[256]{0:T(256)S(1)}, s32[256]{0:T(256)}, u32[]{:S(2)}) copy-start(s32[256]{0:T(256)} %param.18) | copy-start | bytes 3076
  7.2 53.3 %all-gather.7.cloned.1.call-start = ((), (), s32[]{:S(2)}) async-start(), calls=%async_computation | async-start | bytes 1966080 | tf_op jit(solution)/shard_map/all_gather | solution.py:799
  9.4 51.2 %all-gather.9.cloned.1.call-start = ((), (), s32[]{:S(2)}) async-start(), calls=%async_computation.1 | async-start | bytes 2621440 | tf_op jit(solution)/shard_map/all_gather | solution.py:799
  10.1 70.8 %all-gather.11.cloned.1.call-start = ((), (), s32[]{:S(2)}) async-start(), calls=%async_computation.2 | async-start | bytes 2621440 | tf_op jit(solution)/shard_map/all_gather | solution.py:799
  11.4 39.8 %copy-start.1 = (bf16[128,512]{1,0:T(8,128)(2,1)S(1)}, bf16[128,512]{1,0:T(8,128)(2,1)}, u32[]{:S(2)}) copy-start(bf16[128,512]{1,0:T(8,128)(2,1)} %param.31) | copy-start | bytes 393220
  202.9 69.6 %copy-start = (bf16[256,512]{1,0:T(8,128)(2,1)S(1)}, bf16[256,512]{1,0:T(8,128)(2,1)}, u32[]{:S(2)}) copy-start(bf16[256,512]{1,0:T(8,128)(2,1)} %get-tuple-element.150) | copy-start | bytes 786436
Sparse Core Ops, SparseCore 0:
  10.2 22.3 all-gather.6
  34.1 22.5 all-gather.8
  58.3 22.5 all-gather.10

commit v3 on v2

--- a/solution.py
+++ b/solution.py
@@ -15,6 +15,7 @@
 GELU_B = 0.044715
 F32 = jnp.float32
 BF16 = jnp.bfloat16
+MESH = pl.DeviceIdType.MESH
 VMEM_LIMIT = 60 * 1024 * 1024
 
 
@@ -28,6 +29,10 @@
 
 def dot_tn(left, right):
     return lax.dot_general(left, right, (((0,), (0,)), ((), ())), preferred_element_type=F32)
+
+
+def as_column(row):
+    return jnp.transpose(jnp.broadcast_to(row.astype(F32), (128, row.shape[1])))
 
 
 def head_stack(values, heads, factor):
@@ -48,9 +53,17 @@
 
 
 def char_fwd_body(
+    n_dp, cap,
     x_ref, cnt_ref, gains_ref, wqkv_ref, wout_ref, wup_ref, wdown_ref, pool_ref, wproj_ref,
+    src_ref, seg_ref, s_qkv, s_out, s_up, s_down,
     e_ref, n1_ref, p_ref, a_ref, o_ref, n2_ref, rs1_ref, rs2_ref, act_ref, dg_ref, f_ref, aw_ref, pooled_ref,
+    onehot_ref, place_ref, seg_out, g_qkv, g_out, g_up, g_down,
+    row_send, row_got, seg_all, ssem, rsem,
 ):
+    gather_step(
+        n_dp, cap, src_ref, seg_ref, (s_qkv, s_out, s_up, s_down), (g_qkv, g_out, g_up, g_down),
+        onehot_ref, place_ref, seg_out, row_send, row_got, seg_all, ssem, rsem,
+    )
     words, wide = x_ref.shape
     width = wide // CHARS
     blocks = words // 8
@@ -112,12 +125,133 @@
     pooled_ref[...] = pooled
     e_ref[...] = dot_nn(pooled, wproj_ref[...]).astype(BF16)
 
-
-def char_forward(x, counts, gains, wqkv, wout, wup, wdown, pool, wproj, step_words=32):
+    @pl.when(pl.program_id(0) == pl.num_programs(0) - 1)
+    def _():
+        gather_end((g_qkv, g_out, g_up, g_down), (s_qkv, s_out, s_up, s_down), ssem, rsem)
+
+
+def gather_step(
+    n_dp, cap, src_ref, seg_ref, slices, wholes,
+    onehot_ref, place_ref, seg_out, row_send, row_got, seg_all, ssem, rsem,
+):
+    step, last = pl.program_id(0), pl.num_programs(0) - 1
+    dp, mp = lax.axis_index("dp"), lax.axis_index("mp")
+    sibling = mp // 2 * 2 + (mp + 1) % 2
+    across = (mp + 2) % 4
+    mates = [sibling, across, across // 2 * 2 + (across + 1) % 2]
+    words = src_ref.shape[1]
+    slots = n_dp * cap
+    parts = len(slices)
+
+    def copy(src, dst, slot, peer):
+        return pltpu.make_async_remote_copy(
+            src_ref=src, dst_ref=dst, send_sem=ssem.at[slot], recv_sem=rsem.at[slot],
+            device_id=peer, device_id_type=MESH,
+        )
+
+    def far(i):
+        return copy(slices[i], wholes[i].at[mp], i, (dp, across))
+
+    def near(i):
+        return copy(slices[i], wholes[i].at[mp], parts + i, (dp, sibling))
+
+    def relay(i):
+        return copy(wholes[i].at[across], wholes[i].at[across], 2 * parts + i, (dp, sibling))
+
+    def row_copy(k):
+        return copy(row_send.at[k], row_got.at[k], 3 * parts + k, (lax.rem(dp + k, n_dp), mp))
+
+    def seg_copy(j):
+        return copy(seg_all.at[mp], seg_all.at[mp], 3 * parts + n_dp + j, (dp, mates[j]))
+
+    @pl.when(step == 0)
+    def _():
+        barrier = pltpu.get_barrier_semaphore()
+        for k in range(1, n_dp):
+            pl.semaphore_signal(barrier, inc=1, device_id=(lax.rem(dp + k, n_dp), mp), device_id_type=MESH)
+        for mate in mates:
+            pl.semaphore_signal(barrier, inc=1, device_id=(dp, mate), device_id_type=MESH)
+        source = src_ref[...]
+        owner = source // (words * 4)
+        owner_c = as_column(owner)[:, 0:1]
+        index_r = lax.broadcasted_iota(jnp.int32, (words, words), 0)
+        index_c = lax.broadcasted_iota(jnp.int32, (words, words), 1)
+        earlier = (owner_c == owner.astype(F32)) & (index_r < index_c)
+        rank = jnp.sum(jnp.where(earlier, 1.0, 0.0), 0, keepdims=True).astype(jnp.int32)
+        slot_of = lax.rem(owner - dp + n_dp, n_dp) * cap + rank
+        at_slot = lax.broadcasted_iota(jnp.int32, (slots, words), 0) == slot_of
+        onehot_ref[...] = jnp.where(at_slot, 1.0, 0.0).astype(BF16)
+        row_mat = as_column(lax.rem(source, words) + 1).astype(BF16)
+        row_send[...] = dot_nn(onehot_ref[...], row_mat).astype(BF16).reshape(n_dp, cap, 128)
+        seg_all[mp] = jnp.broadcast_to(seg_ref[...], (8, words))
+        pl.semaphore_wait(barrier, n_dp - 1 + 3)
+        far(0).start()
+        far(1).start()
+        for i in range(parts):
+            near(i).start()
+        for k in range(1, n_dp):
+            row_copy(k).start()
+        for j in range(3):
+            seg_copy(j).start()
+        row_got[0] = row_send[0]
+
+    @pl.when(step == 2)
+    def _():
+        far(2).start()
+
+    @pl.when(step == 3)
+    def _():
+        far(0).wait()
+        relay(0).start()
+        far(1).wait()
+        relay(1).start()
+
+    @pl.when(step == 4)
+    def _():
+        far(3).start()
+
+    @pl.when(step == 6)
+    def _():
+        far(2).wait()
+        relay(2).start()
+
+    @pl.when(step == last)
+    def _():
+        far(3).wait()
+        relay(3).start()
+
+    @pl.when(step == last)
+    def _():
+        for k in range(1, n_dp):
+            row_copy(k).wait()
+        for j in range(3):
+            seg_copy(j).wait()
+        at_row = row_got[...].reshape(slots, 128)[:, 0:1].astype(F32) - 1.0
+        lanes = lax.broadcasted_iota(jnp.int32, (slots, words), 1).astype(F32)
+        place_ref[...] = jnp.where(lanes == at_row, 1.0, 0.0).astype(BF16)
+        seg_out[...] = seg_all[...]
+
+
+def gather_end(wholes, slices, ssem, rsem):
+    dp, mp = lax.axis_index("dp"), lax.axis_index("mp")
+    sibling = mp // 2 * 2 + (mp + 1) % 2
+    across = (mp + 2) % 4
+    parts = len(slices)
+    for i in range(parts):
+        for slot, at in ((parts + i, mp), (2 * parts + i, across)):
+            pltpu.make_async_remote_copy(
+                src_ref=slices[i] if slot < 2 * parts else wholes[i].at[across], dst_ref=wholes[i].at[at],
+                send_sem=ssem.at[slot], recv_sem=rsem.at[slot], device_id=(dp, sibling), device_id_type=MESH,
+            ).wait()
+
+
+def char_forward(n_dp, x, counts, gains, wqkv, wout, wup, wdown, pool, wproj, source, segments, slices, step_words=32):
     words, wide = x.shape
     width = wide // CHARS
     rows = words * CHARS
     step_rows = step_words * CHARS
+    cap = -(-2 * words // n_dp // 16) * 16
+    slots = n_dp * cap
     full = lambda arr: pl.BlockSpec(arr.shape, lambda i: (0,) * arr.ndim)
     blk = lambda n, w: pl.BlockSpec((n, w), lambda i: (i, 0))
     hid = wup.shape[1]
@@ -129,117 +263,35 @@
         (rows, step_rows, hid, BF16), (rows, step_rows, hid, BF16), (rows, step_rows, width, BF16),
         (rows, step_rows, 1, F32), (words, step_words, width, BF16),
     ]
+    fixed = [((slots, words), BF16), ((slots, words), BF16), ((4, 8, words), jnp.int32)]
+    any_spec = pl.BlockSpec(memory_space=pl.ANY)
+    n_sem = 3 * len(slices) + n_dp + 3
     return pl.pallas_call(
-        char_fwd_body,
+        functools.partial(char_fwd_body, n_dp, cap),
         grid=(words // step_words,),
-        in_specs=[blk(step_words, wide), blk(step_words, 1)] + [full(w) for w in (gains, wqkv, wout, wup, wdown, pool, wproj)],
-        out_specs=[blk(b, w) for _, b, w, _ in outs],
-        out_shape=[jax.ShapeDtypeStruct((n, w), d) for n, _, w, d in outs],
-        compiler_params=pltpu.CompilerParams(vmem_limit_bytes=VMEM_LIMIT),
+        in_specs=[blk(step_words, wide), blk(step_words, 1)]
+        + [full(w) for w in (gains, wqkv, wout, wup, wdown, pool, wproj, source, segments)]
+        + [any_spec] * len(slices),
+        out_specs=[blk(b, w) for _, b, w, _ in outs]
+        + [pl.BlockSpec(s, lambda i, n=len(s): (0,) * n) for s, _ in fixed]
+        + [any_spec] * len(slices),
+        out_shape=[jax.ShapeDtypeStruct((n, w), d) for n, _, w, d in outs]
+        + [jax.ShapeDtypeStruct(s, d) for s, d in fixed]
+        + [jax.ShapeDtypeStruct((4, *s.shape), s.dtype) for s in slices],
+        scratch_shapes=[
+            pltpu.VMEM((n_dp, cap, 128), BF16), pltpu.VMEM((n_dp, cap, 128), BF16), pltpu.VMEM((4, 8, words), jnp.int32),
+            pltpu.SemaphoreType.DMA((n_sem,)), pltpu.SemaphoreType.DMA((n_sem,)),
+        ],
+        compiler_params=pltpu.CompilerParams(collective_id=2, has_side_effects=True, vmem_limit_bytes=VMEM_LIMIT),
         name="char_forward",
-    )(x, counts, gains, wqkv, wout, wup, wdown, pool, wproj)
-
-
-def char_bwd_body(
-    de_ref, gains_ref, wqkv_ref, wout_ref, wup_ref, wdown_ref, pool_ref, wproj_ref,
-    n1_ref, p_ref, a_ref, o_ref, n2_ref, rs1_ref, rs2_ref, act_ref, dg_ref, f_ref, aw_ref, pooled_ref,
-    dx_ref, gqkv_ref, gout_ref, gup_ref, gdown_ref, gproj_ref, ggain_ref, gpool_ref,
-    dp_ref, do_ref,
-):
-    words = de_ref.shape[0]
-    width = n1_ref.shape[1]
-    blocks = words // 8
-    rows = words * CHARS
-    gains = gains_ref[...].astype(F32)
-
-    @pl.when(pl.program_id(0) == 0)
-    def _():
-        for ref in (gqkv_ref, gout_ref, gup_ref, gdown_ref, gproj_ref, ggain_ref, gpool_ref):
-            ref[...] = jnp.zeros_like(ref)
-
-    de = de_ref[...]
-    gproj_ref[...] += dot_tn(pooled_ref[...], de)
-    dpool = dot_nt(de, wproj_ref[...]).reshape(blocks, 1, 8, width)
-    f = f_ref[...].astype(F32).reshape(blocks, CHARS, 8, width)
-    aw = aw_ref[...].reshape(blocks, CHARS, 8, 1)
-    g = jnp.sum(f * dpool, -1, keepdims=True)
-    dt = aw * (g - jnp.sum(aw * g, 1, keepdims=True))
-    gpool_ref[...] += jnp.sum((dt * f).reshape(rows // 8, 8, width), 0)
-    df = (aw * dpool + dt * pool_ref[...].astype(F32)).reshape(rows, width)
-    dfb = df.astype(BF16)
-    gdown_ref[...] += dot_tn(act_ref[...], dfb)
-    dh = (dg_ref[...].astype(F32) * dot_nt(dfb, wdown_ref[...])).astype(BF16)
-    n2 = n2_ref[...]
-    gup_ref[...] += dot_tn(n2, dh)
-    dn2 = dot_nt(dh, wup_ref[...])
-
-    def norm_back(dn, n, rstd, gain, row):
-        d1 = dn * gain
-        dnn = dn * n.astype(F32)
-        ggain_ref[row] += jnp.sum(dnn.reshape(rows // 8, 8, width), 0)
-        m1 = jnp.mean(d1, -1, keepdims=True)
-        m2 = jnp.mean(dnn, -1, keepdims=True)
-        return rstd * (d1 - m1 - n.astype(F32) * (1.0 / gain) * m2)
-
-    dm = df + norm_back(dn2, n2, rs2_ref[...], gains[1:2], 1)
-    dmb = dm.astype(BF16)
-    gout_ref[...] += dot_tn(o_ref[...], dmb)
-    do_ref[...] = dot_nt(dmb, wout_ref[...]).astype(BF16)
-    scale = (width // CHAR_HEADS) ** -0.5
-    for b in range(blocks):
-        sl = slice(128 * b, 128 * b + 128)
-        q = p_ref[sl, 0:width]
-        k = p_ref[sl, width : 2 * width]
-        v = p_ref[sl, 2 * width : 3 * width]
-        do = do_ref[sl, :]
-        ab = a_ref[CHAR_HEADS * 128 * b : CHAR_HEADS * 128 * (b + 1), :]
-        a = ab.astype(F32).reshape(CHAR_HEADS, CHARS, 8, 128)
-        dpt = dot_nt(head_stack(v, CHAR_HEADS, 1.0), do).reshape(CHAR_HEADS, CHARS, 8, 128)
-        delta = jnp.sum(a * dpt, 1, keepdims=True)
-        ds = (a * (dpt - delta)).reshape(CHAR_HEADS * 128, 128).astype(BF16)
-        wide_ds = jnp.concatenate([ds[128 * h : 128 * h + 128] for h in range(CHAR_HEADS)], 1)
-        wide_a = jnp.concatenate([ab[128 * h : 128 * h + 128] for h in range(CHAR_HEADS)], 1)
-        dp_ref[sl, 0:width] = dot_tn(ds, head_stack(k, CHAR_HEADS, scale)).astype(BF16)
-        dp_ref[sl, width : 2 * width] = dot_nn(wide_ds, head_stack(q, CHAR_HEADS, scale)).astype(BF16)
-        dp_ref[sl, 2 * width : 3 * width] = dot_nn(wide_a, head_stack(do, CHAR_HEADS, 1.0)).astype(BF16)
-    n1 = n1_ref[...]
-    dp = dp_ref[...]
-    gqkv_ref[...] += dot_tn(n1, dp)
-    dn1 = dot_nt(dp, wqkv_ref[...])
-    dx = dm + norm_back(dn1, n1, rs1_ref[...], gains[0:1], 0)
-    for b in range(blocks):
-        for c in range(CHARS):
-            dx_ref[8 * b : 8 * b + 8, width * c : width * c + width] = dx[128 * b + 8 * c : 128 * b + 8 * c + 8]
-
-
-def char_backward(de, kept, gains, wqkv, wout, wup, wdown, pool, wproj, step_words=32):
-    words = de.shape[0]
-    width = wout.shape[0]
-    rows = words * CHARS
-    step_rows = step_words * CHARS
-    full = lambda arr: pl.BlockSpec(arr.shape, lambda i: (0,) * arr.ndim)
-    blk = lambda n, w: pl.BlockSpec((n, w), lambda i: (i, 0))
-    steps = words // step_words
-    weights = (gains, wqkv, wout, wup, wdown, pool, wproj)
-    outs = [wqkv.shape, wout.shape, wup.shape, wdown.shape, wproj.shape, (2, 8, width), (8, width)]
-    return pl.pallas_call(
-        char_bwd_body,
-        grid=(steps,),
-        in_specs=[blk(step_words, de.shape[1])] + [full(w) for w in weights]
-        + [blk(r.shape[0] // steps, r.shape[1]) for r in kept],
-        out_specs=[blk(step_words, CHARS * width)]
-        + [pl.BlockSpec(s, lambda i, n=len(s): (0,) * n) for s in outs],
-        out_shape=[jax.ShapeDtypeStruct((words, CHARS * width), F32)]
-        + [jax.ShapeDtypeStruct(s, F32) for s in outs],
-        scratch_shapes=[pltpu.VMEM((step_rows, 3 * width), BF16), pltpu.VMEM((step_rows, width), BF16)],
-        compiler_params=pltpu.CompilerParams(vmem_limit_bytes=VMEM_LIMIT),
-        name="char_backward",
-    )(de, *weights, *kept)
-
-
-MESH = pl.DeviceIdType.MESH
-CHAR_ROWS = 224
+    )(x, counts, gains, wqkv, wout, wup, wdown, pool, wproj, source, segments, *slices)
+
+
+CHAR_A = 160
+CHAR_B = 64
 WORD_ROWS = 768
+WORD_CHUNKS = 4
+ORDERS = ("yxz", "xyz", "yxz", "xyz")
 SEMS = 8
 
 
@@ -269,8 +321,8 @@
 
 
 class Halving:
-    def __init__(self, n_z, work, got, ssem, rsem, base, order):
-        self.n_z, self.work, self.got = n_z, work, got
+    def __init__(self, n_z, sent, work, got, ssem, rsem, base, order):
+        self.n_z, self.sent, self.work, self.got = n_z, sent, work, got
         self.ssem, self.rsem, self.base, self.order = ssem, rsem, base, order
         self.z, self.x, self.y, self.core = coordinates()
 
@@ -280,18 +332,18 @@
         slot = self.base + phase
         step = "c" if phase == 0 else self.order[phase - 1]
         if step == "c":
-            pairs = [(work.at[1 - core], self.got[0], device_of(z, x, y, 1 - core))]
+            pairs = [(self.sent, self.got[0], device_of(z, x, y, 1 - core))]
         elif step == "y":
-            src = work.at[core, 1 - y] if phase == 1 else work.at[core, 1 - y, x]
+            src = work.at[1 - y] if phase == 1 else work.at[1 - y, x]
             pairs = [(src, self.got[phase], device_of(z, x, 1 - y, core))]
         elif step == "x":
-            src = work.at[core, :, 1 - x] if phase == 1 else work.at[core, y, 1 - x]
+            src = work.at[:, 1 - x] if phase == 1 else work.at[y, 1 - x]
             pairs = [(src, self.got[phase], device_of(z, 1 - x, y, core))]
         else:
             pairs = []
             for k in range(1, self.n_z):
                 other = lax.rem(z + k, self.n_z)
-                pairs.append((work.at[core, y, x, other], self.got[3].at[k - 1], device_of(other, x, y, core)))
+                pairs.append((work.at[y, x, other], self.got[3].at[k - 1], device_of(other, x, y, core)))
         return [remote_copy(s, d, self.ssem, self.rsem, slot + i, peer) for i, (s, d, peer) in enumerate(pairs)]
 
     def start(self, phase):
@@ -301,31 +353,31 @@
     def finish(self, phase):
         for copy in self.copies(phase):
             copy.wait()
-        x, y, core = self.x, self.y, self.core
-        work, got, n_z = self.work, self.got[phase], self.n_z
+        x, y = self.x, self.y
+        work, got = self.work, self.got[phase]
         step = "c" if phase == 0 else self.order[phase - 1]
 
         def add(mine, other):
             def body(i, carry):
-                mine[i] = (mine[i].astype(F32) + other[i].astype(F32)).astype(BF16)
+                mine[i] = mine[i] + other[i]
                 return carry
-            lax.fori_loop(0, n_z, body, 0)
+            lax.fori_loop(0, self.n_z, body, 0)
 
         if step == "c":
             for i in range(2):
                 for j in range(2):
-                    add(work.at[core, i, j], got.at[i, j])
+                    add(work.at[i, j], got.at[i, j])
         elif step == "y" and phase == 1:
             for j in range(2):
-                add(work.at[core, y, j], got.at[j])
+                add(work.at[y, j], got.at[j])
         elif step == "x" and phase == 1:
             for i in range(2):
-                add(work.at[core, i, x], got.at[i])
+                add(work.at[i, x], got.at[i])
         elif step in "yx":
-            add(work.at[core, y, x], got)
+            add(work.at[y, x], got)
 
     def total(self):
-        value = self.work[self.core, self.y, self.x, self.z].astype(F32)
+        value = self.work[self.y, self.x, self.z].astype(F32)
         for k in range(self.n_z - 1):
             value += self.got[3][k].astype(F32)
         return value
@@ -338,21 +390,154 @@
         ]
 
 
-def pack_char(n_z, cqkv_ref, cout_ref, cup_ref, cdown_ref, cproj_ref, cbuf):
-    for d in range(2 * n_z):
-        qkv = cqkv_ref[32 * d : 32 * d + 32, :]
-        out = cout_ref[32 * d : 32 * d + 32, :]
-        down = cdown_ref[128 * d : 128 * d + 128, :]
-        for p in range(4):
-            block = cbuf.at[p % 2, p // 2, d % 2, d // 2]
-            part = qkv[:, 192 * p : 192 * p + 192]
-            block[0:32, :] = part[:, 0:128].astype(BF16)
-            block[32:48, :] = fold_half(part[:, 128:192]).astype(BF16)
-            block[48:64, :] = fold_half(out[:, 64 * p : 64 * p + 64]).astype(BF16)
-            block[64:96, :] = cup_ref[32 * d : 32 * d + 32, 256 * p : 256 * p + 128].astype(BF16)
-            block[96:128, :] = cup_ref[32 * d : 32 * d + 32, 256 * p + 128 : 256 * p + 256].astype(BF16)
-            block[128:192, :] = fold_half(down[:, 64 * p : 64 * p + 64]).astype(BF16)
-            block[192:224, :] = cproj_ref[32 * d : 32 * d + 32, 128 * p : 128 * p + 128].astype(BF16)
+class GradientSums:
+    def __init__(self, n_z, gbuf, refs):
+        self.n_z, self.gbuf = n_z, gbuf
+        abuf, bbuf, wbuf, small, sgot, ssem, rsem, lsem, *got = refs
+        self.abuf, self.bbuf, self.wbuf, self.small, self.sgot = abuf, bbuf, wbuf, small, sgot
+        self.ssem, self.rsem, self.lsem = ssem, rsem, lsem
+        self.core = lax.axis_index("mp") % 2
+        part = WORD_ROWS // WORD_CHUNKS
+        sent = gbuf.at[1 - self.core]
+        self.chunks = [
+            Halving(
+                n_z, sent.at[:, :, :, part * i : part * i + part], wbuf.at[:, :, :, part * i : part * i + part],
+                got[4 * i : 4 * i + 4], ssem, rsem, SEMS * i, ORDERS[i],
+            )
+            for i in range(WORD_CHUNKS)
+        ]
+        base = SEMS * WORD_CHUNKS
+        at = 4 * WORD_CHUNKS
+        self.parta = Halving(
+            n_z, abuf.at[1 - self.core], abuf.at[self.core], got[at : at + 4], ssem, rsem, base, "yxz"
+        )
+        self.partb = Halving(
+            n_z, bbuf.at[1 - self.core], bbuf.at[self.core], got[at + 4 : at + 8], ssem, rsem, base + SEMS, "yxz"
+        )
+        self.tiny = base + 2 * SEMS
+
+    @staticmethod
+    def scratch(n_z):
+        n_sem = SEMS * (WORD_CHUNKS + 3)
+        shapes = [
+            pltpu.VMEM((2, 2, 2, n_z, CHAR_A, 128), BF16), pltpu.VMEM((2, 2, 2, n_z, CHAR_B, 128), BF16),
+            pltpu.VMEM((2, 2, n_z, WORD_ROWS, 128), BF16),
+            pltpu.VMEM((4, 16, 128), F32), pltpu.VMEM((2 + n_z, 16, 128), F32),
+            pltpu.SemaphoreType.DMA((n_sem,)), pltpu.SemaphoreType.DMA((n_sem,)), pltpu.SemaphoreType.DMA,
+        ]
+        for _ in range(WORD_CHUNKS):
+            shapes += Halving.got_shapes(n_z, WORD_ROWS // WORD_CHUNKS)
+        return shapes + Halving.got_shapes(n_z, CHAR_A) + Halving.got_shapes(n_z, CHAR_B)
+
+    def begin(self, step):
+        z, x, y, core = coordinates()
+        chunks = self.chunks
+        load = pltpu.make_async_copy(self.gbuf.at[core], self.wbuf, self.lsem)
+
+        def advance(at, moves):
+            @pl.when(step == at)
+            def _():
+                for i, phase in moves:
+                    chunks[i].finish(phase)
+                    if phase < 3:
+                        chunks[i].start(phase + 1)
+
+        @pl.when(step == 0)
+        def _():
+            load.start()
+            barrier = pltpu.get_barrier_semaphore()
+            peers = [device_of(z, x, y, 1 - core), device_of(z, x, 1 - y, core), device_of(z, 1 - x, y, core)]
+            peers += [device_of(lax.rem(z + k, self.n_z), x, y, core) for k in range(1, self.n_z)]
+            for peer in peers:
+                pl.semaphore_signal(barrier, inc=1, device_id=peer, device_id_type=MESH)
+            pl.semaphore_wait(barrier, len(peers))
+            for i in range(WORD_CHUNKS):
+                chunks[i].start(0)
+            load.wait()
+
+        for at, moves in SCHEDULE:
+            advance(at, moves)
+
+    def middle(self, step, half, gup_ref, gdown_ref, gproj_ref):
+        n_z, abuf, part = self.n_z, self.abuf, self.parta
+
+        @pl.when(step == half - 1)
+        def _():
+            for d in range(2 * n_z):
+                down = gdown_ref[128 * d : 128 * d + 128, :]
+                for p in range(4):
+                    block = abuf.at[p % 2, p // 2, d % 2, d // 2]
+                    block[0:32, :] = gup_ref[32 * d : 32 * d + 32, 256 * p : 256 * p + 128].astype(BF16)
+                    block[32:64, :] = gup_ref[32 * d : 32 * d + 32, 256 * p + 128 : 256 * p + 256].astype(BF16)
+                    block[64:128, :] = fold_half(down[:, 64 * p : 64 * p + 64]).astype(BF16)
+                    block[128:160, :] = gproj_ref[32 * d : 32 * d + 32, 128 * p : 128 * p + 128].astype(BF16)
+            part.start(0)
+
+        for phase, at in enumerate(PART_STEPS):
+            @pl.when(step == half + at)
+            def _():
+                part.finish(phase)
+                part.start(phase + 1)
+
+    def end(
+        self, step, gqkv_ref, gout_ref, ggain_ref, gpool_ref, gains_ref, wgain_ref,
+        outa_ref, outb_ref, word_ref, small_ref,
+    ):
+        n_z, bbuf, small, sgot = self.n_z, self.bbuf, self.small, self.sgot
+        z, x, y, core = coordinates()
+        peers = [device_of(z, x, y, 1 - core), device_of(z, x, 1 - y, core), device_of(z, 1 - x, y, core)]
+        z_peers = [device_of(lax.rem(z + k, n_z), x, y, core) for k in range(1, n_z)]
+
+        @pl.when(step == pl.num_programs(0) - 1)
+        def _():
+            for d in range(2 * n_z):
+                qkv = gqkv_ref[32 * d : 32 * d + 32, :]
+                out = gout_ref[32 * d : 32 * d + 32, :]
+                for p in range(4):
+                    block = bbuf.at[p % 2, p // 2, d % 2, d // 2]
+                    own = qkv[:, 192 * p : 192 * p + 192]
+                    block[0:32, :] = own[:, 0:128].astype(BF16)
+                    block[32:48, :] = fold_half(own[:, 128:192]).astype(BF16)
+                    block[48:64, :] = fold_half(out[:, 64 * p : 64 * p + 64]).astype(BF16)
+            self.partb.start(0)
+            small[0] = pack_small(ggain_ref, gpool_ref, gains_ref, wgain_ref)
+            for i in range(3):
+                copy = remote_copy(small.at[i], sgot.at[i], self.ssem, self.rsem, self.tiny + i, peers[i])
+                copy.start()
+                self.partb.finish(i)
+                self.partb.start(i + 1)
+                copy.wait()
+                small[i + 1] = small[i] + sgot[i]
+            tail = [
+                remote_copy(small.at[3], sgot.at[2 + k], self.ssem, self.rsem, self.tiny + 2 + k, z_peers[k - 1])
+                for k in range(1, n_z)
+            ]
+            for copy in tail:
+                copy.start()
+            part = WORD_ROWS // WORD_CHUNKS
+            for i in range(WORD_CHUNKS):
+                word_ref[part * i : part * i + part, :] = self.chunks[i].total()
+            self.parta.finish(3)
+            outa_ref[...] = self.parta.total()
+            for copy in tail:
+                copy.wait()
+            total = small[3]
+            for k in range(1, n_z):
+                total += sgot[2 + k]
+            small_ref[...] = total
+            self.partb.finish(3)
+            outb_ref[...] = self.partb.total()
+
+
+SCHEDULE = (
+    (1, ((0, 0), (1, 0))),
+    (2, ((2, 0), (3, 0))),
+    (5, ((0, 1), (1, 1))),
+    (8, ((2, 1), (3, 1), (0, 2), (1, 2))),
+    (11, ((2, 2), (3, 2))),
+    (14, ((0, 3), (1, 3), (2, 3), (3, 3))),
+)
+PART_STEPS = (0, 3, 5)
 
 
 def pack_small(cgain_ref, cpool_ref, cg_ref, wgain_ref):
@@ -369,100 +554,19 @@
     return jnp.concatenate(rows, 0)
 
 
-def reduce_body(
-    n_z,
-    cqkv_ref, cout_ref, cup_ref, cdown_ref, cproj_ref, cgain_ref, cpool_ref, cg_ref, wbuf_in, wgain_ref,
-    char_ref, word_ref, small_ref,
-    cbuf, *refs,
-):
-    c_got, wa_got, wb_got = refs[0:4], refs[4:8], refs[8:12]
-    wbuf, small, sgot, ssem, rsem, lsem = refs[12:]
-    z, x, y, core = coordinates()
-    peers = [device_of(z, x, y, 1 - core), device_of(z, x, 1 - y, core), device_of(z, 1 - x, y, core)]
-    z_peers = [device_of(lax.rem(z + k, n_z), x, y, core) for k in range(1, n_z)]
-    barrier = pltpu.get_barrier_semaphore()
-    for peer in peers + z_peers:
-        pl.semaphore_signal(barrier, inc=1, device_id=peer, device_id_type=MESH)
-    load = pltpu.make_async_copy(wbuf_in, wbuf, lsem)
-    load.start()
-    half = WORD_ROWS // 2
-    first = Halving(n_z, wbuf.at[:, :, :, :, 0:half], wa_got, ssem, rsem, 0, "yxz")
-    second = Halving(n_z, wbuf.at[:, :, :, :, half:], wb_got, ssem, rsem, SEMS, "xyz")
-    chars = Halving(n_z, cbuf, c_got, ssem, rsem, 2 * SEMS, "yxz")
-    tiny = 3 * SEMS
-    load.wait()
-    pl.semaphore_wait(barrier, len(peers) + len(z_peers))
-    first.start(0)
-    second.start(0)
-    pack_char(n_z, cqkv_ref, cout_ref, cup_ref, cdown_ref, cproj_ref, cbuf)
-    small[0] = pack_small(cgain_ref, cpool_ref, cg_ref, wgain_ref)
-    chars.start(0)
-    for i in range(3):
-        copy = remote_copy(small.at[i], sgot.at[i], ssem, rsem, tiny + i, peers[i])
-        copy.start()
-        for part in (first, second, chars):
-            part.finish(i)
-            part.start(i + 1)
-        copy.wait()
-        small[i + 1] = small[i] + sgot[i]
-    tail = [remote_copy(small.at[3], sgot.at[2 + k], ssem, rsem, tiny + 2 + k, z_peers[k - 1]) for k in range(1, n_z)]
-    for copy in tail:
-        copy.start()
-    for copy in tail:
-        copy.wait()
-    total = small[3]
-    for k in range(1, n_z):
-        total += sgot[2 + k]
-    small_ref[...] = total
-    first.finish(3)
-    word_ref[0:half, :] = first.total()
-    second.finish(3)
-    word_ref[half:, :] = second.total()
-    chars.finish(3)
-    char_ref[...] = chars.total()
-
-
-def reduce_grads(n_dp, char_parts, char_gains, wbuf, wgain):
-    n_z = n_dp // 2
-    vm = pl.BlockSpec(memory_space=pltpu.VMEM)
-    args = (*char_parts, char_gains, wbuf, wgain)
-    specs = [vm] * len(args)
-    specs[-2] = pl.BlockSpec(memory_space=pl.ANY)
-    outs = [(CHAR_ROWS, 128), (WORD_ROWS, 128), (16, 128)]
-    return pl.pallas_call(
-        functools.partial(reduce_body, n_z),
-        in_specs=specs,
-        out_specs=[vm] * len(outs),
-        out_shape=[jax.ShapeDtypeStruct(s, F32) for s in outs],
-        scratch_shapes=[pltpu.VMEM((2, 2, 2, n_z, CHAR_ROWS, 128), BF16)]
-        + Halving.got_shapes(n_z, CHAR_ROWS)
-        + Halving.got_shapes(n_z, WORD_ROWS // 2) * 2
-        + [
-            pltpu.VMEM((2, 2, 2, n_z, WORD_ROWS, 128), BF16),
-            pltpu.VMEM((4, 16, 128), F32),
-            pltpu.VMEM((2 + n_z, 16, 128), F32),
-            pltpu.SemaphoreType.DMA((4 * SEMS,)),
-            pltpu.SemaphoreType.DMA((4 * SEMS,)),
-            pltpu.SemaphoreType.DMA,
-        ],
-        compiler_params=pltpu.CompilerParams(collective_id=1, has_side_effects=True, vmem_limit_bytes=VMEM_LIMIT),
-        name="reduce_gradients",
-    )(*args)
-
-
 def unpack_body(
-    char_ref, word_ref, small_ref,
+    parta_ref, partb_ref, word_ref, small_ref,
     oqkv_ref, oout_ref, oup_ref, odown_ref, oproj_ref, owqkv_ref, owout_ref, owup_ref, owdown_ref,
     ocgain_ref, opool_ref, owgain_ref,
 ):
-    char, word, total = char_ref[...], word_ref[...], small_ref[...]
-    oqkv_ref[:, 0:128] = char[0:32]
-    oqkv_ref[:, 128:192] = unfold_half(char[32:48])
-    oout_ref[...] = unfold_half(char[48:64])
-    oup_ref[:, 0:128] = char[64:96]
-    oup_ref[:, 128:256] = char[96:128]
-    odown_ref[...] = unfold_half(char[128:192])
-    oproj_ref[...] = char[192:224]
+    parta, partb, word, total = parta_ref[...], partb_ref[...], word_ref[...], small_ref[...]
+    oqkv_ref[:, 0:128] = partb[0:32]
+    oqkv_ref[:, 128:192] = unfold_half(partb[32:48])
+    oout_ref[...] = unfold_half(partb[48:64])
+    oup_ref[:, 0:128] = parta[0:32]
+    oup_ref[:, 128:256] = parta[32:64]
+    odown_ref[...] = unfold_half(parta[64:128])
+    oproj_ref[...] = parta[128:160]
     for t in range(3):
         owqkv_ref[t] = word[64 * t : 64 * t + 64]
     owout_ref[...] = word[192:256].T
@@ -478,16 +582,152 @@
         opool_ref[:, 128 * t : 128 * t + 128] = total[4 + t : 5 + t]
 
 
-def unpack_grads(char, word, small):
+def unpack_grads(*sums):
     vm = pl.BlockSpec(memory_space=pltpu.VMEM)
     outs = [(32, 192), (32, 64), (32, 256), (128, 64), (32, 128), (3, 64, 128), (128, 64), (64, 512), (512, 64), (2, 256), (1, 256), (2, 512)]
     return pl.pallas_call(
         unpack_body,
-        in_specs=[vm] * 3,
+        in_specs=[vm] * 4,
         out_specs=[vm] * len(outs),
         out_shape=[jax.ShapeDtypeStruct(s, F32) for s in outs],
         name="unpack_gradients",
-    )(char, word, small)
+    )(*sums)
+
+
+def char_bwd_body(
+    n_dp, fused,
+    de_ref, gains_ref, wqkv_ref, wout_ref, wup_ref, wdown_ref, pool_ref, wproj_ref,
+    n1_ref, p_ref, a_ref, o_ref, n2_ref, rs1_ref, rs2_ref, act_ref, dg_ref, f_ref, aw_ref, pooled_ref,
+    *refs,
+):
+    if fused:
+        gbuf_any, wgain_ref, dx_ref, outa_ref, outb_ref, word_ref, small_ref, *refs = refs
+        dm_ref, dp_ref, do_ref, *refs = refs
+    else:
+        dx_ref, *refs = refs
+    gqkv_ref, gout_ref, gup_ref, gdown_ref, gproj_ref, ggain_ref, gpool_ref, *refs = refs
+    if not fused:
+        dm_ref, dp_ref, do_ref = refs
+    step = pl.program_id(0)
+    half = pl.num_programs(0) // 2
+    words = de_ref.shape[0]
+    width = n1_ref.shape[1]
+    blocks = words // 8
+    rows = words * CHARS
+    gains = gains_ref[...].astype(F32)
+    if fused:
+        sums = GradientSums(n_dp // 2, gbuf_any, refs)
+        sums.begin(step)
+
+    @pl.when(step == 0)
+    def _():
+        for ref in (gqkv_ref, gout_ref, gup_ref, gdown_ref, gproj_ref, ggain_ref, gpool_ref):
+            ref[...] = jnp.zeros_like(ref)
+
+    def norm_back(dn, n, rstd, gain, row):
+        d1 = dn * gain
+        dnn = dn * n.astype(F32)
+        ggain_ref[row] += jnp.sum(dnn.reshape(rows // 8, 8, width), 0)
+        m1 = jnp.mean(d1, -1, keepdims=True)
+        m2 = jnp.mean(dnn, -1, keepdims=True)
+        return rstd * (d1 - m1 - n.astype(F32) * (1.0 / gain) * m2)
+
+    @pl.when(step < half)
+    def _():
+        de = de_ref[...]
+        gproj_ref[...] += dot_tn(pooled_ref[...], de)
+        dpool = dot_nt(de, wproj_ref[...]).reshape(blocks, 1, 8, width)
+        f = f_ref[...].astype(F32).reshape(blocks, CHARS, 8, width)
+        aw = aw_ref[...].reshape(blocks, CHARS, 8, 1)
+        g = jnp.sum(f * dpool, -1, keepdims=True)
+        dt = aw * (g - jnp.sum(aw * g, 1, keepdims=True))
+        gpool_ref[...] += jnp.sum((dt * f).reshape(rows // 8, 8, width), 0)
+        df = (aw * dpool + dt * pool_ref[...].astype(F32)).reshape(rows, width)
+        dfb = df.astype(BF16)
+        gdown_ref[...] += dot_tn(act_ref[...], dfb)
+        dh = (dg_ref[...].astype(F32) * dot_nt(dfb, wdown_ref[...])).astype(BF16)
+        n2 = n2_ref[...]
+        gup_ref[...] += dot_tn(n2, dh)
+        dn2 = dot_nt(dh, wup_ref[...])
+        dm_ref[pl.ds(pl.multiple_of(step * rows, rows), rows), :] = df + norm_back(dn2, n2, rs2_ref[...], gains[1:2], 1)
+
+    @pl.when(step >= half)
+    def _():
+        dm = dm_ref[pl.ds(pl.multiple_of((step - half) * rows, rows), rows), :]
+        dmb = dm.astype(BF16)
+        gout_ref[...] += dot_tn(o_ref[...], dmb)
+        do_ref[...] = dot_nt(dmb, wout_ref[...]).astype(BF16)
+        scale = (width // CHAR_HEADS) ** -0.5
+        for b in range(blocks):
+            sl = slice(128 * b, 128 * b + 128)
+            q = p_ref[sl, 0:width]
+            k = p_ref[sl, width : 2 * width]
+            v = p_ref[sl, 2 * width : 3 * width]
+            do = do_ref[sl, :]
+            ab = a_ref[CHAR_HEADS * 128 * b : CHAR_HEADS * 128 * (b + 1), :]
+            a = ab.astype(F32).reshape(CHAR_HEADS, CHARS, 8, 128)
+            dpt = dot_nt(head_stack(v, CHAR_HEADS, 1.0), do).reshape(CHAR_HEADS, CHARS, 8, 128)
+            delta = jnp.sum(a * dpt, 1, keepdims=True)
+            ds = (a * (dpt - delta)).reshape(CHAR_HEADS * 128, 128).astype(BF16)
+            wide_ds = jnp.concatenate([ds[128 * h : 128 * h + 128] for h in range(CHAR_HEADS)], 1)
+            wide_a = jnp.concatenate([ab[128 * h : 128 * h + 128] for h in range(CHAR_HEADS)], 1)
+            dp_ref[sl, 0:width] = dot_tn(ds, head_stack(k, CHAR_HEADS, scale)).astype(BF16)
+            dp_ref[sl, width : 2 * width] = dot_nn(wide_ds, head_stack(q, CHAR_HEADS, scale)).astype(BF16)
+            dp_ref[sl, 2 * width : 3 * width] = dot_nn(wide_a, head_stack(do, CHAR_HEADS, 1.0)).astype(BF16)
+        n1 = n1_ref[...]
+        dp = dp_ref[...]
+        gqkv_ref[...] += dot_tn(n1, dp)
+        dn1 = dot_nt(dp, wqkv_ref[...])
+        dx = dm + norm_back(dn1, n1, rs1_ref[...], gains[0:1], 0)
+        for b in range(blocks):
+            for c in range(CHARS):
+                dx_ref[8 * b : 8 * b + 8, width * c : width * c + width] = dx[128 * b + 8 * c : 128 * b + 8 * c + 8]
+
+    if fused:
+        sums.middle(step, half, gup_ref, gdown_ref, gproj_ref)
+        sums.end(
+            step, gqkv_ref, gout_ref, ggain_ref, gpool_ref, gains_ref, wgain_ref,
+            outa_ref, outb_ref, word_ref, small_ref,
+        )
+
+
+def char_backward(n_dp, de, kept, gains, wqkv, wout, wup, wdown, pool, wproj, gbuf, wgain, step_words=32):
+    words = de.shape[0]
+    width = wout.shape[0]
+    rows = words * CHARS
+    step_rows = step_words * CHARS
+    steps = words // step_words
+    fused = gbuf is not None
+    full = lambda arr: pl.BlockSpec(arr.shape, lambda i: (0,) * arr.ndim)
+    fixed = lambda s: pl.BlockSpec(s, lambda i: (0,) * len(s))
+    early = lambda n, w: pl.BlockSpec((n, w), lambda i: (lax.min(i, steps - 1), 0))
+    late = lambda n, w: pl.BlockSpec((n, w), lambda i: (lax.max(i - steps, 0), 0))
+    weights = (gains, wqkv, wout, wup, wdown, pool, wproj)
+    when = [late, late, late, late, early, late, early, early, early, early, early, early]
+    grads = [wqkv.shape, wout.shape, wup.shape, wdown.shape, wproj.shape, (2, 8, width), (8, width)]
+    scratch = [pltpu.VMEM((rows, width), F32), pltpu.VMEM((step_rows, 3 * width), BF16), pltpu.VMEM((step_rows, width), BF16)]
+    args = [de, *weights, *kept]
+    in_specs = [early(step_words, de.shape[1])] + [full(w) for w in weights]
+    in_specs += [f(r.shape[0] // steps, r.shape[1]) for f, r in zip(when, kept)]
+    params = dict(vmem_limit_bytes=VMEM_LIMIT)
+    if fused:
+        outs = [(CHAR_A, 128), (CHAR_B, 128), (WORD_ROWS, 128), (16, 128)]
+        args += [gbuf, wgain]
+        in_specs += [pl.BlockSpec(memory_space=pl.ANY), full(wgain)]
+        scratch += [pltpu.VMEM(s, F32) for s in grads] + GradientSums.scratch(n_dp // 2)
+        params.update(collective_id=1, has_side_effects=True)
+    else:
+        outs = grads
+    return pl.pallas_call(
+        functools.partial(char_bwd_body, n_dp, fused),
+        grid=(2 * steps,),
+        in_specs=in_specs,
+        out_specs=[late(step_words, CHARS * width)] + [fixed(s) for s in outs],
+        out_shape=[jax.ShapeDtypeStruct((words, CHARS * width), F32)] + [jax.ShapeDtypeStruct(s, F32) for s in outs],
+        scratch_shapes=scratch,
+        compiler_params=pltpu.CompilerParams(**params),
+        name="char_backward",
+    )(*args)
 
 
 def norm_fwd(values, gain):
@@ -506,24 +746,20 @@
     return rstd * (d1 - m1 - n * (1.0 / gain) * m2), jnp.sum(dnn, 0, keepdims=True) / gain
 
 
-def as_column(row):
-    return jnp.transpose(jnp.broadcast_to(row.astype(F32), (128, row.shape[1])))
-
-
 def word_body(
     n_dp, cap, packed,
-    e_ref, src_ref, seg_ref, cot_ref, gains_ref, wqkv_ref, wout_ref, wup_ref, wdown_ref,
-    *refs,
+    e_ref, onehot, place, seg_all, cot_ref, gains_ref, *refs,
 ):
+    slices, wholes, refs = refs[:4], refs[4:8], refs[8:]
     if packed:
         out_ref, de_ref, gbuf_ref, ggain_ref, *refs = refs
     else:
         out_ref, de_ref, gqkv_ref, gout_ref, gup_ref, gdown_ref, ggain_ref, *refs = refs
     (
-        onehot, place, vec_send, vec_got, row_send, row_got, seg_all, segc_all, rows_ref, normed, rstd_a,
+        wqkv_ref, wout_ref, wup_ref, wdown_ref, vec_send, vec_got, segc_all, rows_ref, normed, rstd_a,
         qkv_send, qkv_all, weights, o_send, o_all, act_ref, dh_ref, dact_ref, dm_ref,
         do_send, do_all, dk_acc, dv_acc, dqkv_send, dqkv_all, back_send, ret,
-        ssem, rsem,
+        ssem, rsem, lsem,
     ) = refs
     dp, mp = lax.axis_index("dp"), lax.axis_index("mp")
     n_mp = 4
@@ -551,39 +787,29 @@
         copy.start()
         return copy
 
-    source = src_ref[...]
-    owner = source // (words * n_mp)
-    owner_c = as_column(owner)[:, 0:1]
-    index_r = lax.broadcasted_iota(jnp.int32, (words, words), 0)
-    index_c = lax.broadcasted_iota(jnp.int32, (words, words), 1)
-    earlier = (owner_c == owner.astype(F32)) & (index_r < index_c)
-    rank = jnp.sum(jnp.where(earlier, 1.0, 0.0), 0, keepdims=True).astype(jnp.int32)
-    slot_of = lax.rem(owner - dp + n_dp, n_dp) * cap + rank
-    onehot[...] = jnp.where(lax.broadcasted_iota(jnp.int32, (slots, words), 0) == slot_of, 1.0, 0.0).astype(BF16)
-    row_mat = as_column(lax.rem(source, words) + 1).astype(BF16)
-    row_send[...] = dot_nn(onehot[...], row_mat).astype(BF16).reshape(n_dp, cap, 128)
-    seg_all[mp] = jnp.broadcast_to(seg_ref[...], (8, words))
+    loads = []
+    for i, held in ((3, wdown_ref), (0, wqkv_ref), (1, wout_ref), (2, wup_ref)):
+        loads.append([pltpu.make_async_copy(slices[i], held.at[mp], lsem.at[i, 0])])
+        loads[-1] += [
+            pltpu.make_async_copy(wholes[i].at[mate], held.at[mate], lsem.at[i, 1 + j]) for j, mate in enumerate(mates)
+        ]
+        for load in loads[-1]:
+            load.start()
     vec_send[...] = dot_nn(onehot[...], e_ref[...]).astype(BF16).reshape(n_dp, cap, width)
 
     pl.semaphore_wait(barrier, n_dp - 1 + 3)
-    row_copies = [send(row_send.at[k], row_got.at[k], to_dp[k]) for k in range(1, n_dp)]
     vec_copies = [send(vec_send.at[k], vec_got.at[k], to_dp[k]) for k in range(1, n_dp)]
-    seg_copies = [send(seg_all.at[mp], seg_all.at[mp], (dp, mate)) for mate in mates]
-    row_got[0] = row_send[0]
     vec_got[0] = vec_send[0]
     gains = gains_ref[...].astype(F32)
     cot = cot_ref[...]
+    for load in loads[0]:
+        load.wait()
     for p in range(n_mp):
         dact_ref[p] = dot_nt(cot, wdown_ref[p])
-    for copy in seg_copies:
-        copy.wait()
     for j in range(n_mp):
         segc_all[words * j : words * j + words, :] = as_column(seg_all[j, 0:1, :])
-    for copy in row_copies:
-        copy.wait()
-    at_row = row_got[...].reshape(slots, 128)[:, 0:1].astype(F32) - 1.0
-    lanes = lax.broadcasted_iota(jnp.int32, (slots, words), 1).astype(F32)
-    place[...] = jnp.where(lanes == at_row, 1.0, 0.0).astype(BF16)
+    for load in loads[1] + loads[2] + loads[3]:
+        load.wait()
     for copy in vec_copies:
         copy.wait()
     rows = dot_tn(place[...], vec_got[...].reshape(slots, width))
@@ -715,8 +941,9 @@
     de_ref[...] = dot_tn(onehot[...], ret[...].reshape(slots, width)).astype(BF16)
 
 
-def word_layer(n_dp, word_vec, source, segments, cotangent, gains, wqkv, wout, wup, wdown):
+def word_layer(n_dp, word_vec, onehot, place, segments, cotangent, gains, slices, wholes):
     words, width = word_vec.shape
+    wqkv, wout, wup, wdown = wholes
     n_mp = wqkv.shape[0]
     cap = -(-2 * words // n_dp // 16) * 16
     slots = cap * n_dp
@@ -729,12 +956,12 @@
         outs += [((n_mp, width, n), F32) for n in (3 * pair, pair, wup.shape[2], wup.shape[2])]
     outs.append(((2, width), F32))
     hid = wup.shape[2]
-    n_sem = 3 * (n_dp - 1) + 5 * 3
+    n_sem = 2 * (n_dp - 1) + 4 * 3
     vm = pl.BlockSpec(memory_space=pltpu.VMEM)
-    args = (word_vec, source.reshape(1, -1), segments.reshape(1, -1), cotangent, gains, wqkv, wout, wup, wdown)
+    args = (word_vec, onehot, place, segments, cotangent, gains, *slices, *wholes)
     shapes = [
-        ((slots, words), BF16), ((slots, words), BF16), ((n_dp, cap, width), BF16), ((n_dp, cap, width), BF16),
-        ((n_dp, cap, 128), BF16), ((n_dp, cap, 128), BF16), ((n_mp, 8, words), jnp.int32), ((n_mp * words, 128), F32),
+        (wqkv.shape, BF16), (wout.shape, BF16), (wup.shape, BF16), (wdown.shape, BF16),
+        ((n_dp, cap, width), BF16), ((n_dp, cap, width), BF16), ((n_mp * words, 128), F32),
         ((words, width), F32), ((2, words, width), BF16), ((1, words, 1), F32),
         ((n_mp, words, 3 * pair), BF16), ((n_mp, words, 3 * pair), BF16), ((n_mp, 2, n_mp * words, words), BF16),
         ((n_mp, words, pair), BF16), ((n_mp, words, pair), BF16),
@@ -744,11 +971,11 @@
     ]
     return pl.pallas_call(
         functools.partial(word_body, n_dp, cap, packed),
-        in_specs=[vm] * len(args),
+        in_specs=[vm] * (len(args) - 8) + [pl.BlockSpec(memory_space=pl.ANY)] * 8,
         out_specs=[vm] * len(outs),
         out_shape=[jax.ShapeDtypeStruct(s, d) for s, d in outs],
         scratch_shapes=[pltpu.VMEM(s, d) for s, d in shapes]
-        + [pltpu.SemaphoreType.DMA((n_sem,)), pltpu.SemaphoreType.DMA((n_sem,))],
+        + [pltpu.SemaphoreType.DMA((n_sem,)), pltpu.SemaphoreType.DMA((n_sem,)), pltpu.SemaphoreType.DMA((4, 4))],
         compiler_params=pltpu.CompilerParams(collective_id=0, has_side_effects=True, vmem_limit_bytes=VMEM_LIMIT),
         name="word_layer",
     )(*args)
@@ -795,20 +1022,23 @@
     char_weights = (
         char_norm_gains, char_qkv, char_out, char_up, char_down, pool_vector.reshape(1, -1), char_proj
     )
-    word_weights = [
-        lax.all_gather(w, "mp", axis=0, tiled=False)
-        for w in (
-            jnp.transpose(word_qkv, (1, 0, 2)).reshape(word_qkv.shape[1], -1), word_out, word_up, word_down,
-        )
-    ]
-    word_vec, *char_kept = char_forward(char_input, char_counts.reshape(-1, 1), *char_weights)
+    slices = (
+        jnp.transpose(word_qkv, (1, 0, 2)).reshape(word_qkv.shape[1], -1), word_out, word_up, word_down,
+    )
+    word_vec, *kept = char_forward(
+        groups, char_input, char_counts.reshape(-1, 1), *char_weights,
+        word_source.reshape(1, -1), segment_ids.reshape(1, -1), slices,
+    )
+    char_kept, (onehot, place, segments, *word_weights) = kept[:12], kept[12:]
     output, d_word, *word_parts, word_gains = word_layer(
-        groups, word_vec, word_source, segment_ids, cotangent, word_norm_gains, *word_weights
+        groups, word_vec, onehot, place, segments, cotangent, word_norm_gains, slices, word_weights
     )
-    d_chars, *char_parts = char_backward(d_word, char_kept, *char_weights)
-    if groups == 8:
-        sums = reduce_grads(groups, char_parts, char_norm_gains, word_parts[0], word_gains)
-        grads = unpack_grads(*sums)
+    fused = groups == 8
+    d_chars, *char_parts = char_backward(
+        groups, d_word, char_kept, *char_weights, word_parts[0] if fused else None, word_gains
+    )
+    if fused:
+        grads = unpack_grads(*char_parts)
     else:
         grads = plain_reduce(char_parts, char_norm_gains, word_parts, word_gains)
     *mats, grad_char_gains, grad_pool, grad_word_gains = grads

time: 280 us -> 214 us (0.76)
  Pallas kernels: 226 us -> 198 us
  waiting for transfers between devices: 21.8 us -> 0 us
  between operations: 13.8 us -> 0.69 us
  blocking collectives: 9.28 us -> 0 us
  local copies, waits for them, and re-layouts: 8.96 us -> 14.9 us
    all_gather x3 -> x0, waiting for transfers between devices: 20.4 us -> none  [per_device(): lax.all_gather(w, 'mp', axis=0, tiled=False)]
    pallas_call x4 -> x3, Pallas kernels: 147 us -> 127 us  [the longest x1 73.8 us: char_backward(): pl.pallas_call(functools.partial(char_bwd_body, n_dp, fused), grid=(2 * s...]
    all_gather x1 -> x0, blocking collectives: 9.28 us -> none  [per_device(): lax.all_gather(w, 'mp', axis=0, tiled=False)]
    pallas_call x1, Pallas kernels: 78.4 us -> 70.2 us  [word_layer(): pl.pallas_call(functools.partial(word_body, n_dp, cap, packed), in_specs=...]
    unnamed x13 -> x8, local copies, waits for them, and re-layouts: 6.68 us -> 11.3 us
  transfers between devices with their start and end apart: 3 -> 0, of which waited for: 1 -> 0; matrix products, arithmetic and copies ran while one was open for 0% -> 0% of each run, Pallas kernels for 14% -> 0%
where the time goes in v3:
time: 214 us; the launch traced here: 213 us
  Pallas kernels  198 us (93%)
  local copies, waits for them, and re-layouts  14.9 us (7%)
    pallas_call x1, Pallas kernels, char_backward(): pl.pallas_call(functools.partial(char_bwd_body, n_dp, fused), grid=(2 * s...  73.8 us
    pallas_call x1, Pallas kernels, word_layer(): pl.pallas_call(functools.partial(word_body, n_dp, cap, packed), in_specs=...  70.2 us
    pallas_call x1, Pallas kernels, char_forward(): pl.pallas_call(functools.partial(char_fwd_body, n_dp, cap), grid=(words /...  51.6 us
    unnamed x8, local copies, waits for them, and re-layouts  11.3 us

profile of v3, /device:TPU:0, one launch (start us, length us, event | category | flops | bytes accessed | tf_op | source)
XLA Modules:
  0.0 213.3 jit_solution(18421653401443544863)
XLA Ops:
  0.6 1.2 reshape.47.pool_ref
  1.9 1.5 copy.36.cnt_ref
  3.3 1.2 copy.35
  4.5 0.9 copy.37.s_qkv.refs_0_
  5.4 51.6 %char_forward.1 = (bf16[256,512]{1,0:T(8,128)(2,1)}, bf16[4096,256]{1,0:T(8,128)(2,1)}, bf16[4096,768]{1,0:T(8,128)(2,1)}, bf16[16384,128]{1,0:T(8,128)(2,1)}, b...) custom-call(bf16[256,4096]{1,0:T(8,128)(2,1)} %x_ref.1, ...), custom_call_target="tpu_custom_call" | custom-call | tf_op jit(solution)/shard_map/char_forward/pallas_call | solution.py:269
  57.0 70.2 %word_layer.1 = (bf16[256,512]{1,0:T(8,128)(2,1)}, bf16[256,512]{1,0:T(8,128)(2,1)}, bf16[2,2,2,4,768,128]{5,4,3,2,1,0:T(8,128)(2,1)}, f32[2,512]{1,0:T(2,128)}) custom-call(bf16[256,512]{1,0:T(8,128)(2,1)} %get-tuple-element.55.e_ref, bf16[512,256]{1,0:T(8,128)(2,1)} %get-tuple-element.56.onehot, bf16[512,256]{1,0:T(8,128)(2,1)} %get-tuple-element.57.place, ...), custom_call_target="tpu_custom_call" | custom-call | tf_op jit(solution)/shard_map/word_layer/pallas_call | solution.py:972
  127.3 0.0 copy-start
  127.3 73.8 %char_backward.1 = (f32[256,4096]{1,0:T(8,128)}, f32[160,128]{1,0:T(8,128)}, f32[64,128]{1,0:T(8,128)}, f32[768,128]{1,0:T(8,128)}, f32[16,128]{1,0:T(8,128)}) custom-call(bf16[256,512]{1,0:T(8,128)(2,1)} %get-tuple-element.64.de_ref, bf16[2,256]{1,0:T(2,128)(2,1)} %gains_ref.5, bf16[256,768]{1,0:T(8,128)(2,1)} %wqkv_ref.3, bf16[256,256]{1,0:T(8,128)(2,1)} %wout_ref.3, ...), custom_call_target="tpu_custom_call" | custom-call | tf_op jit(solution)/shard_map/char_backward/pallas_call | solution.py:721
  201.1 2.0 unpack_gradients.1
  203.1 1.5 copy.39
  204.7 1.5 copy.40
  206.2 1.7 copy.41
  207.9 0.0 copy-done
  207.9 0.7 copy.44
  208.6 4.7 %copy.45 = f32[256,4096]{1,0:T(8,128)} copy(f32[256,4096]{1,0:T(8,128)} %get-tuple-element.139) | data formatting | bytes 8388608
Async XLA Ops:
  127.3 80.7 %copy-start = (bf16[256,512]{1,0:T(8,128)(2,1)S(1)}, bf16[256,512]{1,0:T(8,128)(2,1)}, u32[]{:S(2)}) copy-start(bf16[256,512]{1,0:T(8,128)(2,1)} %get-tuple-element.138) | copy-start | bytes 786436

commit v4 on v3

v4 whole, which is shorter than its diff:
```python
import functools
import jax
import jax.numpy as jnp
from jax import lax
from jax.experimental import pallas as pl
from jax.experimental.pallas import tpu as pltpu
from jax.sharding import PartitionSpec as P

HEADS = 8
CHARS = 16
CHAR_HEADS = 4
EPSILON = 1e-05
NEGATIVE = -1e30
GELU_A = 0.7978845608028654
GELU_B = 0.044715
F32 = jnp.float32
BF16 = jnp.bfloat16
MESH = pl.DeviceIdType.MESH
VMEM_LIMIT = 62 * 1024 * 1024
STEP_WORDS = 64
HIDDEN_CUT = 256


def dot_nn(left, right):
    return jnp.dot(left, right, preferred_element_type=F32)


def dot_nt(left, right):
    return lax.dot_general(left, right, (((1,), (1,)), ((), ())), preferred_element_type=F32)


def dot_tn(left, right):
    return lax.dot_general(left, right, (((0,), (0,)), ((), ())), preferred_element_type=F32)


def as_column(row):
    return jnp.transpose(jnp.broadcast_to(row.astype(F32), (128, row.shape[1])))


def head_stack(values, heads, factor):
    width = values.shape[1] // heads
    lane = lax.broadcasted_iota(jnp.int32, (1, values.shape[1]), 1) // width
    return jnp.concatenate(
        [values * jnp.where(lane == h, factor, 0.0).astype(values.dtype) for h in range(heads)], 0
    )


def gelu_both(hidden):
    c = lambda value: jnp.asarray(value, hidden.dtype)
    square = hidden * hidden
    tanh = jnp.tanh(hidden * (c(GELU_A) + c(GELU_A * GELU_B) * square))
    half = c(0.5) + c(0.5) * tanh
    slope = half + (c(0.5) * hidden) * (c(1.0) - tanh * tanh) * (c(GELU_A) + c(3.0 * GELU_A * GELU_B) * square)
    return hidden * half, slope


def norm_fwd(values, gain):
    mean = jnp.mean(values, -1, keepdims=True)
    centered = values - mean
    rstd = lax.rsqrt(jnp.mean(centered * centered, -1, keepdims=True) + EPSILON)
    return (centered * rstd * gain).astype(BF16), rstd


def norm_bwd(dn, n, rstd, gain):
    n = n.astype(F32)
    d1 = dn * gain
    dnn = dn * n
    m1 = jnp.mean(d1, -1, keepdims=True)
    m2 = jnp.mean(dnn, -1, keepdims=True)
    return rstd * (d1 - m1 - n * (1.0 / gain) * m2), dnn


def coordinates():
    dp, mp = lax.axis_index("dp"), lax.axis_index("mp")
    return dp // 2, dp % 2, mp // 2, mp % 2


def device_of(z, x, y, core):
    return (z * 2 + x, y * 2 + core)


def remote_copy(src, dst, ssem, rsem, slot, peer):
    return pltpu.make_async_remote_copy(
        src_ref=src, dst_ref=dst, send_sem=ssem.at[slot], recv_sem=rsem.at[slot],
        device_id=peer, device_id_type=MESH,
    )


class WeightGather:
    def __init__(self, slices, wholes, ssem, rsem):
        self.slices, self.wholes, self.ssem, self.rsem = slices, wholes, ssem, rsem
        self.z, self.x, self.y, self.core = coordinates()
        self.mp = self.y * 2 + self.core
        self.across = (1 - self.y) * 2 + self.core

    @staticmethod
    def half(ref, axis, which):
        rows = ref.shape[axis] // 2
        return ref.at[(slice(None),) * axis + (pl.ds(pl.multiple_of(which * rows, rows), rows),)]

    def copy(self, i, kind):
        z, x, y, core = self.z, self.x, self.y, self.core
        piece, whole = self.slices[i], self.wholes[i]
        axis = len(piece.shape) - 2
        far = whole.at[self.across]
        if kind == "far":
            src, dst = self.half(piece, axis, x), self.half(whole.at[self.mp], axis, x)
            peer = device_of(z, x, 1 - y, core)
        elif kind == "near":
            src, dst, peer = piece, whole.at[self.mp], device_of(z, x, y, 1 - core)
        else:
            which = 1 - x if kind == "late" else x
            src = dst = self.half(far, axis, which)
            peer = device_of(z, 1 - x, y, core) if kind == "side" else device_of(z, x, y, 1 - core)
        slot = i * 5 + ("far", "near", "side", "early", "late").index(kind)
        return remote_copy(src, dst, self.ssem, self.rsem, slot, peer)

    def peers(self):
        z, x, y, core = self.z, self.x, self.y, self.core
        return [device_of(z, x, 1 - y, core), device_of(z, x, y, 1 - core), device_of(z, 1 - x, y, core)]

    def begin(self):
        for i in range(len(self.slices)):
            self.copy(i, "far").start()
        for i in range(len(self.slices)):
            self.copy(i, "near").start()

    def pass_on(self, i):
        self.copy(i, "far").wait()
        self.copy(i, "side").start()
        self.copy(i, "early").start()

    def pass_last(self, i):
        self.copy(i, "side").wait()
        self.copy(i, "late").start()

    def finish(self):
        for i in range(len(self.slices)):
            for kind in ("near", "early", "late"):
                self.copy(i, kind).wait()


def char_fwd_body(
    n_dp, cap,
    x_ref, cnt_ref, gains_ref, wqkv_ref, wout_ref, wup_ref, wdown_ref, pool_ref, wproj_ref,
    src_ref, seg_ref, s_qkv, s_out, s_up, s_down,
    e_ref, n1_ref, p_ref, a_ref, o_ref, n2_ref, rs1_ref, rs2_ref, act_ref, dg_ref, f_ref, aw_ref, pooled_ref,
    onehot_ref, place_ref, seg_out, g_qkv, g_out, g_up, g_down,
    cnt_col, row_send, row_got, seg_all, ssem, rsem, wsend, wrecv,
):
    step, last = pl.program_id(0), pl.num_programs(0) - 1
    dp, mp = lax.axis_index("dp"), lax.axis_index("mp")
    gather = WeightGather((s_qkv, s_out, s_up, s_down), (g_qkv, g_out, g_up, g_down), wsend, wrecv)
    mates = [mp // 2 * 2 + (mp + 1) % 2, (mp + 2) % 4, (mp // 2 * 2 + 2) % 4 + (mp + 1) % 2]
    all_words = src_ref.shape[1]
    slots = n_dp * cap
    row_copy = lambda k: remote_copy(row_send.at[k], row_got.at[k], ssem, rsem, k, (lax.rem(dp + k, n_dp), mp))
    seg_copy = lambda j: remote_copy(seg_all.at[mp], seg_all.at[mp], ssem, rsem, n_dp + j, (dp, mates[j]))

    @pl.when(step == 0)
    def _():
        barrier = pltpu.get_barrier_semaphore()
        greeted = [(lax.rem(dp + k, n_dp), mp) for k in range(1, n_dp)] + [(dp, mate) for mate in mates]
        for peer in greeted:
            pl.semaphore_signal(barrier, inc=1, device_id=peer, device_id_type=MESH)
        source = src_ref[...]
        owner = source // (all_words * 4)
        owner_c = as_column(owner)[:, 0:1]
        index_r = lax.broadcasted_iota(jnp.int32, (all_words, all_words), 0)
        index_c = lax.broadcasted_iota(jnp.int32, (all_words, all_words), 1)
        earlier = (owner_c == owner.astype(F32)) & (index_r < index_c)
        rank = jnp.sum(jnp.where(earlier, 1.0, 0.0), 0, keepdims=True).astype(jnp.int32)
        slot_of = lax.rem(owner - dp + n_dp, n_dp) * cap + rank
        at_slot = lax.broadcasted_iota(jnp.int32, (slots, all_words), 0) == slot_of
        onehot_ref[...] = jnp.where(at_slot, 1.0, 0.0).astype(BF16)
        row_mat = as_column(lax.rem(source, all_words) + 1).astype(BF16)
        row_send[...] = dot_nn(onehot_ref[...], row_mat).astype(BF16).reshape(n_dp, cap, 128)
        seg_all[mp] = jnp.broadcast_to(seg_ref[...], (8, all_words))
        cnt_col[...] = as_column(cnt_ref[...])
        pl.semaphore_wait(barrier, len(greeted))
        gather.begin()
        for k in range(1, n_dp):
            row_copy(k).start()
        for j in range(3):
            seg_copy(j).start()
        row_got[0] = row_send[0]

    @pl.when(step == 2)
    def _():
        gather.pass_on(0)
        gather.pass_on(1)

    words, wide = x_ref.shape
    width = wide // CHARS
    blocks = words // 8
    gains = gains_ref[...].astype(F32)
    counts_here = cnt_col[pl.ds(pl.multiple_of(step * words, words), words), :].astype(jnp.int32)
    pieces = []
    for g in range(words // 16):
        xt = x_ref[16 * g : 16 * g + 16, :].astype(F32)
        for half in range(2):
            for c in range(CHARS):
                pieces.append(xt[8 * half : 8 * half + 8, width * c : width * c + width])
    x = jnp.concatenate(pieces, 0)
    n1, rs1 = norm_fwd(x, gains[0:1])
    n1_ref[...] = n1
    rs1_ref[...] = rs1
    p_ref[...] = dot_nn(n1, wqkv_ref[...]).astype(BF16)
    row_w = lax.broadcasted_iota(jnp.int32, (8, 128), 0)
    lane_w = lax.broadcasted_iota(jnp.int32, (8, 128), 1) % 8
    same = row_w == lane_w
    slot = lax.broadcasted_iota(jnp.int32, (CHARS, 8, 128), 0)
    size = CHAR_HEADS * 128
    scale = (width // CHAR_HEADS) ** -0.5
    scores = []
    for b in range(blocks):
        sl = slice(128 * b, 128 * b + 128)
        scores.append(dot_nt(head_stack(p_ref[sl, width : 2 * width], CHAR_HEADS, scale), p_ref[sl, 0:width]))
    for b in range(blocks):
        here = slot < counts_here[8 * b : 8 * b + 8][None]
        st = jnp.where(here[None], scores[b].reshape(CHAR_HEADS, CHARS, 8, 128), NEGATIVE)
        e = jnp.exp(st - jnp.max(st, 1, keepdims=True))
        r = jnp.where(same[None, None], 1.0 / jnp.sum(e, 1, keepdims=True), 0.0)
        a_ref[size * b : size * b + size, :] = (e * r).reshape(size, 128).astype(BF16)
    for b in range(blocks):
        sl = slice(128 * b, 128 * b + 128)
        a = a_ref[size * b : size * b + size, :]
        o_ref[sl, :] = dot_tn(a, head_stack(p_ref[sl, 2 * width : 3 * width], CHAR_HEADS, 1.0)).astype(BF16)
    m = x + dot_nn(o_ref[...], wout_ref[...])
    n2, rs2 = norm_fwd(m, gains[1:2])
    n2_ref[...] = n2
    rs2_ref[...] = rs2

    f = m
    for j in range(0, wup_ref.shape[1], HIDDEN_CUT):
        cut = slice(j, j + HIDDEN_CUT)
        act, slope = gelu_both(dot_nn(n2, wup_ref[:, cut]).astype(BF16))
        act_ref[:, cut] = act
        dg_ref[:, cut] = slope
        f = f + dot_nn(act, wdown_ref[cut, :])
    f_ref[...] = f.astype(BF16)
    t = jnp.sum(f * pool_ref[...].astype(F32).reshape(1, width), -1, keepdims=True).reshape(blocks, CHARS, 8, 1)
    counts = counts_here[:, 0:1].reshape(blocks, 1, 8, 1)
    t = jnp.where(lax.broadcasted_iota(jnp.int32, t.shape, 1) < counts, t, NEGATIVE)
    et = jnp.exp(t - jnp.max(t, 1, keepdims=True))
    aw = et / jnp.sum(et, 1, keepdims=True)
    aw_ref[...] = aw.reshape(words * CHARS, 1)
    pooled = jnp.sum(aw * f.reshape(blocks, CHARS, 8, width), 1).reshape(words, width).astype(BF16)
    pooled_ref[...] = pooled
    e_ref[...] = dot_nn(pooled, wproj_ref[...]).astype(BF16)

    @pl.when(step == 2)
    def _():
        gather.pass_on(2)

    @pl.when(step == last)
    def _():
        gather.pass_on(3)
        for i in range(3):
            gather.pass_last(i)
        for k in range(1, n_dp):
            row_copy(k).wait()
        for j in range(3):
            seg_copy(j).wait()
        at_row = row_got[...].reshape(slots, 128)[:, 0:1].astype(F32) - 1.0
        lanes = lax.broadcasted_iota(jnp.int32, (slots, all_words), 1).astype(F32)
        place_ref[...] = jnp.where(lanes == at_row, 1.0, 0.0).astype(BF16)
        seg_out[...] = seg_all[...]
        gather.pass_last(3)
        gather.finish()


def char_forward(n_dp, x, counts, gains, wqkv, wout, wup, wdown, pool, wproj, source, segments, slices):
    words, wide = x.shape
    width = wide // CHARS
    rows = words * CHARS
    step_rows = STEP_WORDS * CHARS
    cap = -(-2 * words // n_dp // 16) * 16
    slots = n_dp * cap
    full = lambda arr: pl.BlockSpec(arr.shape, lambda i: (0,) * arr.ndim)
    blk = lambda n, w: pl.BlockSpec((n, w), lambda i: (i, 0))
    hid = wup.shape[1]
    dw = wproj.shape[1]
    outs = [
        (words, STEP_WORDS, dw, BF16), (rows, step_rows, width, BF16), (rows, step_rows, 3 * width, BF16),
        (rows * CHAR_HEADS, step_rows * CHAR_HEADS, 128, BF16), (rows, step_rows, width, BF16),
        (rows, step_rows, width, BF16), (rows, step_rows, 1, F32), (rows, step_rows, 1, F32),
        (rows, step_rows, hid, BF16), (rows, step_rows, hid, BF16), (rows, step_rows, width, BF16),
        (rows, step_rows, 1, F32), (words, STEP_WORDS, width, BF16),
    ]
    fixed = [((slots, words), BF16), ((slots, words), BF16), ((4, 8, words), jnp.int32)]
    any_spec = pl.BlockSpec(memory_space=pl.ANY)
    return pl.pallas_call(
        functools.partial(char_fwd_body, n_dp, cap),
        grid=(words // STEP_WORDS,),
        in_specs=[blk(STEP_WORDS, wide)]
        + [full(w) for w in (counts, gains, wqkv, wout, wup, wdown, pool, wproj, source, segments)]
        + [any_spec] * len(slices),
        out_specs=[blk(b, w) for _, b, w, _ in outs]
        + [pl.BlockSpec(s, lambda i, n=len(s): (0,) * n) for s, _ in fixed]
        + [any_spec] * len(slices),
        out_shape=[jax.ShapeDtypeStruct((n, w), d) for n, _, w, d in outs]
        + [jax.ShapeDtypeStruct(s, d) for s, d in fixed]
        + [jax.ShapeDtypeStruct((4, *s.shape), s.dtype) for s in slices],
        scratch_shapes=[
            pltpu.VMEM((words, 128), F32),
            pltpu.VMEM((n_dp, cap, 128), BF16), pltpu.VMEM((n_dp, cap, 128), BF16), pltpu.VMEM((4, 8, words), jnp.int32),
            pltpu.SemaphoreType.DMA((n_dp + 3,)), pltpu.SemaphoreType.DMA((n_dp + 3,)),
            pltpu.SemaphoreType.DMA((5 * len(slices),)), pltpu.SemaphoreType.DMA((5 * len(slices),)),
        ],
        compiler_params=pltpu.CompilerParams(collective_id=2, has_side_effects=True, vmem_limit_bytes=VMEM_LIMIT),
        name="char_forward",
    )(x, counts, gains, wqkv, wout, wup, wdown, pool, wproj, source, segments, *slices)


CHAR_A = 176
CHAR_B = 48
WORD_ROWS = 768
CHUNK_ROWS = 192
SEMS = 8


def fold_half(block):
    half = block.shape[0] // 2
    return jnp.concatenate([block[:half], block[half:]], 1)


def unfold_half(block):
    return jnp.concatenate([block[:, :64], block[:, 64:]], 0)


class Halving:
    def __init__(self, n_z, sent, work, got, ssem, rsem, base, order):
        self.n_z, self.sent, self.work, self.got = n_z, sent, work, got
        self.ssem, self.rsem, self.base, self.order = ssem, rsem, base, order
        self.z, self.x, self.y, self.core = coordinates()

    def copies(self, phase):
        z, x, y, core = self.z, self.x, self.y, self.core
        work = self.work
        step = "c" if phase == 0 else self.order[phase - 1]
        if step == "c":
            pairs = [(self.sent, self.got[0], device_of(z, x, y, 1 - core))]
        elif step == "y":
            src = work.at[1 - y] if phase == 1 else work.at[1 - y, x]
            pairs = [(src, self.got[phase], device_of(z, x, 1 - y, core))]
        elif step == "x":
            src = work.at[:, 1 - x] if phase == 1 else work.at[y, 1 - x]
            pairs = [(src, self.got[phase], device_of(z, 1 - x, y, core))]
        else:
            pairs = []
            for k in range(1, self.n_z):
                other = lax.rem(z + k, self.n_z)
                pairs.append((work.at[y, x, other], self.got[3].at[k - 1], device_of(other, x, y, core)))
        return [
            remote_copy(src, dst, self.ssem, self.rsem, self.base + phase + i, peer)
            for i, (src, dst, peer) in enumerate(pairs)
        ]

    def start(self, phase):
        for copy in self.copies(phase):
            copy.start()

    def finish(self, phase):
        for copy in self.copies(phase):
            copy.wait()
        x, y = self.x, self.y
        work, got = self.work, self.got[phase]
        step = "c" if phase == 0 else self.order[phase - 1]

        def add(mine, other):
            def body(i, carry):
                mine[i] = mine[i] + other[i]
                return carry
            lax.fori_loop(0, self.n_z, body, 0)

        if step == "c":
            for i in range(2):
                for j in range(2):
                    add(work.at[i, j], got.at[i, j])
        elif step == "y" and phase == 1:
            for j in range(2):
                add(work.at[y, j], got.at[j])
        elif step == "x" and phase == 1:
            for i in range(2):
                add(work.at[i, x], got.at[i])
        elif step in "yx":
            add(work.at[y, x], got)

    def advance(self, phase):
        self.finish(phase)
        self.start(phase + 1)

    def total(self):
        value = self.work[self.y, self.x, self.z].astype(F32)
        for k in range(self.n_z - 1):
            value += self.got[3][k].astype(F32)
        return value

    @staticmethod
    def got_shapes(n_z, rows, first=0):
        shapes = [(2, 2, n_z, rows, 128), (2, n_z, rows, 128), (n_z, rows, 128), (n_z - 1, rows, 128)]
        return [pltpu.VMEM(s, BF16) for s in shapes[first:]]


class GradientSums:
    def __init__(self, n_z, word_sum, refs):
        self.n_z, self.word_sum = n_z, word_sum
        abuf, bbuf, wbuf, small, sgot, ssem, rsem, lsem, *got = refs
        self.abuf, self.bbuf, self.wbuf, self.small, self.sgot = abuf, bbuf, wbuf, small, sgot
        self.ssem, self.rsem, self.lsem = ssem, rsem, lsem
        self.z, self.x, self.y, self.core = coordinates()
        self.chunks = []
        for i, order in enumerate(("xyz", "yxz", "yxz", "yxz")):
            rows = wbuf.at[:, :, :, CHUNK_ROWS * i : CHUNK_ROWS * i + CHUNK_ROWS]
            self.chunks.append(
                Halving(n_z, None, rows, [None, *got[3 * i : 3 * i + 3]], ssem, rsem, SEMS * i, order)
            )
        core = self.core
        self.parta = Halving(n_z, abuf.at[1 - core], abuf.at[core], got[12:16], ssem, rsem, 4 * SEMS, "yxz")
        self.partb = Halving(n_z, bbuf.at[1 - core], bbuf.at[core], got[16:20], ssem, rsem, 5 * SEMS, "yxz")
        self.tiny = 6 * SEMS

    @staticmethod
    def scratch(n_z):
        n_sem = 7 * SEMS
        shapes = [
            pltpu.VMEM((2, 2, 2, n_z, CHAR_A, 128), BF16), pltpu.VMEM((2, 2, 2, n_z, CHAR_B, 128), BF16),
            pltpu.VMEM((2, 2, n_z, WORD_ROWS, 128), BF16),
            pltpu.VMEM((4, 16, 128), F32), pltpu.VMEM((2 + n_z, 16, 128), F32),
            pltpu.SemaphoreType.DMA((n_sem,)), pltpu.SemaphoreType.DMA((n_sem,)), pltpu.SemaphoreType.DMA,
        ]
        for _ in range(4):
            shapes += Halving.got_shapes(n_z, CHUNK_ROWS, 1)
        return shapes + Halving.got_shapes(n_z, CHAR_A) + Halving.got_shapes(n_z, CHAR_B)

    def peers(self):
        z, x, y, core = self.z, self.x, self.y, self.core
        near = [device_of(z, x, y, 1 - core), device_of(z, x, 1 - y, core), device_of(z, 1 - x, y, core)]
        return near, [device_of(lax.rem(z + k, self.n_z), x, y, core) for k in range(1, self.n_z)]

    def begin(self):
        load = pltpu.make_async_copy(self.word_sum, self.wbuf, self.lsem)
        load.start()
        near, along = self.peers()
        barrier = pltpu.get_barrier_semaphore()
        for peer in near + along:
            pl.semaphore_signal(barrier, inc=1, device_id=peer, device_id_type=MESH)
        pl.semaphore_wait(barrier, len(near + along))
        load.wait()
        self.chunks[0].start(1)
        self.chunks[1].start(1)
        self.chunks[3].start(2)

    def pack_a(self, gup_ref, gdown_ref, gproj_ref, gout_ref):
        for d in range(2 * self.n_z):
            down = gdown_ref[128 * d : 128 * d + 128, :]
            out = gout_ref[32 * d : 32 * d + 32, :]
            for p in range(4):
                block = self.abuf.at[p % 2, p // 2, d % 2, d // 2]
                block[0:32, :] = gup_ref[32 * d : 32 * d + 32, 256 * p : 256 * p + 128].astype(BF16)
                block[32:64, :] = gup_ref[32 * d : 32 * d + 32, 256 * p + 128 : 256 * p + 256].astype(BF16)
                block[64:128, :] = fold_half(down[:, 64 * p : 64 * p + 64]).astype(BF16)
                block[128:160, :] = gproj_ref[32 * d : 32 * d + 32, 128 * p : 128 * p + 128].astype(BF16)
                block[160:176, :] = fold_half(out[:, 64 * p : 64 * p + 64]).astype(BF16)
        self.parta.start(0)

    def pack_b(self, gqkv_ref):
        for d in range(2 * self.n_z):
            qkv = gqkv_ref[32 * d : 32 * d + 32, :]
            for p in range(4):
                block = self.bbuf.at[p % 2, p // 2, d % 2, d // 2]
                own = qkv[:, 192 * p : 192 * p + 192]
                block[0:32, :] = own[:, 0:128].astype(BF16)
                block[32:48, :] = fold_half(own[:, 128:192]).astype(BF16)
        self.partb.start(0)

    def tiny_copies(self, phase):
        near, along = self.peers()
        small, sgot = self.small, self.sgot
        if phase < 3:
            return [remote_copy(small.at[phase], sgot.at[phase], self.ssem, self.rsem, self.tiny + phase, near[phase])]
        return [
            remote_copy(small.at[3], sgot.at[3 + k], self.ssem, self.rsem, self.tiny + 3 + k, peer)
            for k, peer in enumerate(along)
        ]

    def tiny_start(self, phase):
        for copy in self.tiny_copies(phase):
            copy.start()

    def tiny_finish(self, phase):
        for copy in self.tiny_copies(phase):
            copy.wait()
        small, sgot = self.small, self.sgot
        if phase < 3:
            small[phase + 1] = small[phase] + sgot[phase]
            return None
        total = small[3]
        for k in range(1, self.n_z):
            total += sgot[2 + k]
        return total


def pack_small(cgain_ref, cpool_ref, gqkv_ref, wqkv_ref, gains_ref, wgain_ref):
    gains = gains_ref[...].astype(F32)
    width = gains.shape[1]
    first = jnp.sum(gqkv_ref[...] * wqkv_ref[...].astype(F32), -1, keepdims=True)
    first = jnp.transpose(jnp.broadcast_to(first, (width, 128)))[0:1, :]
    sums = [
        first / gains[0:1], jnp.sum(cgain_ref[...], 0, keepdims=True) / gains[1:2],
        jnp.sum(cpool_ref[...], 0, keepdims=True), wgain_ref[0:1, :], wgain_ref[1:2, :],
    ]
    rows = [v[:, t : t + 128] for v in sums for t in range(0, v.shape[1], 128)]
    rows.append(jnp.zeros((2, 128), F32))
    return jnp.concatenate(rows, 0)


def finish_body(
    dx_ref, wide_ref, parta_ref, partb_ref, word_ref, small_ref,
    odx_ref, owide_ref, oqkv_ref, oout_ref, oup_ref, odown_ref, oproj_ref, owqkv_ref, owout_ref, owup_ref, owdown_ref,
    ocgain_ref, opool_ref, owgain_ref,
):
    odx_ref[...] = dx_ref[...].astype(F32)

    @pl.when(pl.program_id(0) == 0)
    def _():
        parta, partb, word, total = parta_ref[...], partb_ref[...], word_ref[...], small_ref[...]
        owide_ref[...] = wide_ref[...]
        oqkv_ref[:, 0:128] = partb[0:32]
        oqkv_ref[:, 128:192] = unfold_half(partb[32:48])
        oout_ref[...] = unfold_half(parta[160:176])
        oup_ref[:, 0:128] = parta[0:32]
        oup_ref[:, 128:256] = parta[32:64]
        odown_ref[...] = unfold_half(parta[64:128]).T
        oproj_ref[...] = parta[128:160]
        for t in range(3):
            owqkv_ref[t] = word[64 * t : 64 * t + 64]
        owout_ref[...] = word[192:256]
        for t in range(4):
            owup_ref[:, 128 * t : 128 * t + 128] = word[256 + 64 * t : 320 + 64 * t]
            owdown_ref[:, 128 * t : 128 * t + 128] = word[512 + 64 * t : 576 + 64 * t]
        for j in range(2):
            for t in range(2):
                ocgain_ref[j : j + 1, 128 * t : 128 * t + 128] = total[2 * j + t : 2 * j + t + 1]
            for t in range(4):
                owgain_ref[j : j + 1, 128 * t : 128 * t + 128] = total[6 + 4 * j + t : 7 + 4 * j + t]
        for t in range(2):
            opool_ref[:, 128 * t : 128 * t + 128] = total[4 + t : 5 + t]


def finish(d_chars, word_out, *sums):
    words, wide = d_chars.shape
    steps = words // STEP_WORDS
    full = lambda s: pl.BlockSpec(s, lambda i: (0,) * len(s))
    blk = pl.BlockSpec((STEP_WORDS, wide), lambda i: (i, 0))
    outs = [
        word_out.shape, (32, 192), (32, 64), (32, 256), (64, 128), (32, 128),
        (3, 64, 128), (64, 128), (64, 512), (64, 512), (2, 256), (1, 256), (2, 512),
    ]
    result = pl.pallas_call(
        finish_body,
        grid=(steps,),
        in_specs=[blk, full(word_out.shape)] + [full(s.shape) for s in sums],
        out_specs=[blk] + [full(s) for s in outs],
        out_shape=[jax.ShapeDtypeStruct((words, wide), F32), jax.ShapeDtypeStruct(outs[0], BF16)]
        + [jax.ShapeDtypeStruct(s, F32) for s in outs[1:]],
        compiler_params=pltpu.CompilerParams(vmem_limit_bytes=VMEM_LIMIT),
        name="finish",
    )(d_chars, word_out, *sums)
    dx, out, qkv, cout, up, down, proj, wqkv, wout, wup, wdown, cgain, pool, wgain = result
    return (out, dx, qkv, cout, up, down.T, proj, wqkv, wout.T, wup, wdown.T, cgain, pool.reshape(-1), wgain)


def char_bwd_body(
    n_dp, fused,
    de_ref, gains_ref, wqkv_ref, wout_ref, wup_ref, wdown_ref, pool_ref, wproj_ref,
    n1_ref, p_ref, a_ref, o_ref, n2_ref, rs1_ref, rs2_ref, act_ref, dg_ref, f_ref, aw_ref, pooled_ref,
    *refs,
):
    if fused:
        word_sum, wgain_ref, dx_ref, outa_ref, outb_ref, word_ref, small_ref, *refs = refs
    else:
        dx_ref, *refs = refs
        outs, refs = refs[:7], refs[7:]
    gqkv_ref, gout_ref, gup_ref, gdown_ref, gproj_ref, ggain_ref, gpool_ref, *refs = refs
    dm_ref, dp_ref, do_ref, ds_ref, *refs = refs
    step = pl.program_id(0)
    part = pl.num_programs(0) // 3
    words = de_ref.shape[0]
    width = n1_ref.shape[1]
    blocks = words // 8
    rows = words * CHARS
    size = CHAR_HEADS * 128
    gains = gains_ref[...].astype(F32)
    here = pl.ds(pl.multiple_of(lax.rem(step, part) * rows, rows), rows)
    sums = GradientSums(n_dp // 2, word_sum, refs) if fused else None
    chunks = sums.chunks if fused else None

    def at(when, act):
        if fused:
            pl.when(step == when)(act)

    @pl.when(step == 0)
    def _():
        if fused:
            sums.begin()
        for ref in (gqkv_ref, gout_ref, gup_ref, gdown_ref, gproj_ref, ggain_ref, gpool_ref):
            ref[...] = jnp.zeros_like(ref)

    def events_start():
        def second():
            chunks[3].advance(2)
            chunks[0].advance(1)
            chunks[1].advance(1)
            chunks[2].start(1)
        at(2, second)

        def third():
            chunks[3].finish(3)
            chunks[0].advance(2)
            chunks[1].advance(2)
        at(3, third)

        def fourth():
            chunks[2].advance(1)
            sums.parta.advance(0)
        at(4, fourth)

        def sixth():
            chunks[2].advance(2)
            chunks[0].finish(3)
            chunks[1].finish(3)
        at(6, sixth)

        def seventh():
            sums.parta.advance(1)
        at(7, seventh)

        def ninth():
            sums.partb.advance(0)
            sums.tiny_finish(0)
            sums.tiny_start(1)
            sums.parta.advance(2)
        at(9, ninth)

        def eleventh():
            sums.partb.advance(1)
            sums.tiny_finish(1)
            sums.tiny_start(2)
            chunks[2].finish(3)
            for i in range(4):
                word_ref[CHUNK_ROWS * i : CHUNK_ROWS * i + CHUNK_ROWS, :] = chunks[i].total()
        at(11, eleventh)

    events_start()

    @pl.when(step < part)
    def _():
        de = de_ref[...]
        gproj_ref[...] += dot_tn(pooled_ref[...], de)
        dpool = dot_nt(de, wproj_ref[...]).reshape(blocks, 1, 8, width)
        f = f_ref[...].astype(F32).reshape(blocks, CHARS, 8, width)
        aw = aw_ref[...].reshape(blocks, CHARS, 8, 1)
        g = jnp.sum(f * dpool, -1, keepdims=True)
        dt = aw * (g - jnp.sum(aw * g, 1, keepdims=True))
        gpool_ref[...] += jnp.sum((dt * f).reshape(rows // 8, 8, width), 0)
        df = (aw * dpool + dt * pool_ref[...].astype(F32).reshape(1, width)).reshape(rows, width)
        dfb = df.astype(BF16)
        n2 = n2_ref[...]
        dn2 = None
        for j in range(0, wup_ref.shape[1], HIDDEN_CUT):
            cut = slice(j, j + HIDDEN_CUT)
            gdown_ref[cut, :] += dot_tn(act_ref[:, cut], dfb)
            dh = dg_ref[:, cut] * dot_nt(dfb, wdown_ref[cut, :]).astype(BF16)
            gup_ref[:, cut] += dot_tn(n2, dh)
            term = dot_nt(dh, wup_ref[:, cut])
            dn2 = term if dn2 is None else dn2 + term
        d_norm, dnn = norm_bwd(dn2, n2, rs2_ref[...], gains[1:2])
        ggain_ref[...] += jnp.sum(dnn.reshape(rows // 8, 8, width), 0)
        dm = df + d_norm
        dm_ref[here, :] = dm
        dmb = dm.astype(BF16)
        gout_ref[...] += dot_tn(o_ref[...], dmb)
        do_ref[here, :] = dot_nt(dmb, wout_ref[...]).astype(BF16)

    at(part - 1, lambda: sums.pack_a(gup_ref, gdown_ref, gproj_ref, gout_ref))

    @pl.when((step >= part) & (step < 2 * part))
    def _():
        scale = (width // CHAR_HEADS) ** -0.5
        base = lax.rem(step, part) * rows
        spot = lambda b: pl.ds(pl.multiple_of(base + 128 * b, 128), 128)
        raw = []
        for b in range(blocks):
            sl = slice(128 * b, 128 * b + 128)
            raw.append(dot_nt(head_stack(p_ref[sl, 2 * width : 3 * width], CHAR_HEADS, 1.0), do_ref[spot(b), :]))
        for b in range(blocks):
            a = a_ref[size * b : size * b + size, :].astype(F32).reshape(CHAR_HEADS, CHARS, 8, 128)
            dpt = raw[b].reshape(CHAR_HEADS, CHARS, 8, 128)
            delta = jnp.sum(a * dpt, 1, keepdims=True)
            ds_ref[size * b : size * b + size, :] = (a * (dpt - delta)).reshape(size, 128).astype(BF16)
        for b in range(blocks):
            sl = slice(128 * b, 128 * b + 128)
            ds = ds_ref[size * b : size * b + size, :]
            k = head_stack(p_ref[sl, width : 2 * width], CHAR_HEADS, scale)
            dp_ref[spot(b), 0:width] = dot_tn(ds, k).astype(BF16)
        for b in range(blocks):
            sl = slice(128 * b, 128 * b + 128)
            cut = lambda h: ds_ref[size * b + 128 * h : size * b + 128 * h + 128, :]
            wide = jnp.concatenate([cut(h) for h in range(CHAR_HEADS)], 1)
            q = head_stack(p_ref[sl, 0:width], CHAR_HEADS, scale)
            dp_ref[spot(b), width : 2 * width] = dot_nn(wide, q).astype(BF16)
        for b in range(blocks):
            cut = lambda h: a_ref[size * b + 128 * h : size * b + 128 * h + 128, :]
            wide = jnp.concatenate([cut(h) for h in range(CHAR_HEADS)], 1)
            do = head_stack(do_ref[spot(b), :], CHAR_HEADS, 1.0)
            dp_ref[spot(b), 2 * width : 3 * width] = dot_nn(wide, do).astype(BF16)
        gqkv_ref[...] += dot_tn(n1_ref[...], dp_ref[here, :])

    def begin_b():
        sums.pack_b(gqkv_ref)
        sums.small[0] = pack_small(ggain_ref, gpool_ref, gqkv_ref, wqkv_ref, gains_ref, wgain_ref)
        sums.tiny_start(0)
    at(2 * part - 1, begin_b)

    @pl.when(step >= 2 * part)
    def _():
        dn1 = dot_nt(dp_ref[here, :], wqkv_ref[...])
        d_norm, _ = norm_bwd(dn1, n1_ref[...], rs1_ref[...], gains[0:1])
        dx = dm_ref[here, :] + d_norm
        for b in range(0, blocks, 2):
            for c in range(CHARS):
                pair = [dx[128 * i + 8 * c : 128 * i + 8 * c + 8] for i in (b, b + 1)]
                dx_ref[8 * b : 8 * b + 16, width * c : width * c + width] = jnp.concatenate(pair, 0).astype(BF16)

    def end():
        sums.partb.advance(2)
        sums.tiny_finish(2)
        sums.tiny_start(3)
        sums.parta.finish(3)
        outa_ref[...] = sums.parta.total()
        small_ref[...] = sums.tiny_finish(3)
        sums.partb.finish(3)
        outb_ref[...] = sums.partb.total()
    at(3 * part - 1, end)

    if not fused:
        @pl.when(step == 3 * part - 1)
        def _():
            for out, ref in zip(outs, (gqkv_ref, gout_ref, gup_ref, gdown_ref, gproj_ref, ggain_ref, gpool_ref)):
                out[...] = ref[...]


def char_backward(n_dp, de, kept, gains, wqkv, wout, wup, wdown, pool, wproj, word_sum, wgain):
    words = de.shape[0]
    width = wout.shape[0]
    rows = words * CHARS
    step_rows = STEP_WORDS * CHARS
    steps = words // STEP_WORDS
    fused = word_sum is not None
    full = lambda arr: pl.BlockSpec(arr.shape, lambda i: (0,) * arr.ndim)
    fixed = lambda s: pl.BlockSpec(s, lambda i: (0,) * len(s))
    first = lambda n, w: pl.BlockSpec((n, w), lambda i: (lax.min(i, steps - 1), 0))
    second = lambda n, w: pl.BlockSpec((n, w), lambda i: (lax.clamp(0, i - steps, steps - 1), 0))
    third = lambda n, w: pl.BlockSpec((n, w), lambda i: (lax.max(i - 2 * steps, 0), 0))
    twice = lambda n, w: pl.BlockSpec((n, w), lambda i: (lax.rem(lax.max(i - steps, 0), steps), 0))
    weights = (gains, wqkv, wout, wup, wdown, pool, wproj)
    when = [twice, second, second, first, first, third, first, first, first, first, first, first]
    grads = [wqkv.shape, wout.shape, wup.shape, wdown.shape, wproj.shape, (8, width), (8, width)]
    scratch = [pltpu.VMEM(s, F32) for s in grads] + [
        pltpu.VMEM((rows, width), F32), pltpu.VMEM((rows, 3 * width), BF16), pltpu.VMEM((rows, width), BF16),
        pltpu.VMEM((step_rows * CHAR_HEADS, 128), BF16),
    ]
    args = [de, *weights, *kept]
    in_specs = [first(STEP_WORDS, de.shape[1])] + [full(w) for w in weights]
    in_specs += [f(r.shape[0] // steps, r.shape[1]) for f, r in zip(when, kept)]
    params = dict(vmem_limit_bytes=VMEM_LIMIT)
    if fused:
        outs = [(CHAR_A, 128), (CHAR_B, 128), (WORD_ROWS, 128), (16, 128)]
        args += [word_sum, wgain]
        in_specs += [pl.BlockSpec(memory_space=pl.ANY), full(wgain)]
        scratch += GradientSums.scratch(n_dp // 2)
        params.update(collective_id=1, has_side_effects=True)
    else:
        outs = grads
    return pl.pallas_call(
        functools.partial(char_bwd_body, n_dp, fused),
        grid=(3 * steps,),
        in_specs=in_specs,
        out_specs=[third(STEP_WORDS, CHARS * width)] + [fixed(s) for s in outs],
        out_shape=[jax.ShapeDtypeStruct((words, CHARS * width), BF16)] + [jax.ShapeDtypeStruct(s, F32) for s in outs],
        scratch_shapes=scratch,
        compiler_params=pltpu.CompilerParams(**params),
        name="char_backward",
    )(*args)


def word_body(
    n_dp, cap, packed,
    e_ref, onehot, place, seg_all, cot_ref, gains_ref, *refs,
):
    slices, wholes, refs = refs[:4], refs[4:8], refs[8:]
    if packed:
        out_ref, de_ref, gsum_ref, ggain_ref, gbuf_ref, got_a, got_y, *refs = refs
    else:
        out_ref, de_ref, gqkv_ref, gout_ref, gup_ref, gdown_ref, ggain_ref, *refs = refs
    (
        wqkv_ref, wout_ref, wup_ref, wdown_ref, vec_send, vec_got, segc_all, rows_ref, normed, rstd_a,
        qkv_send, qkv_all, weights, o_send, o_all, act_ref, dh_ref, dact_ref, dm_ref,
        do_send, do_all, dk_acc, dv_acc, dqkv_send, dqkv_all, back_send, ret,
        ssem, rsem, lsem,
    ) = refs
    dp, mp = lax.axis_index("dp"), lax.axis_index("mp")
    n_mp = 4
    words, width = e_ref.shape
    slots = n_dp * cap
    pair = 2 * (width // HEADS)
    scale = (width // HEADS) ** -0.5
    to_dp = [(lax.rem(dp + k, n_dp), mp) for k in range(n_dp)]
    from_dp = [(lax.rem(dp + n_dp - k, n_dp), mp) for k in range(n_dp)]
    mates = [(mp // 2 * 2 + (mp + 1) % 2), (mp + 2) % 4, ((mp // 2 * 2 + 2) % 4 + (mp + 1) % 2)]
    barrier = pltpu.get_barrier_semaphore()
    for k in range(1, n_dp):
        pl.semaphore_signal(barrier, inc=1, device_id=to_dp[k], device_id_type=MESH)
    for mate in mates:
        pl.semaphore_signal(barrier, inc=1, device_id=(dp, mate), device_id_type=MESH)
    next_slot = [0]

    def send(src, dst, peer):
        slot = next_slot[0]
        next_slot[0] += 1
        copy = pltpu.make_async_remote_copy(
            src_ref=src, dst_ref=dst, send_sem=ssem.at[slot], recv_sem=rsem.at[slot],
            device_id=peer, device_id_type=MESH,
        )
        copy.start()
        return copy

    loads = []
    for i, held in ((3, wdown_ref), (0, wqkv_ref), (1, wout_ref), (2, wup_ref)):
        loads.append([])
        for j, at in enumerate([mp, *mates]):
            src = slices[i] if j == 0 else wholes[i].at[at]
            if i == 0:
                for t in range(3):
                    dst = held.at[at, :, pair * t : pair * t + pair]
                    loads[-1].append(pltpu.make_async_copy(src.at[t], dst, lsem.at[4 + t, j]))
            else:
                loads[-1].append(pltpu.make_async_copy(src, held.at[at], lsem.at[i, j]))
        for load in loads[-1]:
            load.start()
    vec_send[...] = dot_nn(onehot[...], e_ref[...]).astype(BF16).reshape(n_dp, cap, width)

    pl.semaphore_wait(barrier, n_dp - 1 + 3)
    vec_copies = [send(vec_send.at[k], vec_got.at[k], to_dp[k]) for k in range(1, n_dp)]
    vec_got[0] = vec_send[0]
    gains = gains_ref[...].astype(F32)
    cot = cot_ref[...]
    for load in loads[0]:
        load.wait()
    for p in range(n_mp):
        dact_ref[p] = dot_nt(cot, wdown_ref[p]).astype(BF16)
    for j in range(n_mp):
        segc_all[words * j : words * j + words, :] = as_column(seg_all[j, 0:1, :])
    for load in loads[1] + loads[2] + loads[3]:
        load.wait()
    for copy in vec_copies:
        copy.wait()
    rows = dot_tn(place[...], vec_got[...].reshape(slots, width))
    rows_ref[...] = rows
    n_w, rstd = norm_fwd(rows, gains[0:1])
    normed[0] = n_w
    rstd_a[0] = rstd
    qkv_copies = []
    for mate in reversed(mates):
        qkv_send[mate] = dot_nn(n_w, wqkv_ref[mate]).astype(BF16)
        qkv_copies.append(send(qkv_send.at[mate], qkv_all.at[mp], (dp, mate)))
    qkv_all[mp] = dot_nn(n_w, wqkv_ref[mp]).astype(BF16)
    for copy in qkv_copies:
        copy.wait()

    head_lane = lax.broadcasted_iota(jnp.int32, (1, pair), 1) // (pair // 2)
    head_mask = [jnp.where(head_lane == h, 1.0, 0.0).astype(BF16) for h in range(2)]
    o_copies = []
    for i in reversed(range(n_mp)):
        keys = words * (i + 1)
        q = qkv_all[i, :, 0:pair]
        k = qkv_all[0 : i + 1, :, pair : 2 * pair].reshape(keys, pair)
        v = qkv_all[0 : i + 1, :, 2 * pair : 3 * pair].reshape(keys, pair)
        same = segc_all[0:keys, 0:1] == seg_all[i, 0:1, :].astype(F32)
        key_at = lax.broadcasted_iota(jnp.int32, (keys, words), 0)
        query_at = lax.broadcasted_iota(jnp.int32, (keys, words), 1) + words * i
        allowed = same & (key_at <= query_at)
        total = None
        for h in range(2):
            st = dot_nt(k * (head_mask[h] * scale).astype(BF16), q)
            st = jnp.where(allowed, st, NEGATIVE)
            ex = jnp.exp(st - jnp.max(st, 0, keepdims=True))
            at = (ex * (1.0 / jnp.sum(ex, 0, keepdims=True))).astype(BF16)
            weights[i, h, 0:keys, :] = at
            part = dot_tn(at, v * head_mask[h])
            total = part if total is None else total + part
        o_send[i] = total.astype(BF16)
    for mate in reversed(mates):
        o_copies.append(send(o_send.at[mate], o_all.at[mp], (dp, mate)))
    o_all[mp] = o_send[mp]
    for copy in o_copies:
        copy.wait()
    attended = jnp.concatenate([o_all[p] for p in range(n_mp)], 1)
    mid = rows_ref[...] + dot_nn(attended, wout_ref[...].reshape(width, width))
    n_w2, rstd2 = norm_fwd(mid, gains[1:2])
    normed[1] = n_w2
    out = mid
    dn2 = jnp.zeros((words, width), F32)
    for p in range(n_mp):
        act, slope = gelu_both(dot_nn(n_w2, wup_ref[p]).astype(BF16))
        act_ref[p] = act
        dh = slope * dact_ref[p]
        dh_ref[p] = dh
        out = out + dot_nn(act, wdown_ref[p])
        dn2 = dn2 + dot_nt(dh, wup_ref[p])
    out_ref[...] = out.astype(BF16)
    d_norm, dnn = norm_bwd(dn2, n_w2, rstd2, gains[1:2])
    gain_b = jnp.sum(dnn, 0, keepdims=True) / gains[1:2]
    d_mid = cot.astype(F32) + d_norm
    dm_ref[...] = d_mid
    d_att = d_mid.astype(BF16)
    do_copies = []
    for mate in reversed(mates):
        do_send[mate] = dot_nt(d_att, wout_ref[mate]).astype(BF16)
        do_copies.append(send(do_send.at[mate], do_all.at[mp], (dp, mate)))
    do_all[mp] = dot_nt(d_att, wout_ref[mp]).astype(BF16)

    z, x, y, core = coordinates()

    def pair_sum(low, high):
        src = gbuf_ref.at[1 - core, :, :, :, low:high]
        return send(src, got_a.at[:, :, :, low:high], device_of(z, x, y, 1 - core))

    def pair_add(low, high):
        def add(i, carry):
            b, c, d = i // n_dp, (i // (n_dp // 2)) % 2, lax.rem(i, n_dp // 2)
            gsum_ref[b, c, d, low:high] = gbuf_ref[core, b, c, d, low:high] + got_a[b, c, d, low:high]
            return carry
        lax.fori_loop(0, 2 * n_dp, add, 0)

    def put(base, p, grad):
        if packed:
            block = words // 4
            for d in range(n_dp):
                for t in range(grad.shape[1] // 128):
                    gbuf_ref[p % 2, p // 2, d % 2, d // 2, base + block * t : base + block * t + block, :] = (
                        grad[block * d : block * d + block, 128 * t : 128 * t + 128].astype(BF16)
                    )
        else:
            ref = {0: gqkv_ref, 192: gout_ref, 256: gup_ref, 512: gdown_ref}[base]
            ref[p] = grad

    for p in range(n_mp):
        put(512, p, dot_tn(cot, act_ref[p]))
        put(256, p, dot_tn(n_w2, dh_ref[p]))
        put(192, p, dot_tn(d_att, o_all[p]))
    if packed:
        early_sum = pair_sum(CHUNK_ROWS, WORD_ROWS)
    dk_acc[...] = jnp.zeros_like(dk_acc)
    dv_acc[...] = jnp.zeros_like(dv_acc)
    for copy in do_copies:
        copy.wait()
    for i in reversed(range(n_mp)):
        keys = words * (i + 1)
        q = qkv_all[i, :, 0:pair]
        k = qkv_all[0 : i + 1, :, pair : 2 * pair].reshape(keys, pair)
        v = qkv_all[0 : i + 1, :, 2 * pair : 3 * pair].reshape(keys, pair)
        do = do_all[i]
        dq = None
        for h in range(2):
            at = weights[i, h, 0:keys, :]
            dpt = dot_nt(v * head_mask[h], do)
            af = at.astype(F32)
            delta = jnp.sum(af * dpt, 0, keepdims=True)
            ds = (af * (dpt - delta)).astype(BF16)
            scaled = (head_mask[h] * scale).astype(BF16)
            part = dot_tn(ds, k * scaled)
            dq = part if dq is None else dq + part
            dk_acc[0:keys, :] += dot_nn(ds, q * scaled)
            dv_acc[0:keys, :] += dot_nn(at, do * head_mask[h])
        dqkv_send[i, :, 0:pair] = dq.astype(BF16)
        dqkv_send[i, :, pair : 2 * pair] = dk_acc[words * i : keys, :].astype(BF16)
        dqkv_send[i, :, 2 * pair : 3 * pair] = dv_acc[words * i : keys, :].astype(BF16)
    dqkv_copies = []
    for mate in reversed(mates):
        dqkv_copies.append(send(dqkv_send.at[mate], dqkv_all.at[mp], (dp, mate)))
    dqkv_all[mp] = dqkv_send[mp]
    if packed:
        early_sum.wait()
        pair_add(CHUNK_ROWS, WORD_ROWS)
    for copy in dqkv_copies:
        copy.wait()
    if packed:
        y_sum = send(gsum_ref.at[1 - y, :, :, WORD_ROWS - CHUNK_ROWS :], got_y, device_of(z, x, 1 - y, core))
    d_normed = jnp.zeros((words, width), F32)
    for p in range(n_mp):
        d_normed = d_normed + dot_nt(dqkv_all[p], wqkv_ref[p])
    d_first, dnn = norm_bwd(d_normed, normed[0], rstd_a[0], gains[0:1])
    gain_a = jnp.sum(dnn, 0, keepdims=True) / gains[0:1]
    d_rows = (dm_ref[...] + d_first).astype(BF16)
    ggain_ref[0:1, :] = gain_a
    ggain_ref[1:2, :] = gain_b
    back_send[...] = dot_nn(place[...], d_rows).astype(BF16).reshape(n_dp, cap, width)
    back_copies = [send(back_send.at[k], ret.at[k], from_dp[k]) for k in range(1, n_dp)]
    ret[0] = back_send[0]
    for p in range(n_mp):
        put(0, p, dot_tn(normed[0], dqkv_all[p]))
    if packed:
        late_sum = pair_sum(0, CHUNK_ROWS)
        late_sum.wait()
        pair_add(0, CHUNK_ROWS)
        y_sum.wait()
        for c in range(2):
            for d in range(n_dp // 2):
                gsum_ref[y, c, d, WORD_ROWS - CHUNK_ROWS :] += got_y[c, d]
    for copy in back_copies:
        copy.wait()
    de_ref[...] = dot_tn(onehot[...], ret[...].reshape(slots, width)).astype(BF16)


def word_layer(n_dp, word_vec, onehot, place, segments, cotangent, gains, slices, wholes):
    words, width = word_vec.shape
    wqkv, wout, wup, wdown = wholes
    n_mp = wqkv.shape[0]
    cap = -(-2 * words // n_dp // 16) * 16
    slots = cap * n_dp
    pair = 2 * (width // HEADS)
    packed = n_dp == 8
    outs = [((words, width), BF16), ((words, width), BF16)]
    if packed:
        outs.append(((2, 2, n_dp // 2, WORD_ROWS, 128), BF16))
    else:
        outs += [((n_mp, width, n), F32) for n in (3 * pair, pair, wup.shape[2], wup.shape[2])]
    outs.append(((2, width), F32))
    hid = wup.shape[2]
    n_sem = 2 * (n_dp - 1) + 4 * 3 + 3
    vm = pl.BlockSpec(memory_space=pltpu.VMEM)
    args = (word_vec, onehot, place, segments, cotangent, gains, *slices, *wholes)
    shapes = [
        ((n_mp, width, 3 * pair), BF16), (wout.shape, BF16), (wup.shape, BF16), (wdown.shape, BF16),
        ((n_dp, cap, width), BF16), ((n_dp, cap, width), BF16), ((n_mp * words, 128), F32),
        ((words, width), F32), ((2, words, width), BF16), ((1, words, 1), F32),
        ((n_mp, words, 3 * pair), BF16), ((n_mp, words, 3 * pair), BF16), ((n_mp, 2, n_mp * words, words), BF16),
        ((n_mp, words, pair), BF16), ((n_mp, words, pair), BF16),
        ((n_mp, words, hid), BF16), ((n_mp, words, hid), BF16), ((n_mp, words, hid), BF16), ((words, width), F32),
        ((n_mp, words, pair), BF16), ((n_mp, words, pair), BF16), ((n_mp * words, pair), F32), ((n_mp * words, pair), F32),
        ((n_mp, words, 3 * pair), BF16), ((n_mp, words, 3 * pair), BF16), ((n_dp, cap, width), BF16), ((n_dp, cap, width), BF16),
    ]
    if packed:
        shapes = [
            ((2, 2, 2, n_dp // 2, WORD_ROWS, 128), BF16), ((2, 2, n_dp // 2, WORD_ROWS, 128), BF16),
            ((2, n_dp // 2, CHUNK_ROWS, 128), BF16), *shapes,
        ]
    return pl.pallas_call(
        functools.partial(word_body, n_dp, cap, packed),
        in_specs=[vm] * (len(args) - 8) + [pl.BlockSpec(memory_space=pl.ANY)] * 8,
        out_specs=[vm] * len(outs),
        out_shape=[jax.ShapeDtypeStruct(s, d) for s, d in outs],
        scratch_shapes=[pltpu.VMEM(s, d) for s, d in shapes]
        + [pltpu.SemaphoreType.DMA((n_sem,)), pltpu.SemaphoreType.DMA((n_sem,)), pltpu.SemaphoreType.DMA((7, 4))],
        compiler_params=pltpu.CompilerParams(collective_id=0, has_side_effects=True, vmem_limit_bytes=VMEM_LIMIT),
        name="word_layer",
    )(*args)


def plain_reduce(char_parts, char_gains, char_qkv, word_parts, word_gains):
    *char_mats, gain_rows, pool_rows = char_parts
    gain_sums = jnp.stack([jnp.sum(char_mats[0] * char_qkv.astype(F32), 1), jnp.sum(gain_rows, 0)]) / char_gains.astype(F32)
    small = lax.psum((gain_sums, jnp.sum(pool_rows, 0), word_gains), ("dp", "mp"))
    mats = []
    for grad in char_mats:
        part = lax.psum_scatter(grad, "dp", scatter_dimension=0, tiled=True)
        part = lax.psum_scatter(part.astype(BF16), "mp", scatter_dimension=1, tiled=True)
        mats.append(part.astype(F32))
    words = []
    for grad in word_parts:
        part = lax.psum_scatter(grad, "dp", scatter_dimension=1, tiled=True)
        words.append(lax.psum_scatter(part, "mp", scatter_dimension=0, tiled=False))
    qkv, out, up, down = words
    qkv = jnp.transpose(qkv.reshape(qkv.shape[0], 3, -1), (1, 0, 2))
    return (*mats, qkv, out.T, up, down.T, *small)


def per_device(
    char_input,
    char_counts,
    word_source,
    segment_ids,
    cotangent,
    char_norm_gains,
    char_qkv,
    char_out,
    char_up,
    char_down,
    pool_vector,
    char_proj,
    word_norm_gains,
    word_qkv,
    word_out,
    word_up,
    word_down,
):
    groups = lax.axis_size("dp")
    char_weights = (char_norm_gains, char_qkv, char_out, char_up, char_down, pool_vector, char_proj)
    slices = (word_qkv, word_out, word_up, word_down)
    word_vec, *kept = char_forward(
        groups, char_input, char_counts.reshape(1, -1), *char_weights,
        word_source.reshape(1, -1), segment_ids.reshape(1, -1), slices,
    )
    char_kept, (onehot, place, segments, *word_weights) = kept[:12], kept[12:]
    output, d_word, *word_parts, word_gains = word_layer(
        groups, word_vec, onehot, place, segments, cotangent, word_norm_gains, slices, word_weights
    )
    fused = groups == 8
    d_chars, *char_parts = char_backward(
        groups, d_word, char_kept, *char_weights, word_parts[0] if fused else None, word_gains
    )
    if fused:
        return finish(d_chars, output, *char_parts)
    *mats, grad_char_gains, grad_pool, grad_word_gains = plain_reduce(
        char_parts, char_norm_gains, char_qkv, word_parts, word_gains
    )
    return (output, d_chars.astype(F32), *mats, grad_char_gains, grad_pool, grad_word_gains)


def solution(mesh):
    placed = (
        P(("dp", "mp"), None),
        P(("dp", "mp")),
        P(("dp", "mp")),
        P(("dp", "mp")),
        P(("dp", "mp"), None),
        P(),
        P(),
        P(),
        P(),
        P(),
        P(),
        P(),
        P(),
        P(None, None, "mp"),
        P("mp", None),
        P(None, "mp"),
        P("mp", None),
    )
    return jax.shard_map(
        per_device,
        mesh=mesh,
        in_specs=placed,
        out_specs=(
            P(("dp", "mp"), None),
            P(("dp", "mp"), None),
            P("dp", "mp"),
            P("dp", "mp"),
            P("dp", "mp"),
            P("dp", "mp"),
            P("dp", "mp"),
            P(None, "dp", "mp"),
            P("mp", "dp"),
            P("dp", "mp"),
            P("mp", "dp"),
            P(),
            P(),
            P(),
        ),
        check_vma=False,
    )
```

time: 214 us -> 182 us (0.85)
  Pallas kernels: 198 us -> 181 us
  local copies, waits for them, and re-layouts: 14.9 us -> 0 us
    unnamed x8 -> x0, local copies, waits for them, and re-layouts: 11.3 us -> none
    pallas_call x1, Pallas kernels: 51.6 us -> 41.7 us  [char_forward(): pl.pallas_call(functools.partial(char_fwd_body, n_dp, cap), grid=(words /...]
    pallas_call x2, Pallas kernels: 75.9 us -> 68.2 us  [the longest x1 63.4 us: char_backward(): pl.pallas_call(functools.partial(char_bwd_body, n_dp, fused), grid=(3 * s...]
    reshape x3 -> x0, local copies, waits for them, and re-layouts: 3.61 us -> none  [the longest x1 1.47 us: per_device(): char_counts.reshape(-1, 1)]
where the time goes in v4:
time: 182 us
  Pallas kernels  181 us (99%)
    pallas_call x1, Pallas kernels, word_layer(): pl.pallas_call(functools.partial(word_body, n_dp, cap, packed), in_specs=...  71.2 us
    pallas_call x1, Pallas kernels, char_backward(): pl.pallas_call(functools.partial(char_bwd_body, n_dp, fused), grid=(3 * s...  63.4 us
    pallas_call x1, Pallas kernels, char_forward(): pl.pallas_call(functools.partial(char_fwd_body, n_dp, cap), grid=(words /...  41.7 us
    pallas_call x1, Pallas kernels, finish(): pl.pallas_call(finish_body, grid=(steps,), in_specs=[blk, full(word_out.s...  4.84 us

profile of v4, /device:TPU:0, one launch (start us, length us, event | category | flops | bytes accessed | tf_op | source)
XLA Modules:
  0.0 181.9 jit_solution(12717351685381657365)
XLA Ops:
  0.6 41.7 %char_forward.1 = (bf16[256,512]{1,0:T(8,128)(2,1)}, bf16[4096,256]{1,0:T(8,128)(2,1)}, bf16[4096,768]{1,0:T(8,128)(2,1)}, bf16[16384,128]{1,0:T(8,128)(2,1)}, b...) custom-call(bf16[256,4096]{1,0:T(8,128)(2,1)} %x_ref.1, ...), custom_call_target="tpu_custom_call" | custom-call | tf_op jit(solution)/shard_map/char_forward/pallas_call | solution.py:293
  42.3 71.2 %word_layer.1 = (bf16[256,512]{1,0:T(8,128)(2,1)}, bf16[256,512]{1,0:T(8,128)(2,1)}, bf16[2,2,4,768,128]{4,3,2,1,0:T(8,128)(2,1)}, f32[2,512]{1,0:T(2,128)}) custom-call(bf16[256,512]{1,0:T(8,128)(2,1)} %get-tuple-element.57.e_ref, bf16[512,256]{1,0:T(8,128)(2,1)} %get-tuple-element.58.onehot, bf16[512,256]{1,0:T(8,128)(2,1)} %get-tuple-element.59.place, ...), custom_call_target="tpu_custom_call" | custom-call | tf_op jit(solution)/shard_map/word_layer/pallas_call | solution.py:1061
  113.5 63.4 %char_backward.1 = (bf16[256,4096]{1,0:T(8,128)(2,1)}, f32[176,128]{1,0:T(8,128)}, f32[48,128]{1,0:T(8,128)}, f32[768,128]{1,0:T(8,128)}, f32[16,128]{1,0:T(8,128)}) custom-call(bf16[256,512]{1,0:T(8,128)(2,1)} %get-tuple-element.65.de_ref, bf16[2,256]{1,0:T(2,128)(2,1)} %gains_ref.5, bf16[256,768]{1,0:T(8,128)(2,1)} %wqkv_ref.3, bf16[256,256]{1,0:T(8,128)(2,1)} %wout_ref.3, ...), custom_call_target="tpu_custom_call" | custom-call | tf_op jit(solution)/shard_map/char_backward/pallas_call | solution.py:787
  176.9 4.8 %finish.1 = (f32[256,4096]{1,0:T(8,128)}, bf16[256,512]{1,0:T(8,128)(2,1)}, f32[32,192]{1,0:T(8,128)}, f32[32,64]{1,0:T(8,128)}, f32[32,256]{1,0:T(8,128)}, /*in...) custom-call(bf16[256,4096]{1,0:T(8,128)(2,1)} %get-tuple-element.80., ...), custom_call_target="tpu_custom_call" | custom-call | tf_op jit(solution)/shard_map/finish/pallas_call | solution.py:561

commit v5 on v4

--- a/solution.py
+++ b/solution.py
@@ -120,14 +120,18 @@
         return [device_of(z, x, 1 - y, core), device_of(z, x, y, 1 - core), device_of(z, 1 - x, y, core)]
 
     def begin(self):
-        for i in range(len(self.slices)):
-            self.copy(i, "far").start()
+        self.copy(0, "far").start()
+        self.copy(1, "far").start()
         for i in range(len(self.slices)):
             self.copy(i, "near").start()
 
+    def begin_far(self, i):
+        self.copy(i, "far").start()
+
     def pass_on(self, i):
         self.copy(i, "far").wait()
-        self.copy(i, "side").start()
+        if i < len(self.slices) - 1:
+            self.copy(i, "side").start()
         self.copy(i, "early").start()
 
     def pass_last(self, i):
@@ -136,15 +140,15 @@
 
     def finish(self):
         for i in range(len(self.slices)):
-            for kind in ("near", "early", "late"):
+            for kind in ("near", "early", "late")[: 3 - (i == len(self.slices) - 1)]:
                 self.copy(i, kind).wait()
 
 
 def char_fwd_body(
     n_dp, cap,
-    x_ref, cnt_ref, gains_ref, wqkv_ref, wout_ref, wup_ref, wdown_ref, pool_ref, wproj_ref,
+    x_ref, cnt_ref, gains_ref, wqkv_ref, wout_ref, wup_ref, wdown_ref, pool_ref,
     src_ref, seg_ref, s_qkv, s_out, s_up, s_down,
-    e_ref, n1_ref, p_ref, a_ref, o_ref, n2_ref, rs1_ref, rs2_ref, act_ref, dg_ref, f_ref, aw_ref, pooled_ref,
+    pooled_ref, n1_ref, p_ref, a_ref, o_ref, n2_ref, rs1_ref, rs2_ref, act_ref, dg_ref, f_ref, aw_ref,
     onehot_ref, place_ref, seg_out, g_qkv, g_out, g_up, g_down,
     cnt_col, row_send, row_got, seg_all, ssem, rsem, wsend, wrecv,
 ):
@@ -185,10 +189,10 @@
             seg_copy(j).start()
         row_got[0] = row_send[0]
 
-    @pl.when(step == 2)
+    @pl.when(step == last)
     def _():
-        gather.pass_on(0)
-        gather.pass_on(1)
+        gather.pass_last(0)
+        gather.pass_last(1)
 
     words, wide = x_ref.shape
     width = wide // CHARS
@@ -231,6 +235,25 @@
     n2_ref[...] = n2
     rs2_ref[...] = rs2
 
+    @pl.when(step == 0)
+    def _():
+        gather.begin_far(2)
+
+    @pl.when(step == 1)
+    def _():
+        gather.pass_on(0)
+        gather.pass_on(1)
+        gather.begin_far(3)
+
+    @pl.when(step == 2)
+    def _():
+        gather.pass_on(2)
+
+    @pl.when(step == last)
+    def _():
+        gather.pass_last(2)
+        gather.pass_on(3)
+
     f = m
     for j in range(0, wup_ref.shape[1], HIDDEN_CUT):
         cut = slice(j, j + HIDDEN_CUT)
@@ -245,19 +268,10 @@
     et = jnp.exp(t - jnp.max(t, 1, keepdims=True))
     aw = et / jnp.sum(et, 1, keepdims=True)
     aw_ref[...] = aw.reshape(words * CHARS, 1)
-    pooled = jnp.sum(aw * f.reshape(blocks, CHARS, 8, width), 1).reshape(words, width).astype(BF16)
-    pooled_ref[...] = pooled
-    e_ref[...] = dot_nn(pooled, wproj_ref[...]).astype(BF16)
-
-    @pl.when(step == 2)
-    def _():
-        gather.pass_on(2)
+    pooled_ref[...] = jnp.sum(aw * f.reshape(blocks, CHARS, 8, width), 1).reshape(words, width).astype(BF16)
 
     @pl.when(step == last)
     def _():
-        gather.pass_on(3)
-        for i in range(3):
-            gather.pass_last(i)
         for k in range(1, n_dp):
             row_copy(k).wait()
         for j in range(3):
@@ -266,11 +280,10 @@
         lanes = lax.broadcasted_iota(jnp.int32, (slots, all_words), 1).astype(F32)
         place_ref[...] = jnp.where(lanes == at_row, 1.0, 0.0).astype(BF16)
         seg_out[...] = seg_all[...]
-        gather.pass_last(3)
         gather.finish()
 
 
-def char_forward(n_dp, x, counts, gains, wqkv, wout, wup, wdown, pool, wproj, source, segments, slices):
+def char_forward(n_dp, x, counts, gains, wqkv, wout, wup, wdown, pool, source, segments, slices):
     words, wide = x.shape
     width = wide // CHARS
     rows = words * CHARS
@@ -280,13 +293,12 @@
     full = lambda arr: pl.BlockSpec(arr.shape, lambda i: (0,) * arr.ndim)
     blk = lambda n, w: pl.BlockSpec((n, w), lambda i: (i, 0))
     hid = wup.shape[1]
-    dw = wproj.shape[1]
     outs = [
-        (words, STEP_WORDS, dw, BF16), (rows, step_rows, width, BF16), (rows, step_rows, 3 * width, BF16),
+        (words, STEP_WORDS, width, BF16), (rows, step_rows, width, BF16), (rows, step_rows, 3 * width, BF16),
         (rows * CHAR_HEADS, step_rows * CHAR_HEADS, 128, BF16), (rows, step_rows, width, BF16),
         (rows, step_rows, width, BF16), (rows, step_rows, 1, F32), (rows, step_rows, 1, F32),
         (rows, step_rows, hid, BF16), (rows, step_rows, hid, BF16), (rows, step_rows, width, BF16),
-        (rows, step_rows, 1, F32), (words, STEP_WORDS, width, BF16),
+        (rows, step_rows, 1, F32),
     ]
     fixed = [((slots, words), BF16), ((slots, words), BF16), ((4, 8, words), jnp.int32)]
     any_spec = pl.BlockSpec(memory_space=pl.ANY)
@@ -294,7 +306,7 @@
         functools.partial(char_fwd_body, n_dp, cap),
         grid=(words // STEP_WORDS,),
         in_specs=[blk(STEP_WORDS, wide)]
-        + [full(w) for w in (counts, gains, wqkv, wout, wup, wdown, pool, wproj, source, segments)]
+        + [full(w) for w in (counts, gains, wqkv, wout, wup, wdown, pool, source, segments)]
         + [any_spec] * len(slices),
         out_specs=[blk(b, w) for _, b, w, _ in outs]
         + [pl.BlockSpec(s, lambda i, n=len(s): (0,) * n) for s, _ in fixed]
@@ -310,13 +322,16 @@
         ],
         compiler_params=pltpu.CompilerParams(collective_id=2, has_side_effects=True, vmem_limit_bytes=VMEM_LIMIT),
         name="char_forward",
-    )(x, counts, gains, wqkv, wout, wup, wdown, pool, wproj, source, segments, *slices)
-
-
-CHAR_A = 176
+    )(x, counts, gains, wqkv, wout, wup, wdown, pool, source, segments, *slices)
+
+
+CHAR_A = 144
+CHAR_CUT = 80
 CHAR_B = 48
-WORD_ROWS = 768
+WORD_ROWS = 800
 CHUNK_ROWS = 192
+CHUNKS = ((0, 224), (224, 416), (416, 608), (608, 800))
+ROW_QKV, ROW_PROJ, ROW_OUT, ROW_UP, ROW_DOWN = 0, 192, 224, 288, 544
 SEMS = 8
 
 
@@ -403,56 +418,104 @@
         return [pltpu.VMEM(s, BF16) for s in shapes[first:]]
 
 
+class DirectSum:
+    def __init__(self, n_dp, buf, got_mp, held, got_dp, ssem, rsem, base):
+        self.n_dp, self.buf, self.got_mp, self.held, self.got_dp = n_dp, buf, got_mp, held, got_dp
+        self.ssem, self.rsem, self.base = ssem, rsem, base
+        self.dp, self.mp = lax.axis_index("dp"), lax.axis_index("mp")
+
+    def copies(self, phase):
+        dp, mp, n_dp = self.dp, self.mp, self.n_dp
+        make = lambda src, dst, slot, peer: remote_copy(src, dst, self.ssem, self.rsem, self.base + slot, peer)
+        if phase == 0:
+            to = [lax.rem(mp + k, 4) for k in range(1, 4)]
+            return [make(self.buf.at[p], self.got_mp.at[k], k, (dp, p)) for k, p in enumerate(to)]
+        to = [lax.rem(dp + k, n_dp) for k in range(1, n_dp)]
+        return [make(self.held.at[d], self.got_dp.at[k], 3 + k, (d, mp)) for k, d in enumerate(to)]
+
+    def start(self, phase):
+        for copy in self.copies(phase):
+            copy.start()
+
+    def advance(self):
+        for copy in self.copies(0):
+            copy.wait()
+        got, buf, mp = self.got_mp, self.buf, self.mp
+
+        def add(d, carry):
+            total = buf[mp, d].astype(F32) + got[0, d].astype(F32)
+            total = total + got[1, d].astype(F32) + got[2, d].astype(F32)
+            self.held[d] = total.astype(self.held.dtype)
+            return carry
+        lax.fori_loop(0, self.n_dp, add, 0)
+        self.start(1)
+
+    def total(self):
+        for copy in self.copies(1):
+            copy.wait()
+        value = self.held[self.dp].astype(F32)
+        for k in range(self.n_dp - 1):
+            value += self.got_dp[k].astype(F32)
+        return value
+
+    @staticmethod
+    def shapes(n_dp, rows, dtype):
+        shapes = [(4, n_dp, rows, 128), (3, n_dp, rows, 128), (n_dp, rows, 128), (n_dp - 1, rows, 128)]
+        return [pltpu.VMEM(s, dtype) for s in shapes]
+
+
 class GradientSums:
     def __init__(self, n_z, word_sum, refs):
         self.n_z, self.word_sum = n_z, word_sum
-        abuf, bbuf, wbuf, small, sgot, ssem, rsem, lsem, *got = refs
-        self.abuf, self.bbuf, self.wbuf, self.small, self.sgot = abuf, bbuf, wbuf, small, sgot
+        abuf, wbuf, small, sgot, ssem, rsem, lsem, *got = refs
+        self.abuf, self.wbuf, self.small, self.sgot = abuf, wbuf, small, sgot
         self.ssem, self.rsem, self.lsem = ssem, rsem, lsem
         self.z, self.x, self.y, self.core = coordinates()
         self.chunks = []
-        for i, order in enumerate(("xyz", "yxz", "yxz", "yxz")):
-            rows = wbuf.at[:, :, :, CHUNK_ROWS * i : CHUNK_ROWS * i + CHUNK_ROWS]
+        for i, order in enumerate(("yxz", "yxz", "xyz", "xyz")):
+            rows = wbuf.at[:, :, :, CHUNKS[i][0] : CHUNKS[i][1]]
             self.chunks.append(
                 Halving(n_z, None, rows, [None, *got[3 * i : 3 * i + 3]], ssem, rsem, SEMS * i, order)
             )
         core = self.core
-        self.parta = Halving(n_z, abuf.at[1 - core], abuf.at[core], got[12:16], ssem, rsem, 4 * SEMS, "yxz")
-        self.partb = Halving(n_z, bbuf.at[1 - core], bbuf.at[core], got[16:20], ssem, rsem, 5 * SEMS, "yxz")
-        self.tiny = 6 * SEMS
+        self.parts = []
+        for i, (low, high, order) in enumerate(((0, CHAR_CUT, "yxz"), (CHAR_CUT, CHAR_A, "xyz"))):
+            rows = abuf.at[:, :, :, :, low:high]
+            at = 12 + 4 * i
+            self.parts.append(
+                Halving(n_z, rows.at[1 - core], rows.at[core], got[at : at + 4], ssem, rsem, (4 + i) * SEMS, order)
+            )
+        self.partb = DirectSum(2 * n_z, *got[20:24], ssem, rsem, 6 * SEMS)
+        self.tiny = 8 * SEMS
 
     @staticmethod
     def scratch(n_z):
-        n_sem = 7 * SEMS
+        n_sem = 10 * SEMS
         shapes = [
-            pltpu.VMEM((2, 2, 2, n_z, CHAR_A, 128), BF16), pltpu.VMEM((2, 2, 2, n_z, CHAR_B, 128), BF16),
-            pltpu.VMEM((2, 2, n_z, WORD_ROWS, 128), BF16),
-            pltpu.VMEM((4, 16, 128), F32), pltpu.VMEM((2 + n_z, 16, 128), F32),
+            pltpu.VMEM((2, 2, 2, n_z, CHAR_A, 128), BF16), pltpu.VMEM((2, 2, n_z, WORD_ROWS, 128), BF16),
+            pltpu.VMEM((2, 16, 128), F32), pltpu.VMEM((2 + 2 * n_z, 16, 128), F32),
             pltpu.SemaphoreType.DMA((n_sem,)), pltpu.SemaphoreType.DMA((n_sem,)), pltpu.SemaphoreType.DMA,
         ]
-        for _ in range(4):
-            shapes += Halving.got_shapes(n_z, CHUNK_ROWS, 1)
-        return shapes + Halving.got_shapes(n_z, CHAR_A) + Halving.got_shapes(n_z, CHAR_B)
-
-    def peers(self):
-        z, x, y, core = self.z, self.x, self.y, self.core
-        near = [device_of(z, x, y, 1 - core), device_of(z, x, 1 - y, core), device_of(z, 1 - x, y, core)]
-        return near, [device_of(lax.rem(z + k, self.n_z), x, y, core) for k in range(1, self.n_z)]
+        for low, high in CHUNKS:
+            shapes += Halving.got_shapes(n_z, high - low, 1)
+        for rows in (CHAR_CUT, CHAR_A - CHAR_CUT):
+            shapes += Halving.got_shapes(n_z, rows)
+        return shapes + DirectSum.shapes(2 * n_z, CHAR_B, BF16)
 
     def begin(self):
         load = pltpu.make_async_copy(self.word_sum, self.wbuf, self.lsem)
         load.start()
-        near, along = self.peers()
+        dp, mp, n_dp = self.partb.dp, self.partb.mp, 2 * self.n_z
+        peers = [(lax.rem(dp + k, n_dp), mp) for k in range(1, n_dp)] + [(dp, lax.rem(mp + k, 4)) for k in range(1, 4)]
         barrier = pltpu.get_barrier_semaphore()
-        for peer in near + along:
+        for peer in peers:
             pl.semaphore_signal(barrier, inc=1, device_id=peer, device_id_type=MESH)
-        pl.semaphore_wait(barrier, len(near + along))
+        pl.semaphore_wait(barrier, len(peers))
         load.wait()
-        self.chunks[0].start(1)
-        self.chunks[1].start(1)
-        self.chunks[3].start(2)
-
-    def pack_a(self, gup_ref, gdown_ref, gproj_ref, gout_ref):
+        for i, phase in enumerate((1, 2, 2, 2)):
+            self.chunks[i].start(phase)
+
+    def pack_a(self, gup_ref, gdown_ref, gout_ref):
         for d in range(2 * self.n_z):
             down = gdown_ref[128 * d : 128 * d + 128, :]
             out = gout_ref[32 * d : 32 * d + 32, :]
@@ -461,28 +524,29 @@
                 block[0:32, :] = gup_ref[32 * d : 32 * d + 32, 256 * p : 256 * p + 128].astype(BF16)
                 block[32:64, :] = gup_ref[32 * d : 32 * d + 32, 256 * p + 128 : 256 * p + 256].astype(BF16)
                 block[64:128, :] = fold_half(down[:, 64 * p : 64 * p + 64]).astype(BF16)
-                block[128:160, :] = gproj_ref[32 * d : 32 * d + 32, 128 * p : 128 * p + 128].astype(BF16)
-                block[160:176, :] = fold_half(out[:, 64 * p : 64 * p + 64]).astype(BF16)
-        self.parta.start(0)
+                block[128:144, :] = fold_half(out[:, 64 * p : 64 * p + 64]).astype(BF16)
+        for part in self.parts:
+            part.start(0)
 
     def pack_b(self, gqkv_ref):
         for d in range(2 * self.n_z):
             qkv = gqkv_ref[32 * d : 32 * d + 32, :]
             for p in range(4):
-                block = self.bbuf.at[p % 2, p // 2, d % 2, d // 2]
                 own = qkv[:, 192 * p : 192 * p + 192]
-                block[0:32, :] = own[:, 0:128].astype(BF16)
-                block[32:48, :] = fold_half(own[:, 128:192]).astype(BF16)
+                self.partb.buf[p, d, 0:32, :] = own[:, 0:128].astype(BF16)
+                self.partb.buf[p, d, 32:48, :] = fold_half(own[:, 128:192]).astype(BF16)
         self.partb.start(0)
 
     def tiny_copies(self, phase):
-        near, along = self.peers()
-        small, sgot = self.small, self.sgot
-        if phase < 3:
-            return [remote_copy(small.at[phase], sgot.at[phase], self.ssem, self.rsem, self.tiny + phase, near[phase])]
+        dp, mp, n_dp = self.partb.dp, self.partb.mp, 2 * self.n_z
+        if phase == 0:
+            peers = [(dp, lax.rem(mp + k, 4)) for k in range(1, 4)]
+        else:
+            peers = [(lax.rem(dp + k, n_dp), mp) for k in range(1, n_dp)]
+        at = 3 * phase
         return [
-            remote_copy(small.at[3], sgot.at[3 + k], self.ssem, self.rsem, self.tiny + 3 + k, peer)
-            for k, peer in enumerate(along)
+            remote_copy(self.small.at[phase], self.sgot.at[at + k], self.ssem, self.rsem, self.tiny + at + k, peer)
+            for k, peer in enumerate(peers)
         ]
 
     def tiny_start(self, phase):
@@ -490,15 +554,12 @@
             copy.start()
 
     def tiny_finish(self, phase):
-        for copy in self.tiny_copies(phase):
+        copies = self.tiny_copies(phase)
+        for copy in copies:
             copy.wait()
-        small, sgot = self.small, self.sgot
-        if phase < 3:
-            small[phase + 1] = small[phase] + sgot[phase]
-            return None
-        total = small[3]
-        for k in range(1, self.n_z):
-            total += sgot[2 + k]
+        total = self.small[phase]
+        for k in range(len(copies)):
+            total += self.sgot[3 * phase + k]
         return total
 
 
@@ -529,17 +590,17 @@
         owide_ref[...] = wide_ref[...]
         oqkv_ref[:, 0:128] = partb[0:32]
         oqkv_ref[:, 128:192] = unfold_half(partb[32:48])
-        oout_ref[...] = unfold_half(parta[160:176])
+        oout_ref[...] = unfold_half(parta[128:144])
         oup_ref[:, 0:128] = parta[0:32]
         oup_ref[:, 128:256] = parta[32:64]
         odown_ref[...] = unfold_half(parta[64:128]).T
-        oproj_ref[...] = parta[128:160]
+        oproj_ref[...] = word[ROW_PROJ : ROW_PROJ + 32]
         for t in range(3):
             owqkv_ref[t] = word[64 * t : 64 * t + 64]
-        owout_ref[...] = word[192:256]
+        owout_ref[...] = word[ROW_OUT : ROW_OUT + 64]
         for t in range(4):
-            owup_ref[:, 128 * t : 128 * t + 128] = word[256 + 64 * t : 320 + 64 * t]
-            owdown_ref[:, 128 * t : 128 * t + 128] = word[512 + 64 * t : 576 + 64 * t]
+            owup_ref[:, 128 * t : 128 * t + 128] = word[ROW_UP + 64 * t : ROW_UP + 64 * t + 64]
+            owdown_ref[:, 128 * t : 128 * t + 128] = word[ROW_DOWN + 64 * t : ROW_DOWN + 64 * t + 64]
         for j in range(2):
             for t in range(2):
                 ocgain_ref[j : j + 1, 128 * t : 128 * t + 128] = total[2 * j + t : 2 * j + t + 1]
@@ -574,20 +635,20 @@
 
 def char_bwd_body(
     n_dp, fused,
-    de_ref, gains_ref, wqkv_ref, wout_ref, wup_ref, wdown_ref, pool_ref, wproj_ref,
-    n1_ref, p_ref, a_ref, o_ref, n2_ref, rs1_ref, rs2_ref, act_ref, dg_ref, f_ref, aw_ref, pooled_ref,
+    dpool_ref, gains_ref, wqkv_ref, wout_ref, wup_ref, wdown_ref, pool_ref,
+    n1_ref, p_ref, a_ref, o_ref, n2_ref, rs1_ref, rs2_ref, act_ref, dg_ref, f_ref, aw_ref,
     *refs,
 ):
     if fused:
         word_sum, wgain_ref, dx_ref, outa_ref, outb_ref, word_ref, small_ref, *refs = refs
     else:
         dx_ref, *refs = refs
-        outs, refs = refs[:7], refs[7:]
-    gqkv_ref, gout_ref, gup_ref, gdown_ref, gproj_ref, ggain_ref, gpool_ref, *refs = refs
+        outs, refs = refs[:6], refs[6:]
+    gqkv_ref, gout_ref, gup_ref, gdown_ref, ggain_ref, gpool_ref, *refs = refs
     dm_ref, dp_ref, do_ref, ds_ref, *refs = refs
     step = pl.program_id(0)
     part = pl.num_programs(0) // 3
-    words = de_ref.shape[0]
+    words = dpool_ref.shape[0]
     width = n1_ref.shape[1]
     blocks = words // 8
     rows = words * CHARS
@@ -605,61 +666,30 @@
     def _():
         if fused:
             sums.begin()
-        for ref in (gqkv_ref, gout_ref, gup_ref, gdown_ref, gproj_ref, ggain_ref, gpool_ref):
+        for ref in (gqkv_ref, gout_ref, gup_ref, gdown_ref, ggain_ref, gpool_ref):
             ref[...] = jnp.zeros_like(ref)
 
-    def events_start():
-        def second():
-            chunks[3].advance(2)
-            chunks[0].advance(1)
-            chunks[1].advance(1)
-            chunks[2].start(1)
-        at(2, second)
-
-        def third():
-            chunks[3].finish(3)
-            chunks[0].advance(2)
-            chunks[1].advance(2)
-        at(3, third)
-
-        def fourth():
-            chunks[2].advance(1)
-            sums.parta.advance(0)
-        at(4, fourth)
-
-        def sixth():
-            chunks[2].advance(2)
-            chunks[0].finish(3)
-            chunks[1].finish(3)
-        at(6, sixth)
-
-        def seventh():
-            sums.parta.advance(1)
-        at(7, seventh)
-
-        def ninth():
-            sums.partb.advance(0)
-            sums.tiny_finish(0)
-            sums.tiny_start(1)
-            sums.parta.advance(2)
-        at(9, ninth)
-
-        def eleventh():
-            sums.partb.advance(1)
-            sums.tiny_finish(1)
-            sums.tiny_start(2)
-            chunks[2].finish(3)
-            for i in range(4):
-                word_ref[CHUNK_ROWS * i : CHUNK_ROWS * i + CHUNK_ROWS, :] = chunks[i].total()
-        at(11, eleventh)
-
-    events_start()
+    def event(when, *moves):
+        def act():
+            for sum_of, phase in moves:
+                if phase < 3:
+                    sum_of.advance(phase)
+                else:
+                    sum_of.finish(3)
+        at(when, act)
+
+    if fused:
+        first, other = sums.parts
+        event(2, (chunks[1], 2))
+        event(4, (chunks[2], 2), (chunks[3], 2), (chunks[0], 1))
+        event(5, (first, 0), (other, 0))
+        event(6, (chunks[0], 2))
+        event(8, (first, 1), (other, 1))
+        event(11, (first, 2), (other, 2))
 
     @pl.when(step < part)
     def _():
-        de = de_ref[...]
-        gproj_ref[...] += dot_tn(pooled_ref[...], de)
-        dpool = dot_nt(de, wproj_ref[...]).reshape(blocks, 1, 8, width)
+        dpool = dpool_ref[...].astype(F32).reshape(blocks, 1, 8, width)
         f = f_ref[...].astype(F32).reshape(blocks, CHARS, 8, width)
         aw = aw_ref[...].reshape(blocks, CHARS, 8, 1)
         g = jnp.sum(f * dpool, -1, keepdims=True)
@@ -684,7 +714,7 @@
         gout_ref[...] += dot_tn(o_ref[...], dmb)
         do_ref[here, :] = dot_nt(dmb, wout_ref[...]).astype(BF16)
 
-    at(part - 1, lambda: sums.pack_a(gup_ref, gdown_ref, gproj_ref, gout_ref))
+    at(part - 1, lambda: sums.pack_a(gup_ref, gdown_ref, gout_ref))
 
     @pl.when((step >= part) & (step < 2 * part))
     def _():
@@ -735,25 +765,28 @@
                 dx_ref[8 * b : 8 * b + 16, width * c : width * c + width] = jnp.concatenate(pair, 0).astype(BF16)
 
     def end():
-        sums.partb.advance(2)
-        sums.tiny_finish(2)
-        sums.tiny_start(3)
-        sums.parta.finish(3)
-        outa_ref[...] = sums.parta.total()
-        small_ref[...] = sums.tiny_finish(3)
-        sums.partb.finish(3)
+        sums.partb.advance()
+        sums.small[1] = sums.tiny_finish(0)
+        sums.tiny_start(1)
+        for i in range(4):
+            chunks[i].finish(3)
+            word_ref[CHUNKS[i][0] : CHUNKS[i][1], :] = chunks[i].total()
+        for i, (low, high) in enumerate(((0, CHAR_CUT), (CHAR_CUT, CHAR_A))):
+            sums.parts[i].finish(3)
+            outa_ref[low:high, :] = sums.parts[i].total()
+        small_ref[...] = sums.tiny_finish(1)
         outb_ref[...] = sums.partb.total()
     at(3 * part - 1, end)
 
     if not fused:
         @pl.when(step == 3 * part - 1)
         def _():
-            for out, ref in zip(outs, (gqkv_ref, gout_ref, gup_ref, gdown_ref, gproj_ref, ggain_ref, gpool_ref)):
+            for out, ref in zip(outs, (gqkv_ref, gout_ref, gup_ref, gdown_ref, ggain_ref, gpool_ref)):
                 out[...] = ref[...]
 
 
-def char_backward(n_dp, de, kept, gains, wqkv, wout, wup, wdown, pool, wproj, word_sum, wgain):
-    words = de.shape[0]
+def char_backward(n_dp, dpool, kept, gains, wqkv, wout, wup, wdown, pool, word_sum, wgain):
+    words = dpool.shape[0]
     width = wout.shape[0]
     rows = words * CHARS
     step_rows = STEP_WORDS * CHARS
@@ -765,15 +798,15 @@
     second = lambda n, w: pl.BlockSpec((n, w), lambda i: (lax.clamp(0, i - steps, steps - 1), 0))
     third = lambda n, w: pl.BlockSpec((n, w), lambda i: (lax.max(i - 2 * steps, 0), 0))
     twice = lambda n, w: pl.BlockSpec((n, w), lambda i: (lax.rem(lax.max(i - steps, 0), steps), 0))
-    weights = (gains, wqkv, wout, wup, wdown, pool, wproj)
-    when = [twice, second, second, first, first, third, first, first, first, first, first, first]
-    grads = [wqkv.shape, wout.shape, wup.shape, wdown.shape, wproj.shape, (8, width), (8, width)]
+    weights = (gains, wqkv, wout, wup, wdown, pool)
+    when = [twice, second, second, first, first, third, first, first, first, first, first]
+    grads = [wqkv.shape, wout.shape, wup.shape, wdown.shape, (8, width), (8, width)]
     scratch = [pltpu.VMEM(s, F32) for s in grads] + [
         pltpu.VMEM((rows, width), F32), pltpu.VMEM((rows, 3 * width), BF16), pltpu.VMEM((rows, width), BF16),
         pltpu.VMEM((step_rows * CHAR_HEADS, 128), BF16),
     ]
-    args = [de, *weights, *kept]
-    in_specs = [first(STEP_WORDS, de.shape[1])] + [full(w) for w in weights]
+    args = [dpool, *weights, *kept]
+    in_specs = [first(STEP_WORDS, width)] + [full(w) for w in weights]
     in_specs += [f(r.shape[0] // steps, r.shape[1]) for f, r in zip(when, kept)]
     params = dict(vmem_limit_bytes=VMEM_LIMIT)
     if fused:
@@ -798,22 +831,23 @@
 
 def word_body(
     n_dp, cap, packed,
-    e_ref, onehot, place, seg_all, cot_ref, gains_ref, *refs,
+    pooled_ref, onehot, place, seg_all, cot_ref, gains_ref, wproj_ref, *refs,
 ):
     slices, wholes, refs = refs[:4], refs[4:8], refs[8:]
     if packed:
-        out_ref, de_ref, gsum_ref, ggain_ref, gbuf_ref, got_a, got_y, *refs = refs
+        out_ref, dpool_ref, gsum_ref, ggain_ref, gbuf_ref, got_a, got_x, got_y, *refs = refs
     else:
-        out_ref, de_ref, gqkv_ref, gout_ref, gup_ref, gdown_ref, ggain_ref, *refs = refs
+        out_ref, dpool_ref, gqkv_ref, gout_ref, gup_ref, gdown_ref, gproj_ref, ggain_ref, *refs = refs
     (
-        wqkv_ref, wout_ref, wup_ref, wdown_ref, vec_send, vec_got, segc_all, rows_ref, normed, rstd_a,
+        wqkv_ref, wout_ref, wup_ref, wdown_ref, vec_send, vec_got, segc_all, pooled_rows, rows_ref, normed, rstd_a,
         qkv_send, qkv_all, weights, o_send, o_all, act_ref, dh_ref, dact_ref, dm_ref,
         do_send, do_all, dk_acc, dv_acc, dqkv_send, dqkv_all, back_send, ret,
         ssem, rsem, lsem,
     ) = refs
     dp, mp = lax.axis_index("dp"), lax.axis_index("mp")
     n_mp = 4
-    words, width = e_ref.shape
+    words, narrow = pooled_ref.shape
+    width = cot_ref.shape[1]
     slots = n_dp * cap
     pair = 2 * (width // HEADS)
     scale = (width // HEADS) ** -0.5
@@ -837,6 +871,7 @@
         copy.start()
         return copy
 
+    z, x, y, core = coordinates()
     loads = []
     for i, held in ((3, wdown_ref), (0, wqkv_ref), (1, wout_ref), (2, wup_ref)):
         loads.append([])
@@ -846,28 +881,30 @@
                 for t in range(3):
                     dst = held.at[at, :, pair * t : pair * t + pair]
                     loads[-1].append(pltpu.make_async_copy(src.at[t], dst, lsem.at[4 + t, j]))
+            elif i == 3 and j > 1:
+                src, dst = WeightGather.half(src, 0, x), WeightGather.half(held.at[at], 0, x)
+                loads[-1].append(pltpu.make_async_copy(src, dst, lsem.at[i, j]))
             else:
                 loads[-1].append(pltpu.make_async_copy(src, held.at[at], lsem.at[i, j]))
         for load in loads[-1]:
             load.start()
-    vec_send[...] = dot_nn(onehot[...], e_ref[...]).astype(BF16).reshape(n_dp, cap, width)
+    vec_send[...] = dot_nn(onehot[...], pooled_ref[...]).astype(BF16).reshape(n_dp, cap, narrow)
 
     pl.semaphore_wait(barrier, n_dp - 1 + 3)
     vec_copies = [send(vec_send.at[k], vec_got.at[k], to_dp[k]) for k in range(1, n_dp)]
+    source = WeightGather.half(wholes[3].at[mates[1]], 0, x)
+    down_side = send(source, WeightGather.half(wdown_ref.at[mates[1]], 0, x), device_of(z, 1 - x, y, core))
     vec_got[0] = vec_send[0]
     gains = gains_ref[...].astype(F32)
     cot = cot_ref[...]
-    for load in loads[0]:
-        load.wait()
-    for p in range(n_mp):
-        dact_ref[p] = dot_nt(cot, wdown_ref[p]).astype(BF16)
     for j in range(n_mp):
         segc_all[words * j : words * j + words, :] = as_column(seg_all[j, 0:1, :])
     for load in loads[1] + loads[2] + loads[3]:
         load.wait()
     for copy in vec_copies:
         copy.wait()
-    rows = dot_tn(place[...], vec_got[...].reshape(slots, width))
+    pooled_rows[...] = dot_tn(place[...], vec_got[...].reshape(slots, narrow)).astype(BF16)
+    rows = dot_nn(pooled_rows[...], wproj_ref[...]).astype(BF16).astype(F32)
     rows_ref[...] = rows
     n_w, rstd = norm_fwd(rows, gains[0:1])
     normed[0] = n_w
@@ -877,34 +914,43 @@
         qkv_send[mate] = dot_nn(n_w, wqkv_ref[mate]).astype(BF16)
         qkv_copies.append(send(qkv_send.at[mate], qkv_all.at[mp], (dp, mate)))
     qkv_all[mp] = dot_nn(n_w, wqkv_ref[mp]).astype(BF16)
+    down_side.wait()
+    source = WeightGather.half(wdown_ref.at[mates[1]], 0, 1 - x)
+    down_late = send(source, source, (dp, mates[0]))
     for copy in qkv_copies:
         copy.wait()
 
-    head_lane = lax.broadcasted_iota(jnp.int32, (1, pair), 1) // (pair // 2)
-    head_mask = [jnp.where(head_lane == h, 1.0, 0.0).astype(BF16) for h in range(2)]
+    low_lane = lax.broadcasted_iota(jnp.int32, (1, pair), 1) < pair // 2
+    low_mask = jnp.where(low_lane, 1.0, 0.0).astype(BF16)
+    high_mask = jnp.where(low_lane, 0.0, 1.0).astype(BF16)
+
+    def heads(v, factor):
+        return jnp.concatenate([v * (low_mask * factor).astype(BF16), v * (high_mask * factor).astype(BF16)], 0)
+
     o_copies = []
     for i in reversed(range(n_mp)):
         keys = words * (i + 1)
-        q = qkv_all[i, :, 0:pair]
+        q = heads(qkv_all[i, :, 0:pair], scale)
         k = qkv_all[0 : i + 1, :, pair : 2 * pair].reshape(keys, pair)
         v = qkv_all[0 : i + 1, :, 2 * pair : 3 * pair].reshape(keys, pair)
         same = segc_all[0:keys, 0:1] == seg_all[i, 0:1, :].astype(F32)
         key_at = lax.broadcasted_iota(jnp.int32, (keys, words), 0)
         query_at = lax.broadcasted_iota(jnp.int32, (keys, words), 1) + words * i
         allowed = same & (key_at <= query_at)
-        total = None
-        for h in range(2):
-            st = dot_nt(k * (head_mask[h] * scale).astype(BF16), q)
-            st = jnp.where(allowed, st, NEGATIVE)
-            ex = jnp.exp(st - jnp.max(st, 0, keepdims=True))
-            at = (ex * (1.0 / jnp.sum(ex, 0, keepdims=True))).astype(BF16)
-            weights[i, h, 0:keys, :] = at
-            part = dot_tn(at, v * head_mask[h])
-            total = part if total is None else total + part
-        o_send[i] = total.astype(BF16)
+        st = jnp.where(jnp.concatenate([allowed, allowed], 1), dot_nt(k, q), NEGATIVE)
+        ex = jnp.exp(st - jnp.max(st, 0, keepdims=True))
+        at = (ex * (1.0 / jnp.sum(ex, 0, keepdims=True))).astype(BF16)
+        weights[i, 0:keys, :] = at
+        both = dot_tn(at, v)
+        o_send[i] = jnp.where(low_lane, both[:words], both[words:]).astype(BF16)
     for mate in reversed(mates):
         o_copies.append(send(o_send.at[mate], o_all.at[mp], (dp, mate)))
     o_all[mp] = o_send[mp]
+    down_late.wait()
+    for load in loads[0]:
+        load.wait()
+    for p in range(n_mp):
+        dact_ref[p] = dot_nt(cot, wdown_ref[p]).astype(BF16)
     for copy in o_copies:
         copy.wait()
     attended = jnp.concatenate([o_all[p] for p in range(n_mp)], 1)
@@ -932,37 +978,69 @@
         do_copies.append(send(do_send.at[mate], do_all.at[mp], (dp, mate)))
     do_all[mp] = dot_nt(d_att, wout_ref[mp]).astype(BF16)
 
-    z, x, y, core = coordinates()
-
-    def pair_sum(low, high):
+    def pair_sum(i):
+        low, high = CHUNKS[i]
         src = gbuf_ref.at[1 - core, :, :, :, low:high]
         return send(src, got_a.at[:, :, :, low:high], device_of(z, x, y, 1 - core))
 
-    def pair_add(low, high):
+    def pair_add(i):
+        low, high = CHUNKS[i]
+
         def add(i, carry):
             b, c, d = i // n_dp, (i // (n_dp // 2)) % 2, lax.rem(i, n_dp // 2)
             gsum_ref[b, c, d, low:high] = gbuf_ref[core, b, c, d, low:high] + got_a[b, c, d, low:high]
             return carry
         lax.fori_loop(0, 2 * n_dp, add, 0)
 
+    def x_sum(i):
+        low, high = CHUNKS[i]
+        return send(gsum_ref.at[:, 1 - x, :, low:high], got_x.at[i - 2], device_of(z, 1 - x, y, core))
+
+    def x_add(i):
+        low, high = CHUNKS[i]
+        for b in range(2):
+            for d in range(n_dp // 2):
+                gsum_ref[b, x, d, low:high] += got_x[i - 2, b, d]
+
+    def y_sum(i):
+        low, high = CHUNKS[i]
+        return send(gsum_ref.at[1 - y, :, :, low:high], got_y, device_of(z, x, 1 - y, core))
+
+    def y_add(i):
+        low, high = CHUNKS[i]
+        for c in range(2):
+            for d in range(n_dp // 2):
+                gsum_ref[y, c, d, low:high] += got_y[c, d]
+
     def put(base, p, grad):
         if packed:
-            block = words // 4
+            block = grad.shape[0] // n_dp
             for d in range(n_dp):
                 for t in range(grad.shape[1] // 128):
                     gbuf_ref[p % 2, p // 2, d % 2, d // 2, base + block * t : base + block * t + block, :] = (
                         grad[block * d : block * d + block, 128 * t : 128 * t + 128].astype(BF16)
                     )
+        elif base == ROW_PROJ:
+            gproj_ref[:, 128 * p : 128 * p + 128] = grad
         else:
-            ref = {0: gqkv_ref, 192: gout_ref, 256: gup_ref, 512: gdown_ref}[base]
+            ref = {ROW_QKV: gqkv_ref, ROW_OUT: gout_ref, ROW_UP: gup_ref, ROW_DOWN: gdown_ref}[base]
             ref[p] = grad
 
     for p in range(n_mp):
-        put(512, p, dot_tn(cot, act_ref[p]))
-        put(256, p, dot_tn(n_w2, dh_ref[p]))
-        put(192, p, dot_tn(d_att, o_all[p]))
+        put(ROW_DOWN, p, dot_tn(cot, act_ref[p]))
     if packed:
-        early_sum = pair_sum(CHUNK_ROWS, WORD_ROWS)
+        pair_three = pair_sum(3)
+    for p in range(n_mp):
+        put(ROW_UP, p, dot_tn(n_w2, dh_ref[p]))
+    if packed:
+        pair_two = pair_sum(2)
+    for p in range(n_mp):
+        put(ROW_OUT, p, dot_tn(d_att, o_all[p]))
+    if packed:
+        pair_one = pair_sum(1)
+        pair_three.wait()
+        pair_add(3)
+        x_three = x_sum(3)
     dk_acc[...] = jnp.zeros_like(dk_acc)
     dv_acc[...] = jnp.zeros_like(dv_acc)
     for copy in do_copies:
@@ -972,33 +1050,33 @@
         q = qkv_all[i, :, 0:pair]
         k = qkv_all[0 : i + 1, :, pair : 2 * pair].reshape(keys, pair)
         v = qkv_all[0 : i + 1, :, 2 * pair : 3 * pair].reshape(keys, pair)
-        do = do_all[i]
-        dq = None
-        for h in range(2):
-            at = weights[i, h, 0:keys, :]
-            dpt = dot_nt(v * head_mask[h], do)
-            af = at.astype(F32)
-            delta = jnp.sum(af * dpt, 0, keepdims=True)
-            ds = (af * (dpt - delta)).astype(BF16)
-            scaled = (head_mask[h] * scale).astype(BF16)
-            part = dot_tn(ds, k * scaled)
-            dq = part if dq is None else dq + part
-            dk_acc[0:keys, :] += dot_nn(ds, q * scaled)
-            dv_acc[0:keys, :] += dot_nn(at, do * head_mask[h])
+        do = heads(do_all[i], 1.0)
+        at = weights[i, 0:keys, :]
+        af = at.astype(F32)
+        dpt = dot_nt(v, do)
+        ds = (af * (dpt - jnp.sum(af * dpt, 0, keepdims=True))).astype(BF16)
+        both = dot_tn(ds, k)
+        dq = jnp.where(low_lane, both[:words], both[words:]) * scale
+        dk_acc[0:keys, :] += dot_nn(ds, heads(q, scale))
+        dv_acc[0:keys, :] += dot_nn(at, do)
         dqkv_send[i, :, 0:pair] = dq.astype(BF16)
         dqkv_send[i, :, pair : 2 * pair] = dk_acc[words * i : keys, :].astype(BF16)
         dqkv_send[i, :, 2 * pair : 3 * pair] = dv_acc[words * i : keys, :].astype(BF16)
+    if packed:
+        pair_two.wait()
+        pair_add(2)
+        x_two = x_sum(2)
     dqkv_copies = []
     for mate in reversed(mates):
         dqkv_copies.append(send(dqkv_send.at[mate], dqkv_all.at[mp], (dp, mate)))
     dqkv_all[mp] = dqkv_send[mp]
     if packed:
-        early_sum.wait()
-        pair_add(CHUNK_ROWS, WORD_ROWS)
+        pair_one.wait()
+        pair_add(1)
     for copy in dqkv_copies:
         copy.wait()
     if packed:
-        y_sum = send(gsum_ref.at[1 - y, :, :, WORD_ROWS - CHUNK_ROWS :], got_y, device_of(z, x, 1 - y, core))
+        y_one = y_sum(1)
     d_normed = jnp.zeros((words, width), F32)
     for p in range(n_mp):
         d_normed = d_normed + dot_nt(dqkv_all[p], wqkv_ref[p])
@@ -1007,56 +1085,64 @@
     d_rows = (dm_ref[...] + d_first).astype(BF16)
     ggain_ref[0:1, :] = gain_a
     ggain_ref[1:2, :] = gain_b
-    back_send[...] = dot_nn(place[...], d_rows).astype(BF16).reshape(n_dp, cap, width)
+    d_pooled = dot_nt(d_rows, wproj_ref[...]).astype(BF16)
+    back_send[...] = dot_nn(place[...], d_pooled).astype(BF16).reshape(n_dp, cap, narrow)
     back_copies = [send(back_send.at[k], ret.at[k], from_dp[k]) for k in range(1, n_dp)]
     ret[0] = back_send[0]
+    grad_proj = dot_tn(pooled_rows[...], d_rows)
     for p in range(n_mp):
-        put(0, p, dot_tn(normed[0], dqkv_all[p]))
+        put(ROW_QKV, p, dot_tn(normed[0], dqkv_all[p]))
+        put(ROW_PROJ, p, grad_proj[:, 128 * p : 128 * p + 128])
     if packed:
-        late_sum = pair_sum(0, CHUNK_ROWS)
-        late_sum.wait()
-        pair_add(0, CHUNK_ROWS)
-        y_sum.wait()
-        for c in range(2):
-            for d in range(n_dp // 2):
-                gsum_ref[y, c, d, WORD_ROWS - CHUNK_ROWS :] += got_y[c, d]
+        pair_zero = pair_sum(0)
+        x_three.wait()
+        x_add(3)
+        x_two.wait()
+        x_add(2)
+        pair_zero.wait()
+        pair_add(0)
     for copy in back_copies:
         copy.wait()
-    de_ref[...] = dot_tn(onehot[...], ret[...].reshape(slots, width)).astype(BF16)
-
-
-def word_layer(n_dp, word_vec, onehot, place, segments, cotangent, gains, slices, wholes):
-    words, width = word_vec.shape
+    dpool_ref[...] = dot_tn(onehot[...], ret[...].reshape(slots, narrow)).astype(BF16)
+    if packed:
+        y_one.wait()
+        y_add(1)
+
+
+def word_layer(n_dp, pooled, onehot, place, segments, cotangent, gains, wproj, slices, wholes):
+    words, narrow = pooled.shape
+    width = cotangent.shape[1]
     wqkv, wout, wup, wdown = wholes
     n_mp = wqkv.shape[0]
     cap = -(-2 * words // n_dp // 16) * 16
     slots = cap * n_dp
     pair = 2 * (width // HEADS)
     packed = n_dp == 8
-    outs = [((words, width), BF16), ((words, width), BF16)]
+    outs = [((words, width), BF16), ((words, narrow), BF16)]
     if packed:
         outs.append(((2, 2, n_dp // 2, WORD_ROWS, 128), BF16))
     else:
         outs += [((n_mp, width, n), F32) for n in (3 * pair, pair, wup.shape[2], wup.shape[2])]
+        outs.append(((narrow, width), F32))
     outs.append(((2, width), F32))
     hid = wup.shape[2]
-    n_sem = 2 * (n_dp - 1) + 4 * 3 + 3
+    n_sem = 2 * (n_dp - 1) + 4 * 3 + 3 + 7
     vm = pl.BlockSpec(memory_space=pltpu.VMEM)
-    args = (word_vec, onehot, place, segments, cotangent, gains, *slices, *wholes)
+    args = (pooled, onehot, place, segments, cotangent, gains, wproj, *slices, *wholes)
     shapes = [
         ((n_mp, width, 3 * pair), BF16), (wout.shape, BF16), (wup.shape, BF16), (wdown.shape, BF16),
-        ((n_dp, cap, width), BF16), ((n_dp, cap, width), BF16), ((n_mp * words, 128), F32),
+        ((n_dp, cap, narrow), BF16), ((n_dp, cap, narrow), BF16), ((n_mp * words, 128), F32), ((words, narrow), BF16),
         ((words, width), F32), ((2, words, width), BF16), ((1, words, 1), F32),
-        ((n_mp, words, 3 * pair), BF16), ((n_mp, words, 3 * pair), BF16), ((n_mp, 2, n_mp * words, words), BF16),
+        ((n_mp, words, 3 * pair), BF16), ((n_mp, words, 3 * pair), BF16), ((n_mp, n_mp * words, 2 * words), BF16),
         ((n_mp, words, pair), BF16), ((n_mp, words, pair), BF16),
         ((n_mp, words, hid), BF16), ((n_mp, words, hid), BF16), ((n_mp, words, hid), BF16), ((words, width), F32),
         ((n_mp, words, pair), BF16), ((n_mp, words, pair), BF16), ((n_mp * words, pair), F32), ((n_mp * words, pair), F32),
-        ((n_mp, words, 3 * pair), BF16), ((n_mp, words, 3 * pair), BF16), ((n_dp, cap, width), BF16), ((n_dp, cap, width), BF16),
+        ((n_mp, words, 3 * pair), BF16), ((n_mp, words, 3 * pair), BF16), ((n_dp, cap, narrow), BF16), ((n_dp, cap, narrow), BF16),
     ]
     if packed:
         shapes = [
             ((2, 2, 2, n_dp // 2, WORD_ROWS, 128), BF16), ((2, 2, n_dp // 2, WORD_ROWS, 128), BF16),
-            ((2, n_dp // 2, CHUNK_ROWS, 128), BF16), *shapes,
+            ((2, 2, n_dp // 2, CHUNK_ROWS, 128), BF16), ((2, n_dp // 2, CHUNK_ROWS, 128), BF16), *shapes,
         ]
     return pl.pallas_call(
         functools.partial(word_body, n_dp, cap, packed),
@@ -1108,22 +1194,24 @@
     word_down,
 ):
     groups = lax.axis_size("dp")
-    char_weights = (char_norm_gains, char_qkv, char_out, char_up, char_down, pool_vector, char_proj)
+    char_weights = (char_norm_gains, char_qkv, char_out, char_up, char_down, pool_vector)
     slices = (word_qkv, word_out, word_up, word_down)
-    word_vec, *kept = char_forward(
+    pooled, *kept = char_forward(
         groups, char_input, char_counts.reshape(1, -1), *char_weights,
         word_source.reshape(1, -1), segment_ids.reshape(1, -1), slices,
     )
-    char_kept, (onehot, place, segments, *word_weights) = kept[:12], kept[12:]
-    output, d_word, *word_parts, word_gains = word_layer(
-        groups, word_vec, onehot, place, segments, cotangent, word_norm_gains, slices, word_weights
+    char_kept, (onehot, place, segments, *word_weights) = kept[:11], kept[11:]
+    output, d_pooled, *word_parts, word_gains = word_layer(
+        groups, pooled, onehot, place, segments, cotangent, word_norm_gains, char_proj, slices, word_weights
     )
     fused = groups == 8
     d_chars, *char_parts = char_backward(
-        groups, d_word, char_kept, *char_weights, word_parts[0] if fused else None, word_gains
+        groups, d_pooled, char_kept, *char_weights, word_parts[0] if fused else None, word_gains
     )
     if fused:
         return finish(d_chars, output, *char_parts)
+    *word_parts, grad_proj = word_parts
+    char_parts = (*char_parts[:4], grad_proj, *char_parts[4:])
     *mats, grad_char_gains, grad_pool, grad_word_gains = plain_reduce(
         char_parts, char_norm_gains, char_qkv, word_parts, word_gains
     )

time: 182 us -> 157 us (0.86)
  Pallas kernels: 181 us -> 156 us
    pallas_call x1, Pallas kernels: 71.2 us -> 61.8 us  [word_layer(): pl.pallas_call(functools.partial(word_body, n_dp, cap, packed), in_specs=...]
    pallas_call x1, Pallas kernels: 63.4 us -> 54.3 us  [char_backward(): pl.pallas_call(functools.partial(char_bwd_body, n_dp, fused), grid=(3 * s...]
    pallas_call x1, Pallas kernels: 41.7 us -> 35.1 us  [char_forward(): pl.pallas_call(functools.partial(char_fwd_body, n_dp, cap), grid=(words /...]
where the time goes in v5:
time: 157 us
  Pallas kernels  156 us (99%)
    pallas_call x1, Pallas kernels, word_layer(): pl.pallas_call(functools.partial(word_body, n_dp, cap, packed), in_specs=...  61.8 us
    pallas_call x1, Pallas kernels, char_backward(): pl.pallas_call(functools.partial(char_bwd_body, n_dp, fused), grid=(3 * s...  54.3 us
    pallas_call x1, Pallas kernels, char_forward(): pl.pallas_call(functools.partial(char_fwd_body, n_dp, cap), grid=(words /...  35.1 us
    pallas_call x1, Pallas kernels, finish(): pl.pallas_call(finish_body, grid=(steps,), in_specs=[blk, full(word_out.s...  4.84 us

profile of v5, /device:TPU:0, one launch (start us, length us, event | category | flops | bytes accessed | tf_op | source)
XLA Modules:
  0.0 156.9 jit_solution(1425622498639675811)
XLA Ops:
  0.6 35.1 %char_forward.1 = (bf16[256,256]{1,0:T(8,128)(2,1)}, bf16[4096,256]{1,0:T(8,128)(2,1)}, bf16[4096,768]{1,0:T(8,128)(2,1)}, bf16[16384,128]{1,0:T(8,128)(2,1)}, b...) custom-call(bf16[256,4096]{1,0:T(8,128)(2,1)} %x_ref.1, ...), custom_call_target="tpu_custom_call" | custom-call | tf_op jit(solution)/shard_map/char_forward/pallas_call | solution.py:305
  35.7 61.8 %word_layer.1 = (bf16[256,512]{1,0:T(8,128)(2,1)}, bf16[256,256]{1,0:T(8,128)(2,1)}, bf16[2,2,4,800,128]{4,3,2,1,0:T(8,128)(2,1)}, f32[2,512]{1,0:T(2,128)}) custom-call(bf16[256,256]{1,0:T(8,128)(2,1)} %get-tuple-element.56.pooled_ref, bf16[512,256]{1,0:T(8,128)(2,1)} %get-tuple-element.57.onehot, bf16[512,256]{1,0:T(8,128)(2,1)} %get-tuple-element.58.place, ...), custom_call_target="tpu_custom_call" | custom-call | tf_op jit(solution)/shard_map/word_layer/pallas_call | solution.py:1147
  97.6 54.3 %char_backward.1 = (bf16[256,4096]{1,0:T(8,128)(2,1)}, f32[144,128]{1,0:T(8,128)}, f32[48,128]{1,0:T(8,128)}, f32[800,128]{1,0:T(8,128)}, f32[16,128]{1,0:T(8,128)}) custom-call(bf16[256,256]{1,0:T(8,128)(2,1)} %get-tuple-element.64.dpool_ref, bf16[2,256]{1,0:T(2,128)(2,1)} %gains_ref.5, bf16[256,768]{1,0:T(8,128)(2,1)} %wqkv_ref.3, ...), custom_call_target="tpu_custom_call" | custom-call | tf_op jit(solution)/shard_map/char_backward/pallas_call | solution.py:820
  151.9 4.8 %finish.1 = (f32[256,4096]{1,0:T(8,128)}, bf16[256,512]{1,0:T(8,128)(2,1)}, f32[32,192]{1,0:T(8,128)}, f32[32,64]{1,0:T(8,128)}, f32[32,256]{1,0:T(8,128)}, /*in...) custom-call(bf16[256,4096]{1,0:T(8,128)(2,1)} %get-tuple-element.78., ...), custom_call_target="tpu_custom_call" | custom-call | tf_op jit(solution)/shard_map/finish/pallas_call | solution.py:622

commit v6 on v5

--- a/solution.py
+++ b/solution.py
@@ -148,9 +148,9 @@
     n_dp, cap,
     x_ref, cnt_ref, gains_ref, wqkv_ref, wout_ref, wup_ref, wdown_ref, pool_ref,
     src_ref, seg_ref, s_qkv, s_out, s_up, s_down,
-    pooled_ref, n1_ref, p_ref, a_ref, o_ref, n2_ref, rs1_ref, rs2_ref, act_ref, dg_ref, f_ref, aw_ref,
+    pooled_ref, early_ref, late_ref, p_any, a_any, act_any,
     onehot_ref, place_ref, seg_out, g_qkv, g_out, g_up, g_down,
-    cnt_col, row_send, row_got, seg_all, ssem, rsem, wsend, wrecv,
+    cnt_col, row_send, row_got, seg_all, ssem, rsem, wsend, wrecv, p_buf, a_buf, act_buf, osem,
 ):
     step, last = pl.program_id(0), pl.num_programs(0) - 1
     dp, mp = lax.axis_index("dp"), lax.axis_index("mp")
@@ -206,9 +206,36 @@
             for c in range(CHARS):
                 pieces.append(xt[8 * half : 8 * half + 8, width * c : width * c + width])
     x = jnp.concatenate(pieces, 0)
+    hid = wup_ref.shape[1]
+    rows = words * CHARS
+    cuts = range(0, hid, HIDDEN_CUT)
+    held = lax.rem(step, 2)
+    p_ref, a_ref, act_ref = p_buf.at[held], a_buf.at[held], act_buf.at[held]
+
+    def out_copies(of):
+        slot = lax.rem(of, 2)
+        at = lambda n: pl.ds(pl.multiple_of(of * n, n), n)
+        heads = rows * CHAR_HEADS
+        copies = [
+            pltpu.make_async_copy(p_buf.at[slot], p_any.at[at(rows)], osem.at[slot, 0]),
+            pltpu.make_async_copy(a_buf.at[slot], a_any.at[at(heads)], osem.at[slot, 1]),
+        ]
+        for i in range(2 * hid // HIDDEN_CUT):
+            cut = pl.ds(HIDDEN_CUT * i, HIDDEN_CUT)
+            copies.append(pltpu.make_async_copy(act_buf.at[slot, :, cut], act_any.at[at(rows), cut], osem.at[slot, 2 + i]))
+        return copies
+
+    leaving = out_copies(step)
+
+    @pl.when(step >= 2)
+    def _():
+        for copy in out_copies(step - 2):
+            copy.wait()
+
     n1, rs1 = norm_fwd(x, gains[0:1])
-    n1_ref[...] = n1
-    rs1_ref[...] = rs1
+    lane = lax.broadcasted_iota(jnp.int32, (rows, 128), 1)
+    late_ref[:, 0:width] = n1
+    late_ref[:, width:] = jnp.where(lane == 0, rs1, 0.0).astype(BF16)
     p_ref[...] = dot_nn(n1, wqkv_ref[...]).astype(BF16)
     row_w = lax.broadcasted_iota(jnp.int32, (8, 128), 0)
     lane_w = lax.broadcasted_iota(jnp.int32, (8, 128), 1) % 8
@@ -229,11 +256,12 @@
     for b in range(blocks):
         sl = slice(128 * b, 128 * b + 128)
         a = a_ref[size * b : size * b + size, :]
-        o_ref[sl, :] = dot_tn(a, head_stack(p_ref[sl, 2 * width : 3 * width], CHAR_HEADS, 1.0)).astype(BF16)
-    m = x + dot_nn(o_ref[...], wout_ref[...])
+        early_ref[sl, 0:width] = dot_tn(a, head_stack(p_ref[sl, 2 * width : 3 * width], CHAR_HEADS, 1.0)).astype(BF16)
+    leaving[0].start()
+    leaving[1].start()
+    m = x + dot_nn(early_ref[:, 0:width], wout_ref[...])
     n2, rs2 = norm_fwd(m, gains[1:2])
-    n2_ref[...] = n2
-    rs2_ref[...] = rs2
+    early_ref[:, width : 2 * width] = n2
 
     @pl.when(step == 0)
     def _():
@@ -255,19 +283,21 @@
         gather.pass_on(3)
 
     f = m
-    for j in range(0, wup_ref.shape[1], HIDDEN_CUT):
+    for i, j in enumerate(cuts):
         cut = slice(j, j + HIDDEN_CUT)
         act, slope = gelu_both(dot_nn(n2, wup_ref[:, cut]).astype(BF16))
         act_ref[:, cut] = act
-        dg_ref[:, cut] = slope
+        act_ref[:, hid + j : hid + j + HIDDEN_CUT] = slope
+        leaving[2 + i].start()
+        leaving[2 + len(cuts) + i].start()
         f = f + dot_nn(act, wdown_ref[cut, :])
-    f_ref[...] = f.astype(BF16)
+    early_ref[:, 2 * width : 3 * width] = f.astype(BF16)
     t = jnp.sum(f * pool_ref[...].astype(F32).reshape(1, width), -1, keepdims=True).reshape(blocks, CHARS, 8, 1)
     counts = counts_here[:, 0:1].reshape(blocks, 1, 8, 1)
     t = jnp.where(lax.broadcasted_iota(jnp.int32, t.shape, 1) < counts, t, NEGATIVE)
     et = jnp.exp(t - jnp.max(t, 1, keepdims=True))
     aw = et / jnp.sum(et, 1, keepdims=True)
-    aw_ref[...] = aw.reshape(words * CHARS, 1)
+    early_ref[:, 3 * width :] = jnp.where(lane == 0, rs2, aw.reshape(rows, 1)).astype(BF16)
     pooled_ref[...] = jnp.sum(aw * f.reshape(blocks, CHARS, 8, width), 1).reshape(words, width).astype(BF16)
 
     @pl.when(step == last)
@@ -281,6 +311,8 @@
         place_ref[...] = jnp.where(lanes == at_row, 1.0, 0.0).astype(BF16)
         seg_out[...] = seg_all[...]
         gather.finish()
+        for copy in out_copies(step - 1) + leaving:
+            copy.wait()
 
 
 def char_forward(n_dp, x, counts, gains, wqkv, wout, wup, wdown, pool, source, segments, slices):
@@ -294,11 +326,8 @@
     blk = lambda n, w: pl.BlockSpec((n, w), lambda i: (i, 0))
     hid = wup.shape[1]
     outs = [
-        (words, STEP_WORDS, width, BF16), (rows, step_rows, width, BF16), (rows, step_rows, 3 * width, BF16),
-        (rows * CHAR_HEADS, step_rows * CHAR_HEADS, 128, BF16), (rows, step_rows, width, BF16),
-        (rows, step_rows, width, BF16), (rows, step_rows, 1, F32), (rows, step_rows, 1, F32),
-        (rows, step_rows, hid, BF16), (rows, step_rows, hid, BF16), (rows, step_rows, width, BF16),
-        (rows, step_rows, 1, F32),
+        (words, STEP_WORDS, width), (rows, step_rows, 3 * width + 128), (rows, step_rows, width + 128),
+        (rows, None, 3 * width), (rows * CHAR_HEADS, None, 128), (rows, None, 2 * hid),
     ]
     fixed = [((slots, words), BF16), ((slots, words), BF16), ((4, 8, words), jnp.int32)]
     any_spec = pl.BlockSpec(memory_space=pl.ANY)
@@ -308,10 +337,10 @@
         in_specs=[blk(STEP_WORDS, wide)]
         + [full(w) for w in (counts, gains, wqkv, wout, wup, wdown, pool, source, segments)]
         + [any_spec] * len(slices),
-        out_specs=[blk(b, w) for _, b, w, _ in outs]
+        out_specs=[blk(b, w) if b else any_spec for _, b, w in outs]
         + [pl.BlockSpec(s, lambda i, n=len(s): (0,) * n) for s, _ in fixed]
         + [any_spec] * len(slices),
-        out_shape=[jax.ShapeDtypeStruct((n, w), d) for n, _, w, d in outs]
+        out_shape=[jax.ShapeDtypeStruct((n, w), BF16) for n, _, w in outs]
         + [jax.ShapeDtypeStruct(s, d) for s, d in fixed]
         + [jax.ShapeDtypeStruct((4, *s.shape), s.dtype) for s in slices],
         scratch_shapes=[
@@ -319,6 +348,9 @@
             pltpu.VMEM((n_dp, cap, 128), BF16), pltpu.VMEM((n_dp, cap, 128), BF16), pltpu.VMEM((4, 8, words), jnp.int32),
             pltpu.SemaphoreType.DMA((n_dp + 3,)), pltpu.SemaphoreType.DMA((n_dp + 3,)),
             pltpu.SemaphoreType.DMA((5 * len(slices),)), pltpu.SemaphoreType.DMA((5 * len(slices),)),
+            pltpu.VMEM((2, step_rows, 3 * width), BF16), pltpu.VMEM((2, step_rows * CHAR_HEADS, 128), BF16),
+            pltpu.VMEM((2, step_rows, 2 * hid), BF16),
+            pltpu.SemaphoreType.DMA((2, 2 + 2 * (hid // HIDDEN_CUT))),
         ],
         compiler_params=pltpu.CompilerParams(collective_id=2, has_side_effects=True, vmem_limit_bytes=VMEM_LIMIT),
         name="char_forward",
@@ -330,7 +362,7 @@
 CHAR_B = 48
 WORD_ROWS = 800
 CHUNK_ROWS = 192
-CHUNKS = ((0, 224), (224, 416), (416, 608), (608, 800))
+CHUNKS = ((0, 192), (192, 224), (224, 416), (416, 608), (608, 800))
 ROW_QKV, ROW_PROJ, ROW_OUT, ROW_UP, ROW_DOWN = 0, 192, 224, 288, 544
 SEMS = 8
 
@@ -472,7 +504,7 @@
         self.ssem, self.rsem, self.lsem = ssem, rsem, lsem
         self.z, self.x, self.y, self.core = coordinates()
         self.chunks = []
-        for i, order in enumerate(("yxz", "yxz", "xyz", "xyz")):
+        for i, order in enumerate(("yxz", "yxz", "yxz", "xyz", "xyz")):
             rows = wbuf.at[:, :, :, CHUNKS[i][0] : CHUNKS[i][1]]
             self.chunks.append(
                 Halving(n_z, None, rows, [None, *got[3 * i : 3 * i + 3]], ssem, rsem, SEMS * i, order)
@@ -481,16 +513,17 @@
         self.parts = []
         for i, (low, high, order) in enumerate(((0, CHAR_CUT, "yxz"), (CHAR_CUT, CHAR_A, "xyz"))):
             rows = abuf.at[:, :, :, :, low:high]
-            at = 12 + 4 * i
+            at = 3 * len(CHUNKS) + 4 * i
             self.parts.append(
-                Halving(n_z, rows.at[1 - core], rows.at[core], got[at : at + 4], ssem, rsem, (4 + i) * SEMS, order)
+                Halving(n_z, rows.at[1 - core], rows.at[core], got[at : at + 4], ssem, rsem, (5 + i) * SEMS, order)
             )
-        self.partb = DirectSum(2 * n_z, *got[20:24], ssem, rsem, 6 * SEMS)
-        self.tiny = 8 * SEMS
+        at = 3 * len(CHUNKS) + 8
+        self.partb = DirectSum(2 * n_z, *got[at : at + 4], ssem, rsem, 7 * SEMS)
+        self.tiny = 9 * SEMS
 
     @staticmethod
     def scratch(n_z):
-        n_sem = 10 * SEMS
+        n_sem = 11 * SEMS
         shapes = [
             pltpu.VMEM((2, 2, 2, n_z, CHAR_A, 128), BF16), pltpu.VMEM((2, 2, n_z, WORD_ROWS, 128), BF16),
             pltpu.VMEM((2, 16, 128), F32), pltpu.VMEM((2 + 2 * n_z, 16, 128), F32),
@@ -512,7 +545,7 @@
             pl.semaphore_signal(barrier, inc=1, device_id=peer, device_id_type=MESH)
         pl.semaphore_wait(barrier, len(peers))
         load.wait()
-        for i, phase in enumerate((1, 2, 2, 2)):
+        for i, phase in enumerate((3, 1, 1, 1, 2)):
             self.chunks[i].start(phase)
 
     def pack_a(self, gup_ref, gdown_ref, gout_ref):
@@ -578,7 +611,7 @@
 
 
 def finish_body(
-    dx_ref, wide_ref, parta_ref, partb_ref, word_ref, small_ref,
+    dx_ref, wide_ref, sums_ref,
     odx_ref, owide_ref, oqkv_ref, oout_ref, oup_ref, odown_ref, oproj_ref, owqkv_ref, owout_ref, owup_ref, owdown_ref,
     ocgain_ref, opool_ref, owgain_ref,
 ):
@@ -586,21 +619,23 @@
 
     @pl.when(pl.program_id(0) == 0)
     def _():
-        parta, partb, word, total = parta_ref[...], partb_ref[...], word_ref[...], small_ref[...]
+        base = WORD_ROWS
         owide_ref[...] = wide_ref[...]
-        oqkv_ref[:, 0:128] = partb[0:32]
-        oqkv_ref[:, 128:192] = unfold_half(partb[32:48])
-        oout_ref[...] = unfold_half(parta[128:144])
-        oup_ref[:, 0:128] = parta[0:32]
-        oup_ref[:, 128:256] = parta[32:64]
-        odown_ref[...] = unfold_half(parta[64:128]).T
-        oproj_ref[...] = word[ROW_PROJ : ROW_PROJ + 32]
         for t in range(3):
-            owqkv_ref[t] = word[64 * t : 64 * t + 64]
-        owout_ref[...] = word[ROW_OUT : ROW_OUT + 64]
+            owqkv_ref[t] = sums_ref[64 * t : 64 * t + 64, :]
+        oproj_ref[...] = sums_ref[ROW_PROJ : ROW_PROJ + 32, :]
+        owout_ref[...] = sums_ref[ROW_OUT : ROW_OUT + 64, :]
         for t in range(4):
-            owup_ref[:, 128 * t : 128 * t + 128] = word[ROW_UP + 64 * t : ROW_UP + 64 * t + 64]
-            owdown_ref[:, 128 * t : 128 * t + 128] = word[ROW_DOWN + 64 * t : ROW_DOWN + 64 * t + 64]
+            owup_ref[:, 128 * t : 128 * t + 128] = sums_ref[ROW_UP + 64 * t : ROW_UP + 64 * t + 64, :]
+            owdown_ref[:, 128 * t : 128 * t + 128] = sums_ref[ROW_DOWN + 64 * t : ROW_DOWN + 64 * t + 64, :]
+        oup_ref[:, 0:128] = sums_ref[base : base + 32, :]
+        oup_ref[:, 128:256] = sums_ref[base + 32 : base + 64, :]
+        odown_ref[...] = unfold_half(sums_ref[base + 64 : base + 128, :]).T
+        oout_ref[...] = unfold_half(sums_ref[base + 128 : base + 144, :])
+        base = WORD_ROWS + CHAR_A
+        oqkv_ref[:, 0:128] = sums_ref[base : base + 32, :]
+        oqkv_ref[:, 128:192] = unfold_half(sums_ref[base + 32 : base + 48, :])
+        total = sums_ref[base + CHAR_B : base + CHAR_B + 16, :]
         for j in range(2):
             for t in range(2):
                 ocgain_ref[j : j + 1, 128 * t : 128 * t + 128] = total[2 * j + t : 2 * j + t + 1]
@@ -610,11 +645,11 @@
             opool_ref[:, 128 * t : 128 * t + 128] = total[4 + t : 5 + t]
 
 
-def finish(d_chars, word_out, *sums):
+def finish(d_chars, word_out, sums):
     words, wide = d_chars.shape
-    steps = words // STEP_WORDS
+    steps = 2
     full = lambda s: pl.BlockSpec(s, lambda i: (0,) * len(s))
-    blk = pl.BlockSpec((STEP_WORDS, wide), lambda i: (i, 0))
+    blk = pl.BlockSpec((words // steps, wide), lambda i: (i, 0))
     outs = [
         word_out.shape, (32, 192), (32, 64), (32, 256), (64, 128), (32, 128),
         (3, 64, 128), (64, 128), (64, 512), (64, 512), (2, 256), (1, 256), (2, 512),
@@ -622,34 +657,35 @@
     result = pl.pallas_call(
         finish_body,
         grid=(steps,),
-        in_specs=[blk, full(word_out.shape)] + [full(s.shape) for s in sums],
+        in_specs=[blk, full(word_out.shape), full(sums.shape)],
         out_specs=[blk] + [full(s) for s in outs],
         out_shape=[jax.ShapeDtypeStruct((words, wide), F32), jax.ShapeDtypeStruct(outs[0], BF16)]
         + [jax.ShapeDtypeStruct(s, F32) for s in outs[1:]],
         compiler_params=pltpu.CompilerParams(vmem_limit_bytes=VMEM_LIMIT),
         name="finish",
-    )(d_chars, word_out, *sums)
+    )(d_chars, word_out, sums)
     dx, out, qkv, cout, up, down, proj, wqkv, wout, wup, wdown, cgain, pool, wgain = result
     return (out, dx, qkv, cout, up, down.T, proj, wqkv, wout.T, wup, wdown.T, cgain, pool.reshape(-1), wgain)
 
 
 def char_bwd_body(
     n_dp, fused,
-    dpool_ref, gains_ref, wqkv_ref, wout_ref, wup_ref, wdown_ref, pool_ref,
-    n1_ref, p_ref, a_ref, o_ref, n2_ref, rs1_ref, rs2_ref, act_ref, dg_ref, f_ref, aw_ref,
+    dpool_ref, gains_ref, pool_ref, wqkv_any, wout_any, wup_any, wdown_any,
+    early_ref, late_ref, p_ref, a_ref, act_ref,
     *refs,
 ):
     if fused:
-        word_sum, wgain_ref, dx_ref, outa_ref, outb_ref, word_ref, small_ref, *refs = refs
+        word_sum, wgain_ref, dx_ref, sums_ref, *refs = refs
     else:
         dx_ref, *refs = refs
         outs, refs = refs[:6], refs[6:]
     gqkv_ref, gout_ref, gup_ref, gdown_ref, ggain_ref, gpool_ref, *refs = refs
-    dm_ref, dp_ref, do_ref, ds_ref, *refs = refs
+    dm_ref, dp_ref, do_ref, ds_ref, wqkv_ref, wout_ref, wup_ref, wdown_ref, dp_now, do_now, wsem, *refs = refs
     step = pl.program_id(0)
     part = pl.num_programs(0) // 3
     words = dpool_ref.shape[0]
-    width = n1_ref.shape[1]
+    width = wout_ref.shape[0]
+    hid = wup_ref.shape[1]
     blocks = words // 8
     rows = words * CHARS
     size = CHAR_HEADS * 128
@@ -664,8 +700,14 @@
 
     @pl.when(step == 0)
     def _():
+        pairs = ((wdown_any, wdown_ref), (wup_any, wup_ref), (wout_any, wout_ref), (wqkv_any, wqkv_ref))
+        loads = [pltpu.make_async_copy(src, dst, wsem.at[i]) for i, (src, dst) in enumerate(pairs)]
+        for load in loads:
+            load.start()
         if fused:
             sums.begin()
+        for load in loads:
+            load.wait()
         for ref in (gqkv_ref, gout_ref, gup_ref, gdown_ref, ggain_ref, gpool_ref):
             ref[...] = jnp.zeros_like(ref)
 
@@ -680,38 +722,40 @@
 
     if fused:
         first, other = sums.parts
-        event(2, (chunks[1], 2))
-        event(4, (chunks[2], 2), (chunks[3], 2), (chunks[0], 1))
+        event(2, (chunks[1], 1), (chunks[3], 1))
+        event(3, (chunks[2], 1), (chunks[4], 2))
+        event(4, (chunks[1], 2), (chunks[3], 2))
         event(5, (first, 0), (other, 0))
-        event(6, (chunks[0], 2))
+        event(6, (chunks[2], 2))
         event(8, (first, 1), (other, 1))
         event(11, (first, 2), (other, 2))
 
     @pl.when(step < part)
     def _():
         dpool = dpool_ref[...].astype(F32).reshape(blocks, 1, 8, width)
-        f = f_ref[...].astype(F32).reshape(blocks, CHARS, 8, width)
-        aw = aw_ref[...].reshape(blocks, CHARS, 8, 1)
+        f = early_ref[:, 2 * width : 3 * width].astype(F32).reshape(blocks, CHARS, 8, width)
+        stat = early_ref[:, 3 * width :].astype(F32)
+        aw = stat[:, 1:2].reshape(blocks, CHARS, 8, 1)
         g = jnp.sum(f * dpool, -1, keepdims=True)
         dt = aw * (g - jnp.sum(aw * g, 1, keepdims=True))
         gpool_ref[...] += jnp.sum((dt * f).reshape(rows // 8, 8, width), 0)
         df = (aw * dpool + dt * pool_ref[...].astype(F32).reshape(1, width)).reshape(rows, width)
         dfb = df.astype(BF16)
-        n2 = n2_ref[...]
+        n2 = early_ref[:, width : 2 * width]
         dn2 = None
         for j in range(0, wup_ref.shape[1], HIDDEN_CUT):
             cut = slice(j, j + HIDDEN_CUT)
             gdown_ref[cut, :] += dot_tn(act_ref[:, cut], dfb)
-            dh = dg_ref[:, cut] * dot_nt(dfb, wdown_ref[cut, :]).astype(BF16)
+            dh = act_ref[:, hid + j : hid + j + HIDDEN_CUT] * dot_nt(dfb, wdown_ref[cut, :]).astype(BF16)
             gup_ref[:, cut] += dot_tn(n2, dh)
             term = dot_nt(dh, wup_ref[:, cut])
             dn2 = term if dn2 is None else dn2 + term
-        d_norm, dnn = norm_bwd(dn2, n2, rs2_ref[...], gains[1:2])
+        d_norm, dnn = norm_bwd(dn2, n2, stat[:, 0:1], gains[1:2])
         ggain_ref[...] += jnp.sum(dnn.reshape(rows // 8, 8, width), 0)
         dm = df + d_norm
-        dm_ref[here, :] = dm
         dmb = dm.astype(BF16)
-        gout_ref[...] += dot_tn(o_ref[...], dmb)
+        dm_ref[here, :] = dmb
+        gout_ref[...] += dot_tn(early_ref[:, 0:width], dmb)
         do_ref[here, :] = dot_nt(dmb, wout_ref[...]).astype(BF16)
 
     at(part - 1, lambda: sums.pack_a(gup_ref, gdown_ref, gout_ref))
@@ -719,12 +763,11 @@
     @pl.when((step >= part) & (step < 2 * part))
     def _():
         scale = (width // CHAR_HEADS) ** -0.5
-        base = lax.rem(step, part) * rows
-        spot = lambda b: pl.ds(pl.multiple_of(base + 128 * b, 128), 128)
+        do_now[...] = do_ref[here, :]
         raw = []
         for b in range(blocks):
             sl = slice(128 * b, 128 * b + 128)
-            raw.append(dot_nt(head_stack(p_ref[sl, 2 * width : 3 * width], CHAR_HEADS, 1.0), do_ref[spot(b), :]))
+            raw.append(dot_nt(head_stack(p_ref[sl, 2 * width : 3 * width], CHAR_HEADS, 1.0), do_now[128 * b : 128 * b + 128, :]))
         for b in range(blocks):
             a = a_ref[size * b : size * b + size, :].astype(F32).reshape(CHAR_HEADS, CHARS, 8, 128)
             dpt = raw[b].reshape(CHAR_HEADS, CHARS, 8, 128)
@@ -734,19 +777,21 @@
             sl = slice(128 * b, 128 * b + 128)
             ds = ds_ref[size * b : size * b + size, :]
             k = head_stack(p_ref[sl, width : 2 * width], CHAR_HEADS, scale)
-            dp_ref[spot(b), 0:width] = dot_tn(ds, k).astype(BF16)
+            dp_now[128 * b : 128 * b + 128, 0:width] = dot_tn(ds, k).astype(BF16)
         for b in range(blocks):
             sl = slice(128 * b, 128 * b + 128)
             cut = lambda h: ds_ref[size * b + 128 * h : size * b + 128 * h + 128, :]
             wide = jnp.concatenate([cut(h) for h in range(CHAR_HEADS)], 1)
             q = head_stack(p_ref[sl, 0:width], CHAR_HEADS, scale)
-            dp_ref[spot(b), width : 2 * width] = dot_nn(wide, q).astype(BF16)
+            dp_now[128 * b : 128 * b + 128, width : 2 * width] = dot_nn(wide, q).astype(BF16)
         for b in range(blocks):
             cut = lambda h: a_ref[size * b + 128 * h : size * b + 128 * h + 128, :]
             wide = jnp.concatenate([cut(h) for h in range(CHAR_HEADS)], 1)
-            do = head_stack(do_ref[spot(b), :], CHAR_HEADS, 1.0)
-            dp_ref[spot(b), 2 * width : 3 * width] = dot_nn(wide, do).astype(BF16)
-        gqkv_ref[...] += dot_tn(n1_ref[...], dp_ref[here, :])
+            do = head_stack(do_now[128 * b : 128 * b + 128, :], CHAR_HEADS, 1.0)
+            dp_now[128 * b : 128 * b + 128, 2 * width : 3 * width] = dot_nn(wide, do).astype(BF16)
+        dp = dp_now[...]
+        dp_ref[here, :] = dp
+        gqkv_ref[...] += dot_tn(late_ref[:, 0:width], dp)
 
     def begin_b():
         sums.pack_b(gqkv_ref)
@@ -757,8 +802,9 @@
     @pl.when(step >= 2 * part)
     def _():
         dn1 = dot_nt(dp_ref[here, :], wqkv_ref[...])
-        d_norm, _ = norm_bwd(dn1, n1_ref[...], rs1_ref[...], gains[0:1])
-        dx = dm_ref[here, :] + d_norm
+        rstd = late_ref[:, width:].astype(F32)[:, 0:1]
+        d_norm, _ = norm_bwd(dn1, late_ref[:, 0:width], rstd, gains[0:1])
+        dx = dm_ref[here, :].astype(F32) + d_norm
         for b in range(0, blocks, 2):
             for c in range(CHARS):
                 pair = [dx[128 * i + 8 * c : 128 * i + 8 * c + 8] for i in (b, b + 1)]
@@ -768,14 +814,16 @@
         sums.partb.advance()
         sums.small[1] = sums.tiny_finish(0)
         sums.tiny_start(1)
-        for i in range(4):
+        for i, (low, high) in enumerate(CHUNKS):
             chunks[i].finish(3)
-            word_ref[CHUNKS[i][0] : CHUNKS[i][1], :] = chunks[i].total()
+            sums_ref[low:high, :] = chunks[i].total()
+        base = WORD_ROWS
         for i, (low, high) in enumerate(((0, CHAR_CUT), (CHAR_CUT, CHAR_A))):
             sums.parts[i].finish(3)
-            outa_ref[low:high, :] = sums.parts[i].total()
-        small_ref[...] = sums.tiny_finish(1)
-        outb_ref[...] = sums.partb.total()
+            sums_ref[base + low : base + high, :] = sums.parts[i].total()
+        base += CHAR_A
+        sums_ref[base + CHAR_B : base + CHAR_B + 16, :] = sums.tiny_finish(1)
+        sums_ref[base : base + CHAR_B, :] = sums.partb.total()
     at(3 * part - 1, end)
 
     if not fused:
@@ -798,19 +846,19 @@
     second = lambda n, w: pl.BlockSpec((n, w), lambda i: (lax.clamp(0, i - steps, steps - 1), 0))
     third = lambda n, w: pl.BlockSpec((n, w), lambda i: (lax.max(i - 2 * steps, 0), 0))
     twice = lambda n, w: pl.BlockSpec((n, w), lambda i: (lax.rem(lax.max(i - steps, 0), steps), 0))
-    weights = (gains, wqkv, wout, wup, wdown, pool)
-    when = [twice, second, second, first, first, third, first, first, first, first, first]
     grads = [wqkv.shape, wout.shape, wup.shape, wdown.shape, (8, width), (8, width)]
     scratch = [pltpu.VMEM(s, F32) for s in grads] + [
-        pltpu.VMEM((rows, width), F32), pltpu.VMEM((rows, 3 * width), BF16), pltpu.VMEM((rows, width), BF16),
-        pltpu.VMEM((step_rows * CHAR_HEADS, 128), BF16),
+        pltpu.VMEM((rows, width), BF16), pltpu.VMEM((rows, 3 * width), BF16), pltpu.VMEM((rows, width), BF16),
+        pltpu.VMEM((step_rows * CHAR_HEADS, 128), BF16), *[pltpu.VMEM(w.shape, BF16) for w in (wqkv, wout, wup, wdown)],
+        pltpu.VMEM((step_rows, 3 * width), BF16), pltpu.VMEM((step_rows, width), BF16), pltpu.SemaphoreType.DMA((4,)),
     ]
-    args = [dpool, *weights, *kept]
-    in_specs = [first(STEP_WORDS, width)] + [full(w) for w in weights]
-    in_specs += [f(r.shape[0] // steps, r.shape[1]) for f, r in zip(when, kept)]
+    any_spec = pl.BlockSpec(memory_space=pl.ANY)
+    args = [dpool, gains, pool, wqkv, wout, wup, wdown, *kept]
+    in_specs = [first(STEP_WORDS, width), full(gains), full(pool)] + [any_spec] * 4
+    in_specs += [f(r.shape[0] // steps, r.shape[1]) for f, r in zip((first, twice, second, second, first), kept)]
     params = dict(vmem_limit_bytes=VMEM_LIMIT)
     if fused:
-        outs = [(CHAR_A, 128), (CHAR_B, 128), (WORD_ROWS, 128), (16, 128)]
+        outs = [(WORD_ROWS + CHAR_A + CHAR_B + 16, 128)]
         args += [word_sum, wgain]
         in_specs += [pl.BlockSpec(memory_space=pl.ANY), full(wgain)]
         scratch += GradientSums.scratch(n_dp // 2)
@@ -835,12 +883,12 @@
 ):
     slices, wholes, refs = refs[:4], refs[4:8], refs[8:]
     if packed:
-        out_ref, dpool_ref, gsum_ref, ggain_ref, gbuf_ref, got_a, got_x, got_y, *refs = refs
+        out_ref, dpool_ref, gsum_ref, ggain_ref, gbuf_ref, got_a, got_x, gq_ref, got_q, *refs = refs
     else:
         out_ref, dpool_ref, gqkv_ref, gout_ref, gup_ref, gdown_ref, gproj_ref, ggain_ref, *refs = refs
     (
-        wqkv_ref, wout_ref, wup_ref, wdown_ref, vec_send, vec_got, segc_all, pooled_rows, rows_ref, normed, rstd_a,
-        qkv_send, qkv_all, weights, o_send, o_all, act_ref, dh_ref, dact_ref, dm_ref,
+        wqkv_ref, wout_ref, wup_ref, wdown_ref, vec_send, vec_got, segc_all, pooled_rows, rows_ref, normed_all, rstd_a,
+        qkv_all, weights, o_send, o_all, act_ref, dh_ref, dact_ref, dm_ref,
         do_send, do_all, dk_acc, dv_acc, dqkv_send, dqkv_all, back_send, ret,
         ssem, rsem, lsem,
     ) = refs
@@ -903,22 +951,21 @@
         load.wait()
     for copy in vec_copies:
         copy.wait()
-    pooled_rows[...] = dot_tn(place[...], vec_got[...].reshape(slots, narrow)).astype(BF16)
-    rows = dot_nn(pooled_rows[...], wproj_ref[...]).astype(BF16).astype(F32)
-    rows_ref[...] = rows
-    n_w, rstd = norm_fwd(rows, gains[0:1])
-    normed[0] = n_w
-    rstd_a[0] = rstd
-    qkv_copies = []
-    for mate in reversed(mates):
-        qkv_send[mate] = dot_nn(n_w, wqkv_ref[mate]).astype(BF16)
-        qkv_copies.append(send(qkv_send.at[mate], qkv_all.at[mp], (dp, mate)))
-    qkv_all[mp] = dot_nn(n_w, wqkv_ref[mp]).astype(BF16)
+    pooled_rows[mp] = dot_tn(place[...], vec_got[...].reshape(slots, narrow)).astype(BF16)
+    row_copies = [send(pooled_rows.at[mp], pooled_rows.at[mp], (dp, mate)) for mate in reversed(mates)]
+    for turn, at in enumerate([mp, *mates]):
+        if turn > 0:
+            row_copies[3 - turn].wait()
+        rows = dot_nn(pooled_rows[at], wproj_ref[...]).astype(BF16).astype(F32)
+        n_w, rstd = norm_fwd(rows, gains[0:1])
+        normed_all[at] = n_w
+        if turn == 0:
+            rows_ref[...] = rows
+            rstd_a[...] = rstd
+        qkv_all[at] = dot_nn(n_w, wqkv_ref[mp]).astype(BF16)
     down_side.wait()
     source = WeightGather.half(wdown_ref.at[mates[1]], 0, 1 - x)
     down_late = send(source, source, (dp, mates[0]))
-    for copy in qkv_copies:
-        copy.wait()
 
     low_lane = lax.broadcasted_iota(jnp.int32, (1, pair), 1) < pair // 2
     low_mask = jnp.where(low_lane, 1.0, 0.0).astype(BF16)
@@ -956,7 +1003,6 @@
     attended = jnp.concatenate([o_all[p] for p in range(n_mp)], 1)
     mid = rows_ref[...] + dot_nn(attended, wout_ref[...].reshape(width, width))
     n_w2, rstd2 = norm_fwd(mid, gains[1:2])
-    normed[1] = n_w2
     out = mid
     dn2 = jnp.zeros((words, width), F32)
     for p in range(n_mp):
@@ -994,23 +1040,13 @@
 
     def x_sum(i):
         low, high = CHUNKS[i]
-        return send(gsum_ref.at[:, 1 - x, :, low:high], got_x.at[i - 2], device_of(z, 1 - x, y, core))
+        return send(gsum_ref.at[:, 1 - x, :, low:high], got_x, device_of(z, 1 - x, y, core))
 
     def x_add(i):
         low, high = CHUNKS[i]
         for b in range(2):
             for d in range(n_dp // 2):
-                gsum_ref[b, x, d, low:high] += got_x[i - 2, b, d]
-
-    def y_sum(i):
-        low, high = CHUNKS[i]
-        return send(gsum_ref.at[1 - y, :, :, low:high], got_y, device_of(z, x, 1 - y, core))
-
-    def y_add(i):
-        low, high = CHUNKS[i]
-        for c in range(2):
-            for d in range(n_dp // 2):
-                gsum_ref[y, c, d, low:high] += got_y[c, d]
+                gsum_ref[b, x, d, low:high] += got_x[b, d]
 
     def put(base, p, grad):
         if packed:
@@ -1023,24 +1059,24 @@
         elif base == ROW_PROJ:
             gproj_ref[:, 128 * p : 128 * p + 128] = grad
         else:
-            ref = {ROW_QKV: gqkv_ref, ROW_OUT: gout_ref, ROW_UP: gup_ref, ROW_DOWN: gdown_ref}[base]
+            ref = {ROW_OUT: gout_ref, ROW_UP: gup_ref, ROW_DOWN: gdown_ref}[base]
             ref[p] = grad
 
     for p in range(n_mp):
         put(ROW_DOWN, p, dot_tn(cot, act_ref[p]))
     if packed:
-        pair_three = pair_sum(3)
+        pair_three = pair_sum(4)
     for p in range(n_mp):
         put(ROW_UP, p, dot_tn(n_w2, dh_ref[p]))
     if packed:
-        pair_two = pair_sum(2)
+        pair_two = pair_sum(3)
     for p in range(n_mp):
         put(ROW_OUT, p, dot_tn(d_att, o_all[p]))
     if packed:
-        pair_one = pair_sum(1)
+        pair_one = pair_sum(2)
         pair_three.wait()
-        pair_add(3)
-        x_three = x_sum(3)
+        pair_add(4)
+        x_three = x_sum(4)
     dk_acc[...] = jnp.zeros_like(dk_acc)
     dv_acc[...] = jnp.zeros_like(dv_acc)
     for copy in do_copies:
@@ -1062,25 +1098,31 @@
         dqkv_send[i, :, 0:pair] = dq.astype(BF16)
         dqkv_send[i, :, pair : 2 * pair] = dk_acc[words * i : keys, :].astype(BF16)
         dqkv_send[i, :, 2 * pair : 3 * pair] = dv_acc[words * i : keys, :].astype(BF16)
-    if packed:
-        pair_two.wait()
-        pair_add(2)
-        x_two = x_sum(2)
     dqkv_copies = []
     for mate in reversed(mates):
         dqkv_copies.append(send(dqkv_send.at[mate], dqkv_all.at[mp], (dp, mate)))
     dqkv_all[mp] = dqkv_send[mp]
+    grad_qkv = dot_tn(normed_all[...].reshape(n_mp * words, width), dqkv_send[...].reshape(n_mp * words, 3 * pair))
     if packed:
+        block = width // n_dp
+        for d in range(n_dp):
+            for t in range(3):
+                gq_ref[d % 2, d // 2, block * t : block * t + block, :] = (
+                    grad_qkv[block * d : block * d + block, 128 * t : 128 * t + 128].astype(BF16)
+                )
+        q_sum = send(gq_ref.at[1 - x], got_q, device_of(z, 1 - x, y, core))
+        pair_two.wait()
+        pair_add(3)
         pair_one.wait()
-        pair_add(1)
+        pair_add(2)
+    else:
+        gqkv_ref[...] = grad_qkv
     for copy in dqkv_copies:
         copy.wait()
-    if packed:
-        y_one = y_sum(1)
     d_normed = jnp.zeros((words, width), F32)
     for p in range(n_mp):
         d_normed = d_normed + dot_nt(dqkv_all[p], wqkv_ref[p])
-    d_first, dnn = norm_bwd(d_normed, normed[0], rstd_a[0], gains[0:1])
+    d_first, dnn = norm_bwd(d_normed, normed_all[mp], rstd_a[...], gains[0:1])
     gain_a = jnp.sum(dnn, 0, keepdims=True) / gains[0:1]
     d_rows = (dm_ref[...] + d_first).astype(BF16)
     ggain_ref[0:1, :] = gain_a
@@ -1089,24 +1131,21 @@
     back_send[...] = dot_nn(place[...], d_pooled).astype(BF16).reshape(n_dp, cap, narrow)
     back_copies = [send(back_send.at[k], ret.at[k], from_dp[k]) for k in range(1, n_dp)]
     ret[0] = back_send[0]
-    grad_proj = dot_tn(pooled_rows[...], d_rows)
+    grad_proj = dot_tn(pooled_rows[mp], d_rows)
     for p in range(n_mp):
-        put(ROW_QKV, p, dot_tn(normed[0], dqkv_all[p]))
         put(ROW_PROJ, p, grad_proj[:, 128 * p : 128 * p + 128])
     if packed:
-        pair_zero = pair_sum(0)
+        pair_zero = pair_sum(1)
+        q_sum.wait()
+        low, high = CHUNKS[0]
+        gsum_ref[y, x, :, low:high] = gq_ref[x] + got_q[...]
         x_three.wait()
-        x_add(3)
-        x_two.wait()
-        x_add(2)
+        x_add(4)
         pair_zero.wait()
-        pair_add(0)
+        pair_add(1)
     for copy in back_copies:
         copy.wait()
     dpool_ref[...] = dot_tn(onehot[...], ret[...].reshape(slots, narrow)).astype(BF16)
-    if packed:
-        y_one.wait()
-        y_add(1)
 
 
 def word_layer(n_dp, pooled, onehot, place, segments, cotangent, gains, wproj, slices, wholes):
@@ -1122,18 +1161,19 @@
     if packed:
         outs.append(((2, 2, n_dp // 2, WORD_ROWS, 128), BF16))
     else:
-        outs += [((n_mp, width, n), F32) for n in (3 * pair, pair, wup.shape[2], wup.shape[2])]
+        outs.append(((width, 3 * pair), F32))
+        outs += [((n_mp, width, n), F32) for n in (pair, wup.shape[2], wup.shape[2])]
         outs.append(((narrow, width), F32))
     outs.append(((2, width), F32))
     hid = wup.shape[2]
-    n_sem = 2 * (n_dp - 1) + 4 * 3 + 3 + 7
+    n_sem = 2 * (n_dp - 1) + 4 * 3 + 3 + 6
     vm = pl.BlockSpec(memory_space=pltpu.VMEM)
     args = (pooled, onehot, place, segments, cotangent, gains, wproj, *slices, *wholes)
     shapes = [
         ((n_mp, width, 3 * pair), BF16), (wout.shape, BF16), (wup.shape, BF16), (wdown.shape, BF16),
-        ((n_dp, cap, narrow), BF16), ((n_dp, cap, narrow), BF16), ((n_mp * words, 128), F32), ((words, narrow), BF16),
-        ((words, width), F32), ((2, words, width), BF16), ((1, words, 1), F32),
-        ((n_mp, words, 3 * pair), BF16), ((n_mp, words, 3 * pair), BF16), ((n_mp, n_mp * words, 2 * words), BF16),
+        ((n_dp, cap, narrow), BF16), ((n_dp, cap, narrow), BF16), ((n_mp * words, 128), F32), ((n_mp, words, narrow), BF16),
+        ((words, width), F32), ((n_mp, words, width), BF16), ((words, 1), F32),
+        ((n_mp, words, 3 * pair), BF16), ((n_mp, n_mp * words, 2 * words), BF16),
         ((n_mp, words, pair), BF16), ((n_mp, words, pair), BF16),
         ((n_mp, words, hid), BF16), ((n_mp, words, hid), BF16), ((n_mp, words, hid), BF16), ((words, width), F32),
         ((n_mp, words, pair), BF16), ((n_mp, words, pair), BF16), ((n_mp * words, pair), F32), ((n_mp * words, pair), F32),
@@ -1142,7 +1182,8 @@
     if packed:
         shapes = [
             ((2, 2, 2, n_dp // 2, WORD_ROWS, 128), BF16), ((2, 2, n_dp // 2, WORD_ROWS, 128), BF16),
-            ((2, 2, n_dp // 2, CHUNK_ROWS, 128), BF16), ((2, n_dp // 2, CHUNK_ROWS, 128), BF16), *shapes,
+            ((2, n_dp // 2, CHUNK_ROWS, 128), BF16),
+            ((2, n_dp // 2, CHUNK_ROWS, 128), BF16), ((n_dp // 2, CHUNK_ROWS, 128), BF16), *shapes,
         ]
     return pl.pallas_call(
         functools.partial(word_body, n_dp, cap, packed),
@@ -1165,11 +1206,13 @@
         part = lax.psum_scatter(grad, "dp", scatter_dimension=0, tiled=True)
         part = lax.psum_scatter(part.astype(BF16), "mp", scatter_dimension=1, tiled=True)
         mats.append(part.astype(F32))
+    qkv, *rest = word_parts
     words = []
-    for grad in word_parts:
+    for grad in rest:
         part = lax.psum_scatter(grad, "dp", scatter_dimension=1, tiled=True)
         words.append(lax.psum_scatter(part, "mp", scatter_dimension=0, tiled=False))
-    qkv, out, up, down = words
+    out, up, down = words
+    qkv = lax.psum_scatter(qkv, "dp", scatter_dimension=0, tiled=True)
     qkv = jnp.transpose(qkv.reshape(qkv.shape[0], 3, -1), (1, 0, 2))
     return (*mats, qkv, out.T, up, down.T, *small)
 
@@ -1200,7 +1243,7 @@
         groups, char_input, char_counts.reshape(1, -1), *char_weights,
         word_source.reshape(1, -1), segment_ids.reshape(1, -1), slices,
     )
-    char_kept, (onehot, place, segments, *word_weights) = kept[:11], kept[11:]
+    char_kept, (onehot, place, segments, *word_weights) = kept[:5], kept[5:]
     output, d_pooled, *word_parts, word_gains = word_layer(
         groups, pooled, onehot, place, segments, cotangent, word_norm_gains, char_proj, slices, word_weights
     )
@@ -1209,7 +1252,7 @@
         groups, d_pooled, char_kept, *char_weights, word_parts[0] if fused else None, word_gains
     )
     if fused:
-        return finish(d_chars, output, *char_parts)
+        return finish(d_chars, output, char_parts[0])
     *word_parts, grad_proj = word_parts
     char_parts = (*char_parts[:4], grad_proj, *char_parts[4:])
     *mats, grad_char_gains, grad_pool, grad_word_gains = plain_reduce(

time: 157 us -> 150 us (0.955)
  Pallas kernels: 156 us -> 149 us
    pallas_call x1, Pallas kernels: 61.8 us -> 58.4 us  [word_layer(): pl.pallas_call(functools.partial(word_body, n_dp, cap, packed), in_specs=...]
    pallas_call x1, Pallas kernels: 35.1 us -> 33 us  [char_forward(): pl.pallas_call(functools.partial(char_fwd_body, n_dp, cap), grid=(words /...]
where the time goes in v6:
time: 150 us
  Pallas kernels  149 us (99%)
    pallas_call x1, Pallas kernels, word_layer(): pl.pallas_call(functools.partial(word_body, n_dp, cap, packed), in_specs=...  58.4 us
    pallas_call x1, Pallas kernels, char_backward(): pl.pallas_call(functools.partial(char_bwd_body, n_dp, fused), grid=(3 * s...  53.9 us
    pallas_call x1, Pallas kernels, char_forward(): pl.pallas_call(functools.partial(char_fwd_body, n_dp, cap), grid=(words /...  33 us
    pallas_call x1, Pallas kernels, finish(): pl.pallas_call(finish_body, grid=(steps,), in_specs=[blk, full(word_out.s...  3.98 us

profile of v6, /device:TPU:0, one launch (start us, length us, event | category | flops | bytes accessed | tf_op | source)
XLA Modules:
  0.0 150.1 jit_solution(13912955462823463088)
XLA Ops:
  0.6 33.0 %char_forward.1 = (bf16[256,256]{1,0:T(8,128)(2,1)}, bf16[4096,896]{1,0:T(8,128)(2,1)}, bf16[4096,384]{1,0:T(8,128)(2,1)}, bf16[4096,768]{1,0:T(8,128)(2,1)}, bf...) custom-call(bf16[256,4096]{1,0:T(8,128)(2,1)} %x_ref.1, ...), custom_call_target="tpu_custom_call" | custom-call | tf_op jit(solution)/shard_map/char_forward/pallas_call | solution.py:334
  33.7 58.4 %word_layer.1 = (bf16[256,512]{1,0:T(8,128)(2,1)}, bf16[256,256]{1,0:T(8,128)(2,1)}, bf16[2,2,4,800,128]{4,3,2,1,0:T(8,128)(2,1)}, f32[2,512]{1,0:T(2,128)}) custom-call(bf16[256,256]{1,0:T(8,128)(2,1)} %get-tuple-element.47.pooled_ref, bf16[512,256]{1,0:T(8,128)(2,1)} %get-tuple-element.48.onehot, bf16[512,256]{1,0:T(8,128)(2,1)} %get-tuple-element.49.place, ...), custom_call_target="tpu_custom_call" | custom-call | tf_op jit(solution)/shard_map/word_layer/pallas_call | solution.py:1188
  92.1 53.9 %char_backward.1 = (bf16[256,4096]{1,0:T(8,128)(2,1)}, f32[1008,128]{1,0:T(8,128)}) custom-call(bf16[256,256]{1,0:T(8,128)(2,1)} %get-tuple-element.55.dpool_ref, bf16[2,256]{1,0:T(2,128)(2,1)} %gains_ref.5, bf16[256]{0:T(256)(128)(2,1)} %pool_ref.3, bf16[256,768]{1,0:T(8,128)(2,1)} %wqkv_any.1, bf16[256,256]{1,0:T(8,128)(2,1)} %wout_any.1, ...), custom_call_target="tpu_custom_call" | custom-call | tf_op jit(solution)/shard_map/char_backward/pallas_call | solution.py:868
  146.0 4.0 %finish.1 = (f32[256,4096]{1,0:T(8,128)}, bf16[256,512]{1,0:T(8,128)(2,1)}, f32[32,192]{1,0:T(8,128)}, f32[32,64]{1,0:T(8,128)}, f32[32,256]{1,0:T(8,128)}, /*in...) custom-call(bf16[256,4096]{1,0:T(8,128)(2,1)} %get-tuple-element.63., ...), custom_call_target="tpu_custom_call" | custom-call | tf_op jit(solution)/shard_map/finish/pallas_call | solution.py:657

commit v7 on v6

--- a/solution.py
+++ b/solution.py
@@ -87,8 +87,8 @@
 
 
 class WeightGather:
-    def __init__(self, slices, wholes, ssem, rsem):
-        self.slices, self.wholes, self.ssem, self.rsem = slices, wholes, ssem, rsem
+    def __init__(self, slices, wholes, split, ssem, rsem):
+        self.slices, self.wholes, self.split, self.ssem, self.rsem = slices, wholes, split, ssem, rsem
         self.z, self.x, self.y, self.core = coordinates()
         self.mp = self.y * 2 + self.core
         self.across = (1 - self.y) * 2 + self.core
@@ -104,13 +104,15 @@
         axis = len(piece.shape) - 2
         far = whole.at[self.across]
         if kind == "far":
-            src, dst = self.half(piece, axis, x), self.half(whole.at[self.mp], axis, x)
+            src, dst = piece, whole.at[self.mp]
+            if self.split[i]:
+                src, dst = self.half(src, axis, x), self.half(dst, axis, x)
             peer = device_of(z, x, 1 - y, core)
         elif kind == "near":
             src, dst, peer = piece, whole.at[self.mp], device_of(z, x, y, 1 - core)
         else:
             which = 1 - x if kind == "late" else x
-            src = dst = self.half(far, axis, which)
+            src = dst = self.half(far, axis, which) if self.split[i] else far
             peer = device_of(z, 1 - x, y, core) if kind == "side" else device_of(z, x, y, 1 - core)
         slot = i * 5 + ("far", "near", "side", "early", "late").index(kind)
         return remote_copy(src, dst, self.ssem, self.rsem, slot, peer)
@@ -120,17 +122,14 @@
         return [device_of(z, x, 1 - y, core), device_of(z, x, y, 1 - core), device_of(z, 1 - x, y, core)]
 
     def begin(self):
-        self.copy(0, "far").start()
-        self.copy(1, "far").start()
+        for i in range(len(self.slices)):
+            self.copy(i, "far").start()
         for i in range(len(self.slices)):
             self.copy(i, "near").start()
 
-    def begin_far(self, i):
-        self.copy(i, "far").start()
-
     def pass_on(self, i):
         self.copy(i, "far").wait()
-        if i < len(self.slices) - 1:
+        if self.split[i]:
             self.copy(i, "side").start()
         self.copy(i, "early").start()
 
@@ -140,21 +139,21 @@
 
     def finish(self):
         for i in range(len(self.slices)):
-            for kind in ("near", "early", "late")[: 3 - (i == len(self.slices) - 1)]:
+            for kind in ("near", "early", "late")[: 2 + self.split[i]]:
                 self.copy(i, kind).wait()
 
 
 def char_fwd_body(
     n_dp, cap,
     x_ref, cnt_ref, gains_ref, wqkv_ref, wout_ref, wup_ref, wdown_ref, pool_ref,
-    src_ref, seg_ref, s_qkv, s_out, s_up, s_down,
+    src_ref, seg_ref, s_qkv, s_out, s_up,
     pooled_ref, early_ref, late_ref, p_any, a_any, act_any,
-    onehot_ref, place_ref, seg_out, g_qkv, g_out, g_up, g_down,
+    onehot_ref, place_ref, seg_out, g_qkv, g_out, g_up,
     cnt_col, row_send, row_got, seg_all, ssem, rsem, wsend, wrecv, p_buf, a_buf, act_buf, osem,
 ):
     step, last = pl.program_id(0), pl.num_programs(0) - 1
     dp, mp = lax.axis_index("dp"), lax.axis_index("mp")
-    gather = WeightGather((s_qkv, s_out, s_up, s_down), (g_qkv, g_out, g_up, g_down), wsend, wrecv)
+    gather = WeightGather((s_qkv, s_out, s_up), (g_qkv, g_out, g_up), (True, True, False), wsend, wrecv)
     mates = [mp // 2 * 2 + (mp + 1) % 2, (mp + 2) % 4, (mp // 2 * 2 + 2) % 4 + (mp + 1) % 2]
     all_words = src_ref.shape[1]
     slots = n_dp * cap
@@ -263,24 +262,15 @@
     n2, rs2 = norm_fwd(m, gains[1:2])
     early_ref[:, width : 2 * width] = n2
 
-    @pl.when(step == 0)
-    def _():
-        gather.begin_far(2)
-
     @pl.when(step == 1)
     def _():
         gather.pass_on(0)
         gather.pass_on(1)
-        gather.begin_far(3)
-
-    @pl.when(step == 2)
+
+
+    @pl.when(step == last)
     def _():
         gather.pass_on(2)
-
-    @pl.when(step == last)
-    def _():
-        gather.pass_last(2)
-        gather.pass_on(3)
 
     f = m
     for i, j in enumerate(cuts):
@@ -727,8 +717,8 @@
         event(4, (chunks[1], 2), (chunks[3], 2))
         event(5, (first, 0), (other, 0))
         event(6, (chunks[2], 2))
-        event(8, (first, 1), (other, 1))
-        event(11, (first, 2), (other, 2))
+        event(7, (first, 1), (other, 1))
+        event(9, (first, 2), (other, 2))
 
     @pl.when(step < part)
     def _():
@@ -881,7 +871,7 @@
     n_dp, cap, packed,
     pooled_ref, onehot, place, seg_all, cot_ref, gains_ref, wproj_ref, *refs,
 ):
-    slices, wholes, refs = refs[:4], refs[4:8], refs[8:]
+    slices, wholes, refs = refs[:4], refs[4:7], refs[7:]
     if packed:
         out_ref, dpool_ref, gsum_ref, ggain_ref, gbuf_ref, got_a, got_x, gq_ref, got_q, *refs = refs
     else:
@@ -890,7 +880,7 @@
         wqkv_ref, wout_ref, wup_ref, wdown_ref, vec_send, vec_got, segc_all, pooled_rows, rows_ref, normed_all, rstd_a,
         qkv_all, weights, o_send, o_all, act_ref, dh_ref, dact_ref, dm_ref,
         do_send, do_all, dk_acc, dv_acc, dqkv_send, dqkv_all, back_send, ret,
-        ssem, rsem, lsem,
+        ssem, rsem, lsem, wsend, wrecv,
     ) = refs
     dp, mp = lax.axis_index("dp"), lax.axis_index("mp")
     n_mp = 4
@@ -923,15 +913,12 @@
     loads = []
     for i, held in ((3, wdown_ref), (0, wqkv_ref), (1, wout_ref), (2, wup_ref)):
         loads.append([])
-        for j, at in enumerate([mp, *mates]):
+        for j, at in enumerate([mp] if i == 3 else [mp, *mates]):
             src = slices[i] if j == 0 else wholes[i].at[at]
             if i == 0:
                 for t in range(3):
                     dst = held.at[at, :, pair * t : pair * t + pair]
                     loads[-1].append(pltpu.make_async_copy(src.at[t], dst, lsem.at[4 + t, j]))
-            elif i == 3 and j > 1:
-                src, dst = WeightGather.half(src, 0, x), WeightGather.half(held.at[at], 0, x)
-                loads[-1].append(pltpu.make_async_copy(src, dst, lsem.at[i, j]))
             else:
                 loads[-1].append(pltpu.make_async_copy(src, held.at[at], lsem.at[i, j]))
         for load in loads[-1]:
@@ -940,8 +927,8 @@
 
     pl.semaphore_wait(barrier, n_dp - 1 + 3)
     vec_copies = [send(vec_send.at[k], vec_got.at[k], to_dp[k]) for k in range(1, n_dp)]
-    source = WeightGather.half(wholes[3].at[mates[1]], 0, x)
-    down_side = send(source, WeightGather.half(wdown_ref.at[mates[1]], 0, x), device_of(z, 1 - x, y, core))
+    down = WeightGather((slices[3],), (wdown_ref,), (True,), wsend, wrecv)
+    down.begin()
     vec_got[0] = vec_send[0]
     gains = gains_ref[...].astype(F32)
     cot = cot_ref[...]
@@ -960,12 +947,11 @@
         n_w, rstd = norm_fwd(rows, gains[0:1])
         normed_all[at] = n_w
         if turn == 0:
+            down.pass_on(0)
             rows_ref[...] = rows
             rstd_a[...] = rstd
         qkv_all[at] = dot_nn(n_w, wqkv_ref[mp]).astype(BF16)
-    down_side.wait()
-    source = WeightGather.half(wdown_ref.at[mates[1]], 0, 1 - x)
-    down_late = send(source, source, (dp, mates[0]))
+    down.pass_last(0)
 
     low_lane = lax.broadcasted_iota(jnp.int32, (1, pair), 1) < pair // 2
     low_mask = jnp.where(low_lane, 1.0, 0.0).astype(BF16)
@@ -993,7 +979,7 @@
     for mate in reversed(mates):
         o_copies.append(send(o_send.at[mate], o_all.at[mp], (dp, mate)))
     o_all[mp] = o_send[mp]
-    down_late.wait()
+    down.finish()
     for load in loads[0]:
         load.wait()
     for p in range(n_mp):
@@ -1151,7 +1137,7 @@
 def word_layer(n_dp, pooled, onehot, place, segments, cotangent, gains, wproj, slices, wholes):
     words, narrow = pooled.shape
     width = cotangent.shape[1]
-    wqkv, wout, wup, wdown = wholes
+    wqkv, wout, wup = wholes
     n_mp = wqkv.shape[0]
     cap = -(-2 * words // n_dp // 16) * 16
     slots = cap * n_dp
@@ -1170,7 +1156,7 @@
     vm = pl.BlockSpec(memory_space=pltpu.VMEM)
     args = (pooled, onehot, place, segments, cotangent, gains, wproj, *slices, *wholes)
     shapes = [
-        ((n_mp, width, 3 * pair), BF16), (wout.shape, BF16), (wup.shape, BF16), (wdown.shape, BF16),
+        ((n_mp, width, 3 * pair), BF16), (wout.shape, BF16), (wup.shape, BF16), ((n_mp, *slices[3].shape), BF16),
         ((n_dp, cap, narrow), BF16), ((n_dp, cap, narrow), BF16), ((n_mp * words, 128), F32), ((n_mp, words, narrow), BF16),
         ((words, width), F32), ((n_mp, words, width), BF16), ((words, 1), F32),
         ((n_mp, words, 3 * pair), BF16), ((n_mp, n_mp * words, 2 * words), BF16),
@@ -1187,11 +1173,11 @@
         ]
     return pl.pallas_call(
         functools.partial(word_body, n_dp, cap, packed),
-        in_specs=[vm] * (len(args) - 8) + [pl.BlockSpec(memory_space=pl.ANY)] * 8,
+        in_specs=[vm] * (len(args) - 7) + [pl.BlockSpec(memory_space=pl.ANY)] * 7,
         out_specs=[vm] * len(outs),
         out_shape=[jax.ShapeDtypeStruct(s, d) for s, d in outs],
         scratch_shapes=[pltpu.VMEM(s, d) for s, d in shapes]
-        + [pltpu.SemaphoreType.DMA((n_sem,)), pltpu.SemaphoreType.DMA((n_sem,)), pltpu.SemaphoreType.DMA((7, 4))],
+        + [pltpu.SemaphoreType.DMA((n_sem,)), pltpu.SemaphoreType.DMA((n_sem,)), pltpu.SemaphoreType.DMA((7, 4)), pltpu.SemaphoreType.DMA((5,)), pltpu.SemaphoreType.DMA((5,))],
         compiler_params=pltpu.CompilerParams(collective_id=0, has_side_effects=True, vmem_limit_bytes=VMEM_LIMIT),
         name="word_layer",
     )(*args)
@@ -1241,7 +1227,7 @@
     slices = (word_qkv, word_out, word_up, word_down)
     pooled, *kept = char_forward(
         groups, char_input, char_counts.reshape(1, -1), *char_weights,
-        word_source.reshape(1, -1), segment_ids.reshape(1, -1), slices,
+        word_source.reshape(1, -1), segment_ids.reshape(1, -1), slices[:3],
     )
     char_kept, (onehot, place, segments, *word_weights) = kept[:5], kept[5:]
     output, d_pooled, *word_parts, word_gains = word_layer(

time: 150 us -> 147 us (0.980)
  Pallas kernels: 149 us -> 146 us
    pallas_call x1, Pallas kernels: 58.4 us -> 56.8 us  [word_layer(): pl.pallas_call(functools.partial(word_body, n_dp, cap, packed), in_specs=...]
where the time goes in v7:
time: 147 us
  Pallas kernels  146 us (99%)
    pallas_call x1, Pallas kernels, word_layer(): pl.pallas_call(functools.partial(word_body, n_dp, cap, packed), in_specs=...  56.8 us
    pallas_call x1, Pallas kernels, char_backward(): pl.pallas_call(functools.partial(char_bwd_body, n_dp, fused), grid=(3 * s...  53 us
    pallas_call x1, Pallas kernels, char_forward(): pl.pallas_call(functools.partial(char_fwd_body, n_dp, cap), grid=(words /...  31.9 us
    pallas_call x1, Pallas kernels, finish(): pl.pallas_call(finish_body, grid=(steps,), in_specs=[blk, full(word_out.s...  3.98 us

profile of v7, /device:TPU:0, one launch (start us, length us, event | category | flops | bytes accessed | tf_op | source)
XLA Modules:
  0.0 146.5 jit_solution(5834760202774195498)
XLA Ops:
  0.6 31.9 %char_forward.1 = (bf16[256,256]{1,0:T(8,128)(2,1)}, bf16[4096,896]{1,0:T(8,128)(2,1)}, bf16[4096,384]{1,0:T(8,128)(2,1)}, bf16[4096,768]{1,0:T(8,128)(2,1)}, bf...) custom-call(bf16[256,4096]{1,0:T(8,128)(2,1)} %x_ref.1, ...), custom_call_target="tpu_custom_call" | custom-call | tf_op jit(solution)/shard_map/char_forward/pallas_call | solution.py:324
  32.6 56.8 %word_layer.1 = (bf16[256,512]{1,0:T(8,128)(2,1)}, bf16[256,256]{1,0:T(8,128)(2,1)}, bf16[2,2,4,800,128]{4,3,2,1,0:T(8,128)(2,1)}, f32[2,512]{1,0:T(2,128)}) custom-call(bf16[256,256]{1,0:T(8,128)(2,1)} %get-tuple-element.46.pooled_ref, bf16[512,256]{1,0:T(8,128)(2,1)} %get-tuple-element.47.onehot, bf16[512,256]{1,0:T(8,128)(2,1)} %get-tuple-element.48.place, ...), custom_call_target="tpu_custom_call" | custom-call | tf_op jit(solution)/shard_map/word_layer/pallas_call | solution.py:1174
  89.3 53.0 %char_backward.1 = (bf16[256,4096]{1,0:T(8,128)(2,1)}, f32[1008,128]{1,0:T(8,128)}) custom-call(bf16[256,256]{1,0:T(8,128)(2,1)} %get-tuple-element.53.dpool_ref, bf16[2,256]{1,0:T(2,128)(2,1)} %gains_ref.5, bf16[256]{0:T(256)(128)(2,1)} %pool_ref.3, bf16[256,768]{1,0:T(8,128)(2,1)} %wqkv_any.1, bf16[256,256]{1,0:T(8,128)(2,1)} %wout_any.1, ...), custom_call_target="tpu_custom_call" | custom-call | tf_op jit(solution)/shard_map/char_backward/pallas_call | solution.py:858
  142.4 4.0 %finish.1 = (f32[256,4096]{1,0:T(8,128)}, bf16[256,512]{1,0:T(8,128)(2,1)}, f32[32,192]{1,0:T(8,128)}, f32[32,64]{1,0:T(8,128)}, f32[32,256]{1,0:T(8,128)}, /*in...) custom-call(bf16[256,4096]{1,0:T(8,128)(2,1)} %get-tuple-element.61., ...), custom_call_target="tpu_custom_call" | custom-call | tf_op jit(solution)/shard_map/finish/pallas_call | solution.py:647

commit v8 on v7

--- a/solution.py
+++ b/solution.py
@@ -880,7 +880,7 @@
         wqkv_ref, wout_ref, wup_ref, wdown_ref, vec_send, vec_got, segc_all, pooled_rows, rows_ref, normed_all, rstd_a,
         qkv_all, weights, o_send, o_all, act_ref, dh_ref, dact_ref, dm_ref,
         do_send, do_all, dk_acc, dv_acc, dqkv_send, dqkv_all, back_send, ret,
-        ssem, rsem, lsem, wsend, wrecv,
+        ssem, rsem, lsem, wsend, wrecv, qsend, qrecv,
     ) = refs
     dp, mp = lax.axis_index("dp"), lax.axis_index("mp")
     n_mp = 4
@@ -1067,26 +1067,59 @@
     dv_acc[...] = jnp.zeros_like(dv_acc)
     for copy in do_copies:
         copy.wait()
-    for i in reversed(range(n_mp)):
-        keys = words * (i + 1)
-        q = qkv_all[i, :, 0:pair]
-        k = qkv_all[0 : i + 1, :, pair : 2 * pair].reshape(keys, pair)
-        v = qkv_all[0 : i + 1, :, 2 * pair : 3 * pair].reshape(keys, pair)
-        do = heads(do_all[i], 1.0)
-        at = weights[i, 0:keys, :]
-        af = at.astype(F32)
-        dpt = dot_nt(v, do)
-        ds = (af * (dpt - jnp.sum(af * dpt, 0, keepdims=True))).astype(BF16)
-        both = dot_tn(ds, k)
-        dq = jnp.where(low_lane, both[:words], both[words:]) * scale
-        dk_acc[0:keys, :] += dot_nn(ds, heads(q, scale))
-        dv_acc[0:keys, :] += dot_nn(at, do)
-        dqkv_send[i, :, 0:pair] = dq.astype(BF16)
-        dqkv_send[i, :, pair : 2 * pair] = dk_acc[words * i : keys, :].astype(BF16)
-        dqkv_send[i, :, 2 * pair : 3 * pair] = dv_acc[words * i : keys, :].astype(BF16)
-    dqkv_copies = []
-    for mate in reversed(mates):
-        dqkv_copies.append(send(dqkv_send.at[mate], dqkv_all.at[mp], (dp, mate)))
+    parts = (slice(0, pair), slice(pair, 3 * pair))
+
+    def dqkv_copy(part, to, slot):
+        cut = parts[part]
+        return pltpu.make_async_remote_copy(
+            src_ref=dqkv_send.at[to, :, cut], dst_ref=dqkv_all.at[mp, :, cut],
+            send_sem=qsend.at[part, slot], recv_sem=qrecv.at[part, slot],
+            device_id=(dp, to), device_id_type=MESH,
+        )
+
+    def dqkv_start(part, i):
+        @pl.when(mp != i)
+        def _():
+            dqkv_copy(part, i, lax.rem(mp + i, 2) + 2 * lax.rem(mp // 2 + i // 2, 2)).start()
+
+    def keep_sums(i):
+        here = slice(words * i, words * i + words)
+        dqkv_send[i, :, pair : 2 * pair] = dk_acc[here, :].astype(BF16)
+        dqkv_send[i, :, 2 * pair : 3 * pair] = dv_acc[here, :].astype(BF16)
+
+    def attention_back(falling):
+        for i in reversed(range(n_mp)) if falling else range(n_mp):
+            keys = words * (i + 1)
+            q = qkv_all[i, :, 0:pair]
+            k = qkv_all[0 : i + 1, :, pair : 2 * pair].reshape(keys, pair)
+            v = qkv_all[0 : i + 1, :, 2 * pair : 3 * pair].reshape(keys, pair)
+            do = heads(do_all[i], 1.0)
+            at = weights[i, 0:keys, :]
+            af = at.astype(F32)
+            dpt = dot_nt(v, do)
+            ds = (af * (dpt - jnp.sum(af * dpt, 0, keepdims=True))).astype(BF16)
+            both = dot_tn(ds, k)
+            dqkv_send[i, :, 0:pair] = (jnp.where(low_lane, both[:words], both[words:]) * scale).astype(BF16)
+            dqkv_start(0, i)
+            dk_acc[0:keys, :] += dot_nn(ds, heads(q, scale))
+            dv_acc[0:keys, :] += dot_nn(at, do)
+            if falling:
+                keep_sums(i)
+                dqkv_start(1, i)
+        if not falling:
+            for i in range(n_mp):
+                keep_sums(i)
+                dqkv_start(1, i)
+
+    @pl.when(mp // 2 == 0)
+    def _():
+        attention_back(True)
+
+    @pl.when(mp // 2 == 1)
+    def _():
+        attention_back(False)
+
+    dqkv_copies = [dqkv_copy(part, mate, j + 1) for part in range(2) for j, mate in enumerate(mates)]
     dqkv_all[mp] = dqkv_send[mp]
     grad_qkv = dot_tn(normed_all[...].reshape(n_mp * words, width), dqkv_send[...].reshape(n_mp * words, 3 * pair))
     if packed:
@@ -1177,7 +1210,8 @@
         out_specs=[vm] * len(outs),
         out_shape=[jax.ShapeDtypeStruct(s, d) for s, d in outs],
         scratch_shapes=[pltpu.VMEM(s, d) for s, d in shapes]
-        + [pltpu.SemaphoreType.DMA((n_sem,)), pltpu.SemaphoreType.DMA((n_sem,)), pltpu.SemaphoreType.DMA((7, 4)), pltpu.SemaphoreType.DMA((5,)), pltpu.SemaphoreType.DMA((5,))],
+        + [pltpu.SemaphoreType.DMA((n_sem,)), pltpu.SemaphoreType.DMA((n_sem,)), pltpu.SemaphoreType.DMA((7, 4)), pltpu.SemaphoreType.DMA((5,)), pltpu.SemaphoreType.DMA((5,)),
+        pltpu.SemaphoreType.DMA((2, 4)), pltpu.SemaphoreType.DMA((2, 4))],
         compiler_params=pltpu.CompilerParams(collective_id=0, has_side_effects=True, vmem_limit_bytes=VMEM_LIMIT),
         name="word_layer",
     )(*args)

time: 147 us -> 146 us (level)
  Pallas kernels: 146 us -> 144 us
    pallas_call x1, Pallas kernels: 56.8 us -> 54.5 us  [word_layer(): pl.pallas_call(functools.partial(word_body, n_dp, cap, packed), in_specs=...]
where the time goes in v8:
time: 146 us; the launch traced here: 145 us
  Pallas kernels  144 us (99%)
    pallas_call x1, Pallas kernels, word_layer(): pl.pallas_call(functools.partial(word_body, n_dp, cap, packed), in_specs=...  54.5 us
    pallas_call x1, Pallas kernels, char_backward(): pl.pallas_call(functools.partial(char_bwd_body, n_dp, fused), grid=(3 * s...  54 us
    pallas_call x1, Pallas kernels, char_forward(): pl.pallas_call(functools.partial(char_fwd_body, n_dp, cap), grid=(words /...  31.9 us
    pallas_call x1, Pallas kernels, finish(): pl.pallas_call(finish_body, grid=(steps,), in_specs=[blk, full(word_out.s...  3.98 us

profile of v8, /device:TPU:0, one launch (start us, length us, event | category | flops | bytes accessed | tf_op | source)
XLA Modules:
  0.0 145.2 jit_solution(14627620239894948963)
XLA Ops:
  0.6 31.9 %char_forward.1 = (bf16[256,256]{1,0:T(8,128)(2,1)}, bf16[4096,896]{1,0:T(8,128)(2,1)}, bf16[4096,384]{1,0:T(8,128)(2,1)}, bf16[4096,768]{1,0:T(8,128)(2,1)}, bf...) custom-call(bf16[256,4096]{1,0:T(8,128)(2,1)} %x_ref.1, ...), custom_call_target="tpu_custom_call" | custom-call | tf_op jit(solution)/shard_map/char_forward/pallas_call | solution.py:324
  32.6 54.5 %word_layer.1 = (bf16[256,512]{1,0:T(8,128)(2,1)}, bf16[256,256]{1,0:T(8,128)(2,1)}, bf16[2,2,4,800,128]{4,3,2,1,0:T(8,128)(2,1)}, f32[2,512]{1,0:T(2,128)}) custom-call(bf16[256,256]{1,0:T(8,128)(2,1)} %get-tuple-element.46.pooled_ref, bf16[512,256]{1,0:T(8,128)(2,1)} %get-tuple-element.47.onehot, bf16[512,256]{1,0:T(8,128)(2,1)} %get-tuple-element.48.place, ...), custom_call_target="tpu_custom_call" | custom-call | tf_op jit(solution)/shard_map/word_layer/pallas_call | solution.py:1207
  87.0 54.0 %char_backward.1 = (bf16[256,4096]{1,0:T(8,128)(2,1)}, f32[1008,128]{1,0:T(8,128)}) custom-call(bf16[256,256]{1,0:T(8,128)(2,1)} %get-tuple-element.53.dpool_ref, bf16[2,256]{1,0:T(2,128)(2,1)} %gains_ref.5, bf16[256]{0:T(256)(128)(2,1)} %pool_ref.3, bf16[256,768]{1,0:T(8,128)(2,1)} %wqkv_any.1, bf16[256,256]{1,0:T(8,128)(2,1)} %wout_any.1, ...), custom_call_target="tpu_custom_call" | custom-call | tf_op jit(solution)/shard_map/char_backward/pallas_call | solution.py:858
  141.0 4.0 %finish.1 = (f32[256,4096]{1,0:T(8,128)}, bf16[256,512]{1,0:T(8,128)(2,1)}, f32[32,192]{1,0:T(8,128)}, f32[32,64]{1,0:T(8,128)}, f32[32,256]{1,0:T(8,128)}, /*in...) custom-call(bf16[256,4096]{1,0:T(8,128)(2,1)} %get-tuple-element.61., ...), custom_call_target="tpu_custom_call" | custom-call | tf_op jit(solution)/shard_map/finish/pallas_call | solution.py:647

commit v9 on v8

--- a/solution.py
+++ b/solution.py
@@ -459,15 +459,18 @@
         for copy in self.copies(phase):
             copy.start()
 
-    def advance(self):
+    def advance(self, extra):
         for copy in self.copies(0):
             copy.wait()
         got, buf, mp = self.got_mp, self.buf, self.mp
+        rows = buf.shape[2]
+        extra = extra.astype(self.held.dtype)
 
         def add(d, carry):
             total = buf[mp, d].astype(F32) + got[0, d].astype(F32)
             total = total + got[1, d].astype(F32) + got[2, d].astype(F32)
-            self.held[d] = total.astype(self.held.dtype)
+            self.held[d, 0:rows] = total.astype(self.held.dtype)
+            self.held[d, rows:] = extra
             return carry
         lax.fori_loop(0, self.n_dp, add, 0)
         self.start(1)
@@ -482,7 +485,7 @@
 
     @staticmethod
     def shapes(n_dp, rows, dtype):
-        shapes = [(4, n_dp, rows, 128), (3, n_dp, rows, 128), (n_dp, rows, 128), (n_dp - 1, rows, 128)]
+        shapes = [(4, n_dp, rows, 128), (3, n_dp, rows, 128), (n_dp, rows + 16, 128), (n_dp - 1, rows + 16, 128)]
         return [pltpu.VMEM(s, dtype) for s in shapes]
 
 
@@ -516,7 +519,7 @@
         n_sem = 11 * SEMS
         shapes = [
             pltpu.VMEM((2, 2, 2, n_z, CHAR_A, 128), BF16), pltpu.VMEM((2, 2, n_z, WORD_ROWS, 128), BF16),
-            pltpu.VMEM((2, 16, 128), F32), pltpu.VMEM((2 + 2 * n_z, 16, 128), F32),
+            pltpu.VMEM((16, 128), F32), pltpu.VMEM((3, 16, 128), F32),
             pltpu.SemaphoreType.DMA((n_sem,)), pltpu.SemaphoreType.DMA((n_sem,)), pltpu.SemaphoreType.DMA,
         ]
         for low, high in CHUNKS:
@@ -560,30 +563,21 @@
                 self.partb.buf[p, d, 32:48, :] = fold_half(own[:, 128:192]).astype(BF16)
         self.partb.start(0)
 
-    def tiny_copies(self, phase):
-        dp, mp, n_dp = self.partb.dp, self.partb.mp, 2 * self.n_z
-        if phase == 0:
-            peers = [(dp, lax.rem(mp + k, 4)) for k in range(1, 4)]
-        else:
-            peers = [(lax.rem(dp + k, n_dp), mp) for k in range(1, n_dp)]
-        at = 3 * phase
+    def tiny_copies(self):
+        dp, mp = self.partb.dp, self.partb.mp
         return [
-            remote_copy(self.small.at[phase], self.sgot.at[at + k], self.ssem, self.rsem, self.tiny + at + k, peer)
-            for k, peer in enumerate(peers)
+            remote_copy(self.small, self.sgot.at[k], self.ssem, self.rsem, self.tiny + k, (dp, lax.rem(mp + k + 1, 4)))
+            for k in range(3)
         ]
 
-    def tiny_start(self, phase):
-        for copy in self.tiny_copies(phase):
+    def tiny_start(self):
+        for copy in self.tiny_copies():
             copy.start()
 
-    def tiny_finish(self, phase):
-        copies = self.tiny_copies(phase)
-        for copy in copies:
+    def tiny_finish(self):
+        for copy in self.tiny_copies():
             copy.wait()
-        total = self.small[phase]
-        for k in range(len(copies)):
-            total += self.sgot[3 * phase + k]
-        return total
+        return self.small[...] + self.sgot[0] + self.sgot[1] + self.sgot[2]
 
 
 def pack_small(cgain_ref, cpool_ref, gqkv_ref, wqkv_ref, gains_ref, wgain_ref):
@@ -661,7 +655,7 @@
 def char_bwd_body(
     n_dp, fused,
     dpool_ref, gains_ref, pool_ref, wqkv_any, wout_any, wup_any, wdown_any,
-    early_ref, late_ref, p_ref, a_ref, act_ref,
+    early_ref, late_ref, p_any, a_any, act_any,
     *refs,
 ):
     if fused:
@@ -670,7 +664,7 @@
         dx_ref, *refs = refs
         outs, refs = refs[:6], refs[6:]
     gqkv_ref, gout_ref, gup_ref, gdown_ref, ggain_ref, gpool_ref, *refs = refs
-    dm_ref, dp_ref, do_ref, ds_ref, wqkv_ref, wout_ref, wup_ref, wdown_ref, dp_now, do_now, wsem, *refs = refs
+    dm_ref, dp_ref, do_ref, ds_ref, wqkv_ref, wout_ref, wup_ref, wdown_ref, dp_now, do_now, wsem, p_buf, a_buf, pasem, act_buf, actsem, *refs = refs
     step = pl.program_id(0)
     part = pl.num_programs(0) // 3
     words = dpool_ref.shape[0]
@@ -688,6 +682,33 @@
         if fused:
             pl.when(step == when)(act)
 
+    def act_copy(of):
+        slot = lax.rem(of, 2)
+        return pltpu.make_async_copy(
+            act_any.at[pl.ds(pl.multiple_of(of * rows, rows), rows)], act_buf.at[slot], actsem.at[slot]
+        )
+
+    @pl.when(step == 0)
+    def _():
+        act_copy(step).start()
+
+    @pl.when(step + 1 < part)
+    def _():
+        act_copy(step + 1).start()
+
+    def pa_copies(of):
+        slot = lax.rem(of, 2)
+        heads = rows * CHAR_HEADS
+        return [
+            pltpu.make_async_copy(p_any.at[pl.ds(pl.multiple_of(of * rows, rows), rows)], p_buf.at[slot], pasem.at[slot, 0]),
+            pltpu.make_async_copy(a_any.at[pl.ds(pl.multiple_of(of * heads, heads), heads)], a_buf.at[slot], pasem.at[slot, 1]),
+        ]
+
+    @pl.when((step + 1 >= part) & (step + 1 < 2 * part))
+    def _():
+        for copy in pa_copies(step + 1 - part):
+            copy.start()
+
     @pl.when(step == 0)
     def _():
         pairs = ((wdown_any, wdown_ref), (wup_any, wup_ref), (wout_any, wout_ref), (wqkv_any, wqkv_ref))
@@ -732,6 +753,8 @@
         df = (aw * dpool + dt * pool_ref[...].astype(F32).reshape(1, width)).reshape(rows, width)
         dfb = df.astype(BF16)
         n2 = early_ref[:, width : 2 * width]
+        act_copy(step).wait()
+        act_ref = act_buf.at[lax.rem(step, 2)]
         dn2 = None
         for j in range(0, wup_ref.shape[1], HIDDEN_CUT):
             cut = slice(j, j + HIDDEN_CUT)
@@ -753,6 +776,9 @@
     @pl.when((step >= part) & (step < 2 * part))
     def _():
         scale = (width // CHAR_HEADS) ** -0.5
+        for copy in pa_copies(step - part):
+            copy.wait()
+        p_ref, a_ref = p_buf.at[lax.rem(step - part, 2)], a_buf.at[lax.rem(step - part, 2)]
         do_now[...] = do_ref[here, :]
         raw = []
         for b in range(blocks):
@@ -785,8 +811,8 @@
 
     def begin_b():
         sums.pack_b(gqkv_ref)
-        sums.small[0] = pack_small(ggain_ref, gpool_ref, gqkv_ref, wqkv_ref, gains_ref, wgain_ref)
-        sums.tiny_start(0)
+        sums.small[...] = pack_small(ggain_ref, gpool_ref, gqkv_ref, wqkv_ref, gains_ref, wgain_ref)
+        sums.tiny_start()
     at(2 * part - 1, begin_b)
 
     @pl.when(step >= 2 * part)
@@ -801,9 +827,7 @@
                 dx_ref[8 * b : 8 * b + 16, width * c : width * c + width] = jnp.concatenate(pair, 0).astype(BF16)
 
     def end():
-        sums.partb.advance()
-        sums.small[1] = sums.tiny_finish(0)
-        sums.tiny_start(1)
+        sums.partb.advance(sums.tiny_finish())
         for i, (low, high) in enumerate(CHUNKS):
             chunks[i].finish(3)
             sums_ref[low:high, :] = chunks[i].total()
@@ -812,8 +836,7 @@
             sums.parts[i].finish(3)
             sums_ref[base + low : base + high, :] = sums.parts[i].total()
         base += CHAR_A
-        sums_ref[base + CHAR_B : base + CHAR_B + 16, :] = sums.tiny_finish(1)
-        sums_ref[base : base + CHAR_B, :] = sums.partb.total()
+        sums_ref[base : base + CHAR_B + 16, :] = sums.partb.total()
     at(3 * part - 1, end)
 
     if not fused:
@@ -841,11 +864,15 @@
         pltpu.VMEM((rows, width), BF16), pltpu.VMEM((rows, 3 * width), BF16), pltpu.VMEM((rows, width), BF16),
         pltpu.VMEM((step_rows * CHAR_HEADS, 128), BF16), *[pltpu.VMEM(w.shape, BF16) for w in (wqkv, wout, wup, wdown)],
         pltpu.VMEM((step_rows, 3 * width), BF16), pltpu.VMEM((step_rows, width), BF16), pltpu.SemaphoreType.DMA((4,)),
+        pltpu.VMEM((2, step_rows, 3 * width), BF16), pltpu.VMEM((2, step_rows * CHAR_HEADS, 128), BF16), pltpu.SemaphoreType.DMA((2, 2)),
+        pltpu.VMEM((2, step_rows, kept[4].shape[1]), BF16), pltpu.SemaphoreType.DMA((2,)),
     ]
     any_spec = pl.BlockSpec(memory_space=pl.ANY)
     args = [dpool, gains, pool, wqkv, wout, wup, wdown, *kept]
     in_specs = [first(STEP_WORDS, width), full(gains), full(pool)] + [any_spec] * 4
-    in_specs += [f(r.shape[0] // steps, r.shape[1]) for f, r in zip((first, twice, second, second, first), kept)]
+    in_specs += [f(r.shape[0] // steps, r.shape[1]) for f, r in zip((first, twice), kept)]
+    in_specs += [any_spec] * 2
+    in_specs.append(any_spec)
     params = dict(vmem_limit_bytes=VMEM_LIMIT)
     if fused:
         outs = [(WORD_ROWS + CHAR_A + CHAR_B + 16, 128)]

time: 146 us -> 143 us (0.979)
  Pallas kernels: 144 us -> 142 us
    pallas_call x1, Pallas kernels: 54 us -> 51.7 us  [char_backward(): pl.pallas_call(functools.partial(char_bwd_body, n_dp, fused), grid=(3 * s...]
where the time goes in v9:
time: 143 us
  Pallas kernels  142 us (99%)
    pallas_call x1, Pallas kernels, word_layer(): pl.pallas_call(functools.partial(word_body, n_dp, cap, packed), in_specs=...  54.5 us
    pallas_call x1, Pallas kernels, char_backward(): pl.pallas_call(functools.partial(char_bwd_body, n_dp, fused), grid=(3 * s...  51.7 us
    pallas_call x1, Pallas kernels, char_forward(): pl.pallas_call(functools.partial(char_fwd_body, n_dp, cap), grid=(words /...  31.9 us
    pallas_call x1, Pallas kernels, finish(): pl.pallas_call(finish_body, grid=(steps,), in_specs=[blk, full(word_out.s...  3.98 us

profile of v9, /device:TPU:0, one launch (start us, length us, event | category | flops | bytes accessed | tf_op | source)
XLA Modules:
  0.0 142.9 jit_solution(4298375311667417292)
XLA Ops:
  0.6 31.9 %char_forward.1 = (bf16[256,256]{1,0:T(8,128)(2,1)}, bf16[4096,896]{1,0:T(8,128)(2,1)}, bf16[4096,384]{1,0:T(8,128)(2,1)}, bf16[4096,768]{1,0:T(8,128)(2,1)}, bf...) custom-call(bf16[256,4096]{1,0:T(8,128)(2,1)} %x_ref.1, ...), custom_call_target="tpu_custom_call" | custom-call | tf_op jit(solution)/shard_map/char_forward/pallas_call | solution.py:324
  32.6 54.5 %word_layer.1 = (bf16[256,512]{1,0:T(8,128)(2,1)}, bf16[256,256]{1,0:T(8,128)(2,1)}, bf16[2,2,4,800,128]{4,3,2,1,0:T(8,128)(2,1)}, f32[2,512]{1,0:T(2,128)}) custom-call(bf16[256,256]{1,0:T(8,128)(2,1)} %get-tuple-element.46.pooled_ref, bf16[512,256]{1,0:T(8,128)(2,1)} %get-tuple-element.47.onehot, bf16[512,256]{1,0:T(8,128)(2,1)} %get-tuple-element.48.place, ...), custom_call_target="tpu_custom_call" | custom-call | tf_op jit(solution)/shard_map/word_layer/pallas_call | solution.py:1234
  87.0 51.7 %char_backward.1 = (bf16[256,4096]{1,0:T(8,128)(2,1)}, f32[1008,128]{1,0:T(8,128)}) custom-call(bf16[256,256]{1,0:T(8,128)(2,1)} %get-tuple-element.53.dpool_ref, bf16[2,256]{1,0:T(2,128)(2,1)} %gains_ref.5, bf16[256]{0:T(256)(128)(2,1)} %pool_ref.3, bf16[256,768]{1,0:T(8,128)(2,1)} %wqkv_any.1, bf16[256,256]{1,0:T(8,128)(2,1)} %wout_any.1, ...), custom_call_target="tpu_custom_call" | custom-call | tf_op jit(solution)/shard_map/char_backward/pallas_call | solution.py:885
  138.8 4.0 %finish.1 = (f32[256,4096]{1,0:T(8,128)}, bf16[256,512]{1,0:T(8,128)(2,1)}, f32[32,192]{1,0:T(8,128)}, f32[32,64]{1,0:T(8,128)}, f32[32,256]{1,0:T(8,128)}, /*in...) custom-call(bf16[256,4096]{1,0:T(8,128)(2,1)} %get-tuple-element.61., ...), custom_call_target="tpu_custom_call" | custom-call | tf_op jit(solution)/shard_map/finish/pallas_call | solution.py:641
